TPU v7x, 256 devices: a whole 4x4x8 slice. The times are simulated.
256 devices in a mesh: section: 4 (over y), tile: 64 (over z, x, core).
Axes of the slice: x: 4, y: 4, z: 8, core: 2. Of those that a mesh axis runs over, the one named last changes fastest.
Arguments:
- acts: bfloat16 [4, 320, 192, 128], P('section', 'tile'), may hold values from -6 to 6
- cot_top: bfloat16 [320, 192, 128], P('tile'), may hold values from -6 to 6
- land: int32 [320], P('tile'), may hold values from 0 to 1, as said below
- owners: int32 [192], P('tile'), may hold values from 0 to 319, as said below
- dw_kernel: float32 [4, 49, 192], P('section'), may hold values from -0.875 to 0.875
- ln_gain: float32 [4, 192], P('section'), may hold values from 0.5 to 1.5
- w_up: bfloat16 [4, 192, 768], P('section'), may hold values from -0.4375 to 0.4375
- b_up: float32 [4, 768], P('section'), may hold values from -1 to 1
- w_down: bfloat16 [4, 192, 768], P('section'), may hold values from -0.21875 to 0.21875
- layer_scale: float32 [4, 192], P('section'), may hold values from 0.5 to 1.5
Outputs:
- d_input: bfloat16 [4, 192, 192, 128], P('section', 'tile')
- grad_kernel: float32 [4, 49, 192], P('section')
- grad_gain: float32 [4, 192], P('section')
- grad_up: float32 [4, 192, 768], P('section')
- grad_bias: float32 [4, 768], P('section')
- grad_down: float32 [4, 192, 768], P('section')
- grad_scale: float32 [4, 192], P('section')
Inputs may be any that keep to these rules, and one draw needn't show every extreme that they name: `land`: 192 of the 320 tiles are wet; each device's 5 tiles hold between 1 and 5 wet ones. `owners`: the wet tiles in ascending order, 3 to a device; each is listed on its own device or on the next one along tile; at most 2 tiles of one device are listed on the next, and some device hands exactly 2.
All inputs are finite; a program needn't handle non-finite values.
Results may differ from a plain program's by a relative error of at most 0.02.
Values may be sent and summed in bfloat16 or wider, within the bound.
No kernel may reach another device: no remote copies, remote signals or barrier semaphores. Data moves between devices by JAX's collectives and lax.ppermute only.
A program may use at most 128 MiB of HBM per device.

v0:
```python
import math

import jax
import jax.numpy as jnp
from jax import lax
from jax.sharding import PartitionSpec as P

KS = 7
CAP = 2


norm_eps = 1e-06
tanh_root = math.sqrt(2.0 / math.pi)
cubic_coef = 0.044715


def padded_2(cells, sides, width):
    for axis, dim in sides:
        count = lax.axis_size(axis)
        ends = count - 1
        head = lax.slice_in_dim(cells, 0, width, axis=dim)
        tail = lax.slice_in_dim(cells, cells.shape[dim] - width, cells.shape[dim], axis=dim)
        cells = jnp.concatenate(
            [
                lax.ppermute(tail, axis, [(i, (i + 1) % count) for i in range(ends)]),
                cells,
                lax.ppermute(head, axis, [((i + 1) % count, i) for i in range(ends)]),
            ],
            axis=dim,
        )
    return cells


def shifted(value, axis, steps):
    count = lax.axis_size(axis)
    initial, last = (max(0, -steps), min(count, count - steps))
    return lax.ppermute(value, axis, [(source, source + steps) for source in range(initial, last)])


def extend_cols(source, margin):
    return jnp.concatenate([source[..., -margin:], source, source[..., :margin]], axis=-1)


def depthwise(padded, kernel, row_count, col_count):
    running = jnp.zeros((row_count, padded.shape[1], col_count), jnp.float32)
    for tap_row in range(KS):
        for tap_col in range(KS):
            weight_col = kernel[tap_row * KS + tap_col][:, None]
            running = running + weight_col * padded[
                tap_row : tap_row + row_count, :, tap_col : tap_col + col_count
            ].astype(jnp.float32)
    return running


def transpose_conv(padded, kernel, row_count, col_count):
    running = jnp.zeros((row_count, padded.shape[1], col_count), jnp.float32)
    for tap_row in range(KS):
        for tap_col in range(KS):
            weight_col = kernel[tap_row * KS + tap_col][:, None]
            first_row = KS - 1 - tap_row
            first_col = KS - 1 - tap_col
            running = running + weight_col * padded[
                first_row : first_row + row_count, :, first_col : first_col + col_count
            ].astype(jnp.float32)
    return running


def kernel_taps(fieldlow, padded, row_count, col_count):
    grads = []
    source = fieldlow.astype(jnp.float32)
    for tap_row in range(KS):
        for tap_col in range(KS):
            window = padded[tap_row : tap_row + row_count, :, tap_col : tap_col + col_count].astype(
                jnp.float32
            )
            grads.append(jnp.sum(source * window, axis=(0, 2)))
    return jnp.stack(grads)


def normalize(source):
    center = source - jnp.mean(source, axis=1, keepdims=True)
    inverse = 1.0 / jnp.sqrt(jnp.mean(center * center, axis=1, keepdims=True) + norm_eps)
    return (center * inverse, inverse)


def gelu_parts(preact):
    inner = tanh_root * (preact + cubic_coef * preact * preact * preact)
    hyper = jnp.tanh(inner)
    value = 0.5 * preact * (1.0 + hyper)
    slope = 0.5 * (1.0 + hyper) + 0.5 * preact * (1.0 - hyper * hyper) * tanh_root * (
        1.0 + 3.0 * cubic_coef * preact * preact
    )
    return (value, slope)


def body(acts, cot_top, land, owners, dw_kernel, ln_gain, w_up, b_up, w_down, layer_scale):
    source = acts[0]
    kernel = dw_kernel[0]
    gain = ln_gain[0][:, None]
    up_mat = w_up[0]
    bias = b_up[0][:, None]
    down_mat = w_down[0]
    layer = layer_scale[0][:, None]
    tiles_dev = land.shape[0]
    slot_count = owners.shape[0]
    row_count, chan_count, col_count = source.shape
    tile_rows = row_count // tiles_dev
    tile_size = tile_rows * chan_count * col_count
    section_count = lax.axis_size("section")
    section_now = lax.axis_index("section")
    scale = 1.0 / math.sqrt(lax.axis_size("tile") * row_count * col_count)
    offset = lax.axis_index("tile") * tiles_dev
    local = jnp.arange(tiles_dev, dtype=jnp.int32)
    places = jnp.arange(CAP, dtype=jnp.int32)
    slot_ids = jnp.arange(slot_count, dtype=jnp.int32)
    kept_map = owners[None, :] == (offset + local)[:, None]
    kept = jnp.any(kept_map, axis=1)
    sent = (land == 1) & jnp.logical_not(kept)
    sent_int = sent.astype(jnp.int32)
    sent_rank = jnp.cumsum(sent_int) - sent_int
    send_hits = sent[None, :] & (sent_rank[None, :] == places[:, None])
    send_index = jnp.sum(send_hits.astype(jnp.int32) * local[None, :], axis=1)
    send_valid = jnp.any(send_hits, axis=1)
    own_slot = jnp.any(kept_map, axis=0)
    own_index = jnp.sum(kept_map.astype(jnp.int32) * local[:, None], axis=0)
    left_index = jnp.minimum(slot_ids, CAP - 1)
    padded = extend_cols(padded_2(source, (("tile", 0),), 3), 3)
    field = depthwise(padded, kernel, row_count, col_count)
    wet_work = jnp.repeat(land.astype(jnp.float32), tile_rows)[:, None, None]
    nhat, inverse = normalize(field)
    normed = (nhat * gain).astype(jnp.bfloat16)
    preact = jnp.einsum("rcw,cf->rfw", normed, up_mat, preferred_element_type=jnp.float32) + bias
    value, slope = gelu_parts(preact)
    hidden = value.astype(jnp.bfloat16)
    branch = jnp.einsum("rfw,cf->rcw", hidden, down_mat, preferred_element_type=jnp.float32)
    cotangent = cot_top
    for turn in range(section_count):
        active = section_now == section_count - 1 - turn
        cot_work = cotangent
        outgrad = (cot_work.astype(jnp.float32) * layer * wet_work).astype(jnp.bfloat16)
        pregrad = (
            jnp.einsum("rcw,cf->rfw", outgrad, down_mat, preferred_element_type=jnp.float32) * slope
        )
        lowgrad = pregrad.astype(jnp.bfloat16)
        bias_turn = jnp.sum(pregrad, axis=(0, 2))
        featgrad = jnp.einsum("rfw,cf->rcw", lowgrad, up_mat, preferred_element_type=jnp.float32)
        gain_turn = jnp.sum(featgrad * nhat, axis=(0, 2))
        scaled = featgrad * gain
        fieldgrad = inverse * (
            scaled
            - jnp.mean(scaled, axis=1, keepdims=True)
            - nhat * jnp.mean(scaled * nhat, axis=1, keepdims=True)
        )
        fieldlow = fieldgrad.astype(jnp.bfloat16)
        grad_pad = extend_cols(padded_2(fieldlow, (("tile", 0),), 3), 3)
        inputgrad = (
            cotangent.astype(jnp.float32) + transpose_conv(grad_pad, kernel, row_count, col_count)
        ).astype(jnp.bfloat16)
        if turn == 0:
            cot_keep, out_keep, low_keep, bias_keep = (cot_work, outgrad, lowgrad, bias_turn)
            gain_keep, field_keep, input_keep = (gain_turn, fieldlow, inputgrad)
        else:
            cot_keep = jnp.where(active, cot_work, cot_keep)
            out_keep = jnp.where(active, outgrad, out_keep)
            low_keep = jnp.where(active, lowgrad, low_keep)
            bias_keep = jnp.where(active, bias_turn, bias_keep)
            gain_keep = jnp.where(active, gain_turn, gain_keep)
            field_keep = jnp.where(active, fieldlow, field_keep)
            input_keep = jnp.where(active, inputgrad, input_keep)
        if turn + 1 < section_count:
            cotangent = shifted(inputgrad, "section", -1)
    grad_down = jnp.einsum("rcw,rfw->cf", out_keep, hidden, preferred_element_type=jnp.float32)
    grad_up = jnp.einsum("rcw,rfw->cf", normed, low_keep, preferred_element_type=jnp.float32)
    grad_scale = jnp.sum(cot_keep.astype(jnp.float32) * branch * wet_work, axis=(0, 2))
    grad_kernel = kernel_taps(field_keep, padded, row_count, col_count)
    summed = lax.psum((grad_kernel, gain_keep, grad_up, bias_keep, grad_down, grad_scale), "tile")
    flat = input_keep.reshape(tiles_dev, tile_size)
    arrived = shifted(
        jnp.take(flat, send_index, axis=0) * send_valid[:, None].astype(input_keep.dtype), "tile", 1
    )
    arrange_flat = input_keep.reshape(tiles_dev, tile_size)
    mine = jnp.take(arrange_flat, own_index, axis=0) * own_slot[:, None].astype(input_keep.dtype)
    borrowed = jnp.take(arrived, left_index, axis=0) * jnp.logical_not(own_slot)[:, None].astype(
        input_keep.dtype
    )
    slotted = (mine + borrowed).reshape(slot_count * tile_rows, chan_count, col_count)
    return (
        slotted[None],
        (scale * summed[0])[None],
        (scale * summed[1])[None],
        (scale * summed[2])[None],
        (scale * summed[3])[None],
        (scale * summed[4])[None],
        (scale * summed[5])[None],
    )


def solution(mesh):
    in_specs = (
        P("section", "tile", None, None),
        P("tile", None, None),
        P("tile"),
        P("tile"),
        P("section", None, None),
        P("section", None),
        P("section", None, None),
        P("section", None),
        P("section", None, None),
        P("section", None),
    )
    out_specs = (
        P("section", "tile", None, None),
        P("section", None, None),
        P("section", None),
        P("section", None, None),
        P("section", None),
        P("section", None, None),
        P("section", None),
    )
    return jax.shard_map(body, mesh=mesh, in_specs=in_specs, out_specs=out_specs, check_vma=False)
```

profile of v0, /device:TPU:1, one launch (start us, length us, event | category | flops | bytes accessed | tf_op | source)
XLA Modules:
  0.0 601.4 jit_solution(16961418338673354934)
XLA Ops:
  8.3 4.5 collective-permute-start
  12.9 1.9 collective-permute-start.1
  27.1 4.9 fusion.183
  32.9 2.2 fusion.201
  36.5 3.6 collective-permute-start.2
  40.1 1.9 collective-permute-start.3
  42.2 4.4 collective-permute-done.3
  47.6 5.1 fusion.13
  54.8 4.9 collective-permute-done.4
  59.7 2.2 fusion.200
  63.3 4.8 collective-permute-start.5
  68.2 2.1 collective-permute-start.6
  70.9 3.7 collective-permute-done.6
  75.7 5.1 fusion.64
  82.6 5.1 collective-permute-done.7
  87.7 2.2 fusion.199
  91.4 4.4 collective-permute-start.8
  95.8 1.9 collective-permute-start.9
  98.5 3.8 collective-permute-done.9
  103.4 5.6 fusion.67
  112.3 4.1 collective-permute-done.10
  116.3 3.4 fusion.198
  122.6 2.9 fusion.119
  129.1 2.7 multiply_reduce_fusion
  131.9 244.4 %all-reduce = (f32[49,192]{1,0:T(8,128)S(1)}, f32[192]{0:T(256)}, f32[768]{0:T(1024)S(1)}, f32[192]{0:T(256)}) all-reduce(f32[49,192]{1,0:T(8,128)S(1)} %stack.199, f32[192]{0:T(256)S(1)} %select_select_fusion.2, f32[768]{0:T(1024)S(1)} %select_select_fusion.1, ...), channel_id=1, replica_groups=mesh['section'=4,'tile'=64] {'tile'}, use_global_device_ids=true, to_apply=%region_65.66 | all-reduce | flops 10560 | bytes 84480 | tf_op jit(solution)/shard_map/psum | solution.py:176
  378.2 3.6 collective-permute-start.11
  381.8 5.5 collective-permute-start.12
  387.3 2.9 convolution_bitcast_fusion
  393.3 6.3 %select_bitcast_fusion = bf16[1,5,192,128]{3,2,1,0:T(8,128)(2,1)S(1)} fusion(bf16[5,192,128]{2,1,0:T(8,128)(2,1)} %fusion.67, bf16[5,192,128]{2,1,0:T(8,128)(2,1)S(1)} %copy-done.16, bf16[5,192,128]{2,1,0:T(8,128)(2,1)S(1)} %copy-done.14, pred[]{:T(512)S(6)} %eq.43, pred[]{:T(512)S(6)} %eq.42, pred[]{:T(512)S(6)} %eq.41, ...), kind=kLoop, calls=%fused_computation.375 | loop fusion | flops 19415040 | bytes 12129027
  409.0 181.7 %all-reduce.4.cloned.1.call-done = (f32[192,768]{1,0:T(8,128)}, f32[192,768]{1,0:T(8,128)}) async-done(((f32[192,768]{1,0:T(8,128)}, f32[192,768]{1,0:T(8,128)}), (f32[192,768]{1,0:T(8,128)}, f32[192,768]{1,0:T(8,128)})) %all-reduce.4.cloned.1.call-update) | async-done | bytes 1179664 | tf_op jit(solution)/shard_map/psum | solution.py:176
  590.7 1.9 multiply_bitcast_fusion
  592.7 1.9 multiply_bitcast_fusion.1
  (408 shorter events, 48.9 us)
Async XLA Ops:
  7.2 25.5 %copy-start = (bf16[1,192,768]{2,1,0:T(8,128)(2,1)S(1)}, bf16[1,192,768]{2,1,0:T(8,128)(2,1)}, u32[]{:S(2)}) copy-start(bf16[1,192,768]{2,1,0:T(8,128)(2,1)} %param.18) | copy-start | bytes 884740
  7.2 18.4 %copy-start.1 = (bf16[1,5,192,128]{3,2,1,0:T(8,128)(2,1)S(1)}, bf16[1,5,192,128]{3,2,1,0:T(8,128)(2,1)}, u32[]{:S(2)}) copy-start(bf16[1,5,192,128]{3,2,1,0:T(8,128)(2,1)} %param.10) | copy-start | bytes 737284
  7.2 583.5 %all-reduce.4.cloned.1.call-start = ((), (), s32[]{:S(2)}) async-start(), calls=%async_computation | async-start | bytes 2359296 | tf_op jit(solution)/shard_map/psum | solution.py:176
  8.3 15.9 %collective-permute-start = (bf16[3,192,128]{2,1,0:T(8,128)(2,1)S(1)}, bf16[3,192,128]{2,1,0:T(8,128)(2,1)S(1)}, u32[]{:S(2)}, u32[]{:S(2)}) collective-permute-start(bf16[3,192,128]{2,1,0:T(8,128)(2,1)S(1)} %get-tuple-element.116), channel_id=1, source_target_pairs={{0,1},{1,2},{2,3},{3,4},{4,5},{5,6},{6,7},{7,8},{8,9},{9,10},{10,1... | collective-permute-start | bytes 442376 | tf_op jit(solution)/shard_map/ppermute | solution.py:25
  12.9 11.4 %collective-permute-start.1 = (bf16[3,192,128]{2,1,0:T(8,128)(2,1)S(1)}, bf16[3,192,128]{2,1,0:T(8,128)(2,1)S(1)}, u32[]{:S(2)}, u32[]{:S(2)}) collective-permute-start(bf16[3,192,128]{2,1,0:T(8,128)(2,1)S(1)} %get-tuple-element.117), channel_id=1, source_target_pairs={{1,0},{2,1},{3,2},{4,3},{5,4},{6,5},{7,6},{8,7},{9,8},{10,9},{11,1... | collective-permute-start | bytes 442376 | tf_op jit(solution)/shard_map/ppermute | solution.py:27
  16.3 87.0 %copy-start.26 = (f32[1,1,192]{2,0,1:T(1,128)}, f32[1,1,192]{2,0,1:T(1,128)S(1)}, u32[]{:S(2)}) copy-start(f32[1,1,192]{2,0,1:T(1,128)S(1)} %get-tuple-element.122) | copy-start | bytes 2308
  16.3 87.0 %copy-start.28 = (f32[1,1,192]{2,0,1:T(1,128)}, f32[1,1,192]{2,0,1:T(1,128)S(1)}, u32[]{:S(2)}) copy-start(f32[1,1,192]{2,0,1:T(1,128)S(1)} %get-tuple-element.123) | copy-start | bytes 2308
  16.3 87.1 %copy-start.30 = (f32[1,1,192]{2,0,1:T(1,128)}, f32[1,1,192]{2,0,1:T(1,128)S(1)}, u32[]{:S(2)}) copy-start(f32[1,1,192]{2,0,1:T(1,128)S(1)} %get-tuple-element.124) | copy-start | bytes 2308
  16.3 87.1 %copy-start.32 = (f32[1,1,192]{2,0,1:T(1,128)}, f32[1,1,192]{2,0,1:T(1,128)S(1)}, u32[]{:S(2)}) copy-start(f32[1,1,192]{2,0,1:T(1,128)S(1)} %get-tuple-element.125) | copy-start | bytes 2308
  16.3 87.1 %copy-start.34 = (f32[1,1,192]{2,0,1:T(1,128)}, f32[1,1,192]{2,0,1:T(1,128)S(1)}, u32[]{:S(2)}) copy-start(f32[1,1,192]{2,0,1:T(1,128)S(1)} %get-tuple-element.126) | copy-start | bytes 2308
  16.3 87.1 %copy-start.36 = (f32[1,1,192]{2,0,1:T(1,128)}, f32[1,1,192]{2,0,1:T(1,128)S(1)}, u32[]{:S(2)}) copy-start(f32[1,1,192]{2,0,1:T(1,128)S(1)} %get-tuple-element.127) | copy-start | bytes 2308
  16.3 87.1 %copy-start.38 = (f32[1,1,192]{2,0,1:T(1,128)}, f32[1,1,192]{2,0,1:T(1,128)S(1)}, u32[]{:S(2)}) copy-start(f32[1,1,192]{2,0,1:T(1,128)S(1)} %get-tuple-element.128) | copy-start | bytes 2308
  16.3 87.1 %copy-start.40 = (f32[1,1,192]{2,0,1:T(1,128)}, f32[1,1,192]{2,0,1:T(1,128)S(1)}, u32[]{:S(2)}) copy-start(f32[1,1,192]{2,0,1:T(1,128)S(1)} %get-tuple-element.129) | copy-start | bytes 2308
  16.3 87.1 %copy-start.42 = (f32[1,1,192]{2,0,1:T(1,128)}, f32[1,1,192]{2,0,1:T(1,128)S(1)}, u32[]{:S(2)}) copy-start(f32[1,1,192]{2,0,1:T(1,128)S(1)} %get-tuple-element.130) | copy-start | bytes 2308
  16.3 87.1 %copy-start.44 = (f32[1,1,192]{2,0,1:T(1,128)}, f32[1,1,192]{2,0,1:T(1,128)S(1)}, u32[]{:S(2)}) copy-start(f32[1,1,192]{2,0,1:T(1,128)S(1)} %get-tuple-element.131) | copy-start | bytes 2308
  16.3 87.1 %copy-start.46 = (f32[1,1,192]{2,0,1:T(1,128)}, f32[1,1,192]{2,0,1:T(1,128)S(1)}, u32[]{:S(2)}) copy-start(f32[1,1,192]{2,0,1:T(1,128)S(1)} %get-tuple-element.132) | copy-start | bytes 2308
  16.4 87.1 %copy-start.48 = (f32[1,1,192]{2,0,1:T(1,128)}, f32[1,1,192]{2,0,1:T(1,128)S(1)}, u32[]{:S(2)}) copy-start(f32[1,1,192]{2,0,1:T(1,128)S(1)} %get-tuple-element.133) | copy-start | bytes 2308
  32.7 55.1 %copy-start.11 = (f32[5,128,768]{2,1,0:T(8,128)}, f32[5,128,768]{2,1,0:T(8,128)S(1)}, u32[]{:S(2)}) copy-start(f32[5,128,768]{2,1,0:T(8,128)S(1)} %fusion.132) | copy-start | bytes 5898244
  36.5 5.7 collective-permute-start.2
  40.1 6.5 %collective-permute-start.3 = (bf16[3,192,128]{2,1,0:T(8,128)(2,1)S(1)}, bf16[3,192,128]{2,1,0:T(8,128)(2,1)S(1)}, u32[]{:S(2)}, u32[]{:S(2)}) collective-permute-start(bf16[3,192,128]{2,1,0:T(8,128)(2,1)S(1)} %get-tuple-element.114), channel_id=1, source_target_pairs={{1,0},{2,1},{3,2},{4,3},{5,4},{6,5},{7,6},{8,7},{9,8},{10,9},{11,1... | collective-permute-start | bytes 442376 | tf_op jit(solution)/shard_map/ppermute | solution.py:27
  52.8 6.9 %collective-permute-start.4 = (bf16[5,192,128]{2,1,0:T(8,128)(2,1)S(1)}, bf16[5,192,128]{2,1,0:T(8,128)(2,1)S(1)}, u32[]{:S(2)}, u32[]{:S(2)}) collective-permute-start(bf16[5,192,128]{2,1,0:T(8,128)(2,1)S(1)} %fusion.13), channel_id=1, source_target_pairs={{64,0},{128,64},{192,128},{65,1},{129,65},{193,129},{66,2},{130,66... | collective-permute-start | bytes 737288 | tf_op jit(solution)/shard_map/ppermute | solution.py:37
  63.3 7.5 %collective-permute-start.5 = (bf16[3,192,128]{2,1,0:T(8,128)(2,1)S(1)}, bf16[3,192,128]{2,1,0:T(8,128)(2,1)S(1)}, u32[]{:S(2)}, u32[]{:S(2)}) collective-permute-start(bf16[3,192,128]{2,1,0:T(8,128)(2,1)S(1)} %get-tuple-element.113), channel_id=1, source_target_pairs={{0,1},{1,2},{2,3},{3,4},{4,5},{5,6},{6,7},{7,8},{8,9},{9,10},{10,1... | collective-permute-start | bytes 442376 | tf_op jit(solution)/shard_map/ppermute | solution.py:25
  68.2 6.5 %collective-permute-start.6 = (bf16[3,192,128]{2,1,0:T(8,128)(2,1)S(1)}, bf16[3,192,128]{2,1,0:T(8,128)(2,1)S(1)}, u32[]{:S(2)}, u32[]{:S(2)}) collective-permute-start(bf16[3,192,128]{2,1,0:T(8,128)(2,1)S(1)} %get-tuple-element.112), channel_id=1, source_target_pairs={{1,0},{2,1},{3,2},{4,3},{5,4},{6,5},{7,6},{8,7},{9,8},{10,9},{11,1... | collective-permute-start | bytes 442376 | tf_op jit(solution)/shard_map/ppermute | solution.py:27
  80.8 6.9 %collective-permute-start.7 = (bf16[5,192,128]{2,1,0:T(8,128)(2,1)S(1)}, bf16[5,192,128]{2,1,0:T(8,128)(2,1)S(1)}, u32[]{:S(2)}, u32[]{:S(2)}) collective-permute-start(bf16[5,192,128]{2,1,0:T(8,128)(2,1)S(1)} %fusion.64), channel_id=1, source_target_pairs={{64,0},{128,64},{192,128},{65,1},{129,65},{193,129},{66,2},{130,66... | collective-permute-start | bytes 737288 | tf_op jit(solution)/shard_map/ppermute | solution.py:37
  91.4 7.1 %collective-permute-start.8 = (bf16[3,192,128]{2,1,0:T(8,128)(2,1)S(1)}, bf16[3,192,128]{2,1,0:T(8,128)(2,1)S(1)}, u32[]{:S(2)}, u32[]{:S(2)}) collective-permute-start(bf16[3,192,128]{2,1,0:T(8,128)(2,1)S(1)} %get-tuple-element.111), channel_id=1, source_target_pairs={{0,1},{1,2},{2,3},{3,4},{4,5},{5,6},{6,7},{7,8},{8,9},{9,10},{10,1... | collective-permute-start | bytes 442376 | tf_op jit(solution)/shard_map/ppermute | solution.py:25
  95.8 6.5 %collective-permute-start.9 = (bf16[3,192,128]{2,1,0:T(8,128)(2,1)S(1)}, bf16[3,192,128]{2,1,0:T(8,128)(2,1)S(1)}, u32[]{:S(2)}, u32[]{:S(2)}) collective-permute-start(bf16[3,192,128]{2,1,0:T(8,128)(2,1)S(1)} %get-tuple-element.110), channel_id=1, source_target_pairs={{1,0},{2,1},{3,2},{4,3},{5,4},{6,5},{7,6},{8,7},{9,8},{10,9},{11,1... | collective-permute-start | bytes 442376 | tf_op jit(solution)/shard_map/ppermute | solution.py:27
  109.1 7.2 %collective-permute-start.10 = (bf16[5,192,128]{2,1,0:T(8,128)(2,1)}, bf16[5,192,128]{2,1,0:T(8,128)(2,1)}, u32[]{:S(2)}, u32[]{:S(2)}) collective-permute-start(bf16[5,192,128]{2,1,0:T(8,128)(2,1)} %fusion.67), channel_id=1, source_target_pairs={{64,0},{128,64},{192,128},{65,1},{129,65},{193,129},{66,2},{130,66... | collective-permute-start | bytes 737288 | tf_op jit(solution)/shard_map/ppermute | solution.py:37
  129.1 248.3 %copy-start.6 = (bf16[5,192,128]{2,1,0:T(8,128)(2,1)S(1)}, bf16[5,192,128]{2,1,0:T(8,128)(2,1)}, u32[]{:S(2)}) copy-start(bf16[5,192,128]{2,1,0:T(8,128)(2,1)} %get-tuple-element.83) | copy-start | bytes 737284
  129.1 258.2 %copy-start.12 = (f32[5,128,768]{2,1,0:T(8,128)S(1)}, f32[5,128,768]{2,1,0:T(8,128)}, u32[]{:S(2)}) copy-start(f32[5,128,768]{2,1,0:T(8,128)} %copy-done.11) | copy-start | bytes 5898244
  378.2 13.3 %collective-permute-start.11 = (bf16[3,192,128]{2,1,0:T(8,128)(2,1)}, bf16[3,192,128]{2,1,0:T(8,128)(2,1)S(1)}, u32[]{:S(2)}, u32[]{:S(2)}) collective-permute-start(bf16[3,192,128]{2,1,0:T(8,128)(2,1)} %get-tuple-element.108), channel_id=1, source_target_pairs={{0,1},{1,2},{2,3},{3,4},{4,5},{5,6},{6,7},{7,8},{8,9},{9,10},{10,1... | collective-permute-start | bytes 442376 | tf_op jit(solution)/shard_map/ppermute | solution.py:25
  381.8 9.7 %collective-permute-start.12 = (bf16[3,192,128]{2,1,0:T(8,128)(2,1)}, bf16[3,192,128]{2,1,0:T(8,128)(2,1)S(1)}, u32[]{:S(2)}, u32[]{:S(2)}) collective-permute-start(bf16[3,192,128]{2,1,0:T(8,128)(2,1)} %get-tuple-element.109), channel_id=1, source_target_pairs={{1,0},{2,1},{3,2},{4,3},{5,4},{6,5},{7,6},{8,7},{9,8},{10,9},{11,1... | collective-permute-start | bytes 442376 | tf_op jit(solution)/shard_map/ppermute | solution.py:27
  401.5 5.9 collective-permute-start.13
  (140 other events, 365.1 us)
Sparse Core Ops, SparseCore 0:
  390.4 200.3 all-reduce.3
where the time goes:
time: 603 us; the launch traced here: 601 us
  blocking collectives  244 us (40%)
  waiting for transfers between devices  208 us (34%)
  other arithmetic  56.5 us (9%)
  starting transfers between devices  40.4 us (7%)
  matrix products  21.8 us (4%)
  between operations  16.7 us (3%)
  local copies, waits for them, and re-layouts  13.9 us (2%)
    psum x1, blocking collectives, body(): lax.psum((grad_kernel, gain_keep, grad_up, bias_keep, grad_down, grad_sca...  244 us
    psum x1, waiting for transfers between devices, body(): lax.psum((grad_kernel, gain_keep, grad_up, bias_keep, grad_down, grad_sca...  182 us
    ppermute x5, starting transfers between devices, padded_2(): lax.ppermute(tail, axis, [(i, (i + 1) % count) for i in range(ends)])  21 us
    convert_element_type x3, other arithmetic, body(): inputgrad = (cotangent.astype(jnp.float32) + transpose_conv(grad_pad, ker...  15.9 us
    ppermute x4, waiting for transfers between devices, shifted(): lax.ppermute(value, axis, [(source, source + steps) for source in range(i...  14 us
    ppermute x5, starting transfers between devices, padded_2(): lax.ppermute(head, axis, [((i + 1) % count, i) for i in range(ends)])  13.4 us
  transfers between devices with their start and end apart: 15, of which 8 were waited for; matrix products, arithmetic and copies ran while one was open for 5% of the time, Pallas kernels for 0%

commit v1 on v0

v1 whole, which is shorter than its diff:
```python
import functools
import math

import jax
import jax.numpy as jnp
from jax import lax
from jax.experimental import pallas as pl
from jax.experimental.pallas import tpu as pltpu
from jax.sharding import PartitionSpec as P

KS = 7
CAP = 2
SECTIONS = 4
TILES = 64
MARGIN = 3
BLOCK = 16

norm_eps = 1e-06
tanh_root = math.sqrt(2.0 / math.pi)
cubic_coef = 0.044715

f32 = jnp.float32
bf16 = jnp.bfloat16

SECTION, ODD, KEEP, NEAR, MATE, FAR, OFFSET = range(7)


def split_tile(tile):
    return tile % 2, tile // 2 % 4, tile // 8


def flip_x0(x):
    return x ^ 1


def flip_x1(x):
    return 3 - x


def flip_z0(z):
    return z ^ 1


def flip_z1(z):
    return 3 - z if z < 4 else 11 - z


def flip_z2(z):
    return 7 - z


flips = {"x0": flip_x0, "x1": flip_x1, "z0": flip_z0, "z1": flip_z1, "z2": flip_z2}


def moved(value, dims, swap):
    pairs = []
    for tile in range(TILES):
        core, x, z = split_tile(tile)
        dim = dims[core]
        if dim in ("x0", "x1"):
            x = flips[dim](x)
        elif dim:
            z = flips[dim](z)
        core = 1 - core if swap else core
        pairs.append((tile, z * 8 + x * 2 + core))
    return lax.ppermute(value, "tile", pairs)


def halo(inner, outer, sections):
    within, across = [], []
    for section in sections:
        for tile in range(TILES):
            within.append((section * TILES + tile, section * TILES + (tile ^ 1)))
            other = tile + 1 if tile % 2 else tile - 1
            if 0 <= other < TILES:
                across.append((section * TILES + tile, section * TILES + other))
    axes = ("section", "tile")
    outer = lax.ppermute(outer, axes, across)
    inner = lax.ppermute(inner, axes, within)
    return inner, outer


def call(body, out_shape, smem, operands, scratch=(), cost=(0, 0)):
    spec = [pl.BlockSpec(memory_space=pltpu.SMEM)] * smem
    spec += [pl.BlockSpec(memory_space=pltpu.VMEM)] * (len(operands) - smem)
    outs = jax.tree.map(lambda _: pl.BlockSpec(memory_space=pltpu.VMEM), out_shape)
    return pl.pallas_call(
        body,
        out_shape=out_shape,
        in_specs=spec,
        out_specs=outs,
        scratch_shapes=list(scratch),
        compiler_params=pltpu.CompilerParams(vmem_limit_bytes=32 * 1024 * 1024),
        cost_estimate=pl.CostEstimate(flops=cost[0], bytes_accessed=cost[1], transcendentals=0),
    )(*operands)


def shape(dims, dtype):
    return jax.ShapeDtypeStruct(dims, dtype)


def fill_rows(rows_ref, odd, own, inner, outer):
    count = own.shape[0]
    rows_ref[MARGIN : MARGIN + count] = own[...]
    rows_ref[:MARGIN] = jnp.where(odd, inner[...], outer[...])
    rows_ref[MARGIN + count :] = jnp.where(odd, outer[...], inner[...])


def edges(odd, value_ref, inner_ref, outer_ref):
    count = value_ref.shape[0]
    head = value_ref[:MARGIN]
    tail = value_ref[count - MARGIN :]
    inner_ref[...] = jnp.where(odd, head, tail)
    outer_ref[...] = jnp.where(odd, tail, head)


def taps_sum(rows_ref, cols_ref, start, count, backward):
    coefs = cols_ref[pl.ds(start, BLOCK), :]
    rows = [
        rows_ref[row, pl.ds(start, BLOCK), :].astype(f32) for row in range(count + 2 * MARGIN)
    ]
    sums = [None] * count
    for tap_col in range(KS):
        shift = (tap_col - MARGIN if backward else MARGIN - tap_col) % 128
        weights = [
            jnp.broadcast_to(
                coefs[:, tap_row * KS + tap_col : tap_row * KS + tap_col + 1], rows[0].shape
            )
            for tap_row in range(KS)
        ]
        for row in range(count):
            part = None
            for tap_row in range(KS):
                place = row + (KS - 1 - tap_row if backward else tap_row)
                term = weights[tap_row] * rows[place]
                part = term if part is None else part + term
            if shift:
                part = pltpu.roll(part, shift, 1)
            sums[row] = part if sums[row] is None else sums[row] + part
    return sums


def forward_kernel(
    meta, acts, inner, outer, cols, up_t, bias, nhat_ref, inv_ref, hidden_ref, slope_ref, rows_ref, field_ref, normed_ref
):
    count, chans, width = acts.shape
    fill_rows(rows_ref, meta[ODD] == 1, acts, inner, outer)

    def step(index, carry):
        start = pl.multiple_of(index * BLOCK, BLOCK)
        sums = taps_sum(rows_ref, cols, start, count, False)
        for row in range(count):
            field_ref[pl.ds(start, BLOCK), row * width : (row + 1) * width] = sums[row]
        return carry

    lax.fori_loop(0, chans // BLOCK, step, 0)
    gain = cols[:, KS * KS : KS * KS + 1]
    for row in range(count):
        part = slice(row * width, (row + 1) * width)
        field = field_ref[:, part]
        center = field - jnp.mean(field, axis=0, keepdims=True)
        inverse = 1.0 / jnp.sqrt(jnp.mean(center * center, axis=0, keepdims=True) + norm_eps)
        nhat = center * inverse
        nhat_ref[:, part] = nhat
        inv_ref[:, part] = inverse
        normed_ref[:, part] = (nhat * gain).astype(bf16)
    units = up_t.shape[0]
    chunk = 128
    for first in range(0, units, chunk):
        part = slice(first, first + chunk)
        preact = jnp.dot(up_t[part], normed_ref[...], preferred_element_type=f32) + bias[part]
        square = preact * preact
        hyper = jnp.tanh(preact * (tanh_root + tanh_root * cubic_coef * square))
        half = 0.5 + 0.5 * hyper
        hidden_ref[part] = (preact * half).astype(bf16)
        slope = half * (
            1.0 + preact * (1.0 - hyper) * (tanh_root + 3.0 * cubic_coef * tanh_root * square)
        )
        slope_ref[part] = slope.astype(bf16)


def mlp_backward(cots, land, cols, down_t, up, slope, nhat, inv, out_ref, low_ref, field_ref, sums=None):
    width = cots[0].shape[1]
    count = len(cots)
    gain = cols[:, KS * KS : KS * KS + 1]
    layer = cols[:, KS * KS + 1 : KS * KS + 2]
    for row in range(count):
        wet = land[row].astype(f32)
        out_ref[:, row * width : (row + 1) * width] = (cots[row] * layer * wet).astype(bf16)
    units = down_t.shape[0]
    chunk = 128
    for first in range(0, units, chunk):
        part = slice(first, first + chunk)
        pregrad = jnp.dot(down_t[part], out_ref[...], preferred_element_type=f32)
        pregrad = pregrad * slope[part].astype(f32)
        low_ref[part] = pregrad.astype(bf16)
        if sums is not None:
            sums[0][part] = sum(
                pregrad[:, row * width : (row + 1) * width] for row in range(count)
            )
    featgrad = jnp.dot(up[...], low_ref[...], preferred_element_type=f32)
    gains = None
    for row in range(count):
        part = slice(row * width, (row + 1) * width)
        feat = featgrad[:, part]
        own = nhat[:, part]
        scaled = feat * gain
        mean = jnp.mean(scaled, axis=0, keepdims=True)
        cross = jnp.mean(scaled * own, axis=0, keepdims=True)
        field_ref[row] = (inv[:, part] * (scaled - mean - own * cross)).astype(bf16)
        if sums is not None:
            term = feat * own
            gains = term if gains is None else gains + term
    if sums is not None:
        sums[1][...] = gains


def turn_kernel(
    section, meta, land, cot, cols, down_t, up, slope, nhat, inv, field_ref, inner_ref, outer_ref, out_ref, low_ref
):
    @pl.when(meta[SECTION] == section)
    def _():
        cots = [cot[row].astype(f32) for row in range(cot.shape[0])]
        mlp_backward(cots, land, cols, down_t, up, slope, nhat, inv, out_ref, low_ref, field_ref)
        edges(meta[ODD] == 1, field_ref, inner_ref, outer_ref)


def conv_rows(meta, field, inner, outer, cot, cols, result_ref, rows_ref):
    count, chans, width = field.shape
    fill_rows(rows_ref, meta[ODD] == 1, field, inner, outer)

    def step(index, carry):
        start = pl.multiple_of(index * BLOCK, BLOCK)
        sums = taps_sum(rows_ref, cols, start, count, True)
        for row in range(count):
            own = cot[row, pl.ds(start, BLOCK), :].astype(f32)
            result_ref[row, pl.ds(start, BLOCK), :] = (own + sums[row]).astype(bf16)
        return carry

    lax.fori_loop(0, chans // BLOCK, step, 0)


def conv_kernel(section, meta, field, inner, outer, cot, cols, result_ref, rows_ref):
    @pl.when(meta[SECTION] == section)
    def _():
        conv_rows(meta, field, inner, outer, cot, cols, result_ref, rows_ref)


def last_conv_kernel(
    meta, land, owners, field, inner, outer, cot, cols, third, second, first, result_ref, sent_ref, rows_ref
):
    for section, kept in ((3, third), (2, second), (1, first)):

        @pl.when(meta[SECTION] == section)
        def _():
            result_ref[...] = kept[...]

    @pl.when(meta[SECTION] == 0)
    def _():
        conv_rows(meta, field, inner, outer, cot, cols, result_ref, rows_ref)

    sent_ref[...] = jnp.zeros_like(sent_ref)
    rank = jnp.int32(0)
    for local in range(result_ref.shape[0]):
        kept = jnp.bool_(False)
        for slot in range(owners.shape[0]):
            kept = kept | (owners[slot] == meta[OFFSET] + local)
        sent = (land[local] == 1) & jnp.logical_not(kept)
        for place in range(CAP):

            @pl.when(sent & (rank == place))
            def _():
                sent_ref[place] = result_ref[local]

        rank = rank + sent.astype(jnp.int32)


def slots_kernel(meta, owners, result, arrived, slots_ref):
    for slot in range(slots_ref.shape[0]):
        slots_ref[slot] = arrived[min(slot, CAP - 1)]
        for local in range(result.shape[0]):

            @pl.when(owners[slot] == meta[OFFSET] + local)
            def _():
                slots_ref[slot] = result[local]


def last_kernel(
    meta,
    land,
    cot_top,
    cot_2,
    cot_1,
    cot_0,
    cols,
    layer_row,
    down_t,
    down,
    up,
    slope,
    nhat,
    inv,
    hidden,
    acts,
    inner,
    outer,
    field_ref,
    field_inner_ref,
    field_outer_ref,
    keep_ref,
    near_ref,
    mate_ref,
    far_ref,
    out_ref,
    low_ref,
    bias_ref,
    gain_ref,
    rows_ref,
    taps_ref,
    packed_ref,
    cot_ref,
):
    count, chans, width = acts.shape
    units = slope.shape[0]
    odd = meta[ODD] == 1
    for section, cot in ((3, cot_top), (2, cot_2), (1, cot_1), (0, cot_0)):

        @pl.when(meta[SECTION] == section)
        def _():
            cot_ref[...] = cot[...]

    cots = [cot_ref[row].astype(f32) for row in range(count)]
    mlp_backward(
        cots, land, cols, down_t, up, slope, nhat, inv, out_ref, low_ref, field_ref, (bias_ref, gain_ref)
    )
    edges(odd, field_ref, field_inner_ref, field_outer_ref)
    gain = cols[:, KS * KS : KS * KS + 1]
    normed = (nhat[...] * gain).astype(bf16)
    turned = (((1,), (1,)), ((), ()))
    grad_up = lax.dot_general(normed, low_ref[...], turned, preferred_element_type=f32)
    packed_ref[:chans] = grad_up.astype(bf16)
    grad_down = lax.dot_general(out_ref[...], hidden[...], turned, preferred_element_type=f32)
    packed_ref[chans : 2 * chans] = grad_down.astype(bf16)
    product = grad_down * down[...].astype(f32)
    product = sum(product[:, first : first + 128] for first in range(0, units, 128))

    fill_rows(rows_ref, odd, acts, inner, outer)

    def step(index, carry):
        start = pl.multiple_of(index * BLOCK, BLOCK)
        rows = [
            rows_ref[row, pl.ds(start, BLOCK), :].astype(f32) for row in range(count + 2 * MARGIN)
        ]
        fields = [field_ref[row, pl.ds(start, BLOCK), :].astype(f32) for row in range(count)]
        lane = lax.broadcasted_iota(jnp.int32, (BLOCK, 128), 1)
        grads = jnp.zeros((BLOCK, 128), f32)
        for tap_col in range(KS):
            shift = (tap_col - MARGIN) % 128
            turned_fields = [pltpu.roll(field, shift, 1) if shift else field for field in fields]
            for tap_row in range(KS):
                part = None
                for row in range(count):
                    term = turned_fields[row] * rows[row + tap_row]
                    part = term if part is None else part + term
                grads = jnp.where(
                    lane == tap_row * KS + tap_col, jnp.sum(part, axis=1, keepdims=True), grads
                )
        taps_ref[pl.ds(start, BLOCK), :] = grads
        return carry

    lax.fori_loop(0, chans // BLOCK, step, 0)
    base = 2 * chans
    taps = jnp.transpose(taps_ref[...])[:56]
    zeros = jnp.zeros((56, units - chans), f32)
    bias_row = jnp.sum(jnp.transpose(bias_ref[...]), axis=0, keepdims=True)
    gain_row = jnp.sum(jnp.transpose(gain_ref[...]), axis=0, keepdims=True)
    scale_row = jnp.sum(jnp.transpose(product), axis=0, keepdims=True) / layer_row[...]
    gap = jnp.zeros((1, 256 - chans), f32)
    rest = jnp.zeros((1, units - 256 - chans), f32)
    pair_row = jnp.concatenate([gain_row, gap, scale_row, rest], axis=1)
    small = jnp.concatenate(
        [jnp.concatenate([taps, zeros], axis=1), bias_row, pair_row, jnp.zeros((6, units), f32)]
    )
    packed_ref[base : base + 64] = small.astype(bf16)
    part_rows = keep_ref.shape[0]
    for place, target in ((KEEP, keep_ref), (NEAR, near_ref), (MATE, mate_ref), (FAR, far_ref)):
        start = pl.multiple_of(meta[place] * part_rows, 16)
        target[...] = packed_ref[pl.ds(start, part_rows), :]


def finish_kernel(
    scale, meta, keep, near, mate, far, kernel_ref, gain_ref, up_ref, bias_ref, down_ref, scale_ref, packed_ref
):
    part_rows = keep.shape[0]
    for place, source in ((KEEP, keep), (NEAR, near), (MATE, mate), (FAR, far)):
        start = pl.multiple_of(meta[place] * part_rows, 16)
        packed_ref[pl.ds(start, part_rows), :] = source[...]
    chans = up_ref.shape[0]
    up_ref[...] = packed_ref[:chans].astype(f32) * scale
    down_ref[...] = packed_ref[chans : 2 * chans].astype(f32) * scale
    small = packed_ref[2 * chans :].astype(f32) * scale
    kernel_ref[...] = small[: KS * KS, :chans]
    bias_ref[...] = small[56:57]
    gain_ref[...] = small[57:58, :chans]
    scale_ref[...] = small[57:58, 256 : 256 + chans]


def added(*values):
    return sum(value.astype(f32) for value in values).astype(bf16)


def body(acts, cot_top, land, owners, dw_kernel, ln_gain, w_up, b_up, w_down, layer_scale):
    source = acts[0]
    count, chans, width = source.shape
    units = w_up.shape[2]
    cells = count * width
    tile_now = lax.axis_index("tile")
    section_now = lax.axis_index("section")
    scale = 1.0 / math.sqrt(lax.axis_size("tile") * cells)
    core, x, z = split_tile(tile_now)
    bit_x, bit_z = (x + 1) // 2 % 2, (z + 1) // 2 % 2
    bit = jnp.where(core == 0, bit_x, bit_z)
    mate_bit = jnp.where(core == 0, bit_z, bit_x)
    meta = jnp.stack(
        [
            section_now,
            core,
            2 * core + bit,
            2 * core + 1 - bit,
            2 * (1 - core) + mate_bit,
            2 * (1 - core) + 1 - mate_bit,
            tile_now * count,
            core,
        ]
    ).astype(jnp.int32)

    odd = core == 1
    head, tail = source[:MARGIN], source[count - MARGIN :]
    acts_inner, acts_outer = halo(
        jnp.where(odd, head, tail), jnp.where(odd, tail, head), range(SECTIONS)
    )
    cols = jnp.concatenate([dw_kernel[0], ln_gain, layer_scale]).T
    up, down = w_up[0], w_down[0]
    up_t, down_t = up.T, down.T
    bias = b_up.reshape(units, 1)

    padded = pltpu.VMEM((count + 2 * MARGIN, chans, width), bf16)
    nhat, inv, hidden, slope = call(
        forward_kernel,
        (
            shape((chans, cells), f32),
            shape((1, cells), f32),
            shape((units, cells), bf16),
            shape((units, cells), bf16),
        ),
        1,
        (meta, source, acts_inner, acts_outer, cols, up_t, bias),
        (padded, pltpu.VMEM((chans, cells), f32), pltpu.VMEM((chans, cells), bf16)),
    )

    rows_shape = shape((count, chans, width), bf16)
    edge_shape = shape((MARGIN, chans, width), bf16)
    outgrads = pltpu.VMEM((chans, cells), bf16)
    lowgrads = pltpu.VMEM((units, cells), bf16)
    cots, results = [cot_top], []
    for section in range(SECTIONS - 1, 0, -1):
        field, inner, outer = call(
            functools.partial(turn_kernel, section),
            (rows_shape, edge_shape, edge_shape),
            2,
            (meta, land, cots[-1], cols, down_t, up, slope, nhat, inv),
            (outgrads, lowgrads),
        )
        inner, outer = halo(inner, outer, (section,))
        result = call(
            functools.partial(conv_kernel, section),
            rows_shape,
            1,
            (meta, field, inner, outer, cots[-1], cols),
            (padded,),
        )
        results.append(result)
        pairs = [
            (section * TILES + tile, (section - 1) * TILES + tile) for tile in range(TILES)
        ]
        cots.append(lax.ppermute(result, ("section", "tile"), pairs))

    part = shape(((2 * chans + 64) // 4, units), bf16)
    field, inner, outer, keep, near, mate, far = call(
        last_kernel,
        (rows_shape, edge_shape, edge_shape, part, part, part, part),
        2,
        (meta, land, *cots, cols, layer_scale, down_t, down, up, slope, nhat, inv, hidden)
        + (source, acts_inner, acts_outer),
        (
            outgrads,
            lowgrads,
            pltpu.VMEM((units, width), f32),
            pltpu.VMEM((chans, width), f32),
            padded,
            pltpu.VMEM((chans, 128), f32),
            pltpu.VMEM((2 * chans + 64, units), bf16),
            pltpu.VMEM((count, chans, width), bf16),
        ),
    )
    far = moved(far, ("z0", "x0"), True)
    near = moved(near, ("x0", "z0"), False)
    mate = moved(mate, ("", ""), True)
    total = added(keep, near, mate, far)
    for dims in (("x1", "z1"), ("z0", "z2"), ("z1", "x0"), ("z2", "x1")):
        total = added(total, moved(total, dims, False))
    far = moved(total, ("x0", "z0"), True)
    near = moved(total, ("x0", "z0"), False)
    mate = moved(total, ("", ""), True)
    grads = call(
        functools.partial(finish_kernel, scale),
        (
            shape((KS * KS, chans), f32),
            shape((1, chans), f32),
            shape((chans, units), f32),
            shape((1, units), f32),
            shape((chans, units), f32),
            shape((1, chans), f32),
        ),
        1,
        (meta, total, near, mate, far),
        (pltpu.VMEM((2 * chans + 64, units), bf16),),
    )

    inner, outer = halo(inner, outer, (0,))
    result, sent = call(
        last_conv_kernel,
        (rows_shape, shape((CAP, chans, width), bf16)),
        3,
        (meta, land, owners, field, inner, outer, cots[-1], cols, *results),
        (padded,),
    )
    arrived = lax.ppermute(sent, "tile", [(tile, tile + 1) for tile in range(TILES - 1)])
    slotted = call(
        slots_kernel,
        shape((owners.shape[0], chans, width), bf16),
        2,
        (meta, owners, result, arrived),
    )
    grad_kernel, grad_gain, grad_up, grad_bias, grad_down, grad_scale = grads
    return (
        slotted[None],
        grad_kernel[None],
        grad_gain,
        grad_up[None],
        grad_bias,
        grad_down[None],
        grad_scale,
    )


def solution(mesh):
    in_specs = (
        P("section", "tile", None, None),
        P("tile", None, None),
        P("tile"),
        P("tile"),
        P("section", None, None),
        P("section", None),
        P("section", None, None),
        P("section", None),
        P("section", None, None),
        P("section", None),
    )
    out_specs = (
        P("section", "tile", None, None),
        P("section", None, None),
        P("section", None),
        P("section", None, None),
        P("section", None),
        P("section", None, None),
        P("section", None),
    )
    return jax.shard_map(body, mesh=mesh, in_specs=in_specs, out_specs=out_specs, check_vma=False)
```

time: 603 us -> 172 us (0.29)
  the two profiles are of different devices: /device:TPU:1 before, /device:TPU:64 now
where the time goes in v1:
time: 172 us
  waiting for transfers between devices  101 us (59%)
  starting transfers between devices  33.8 us (20%)
  Pallas kernels  30.2 us (18%)
  local copies, waits for them, and re-layouts  4.18 us (2%)
    ppermute x3, waiting for transfers between devices, body(): cots.append(lax.ppermute(result, ('section', 'tile'), pairs))  69.2 us
    pallas_call x11, Pallas kernels, call(): pl.pallas_call(body, out_shape=out_shape, in_specs=spec, out_specs=outs,...  30.2 us
    ppermute x10, waiting for transfers between devices, moved(): return lax.ppermute(value, 'tile', pairs)  19.9 us
    ppermute x10, starting transfers between devices, moved(): return lax.ppermute(value, 'tile', pairs)  17.3 us
    ppermute x5, starting transfers between devices, halo(): outer = lax.ppermute(outer, axes, across)  7.98 us
    ppermute x1, waiting for transfers between devices, body(): lax.ppermute(sent, 'tile', [(tile, tile + 1) for tile in range(TILES - 1)])  6.12 us
    ppermute x5, waiting for transfers between devices, halo(): outer = lax.ppermute(outer, axes, across)  5.44 us
    ppermute x5, starting transfers between devices, halo(): inner = lax.ppermute(inner, axes, within)  4.01 us
  transfers between devices with their start and end apart: 24, of which 8 were waited for; matrix products, arithmetic and copies ran while one was open for 1% of the time, Pallas kernels for 5%

profile of v1, /device:TPU:64, one launch (start us, length us, event | category | flops | bytes accessed | tf_op | source)
XLA Modules:
  0.0 171.6 jit_solution(11197112598232793110)
XLA Ops:
  0.7 1.0 select_bitcast_fusion
  1.7 3.8 %collective-permute-start.1 = (bf16[3,192,128]{2,1,0:T(8,128)(2,1)S(1)}, bf16[3,192,128]{2,1,0:T(8,128)(2,1)S(1)}, u32[]{:S(2)}, u32[]{:S(2)}) collective-permute-start(bf16[3,192,128]{2,1,0:T(8,128)(2,1)S(1)} %get-tuple-element.77), channel_id=1, source_target_pairs={{1,2},{2,1},{3,4},{4,3},{5,6},{6,5},{7,8},{8,7},{9,10},{10,9},{11,... | collective-permute-start | bytes 442376 | tf_op jit(solution)/shard_map/ppermute | solution.py:78
  8.8 1.6 collective-permute-done.1.outer
  10.4 8.3 %shard_map.153 = (f32[192,640]{1,0:T(8,128)S(1)}, f32[1,640]{1,0:T(1,128)S(1)}, bf16[768,640]{1,0:T(8,128)(2,1)S(1)}, bf16[768,640]{1,0:T(8,128)(2,1)S(1)}) custom-call(s32[8]{0:T(128)S(1)} %stack.32.meta, bf16[5,192,128]{2,1,0:T(8,128)(2,1)S(1)} %bitcast.31, bf16[3,192,128]{2,1,0:T(8,128)(2,1)S(1)} %collective-permute-done.inner, ...), custom_call_target="tpu_custom_call" | custom-call | tf_op jit(solution)/shard_map/pallas_call | solution.py:87
  19.9 0.7 collective-permute-start.2
  20.6 0.7 collective-permute-start.3
  21.9 0.7 collective-permute-start.4
  23.1 0.7 collective-permute-start.5
  23.8 0.7 collective-permute-start.6
  25.0 0.7 collective-permute-start.7
  26.3 0.7 collective-permute-start.8
  28.2 1.3 collective-permute-start.10
  29.5 69.2 %collective-permute-done.10.cot_0.cot = bf16[5,192,128]{2,1,0:T(8,128)(2,1)S(1)} collective-permute-done((bf16[5,192,128]{2,1,0:T(8,128)(2,1)S(1)}, bf16[5,192,128]{2,1,0:T(8,128)(2,1)S(1)}, u32[]{:S(2)}, u32[]{:S(2)}) %collective-permute-start.10) | collective-permute-done | bytes 245792 | tf_op jit(solution)/shard_map/ppermute | solution.py:486
  98.7 8.6 %shard_map.160 = (bf16[5,192,128]{2,1,0:T(8,128)(2,1)S(1)}, bf16[3,192,128]{2,1,0:T(8,128)(2,1)S(1)}, bf16[3,192,128]{2,1,0:T(8,128)(2,1)S(1)}, bf16[112,768]{1,...) custom-call(s32[8]{0:T(128)S(1)} %stack.32.meta, ...), custom_call_target="tpu_custom_call" | custom-call | tf_op jit(solution)/shard_map/pallas_call | solution.py:87
  107.6 2.0 %collective-permute-start.16 = (bf16[112,768]{1,0:T(8,128)(2,1)S(1)}, bf16[112,768]{1,0:T(8,128)(2,1)S(1)}, u32[]{:S(2)}, u32[]{:S(2)}) collective-permute-start(bf16[112,768]{1,0:T(8,128)(2,1)S(1)} %get-tuple-element.56), channel_id=1, source_target_pairs={{0,9},{1,2},{2,11},{3,0},{4,13},{5,6},{6,15},{7,4},{8,1},{9,10},{1... | collective-permute-start | bytes 516104 | tf_op jit(solution)/shard_map/ppermute | solution.py:66
  109.6 4.9 %collective-permute-done.14 = bf16[112,768]{1,0:T(8,128)(2,1)S(1)} collective-permute-done((bf16[112,768]{1,0:T(8,128)(2,1)S(1)}, bf16[112,768]{1,0:T(8,128)(2,1)S(1)}, u32[]{:S(2)}, u32[]{:S(2)}) %collective-permute-start.14) | collective-permute-done | bytes 172064 | tf_op jit(solution)/shard_map/ppermute | solution.py:66
  114.7 2.6 %collective-permute-start.17 = (bf16[112,768]{1,0:T(8,128)(2,1)S(1)}, bf16[112,768]{1,0:T(8,128)(2,1)S(1)}, u32[]{:S(2)}, u32[]{:S(2)}) collective-permute-start(bf16[112,768]{1,0:T(8,128)(2,1)S(1)} %add_convert_fusion.4), channel_id=1, source_target_pairs={{0,6},{1,25},{2,4},{3,27},{4,2},{5,29},{6,0},{7,31},{8,14},{9,17},... | collective-permute-start | bytes 516104 | tf_op jit(solution)/shard_map/ppermute | solution.py:66
  117.3 4.3 %collective-permute-done.17 = bf16[112,768]{1,0:T(8,128)(2,1)S(1)} collective-permute-done((bf16[112,768]{1,0:T(8,128)(2,1)S(1)}, bf16[112,768]{1,0:T(8,128)(2,1)S(1)}, u32[]{:S(2)}, u32[]{:S(2)}) %collective-permute-start.17) | collective-permute-done | bytes 172064 | tf_op jit(solution)/shard_map/ppermute | solution.py:66
  121.6 2.0 %collective-permute-start.18 = (bf16[112,768]{1,0:T(8,128)(2,1)S(1)}, bf16[112,768]{1,0:T(8,128)(2,1)S(1)}, u32[]{:S(2)}, u32[]{:S(2)}) collective-permute-start(bf16[112,768]{1,0:T(8,128)(2,1)S(1)} %add_convert_fusion.3), channel_id=1, source_target_pairs={{0,8},{1,57},{2,10},{3,59},{4,12},{5,61},{6,14},{7,63},{8,0},{9,49... | collective-permute-start | bytes 516104 | tf_op jit(solution)/shard_map/ppermute | solution.py:66
  123.6 5.3 %collective-permute-done.18 = bf16[112,768]{1,0:T(8,128)(2,1)S(1)} collective-permute-done((bf16[112,768]{1,0:T(8,128)(2,1)S(1)}, bf16[112,768]{1,0:T(8,128)(2,1)S(1)}, u32[]{:S(2)}, u32[]{:S(2)}) %collective-permute-start.18) | collective-permute-done | bytes 172064 | tf_op jit(solution)/shard_map/ppermute | solution.py:66
  129.2 5.3 %collective-permute-done.19 = bf16[112,768]{1,0:T(8,128)(2,1)S(1)} collective-permute-done((bf16[112,768]{1,0:T(8,128)(2,1)S(1)}, bf16[112,768]{1,0:T(8,128)(2,1)S(1)}, u32[]{:S(2)}, u32[]{:S(2)}) %collective-permute-start.19) | collective-permute-done | bytes 172064 | tf_op jit(solution)/shard_map/ppermute | solution.py:66
  134.5 7.8 %collective-permute-start.20 = (bf16[112,768]{1,0:T(8,128)(2,1)S(1)}, bf16[112,768]{1,0:T(8,128)(2,1)S(1)}, u32[]{:S(2)}, u32[]{:S(2)}) collective-permute-start(bf16[112,768]{1,0:T(8,128)(2,1)S(1)} %add_convert_fusion.1), channel_id=1, source_target_pairs={{0,56},{1,7},{2,58},{3,5},{4,60},{5,3},{6,62},{7,1},{8,48},{9,15},... | collective-permute-start | bytes 516104 | tf_op jit(solution)/shard_map/ppermute | solution.py:66
  142.3 1.9 %collective-permute-start.11 = (bf16[3,192,128]{2,1,0:T(8,128)(2,1)S(1)}, bf16[3,192,128]{2,1,0:T(8,128)(2,1)S(1)}, u32[]{:S(2)}, u32[]{:S(2)}) collective-permute-start(bf16[3,192,128]{2,1,0:T(8,128)(2,1)S(1)} %get-tuple-element.49), channel_id=1, source_target_pairs={{0,1},{1,0},{2,3},{3,2},{4,5},{5,4},{6,7},{7,6},{8,9},{9,8},{10,11... | collective-permute-start | bytes 442376 | tf_op jit(solution)/shard_map/ppermute | solution.py:79
  144.2 2.2 %collective-permute-start.12 = (bf16[3,192,128]{2,1,0:T(8,128)(2,1)S(1)}, bf16[3,192,128]{2,1,0:T(8,128)(2,1)S(1)}, u32[]{:S(2)}, u32[]{:S(2)}) collective-permute-start(bf16[3,192,128]{2,1,0:T(8,128)(2,1)S(1)} %get-tuple-element.50), channel_id=1, source_target_pairs={{1,2},{2,1},{3,4},{4,3},{5,6},{6,5},{7,8},{8,7},{9,10},{10,9},{11,... | collective-permute-start | bytes 442376 | tf_op jit(solution)/shard_map/ppermute | solution.py:78
  146.6 2.4 %collective-permute-start.22 = (bf16[112,768]{1,0:T(8,128)(2,1)S(1)}, bf16[112,768]{1,0:T(8,128)(2,1)S(1)}, u32[]{:S(2)}, u32[]{:S(2)}) collective-permute-start(bf16[112,768]{1,0:T(8,128)(2,1)S(1)} %add_convert_fusion.keep), channel_id=1, source_target_pairs={{0,1},{1,0},{2,3},{3,2},{4,5},{5,4},{6,7},{7,6},{8,9},{9,8},{10,11... | collective-permute-start | bytes 516104 | tf_op jit(solution)/shard_map/ppermute | solution.py:66
  149.0 3.8 %collective-permute-done.12.outer = bf16[3,192,128]{2,1,0:T(8,128)(2,1)S(1)} collective-permute-done((bf16[3,192,128]{2,1,0:T(8,128)(2,1)S(1)}, bf16[3,192,128]{2,1,0:T(8,128)(2,1)S(1)}, u32[]{:S(2)}, u32[]{:S(2)}) %collective-permute-start.12) | collective-permute-done | bytes 147488 | tf_op jit(solution)/shard_map/ppermute | solution.py:78
  152.8 7.0 %shard_map.161 = (bf16[5,192,128]{2,1,0:T(8,128)(2,1)S(1)}, bf16[2,192,128]{2,1,0:T(8,128)(2,1)S(1)}) custom-call(s32[8]{0:T(128)S(1)} %stack.32.meta, s32[5]{0:T(128)S(1)} %copy-done.4, s32[3]{0:T(128)S(1)} %copy-done.6, bf16[5,192,128]{2,1,0:T(8,128)(2,1)S(1)} %get-tuple-element.48.field, bf16[3,192,128]{2,1,0:T(8,128)(2,1)S(1)} %collective-permute-done.11.inner, ...), custom_call_target="tpu_custom_call" | custom-call | tf_op jit(solution)/shard_map/pallas_call | solution.py:87
  159.8 1.9 %collective-permute-start.13 = (bf16[2,192,128]{2,1,0:T(8,128)(2,1)S(1)}, bf16[2,192,128]{2,1,0:T(8,128)(2,1)S(1)}, u32[]{:S(2)}, u32[]{:S(2)}) collective-permute-start(bf16[2,192,128]{2,1,0:T(8,128)(2,1)S(1)} %get-tuple-element.52), channel_id=1, source_target_pairs={{0,1},{1,2},{2,3},{3,4},{4,5},{5,6},{6,7},{7,8},{8,9},{9,10},{10,1... | collective-permute-start | bytes 294920 | tf_op jit(solution)/shard_map/ppermute | solution.py:538
  161.8 6.1 %collective-permute-done.13.arrived = bf16[2,192,128]{2,1,0:T(8,128)(2,1)S(1)} collective-permute-done((bf16[2,192,128]{2,1,0:T(8,128)(2,1)S(1)}, bf16[2,192,128]{2,1,0:T(8,128)(2,1)S(1)}, u32[]{:S(2)}, u32[]{:S(2)}) %collective-permute-start.13) | collective-permute-done | bytes 98336 | tf_op jit(solution)/shard_map/ppermute | solution.py:538
  167.9 1.3 shard_map.162
  169.2 1.7 shard_map.163
  170.9 0.7 copy.35
  (62 shorter events, 8.5 us)
Async XLA Ops:
  0.6 5.1 %copy-start.7 = (f32[1,49,192]{2,0,1:T(1,128)S(1)}, f32[1,49,192]{2,0,1:T(1,128)}, u32[]{:S(2)}) copy-start(f32[1,49,192]{2,0,1:T(1,128)} %param.14) | copy-start | bytes 112900
  1.7 5.5 %copy-start.3 = (bf16[1,192,768]{2,1,0:T(8,128)(2,1)S(1)}, bf16[1,192,768]{2,1,0:T(8,128)(2,1)}, u32[]{:S(2)}) copy-start(bf16[1,192,768]{2,1,0:T(8,128)(2,1)} %param.18) | copy-start | bytes 884740
  1.7 8.7 %collective-permute-start.1 = (bf16[3,192,128]{2,1,0:T(8,128)(2,1)S(1)}, bf16[3,192,128]{2,1,0:T(8,128)(2,1)S(1)}, u32[]{:S(2)}, u32[]{:S(2)}) collective-permute-start(bf16[3,192,128]{2,1,0:T(8,128)(2,1)S(1)} %get-tuple-element.77), channel_id=1, source_target_pairs={{1,2},{2,1},{3,4},{4,3},{5,6},{6,5},{7,8},{8,7},{9,10},{10,9},{11,... | collective-permute-start | bytes 442376 | tf_op jit(solution)/shard_map/ppermute | solution.py:78
  5.5 4.9 %collective-permute-start = (bf16[3,192,128]{2,1,0:T(8,128)(2,1)S(1)}, bf16[3,192,128]{2,1,0:T(8,128)(2,1)S(1)}, u32[]{:S(2)}, u32[]{:S(2)}) collective-permute-start(bf16[3,192,128]{2,1,0:T(8,128)(2,1)S(1)} %get-tuple-element.78), channel_id=1, source_target_pairs={{0,1},{1,0},{2,3},{3,2},{4,5},{5,4},{6,7},{7,6},{8,9},{9,8},{10,11... | collective-permute-start | bytes 442376 | tf_op jit(solution)/shard_map/ppermute | solution.py:79
  5.7 0.7 copy-start.9
  7.2 0.7 copy-start.8
  7.4 1.0 copy-start
  8.5 1.9 %copy-start.1 = (bf16[1,5,192,128]{3,2,1,0:T(8,128)(2,1)S(1)}, bf16[1,5,192,128]{3,2,1,0:T(8,128)(2,1)}, u32[]{:S(2)}) copy-start(bf16[1,5,192,128]{3,2,1,0:T(8,128)(2,1)} %param.10) | copy-start | bytes 737284
  10.4 8.3 %copy-start.2 = (bf16[5,192,128]{2,1,0:T(8,128)(2,1)S(1)}, bf16[5,192,128]{2,1,0:T(8,128)(2,1)}, u32[]{:S(2)}) copy-start(bf16[5,192,128]{2,1,0:T(8,128)(2,1)} %cot_top.1) | copy-start | bytes 737284
  19.9 1.4 collective-permute-start.2
  20.6 0.7 collective-permute-start.3
  21.9 0.7 collective-permute-start.4
  23.1 1.4 collective-permute-start.5
  23.8 0.7 collective-permute-start.6
  25.0 0.7 collective-permute-start.7
  26.3 1.4 collective-permute-start.8
  27.0 0.7 collective-permute-start.9
  28.2 70.5 %collective-permute-start.10 = (bf16[5,192,128]{2,1,0:T(8,128)(2,1)S(1)}, bf16[5,192,128]{2,1,0:T(8,128)(2,1)S(1)}, u32[]{:S(2)}, u32[]{:S(2)}) collective-permute-start(bf16[5,192,128]{2,1,0:T(8,128)(2,1)S(1)} %shard_map.159.first), channel_id=1, source_target_pairs={{64,0},{65,1},{66,2},{67,3},{68,4},{69,5},{70,6},{71,7},{72,8},{73... | collective-permute-start | bytes 737288 | tf_op jit(solution)/shard_map/ppermute | solution.py:486
  107.4 7.2 %collective-permute-start.14 = (bf16[112,768]{1,0:T(8,128)(2,1)S(1)}, bf16[112,768]{1,0:T(8,128)(2,1)S(1)}, u32[]{:S(2)}, u32[]{:S(2)}) collective-permute-start(bf16[112,768]{1,0:T(8,128)(2,1)S(1)} %get-tuple-element.54), channel_id=1, source_target_pairs={{0,2},{1,9},{2,0},{3,11},{4,6},{5,13},{6,4},{7,15},{8,10},{9,1},{1... | collective-permute-start | bytes 516104 | tf_op jit(solution)/shard_map/ppermute | solution.py:66
  107.5 7.1 %collective-permute-start.15 = (bf16[112,768]{1,0:T(8,128)(2,1)S(1)}, bf16[112,768]{1,0:T(8,128)(2,1)S(1)}, u32[]{:S(2)}, u32[]{:S(2)}) collective-permute-start(bf16[112,768]{1,0:T(8,128)(2,1)S(1)} %get-tuple-element.55), channel_id=1, source_target_pairs={{0,1},{1,0},{2,3},{3,2},{4,5},{5,4},{6,7},{7,6},{8,9},{9,8},{10,11... | collective-permute-start | bytes 516104 | tf_op jit(solution)/shard_map/ppermute | solution.py:66
  107.6 7.0 %collective-permute-start.16 = (bf16[112,768]{1,0:T(8,128)(2,1)S(1)}, bf16[112,768]{1,0:T(8,128)(2,1)S(1)}, u32[]{:S(2)}, u32[]{:S(2)}) collective-permute-start(bf16[112,768]{1,0:T(8,128)(2,1)S(1)} %get-tuple-element.56), channel_id=1, source_target_pairs={{0,9},{1,2},{2,11},{3,0},{4,13},{5,6},{6,15},{7,4},{8,1},{9,10},{1... | collective-permute-start | bytes 516104 | tf_op jit(solution)/shard_map/ppermute | solution.py:66
  114.7 6.9 %collective-permute-start.17 = (bf16[112,768]{1,0:T(8,128)(2,1)S(1)}, bf16[112,768]{1,0:T(8,128)(2,1)S(1)}, u32[]{:S(2)}, u32[]{:S(2)}) collective-permute-start(bf16[112,768]{1,0:T(8,128)(2,1)S(1)} %add_convert_fusion.4), channel_id=1, source_target_pairs={{0,6},{1,25},{2,4},{3,27},{4,2},{5,29},{6,0},{7,31},{8,14},{9,17},... | collective-permute-start | bytes 516104 | tf_op jit(solution)/shard_map/ppermute | solution.py:66
  121.6 7.3 %collective-permute-start.18 = (bf16[112,768]{1,0:T(8,128)(2,1)S(1)}, bf16[112,768]{1,0:T(8,128)(2,1)S(1)}, u32[]{:S(2)}, u32[]{:S(2)}) collective-permute-start(bf16[112,768]{1,0:T(8,128)(2,1)S(1)} %add_convert_fusion.3), channel_id=1, source_target_pairs={{0,8},{1,57},{2,10},{3,59},{4,12},{5,61},{6,14},{7,63},{8,0},{9,49... | collective-permute-start | bytes 516104 | tf_op jit(solution)/shard_map/ppermute | solution.py:66
  129.0 5.5 %collective-permute-start.19 = (bf16[112,768]{1,0:T(8,128)(2,1)S(1)}, bf16[112,768]{1,0:T(8,128)(2,1)S(1)}, u32[]{:S(2)}, u32[]{:S(2)}) collective-permute-start(bf16[112,768]{1,0:T(8,128)(2,1)S(1)} %add_convert_fusion.2), channel_id=1, source_target_pairs={{0,24},{1,3},{2,26},{3,1},{4,28},{5,7},{6,30},{7,5},{8,16},{9,11},... | collective-permute-start | bytes 516104 | tf_op jit(solution)/shard_map/ppermute | solution.py:66
  134.5 11.9 %collective-permute-start.20 = (bf16[112,768]{1,0:T(8,128)(2,1)S(1)}, bf16[112,768]{1,0:T(8,128)(2,1)S(1)}, u32[]{:S(2)}, u32[]{:S(2)}) collective-permute-start(bf16[112,768]{1,0:T(8,128)(2,1)S(1)} %add_convert_fusion.1), channel_id=1, source_target_pairs={{0,56},{1,7},{2,58},{3,5},{4,60},{5,3},{6,62},{7,1},{8,48},{9,15},... | collective-permute-start | bytes 516104 | tf_op jit(solution)/shard_map/ppermute | solution.py:66
  142.3 6.7 %collective-permute-start.11 = (bf16[3,192,128]{2,1,0:T(8,128)(2,1)S(1)}, bf16[3,192,128]{2,1,0:T(8,128)(2,1)S(1)}, u32[]{:S(2)}, u32[]{:S(2)}) collective-permute-start(bf16[3,192,128]{2,1,0:T(8,128)(2,1)S(1)} %get-tuple-element.49), channel_id=1, source_target_pairs={{0,1},{1,0},{2,3},{3,2},{4,5},{5,4},{6,7},{7,6},{8,9},{9,8},{10,11... | collective-permute-start | bytes 442376 | tf_op jit(solution)/shard_map/ppermute | solution.py:79
  144.2 8.6 %collective-permute-start.12 = (bf16[3,192,128]{2,1,0:T(8,128)(2,1)S(1)}, bf16[3,192,128]{2,1,0:T(8,128)(2,1)S(1)}, u32[]{:S(2)}, u32[]{:S(2)}) collective-permute-start(bf16[3,192,128]{2,1,0:T(8,128)(2,1)S(1)} %get-tuple-element.50), channel_id=1, source_target_pairs={{1,2},{2,1},{3,4},{4,3},{5,6},{6,5},{7,8},{8,7},{9,10},{10,9},{11,... | collective-permute-start | bytes 442376 | tf_op jit(solution)/shard_map/ppermute | solution.py:78
  146.5 6.3 %copy-start.6 = (s32[3]{0:T(128)S(1)}, s32[3]{0:T(128)}, u32[]{:S(2)}) copy-start(s32[3]{0:T(128)} %owners.3) | copy-start | bytes 40
  146.5 22.7 %collective-permute-start.23 = (bf16[112,768]{1,0:T(8,128)(2,1)S(1)}, bf16[112,768]{1,0:T(8,128)(2,1)S(1)}, u32[]{:S(2)}, u32[]{:S(2)}) collective-permute-start(bf16[112,768]{1,0:T(8,128)(2,1)S(1)} %add_convert_fusion.keep), channel_id=1, source_target_pairs={{0,3},{1,8},{2,1},{3,10},{4,7},{5,12},{6,5},{7,14},{8,11},{9,0},{1... | collective-permute-start | bytes 516104 | tf_op jit(solution)/shard_map/ppermute | solution.py:66
  146.6 22.6 %collective-permute-start.22 = (bf16[112,768]{1,0:T(8,128)(2,1)S(1)}, bf16[112,768]{1,0:T(8,128)(2,1)S(1)}, u32[]{:S(2)}, u32[]{:S(2)}) collective-permute-start(bf16[112,768]{1,0:T(8,128)(2,1)S(1)} %add_convert_fusion.keep), channel_id=1, source_target_pairs={{0,1},{1,0},{2,3},{3,2},{4,5},{5,4},{6,7},{7,6},{8,9},{9,8},{10,11... | collective-permute-start | bytes 516104 | tf_op jit(solution)/shard_map/ppermute | solution.py:66
  149.0 20.2 %collective-permute-start.21 = (bf16[112,768]{1,0:T(8,128)(2,1)S(1)}, bf16[112,768]{1,0:T(8,128)(2,1)S(1)}, u32[]{:S(2)}, u32[]{:S(2)}) collective-permute-start(bf16[112,768]{1,0:T(8,128)(2,1)S(1)} %add_convert_fusion.keep), channel_id=1, source_target_pairs={{0,2},{1,9},{2,0},{3,11},{4,6},{5,13},{6,4},{7,15},{8,10},{9,1},{1... | collective-permute-start | bytes 516104 | tf_op jit(solution)/shard_map/ppermute | solution.py:66
  159.8 8.0 %collective-permute-start.13 = (bf16[2,192,128]{2,1,0:T(8,128)(2,1)S(1)}, bf16[2,192,128]{2,1,0:T(8,128)(2,1)S(1)}, u32[]{:S(2)}, u32[]{:S(2)}) collective-permute-start(bf16[2,192,128]{2,1,0:T(8,128)(2,1)S(1)} %get-tuple-element.52), channel_id=1, source_target_pairs={{0,1},{1,2},{2,3},{3,4},{4,5},{5,6},{6,7},{7,8},{8,9},{9,10},{10,1... | collective-permute-start | bytes 294920 | tf_op jit(solution)/shard_map/ppermute | solution.py:538
  (2 other events, 1.3 us)

commit v2 on v1

--- a/solution.py
+++ b/solution.py
@@ -14,6 +14,7 @@
 TILES = 64
 MARGIN = 3
 BLOCK = 16
+UNROLL = 4
 
 norm_eps = 1e-06
 tanh_root = math.sqrt(2.0 / math.pi)
@@ -22,7 +23,8 @@
 f32 = jnp.float32
 bf16 = jnp.bfloat16
 
-SECTION, ODD, KEEP, NEAR, MATE, FAR, OFFSET = range(7)
+SECTION, ODD, KEEP, NEAR, MATE, FAR, OFFSET, INSIDE = range(8)
+PLACES = 8
 
 
 def split_tile(tile):
@@ -66,17 +68,10 @@
     return lax.ppermute(value, "tile", pairs)
 
 
-def halo(inner, outer, sections):
-    within, across = [], []
-    for section in sections:
-        for tile in range(TILES):
-            within.append((section * TILES + tile, section * TILES + (tile ^ 1)))
-            other = tile + 1 if tile % 2 else tile - 1
-            if 0 <= other < TILES:
-                across.append((section * TILES + tile, section * TILES + other))
-    axes = ("section", "tile")
-    outer = lax.ppermute(outer, axes, across)
-    inner = lax.ppermute(inner, axes, within)
+def halo(inner, outer):
+    across = [(tile, (tile + 1 if tile % 2 else tile - 1) % TILES) for tile in range(TILES)]
+    outer = lax.ppermute(outer, "tile", across)
+    inner = lax.ppermute(inner, "tile", [(tile, tile ^ 1) for tile in range(TILES)])
     return inner, outer
 
 
@@ -99,11 +94,15 @@
     return jax.ShapeDtypeStruct(dims, dtype)
 
 
-def fill_rows(rows_ref, odd, own, inner, outer):
+def fill_rows(rows_ref, meta, own, inner, outer):
     count = own.shape[0]
+    odd = meta[ODD] == 1
+    far_rows = jnp.where(meta[INSIDE] == 1, outer[...], jnp.zeros_like(outer))
+    near_rows = inner[...]
     rows_ref[MARGIN : MARGIN + count] = own[...]
-    rows_ref[:MARGIN] = jnp.where(odd, inner[...], outer[...])
-    rows_ref[MARGIN + count :] = jnp.where(odd, outer[...], inner[...])
+    rows_ref[:MARGIN] = jnp.where(odd, near_rows, far_rows)
+    rows_ref[MARGIN + count : 2 * MARGIN + count] = jnp.where(odd, far_rows, near_rows)
+    rows_ref[2 * MARGIN + count :] = jnp.zeros((1,) + own.shape[1:], bf16)
 
 
 def edges(odd, value_ref, inner_ref, outer_ref):
@@ -114,46 +113,68 @@
     outer_ref[...] = jnp.where(odd, tail, head)
 
 
-def taps_sum(rows_ref, cols_ref, start, count, backward):
-    coefs = cols_ref[pl.ds(start, BLOCK), :]
-    rows = [
-        rows_ref[row, pl.ds(start, BLOCK), :].astype(f32) for row in range(count + 2 * MARGIN)
-    ]
-    sums = [None] * count
-    for tap_col in range(KS):
-        shift = (tap_col - MARGIN if backward else MARGIN - tap_col) % 128
-        weights = [
-            jnp.broadcast_to(
-                coefs[:, tap_row * KS + tap_col : tap_row * KS + tap_col + 1], rows[0].shape
-            )
-            for tap_row in range(KS)
-        ]
-        for row in range(count):
-            part = None
-            for tap_row in range(KS):
-                place = row + (KS - 1 - tap_row if backward else tap_row)
-                term = weights[tap_row] * rows[place]
-                part = term if part is None else part + term
+def prepare_kernel(cols, forth_ref, back_ref):
+    high = cols[...].astype(bf16)
+    low = (cols[...] - high.astype(f32)).astype(bf16)
+    chans, taps = cols.shape
+    wide = KS * 128
+    tap = lax.broadcasted_iota(jnp.int32, (taps, wide), 0)
+    place = lax.broadcasted_iota(jnp.int32, (taps, wide), 1)
+    tap_col, tap_row = place >> 7, (place >> 4) & (PLACES - 1)
+    own = lax.broadcasted_iota(jnp.int32, (chans, wide), 0) & (BLOCK - 1)
+    diagonal = own == (lax.broadcasted_iota(jnp.int32, (chans, wide), 1) & (BLOCK - 1))
+    for target, row in ((forth_ref, tap_row), (back_ref, KS - 1 - tap_row)):
+        hit = (tap == row * KS + tap_col) & (tap_row < KS)
+        spread = jnp.where(hit, 1.0, 0.0).astype(bf16)
+        for half, value in enumerate((high, low)):
+            filled = jnp.dot(value, spread, preferred_element_type=f32)
+            filled = jnp.where(diagonal, filled, 0.0).astype(bf16)
+            for block in range(chans // BLOCK):
+                for col in range(KS):
+                    target[
+                        block, col * BLOCK : (col + 1) * BLOCK, half * 128 : (half + 1) * 128
+                    ] = filled[block * BLOCK : (block + 1) * BLOCK, col * 128 : (col + 1) * 128]
+
+
+def stacked(rows_ref, start, count):
+    rows = [rows_ref[row, pl.ds(start, BLOCK), :] for row in range(count + PLACES - 1)]
+    return jnp.concatenate(
+        [jnp.concatenate(rows[place : place + count], axis=1) for place in range(PLACES)], axis=0
+    )
+
+
+def taps_sum(rows_ref, taps_mat, block, count, backward):
+    windows = stacked(rows_ref, pl.multiple_of(block * BLOCK, BLOCK), count)
+    parts = jnp.dot(
+        taps_mat[block], jnp.concatenate([windows, windows], axis=0), preferred_element_type=f32
+    )
+    sums = []
+    for row in range(count):
+        total = None
+        for tap_col in range(KS):
+            shift = (tap_col - MARGIN if backward else MARGIN - tap_col) % 128
+            part = parts[tap_col * BLOCK : (tap_col + 1) * BLOCK, row * 128 : (row + 1) * 128]
             if shift:
                 part = pltpu.roll(part, shift, 1)
-            sums[row] = part if sums[row] is None else sums[row] + part
+            total = part if total is None else total + part
+        sums.append(total)
     return sums
 
 
 def forward_kernel(
-    meta, acts, inner, outer, cols, up_t, bias, nhat_ref, inv_ref, hidden_ref, slope_ref, rows_ref, field_ref, normed_ref
+    meta, acts, inner, outer, taps_mat, cols, up_t, bias, nhat_ref, inv_ref, hidden_ref, slope_ref, rows_ref, field_ref, normed_ref
 ):
     count, chans, width = acts.shape
-    fill_rows(rows_ref, meta[ODD] == 1, acts, inner, outer)
+    fill_rows(rows_ref, meta, acts, inner, outer)
 
     def step(index, carry):
         start = pl.multiple_of(index * BLOCK, BLOCK)
-        sums = taps_sum(rows_ref, cols, start, count, False)
+        sums = taps_sum(rows_ref, taps_mat, index, count, False)
         for row in range(count):
             field_ref[pl.ds(start, BLOCK), row * width : (row + 1) * width] = sums[row]
         return carry
 
-    lax.fori_loop(0, chans // BLOCK, step, 0)
+    lax.fori_loop(0, chans // BLOCK, step, 0, unroll=UNROLL)
     gain = cols[:, KS * KS : KS * KS + 1]
     for row in range(count):
         part = slice(row * width, (row + 1) * width)
@@ -225,29 +246,29 @@
         edges(meta[ODD] == 1, field_ref, inner_ref, outer_ref)
 
 
-def conv_rows(meta, field, inner, outer, cot, cols, result_ref, rows_ref):
+def conv_rows(meta, field, inner, outer, cot, taps_mat, result_ref, rows_ref):
     count, chans, width = field.shape
-    fill_rows(rows_ref, meta[ODD] == 1, field, inner, outer)
+    fill_rows(rows_ref, meta, field, inner, outer)
 
     def step(index, carry):
         start = pl.multiple_of(index * BLOCK, BLOCK)
-        sums = taps_sum(rows_ref, cols, start, count, True)
+        sums = taps_sum(rows_ref, taps_mat, index, count, True)
         for row in range(count):
             own = cot[row, pl.ds(start, BLOCK), :].astype(f32)
             result_ref[row, pl.ds(start, BLOCK), :] = (own + sums[row]).astype(bf16)
         return carry
 
-    lax.fori_loop(0, chans // BLOCK, step, 0)
-
-
-def conv_kernel(section, meta, field, inner, outer, cot, cols, result_ref, rows_ref):
+    lax.fori_loop(0, chans // BLOCK, step, 0, unroll=UNROLL)
+
+
+def conv_kernel(section, meta, field, inner, outer, cot, taps_mat, result_ref, rows_ref):
     @pl.when(meta[SECTION] == section)
     def _():
-        conv_rows(meta, field, inner, outer, cot, cols, result_ref, rows_ref)
+        conv_rows(meta, field, inner, outer, cot, taps_mat, result_ref, rows_ref)
 
 
 def last_conv_kernel(
-    meta, land, owners, field, inner, outer, cot, cols, third, second, first, result_ref, sent_ref, rows_ref
+    meta, land, owners, field, inner, outer, cot, taps_mat, third, second, first, result_ref, sent_ref, rows_ref
 ):
     for section, kept in ((3, third), (2, second), (1, first)):
 
@@ -257,7 +278,7 @@
 
     @pl.when(meta[SECTION] == 0)
     def _():
-        conv_rows(meta, field, inner, outer, cot, cols, result_ref, rows_ref)
+        conv_rows(meta, field, inner, outer, cot, taps_mat, result_ref, rows_ref)
 
     sent_ref[...] = jnp.zeros_like(sent_ref)
     rank = jnp.int32(0)
@@ -316,7 +337,6 @@
     bias_ref,
     gain_ref,
     rows_ref,
-    taps_ref,
     packed_ref,
     cot_ref,
 ):
@@ -338,54 +358,50 @@
     normed = (nhat[...] * gain).astype(bf16)
     turned = (((1,), (1,)), ((), ()))
     grad_up = lax.dot_general(normed, low_ref[...], turned, preferred_element_type=f32)
-    packed_ref[:chans] = grad_up.astype(bf16)
+    packed_ref[:chans] = grad_up
     grad_down = lax.dot_general(out_ref[...], hidden[...], turned, preferred_element_type=f32)
-    packed_ref[chans : 2 * chans] = grad_down.astype(bf16)
+    packed_ref[chans : 2 * chans] = grad_down
     product = grad_down * down[...].astype(f32)
     product = sum(product[:, first : first + 128] for first in range(0, units, 128))
 
-    fill_rows(rows_ref, odd, acts, inner, outer)
-
-    def step(index, carry):
-        start = pl.multiple_of(index * BLOCK, BLOCK)
-        rows = [
-            rows_ref[row, pl.ds(start, BLOCK), :].astype(f32) for row in range(count + 2 * MARGIN)
-        ]
-        fields = [field_ref[row, pl.ds(start, BLOCK), :].astype(f32) for row in range(count)]
-        lane = lax.broadcasted_iota(jnp.int32, (BLOCK, 128), 1)
-        grads = jnp.zeros((BLOCK, 128), f32)
+    fill_rows(rows_ref, meta, acts, inner, outer)
+    base = 2 * chans
+    shifts = [(tap_col - MARGIN) % 128 for tap_col in range(KS)]
+    own = lax.broadcasted_iota(jnp.int32, (BLOCK, 128), 0)
+    diagonal = own == (lax.broadcasted_iota(jnp.int32, (BLOCK, 128), 1) & (BLOCK - 1))
+    for block in range(chans // BLOCK):
+        start = block * BLOCK
+        windows = stacked(rows_ref, start, count)
+        fields = [field_ref[row, start : start + BLOCK, :].astype(f32) for row in range(count)]
+        rolled = jnp.concatenate(
+            [
+                jnp.concatenate(
+                    [pltpu.roll(field, shift, 1) if shift else field for field in fields], axis=1
+                )
+                for shift in shifts
+            ],
+            axis=0,
+        ).astype(bf16)
+        crossed = lax.dot_general(rolled, windows, turned, preferred_element_type=f32)
+        first = base + block // 6 * 8
+        lanes = slice(block % 6 * 128, block % 6 * 128 + 128)
         for tap_col in range(KS):
-            shift = (tap_col - MARGIN) % 128
-            turned_fields = [pltpu.roll(field, shift, 1) if shift else field for field in fields]
-            for tap_row in range(KS):
-                part = None
-                for row in range(count):
-                    term = turned_fields[row] * rows[row + tap_row]
-                    part = term if part is None else part + term
-                grads = jnp.where(
-                    lane == tap_row * KS + tap_col, jnp.sum(part, axis=1, keepdims=True), grads
-                )
-        taps_ref[pl.ds(start, BLOCK), :] = grads
-        return carry
-
-    lax.fori_loop(0, chans // BLOCK, step, 0)
-    base = 2 * chans
-    taps = jnp.transpose(taps_ref[...])[:56]
-    zeros = jnp.zeros((56, units - chans), f32)
+            part = jnp.where(diagonal, crossed[tap_col * BLOCK : (tap_col + 1) * BLOCK], 0.0)
+            packed_ref[first + tap_col : first + tap_col + 1, lanes] = jnp.sum(
+                part, axis=0, keepdims=True
+            )
+        packed_ref[first + KS : first + PLACES, lanes] = jnp.zeros((1, 128), f32)
     bias_row = jnp.sum(jnp.transpose(bias_ref[...]), axis=0, keepdims=True)
     gain_row = jnp.sum(jnp.transpose(gain_ref[...]), axis=0, keepdims=True)
     scale_row = jnp.sum(jnp.transpose(product), axis=0, keepdims=True) / layer_row[...]
-    gap = jnp.zeros((1, 256 - chans), f32)
-    rest = jnp.zeros((1, units - 256 - chans), f32)
-    pair_row = jnp.concatenate([gain_row, gap, scale_row, rest], axis=1)
-    small = jnp.concatenate(
-        [jnp.concatenate([taps, zeros], axis=1), bias_row, pair_row, jnp.zeros((6, units), f32)]
-    )
-    packed_ref[base : base + 64] = small.astype(bf16)
+    packed_ref[base + 16 :] = jnp.zeros((packed_ref.shape[0] - base - 16, units), f32)
+    packed_ref[base + 16 : base + 17] = bias_row
+    packed_ref[base + 17 : base + 18, :chans] = gain_row
+    packed_ref[base + 17 : base + 18, 256 : 256 + chans] = scale_row
     part_rows = keep_ref.shape[0]
     for place, target in ((KEEP, keep_ref), (NEAR, near_ref), (MATE, mate_ref), (FAR, far_ref)):
-        start = pl.multiple_of(meta[place] * part_rows, 16)
-        target[...] = packed_ref[pl.ds(start, part_rows), :]
+        start = pl.multiple_of(meta[place] * part_rows, 8)
+        target[...] = packed_ref[pl.ds(start, part_rows), :].astype(bf16)
 
 
 def finish_kernel(
@@ -393,16 +409,31 @@
 ):
     part_rows = keep.shape[0]
     for place, source in ((KEEP, keep), (NEAR, near), (MATE, mate), (FAR, far)):
-        start = pl.multiple_of(meta[place] * part_rows, 16)
-        packed_ref[pl.ds(start, part_rows), :] = source[...]
+        start = pl.multiple_of(meta[place] * part_rows, 8)
+        packed_ref[pl.ds(start, part_rows), :] = source[...].astype(f32) * scale
     chans = up_ref.shape[0]
-    up_ref[...] = packed_ref[:chans].astype(f32) * scale
-    down_ref[...] = packed_ref[chans : 2 * chans].astype(f32) * scale
-    small = packed_ref[2 * chans :].astype(f32) * scale
-    kernel_ref[...] = small[: KS * KS, :chans]
-    bias_ref[...] = small[56:57]
-    gain_ref[...] = small[57:58, :chans]
-    scale_ref[...] = small[57:58, 256 : 256 + chans]
+    base = 2 * chans
+    up_ref[...] = packed_ref[:chans]
+    down_ref[...] = packed_ref[chans:base]
+    lane = lax.broadcasted_iota(jnp.int32, (PLACES, 128), 1) >> 4
+    blocks = chans // BLOCK
+    for tap_row in range(KS):
+        halves = []
+        for first in range(0, blocks, PLACES):
+            half = jnp.zeros((PLACES, 128), f32)
+            for block in range(first, min(first + PLACES, blocks)):
+                rows = slice(base + block // 6 * 8, base + block // 6 * 8 + 8)
+                part = packed_ref[rows, block % 6 * 128 : block % 6 * 128 + 128]
+                shift = (block - first - tap_row) * BLOCK % 128
+                if shift:
+                    part = pltpu.roll(part, shift, 1)
+                half = jnp.where(lane == block - first, part, half)
+            halves.append(half)
+        line = jnp.concatenate(halves, axis=1)
+        kernel_ref[tap_row * KS : (tap_row + 1) * KS] = line[:KS, :chans]
+    bias_ref[...] = packed_ref[base + 16 : base + 17]
+    gain_ref[...] = packed_ref[base + 17 : base + 18, :chans]
+    scale_ref[...] = packed_ref[base + 17 : base + 18, 256 : 256 + chans]
 
 
 def added(*values):
@@ -430,21 +461,22 @@
             2 * (1 - core) + mate_bit,
             2 * (1 - core) + 1 - mate_bit,
             tile_now * count,
-            core,
+            jnp.where((tile_now == 0) | (tile_now == TILES - 1), 0, 1),
         ]
     ).astype(jnp.int32)
 
     odd = core == 1
     head, tail = source[:MARGIN], source[count - MARGIN :]
-    acts_inner, acts_outer = halo(
-        jnp.where(odd, head, tail), jnp.where(odd, tail, head), range(SECTIONS)
-    )
-    cols = jnp.concatenate([dw_kernel[0], ln_gain, layer_scale]).T
+    acts_inner, acts_outer = halo(jnp.where(odd, head, tail), jnp.where(odd, tail, head))
+    unused = jnp.zeros((64 - KS * KS - 2, chans), f32)
+    cols = jnp.concatenate([dw_kernel[0], ln_gain, layer_scale, unused]).T
+    taps_shape = shape((chans // BLOCK, KS * BLOCK, 256), bf16)
+    forth, back = call(prepare_kernel, (taps_shape, taps_shape), 0, (cols,), cost=(10**9, 10**7))
     up, down = w_up[0], w_down[0]
     up_t, down_t = up.T, down.T
     bias = b_up.reshape(units, 1)
 
-    padded = pltpu.VMEM((count + 2 * MARGIN, chans, width), bf16)
+    padded = pltpu.VMEM((count + PLACES - 1, chans, width), bf16)
     nhat, inv, hidden, slope = call(
         forward_kernel,
         (
@@ -454,7 +486,7 @@
             shape((units, cells), bf16),
         ),
         1,
-        (meta, source, acts_inner, acts_outer, cols, up_t, bias),
+        (meta, source, acts_inner, acts_outer, forth, cols, up_t, bias),
         (padded, pltpu.VMEM((chans, cells), f32), pltpu.VMEM((chans, cells), bf16)),
     )
 
@@ -471,21 +503,19 @@
             (meta, land, cots[-1], cols, down_t, up, slope, nhat, inv),
             (outgrads, lowgrads),
         )
-        inner, outer = halo(inner, outer, (section,))
+        inner, outer = halo(inner, outer)
         result = call(
             functools.partial(conv_kernel, section),
             rows_shape,
             1,
-            (meta, field, inner, outer, cots[-1], cols),
+            (meta, field, inner, outer, cots[-1], back),
             (padded,),
         )
         results.append(result)
-        pairs = [
-            (section * TILES + tile, (section - 1) * TILES + tile) for tile in range(TILES)
-        ]
-        cots.append(lax.ppermute(result, ("section", "tile"), pairs))
-
-    part = shape(((2 * chans + 64) // 4, units), bf16)
+        pairs = [(place, (place - 1) % SECTIONS) for place in range(SECTIONS)]
+        cots.append(lax.ppermute(result, "section", pairs))
+
+    part = shape(((2 * chans + 32) // 4, units), bf16)
     field, inner, outer, keep, near, mate, far = call(
         last_kernel,
         (rows_shape, edge_shape, edge_shape, part, part, part, part),
@@ -498,8 +528,7 @@
             pltpu.VMEM((units, width), f32),
             pltpu.VMEM((chans, width), f32),
             padded,
-            pltpu.VMEM((chans, 128), f32),
-            pltpu.VMEM((2 * chans + 64, units), bf16),
+            pltpu.VMEM((2 * chans + 32, units), f32),
             pltpu.VMEM((count, chans, width), bf16),
         ),
     )
@@ -507,8 +536,31 @@
     near = moved(near, ("x0", "z0"), False)
     mate = moved(mate, ("", ""), True)
     total = added(keep, near, mate, far)
-    for dims in (("x1", "z1"), ("z0", "z2"), ("z1", "x0"), ("z2", "x1")):
-        total = added(total, moved(total, dims, False))
+    orders = (("x1", "z1"), ("z0", "z2"), ("z1", "x0"), ("z2", "x1"))
+    total, inner, outer = lax.optimization_barrier((total, inner, outer))
+    total = added(total, moved(total, orders[0], False))
+    inner, outer = halo(inner, outer)
+    total, inner, outer = lax.optimization_barrier((total, inner, outer))
+    total = added(total, moved(total, orders[1], False))
+    result, sent = call(
+        last_conv_kernel,
+        (rows_shape, shape((CAP, chans, width), bf16)),
+        3,
+        (meta, land, owners, field, inner, outer, cots[-1], back, *results),
+        (padded,),
+    )
+    total, result, sent = lax.optimization_barrier((total, result, sent))
+    total = added(total, moved(total, orders[2], False))
+    arrived = lax.ppermute(sent, "tile", [(tile, (tile + 1) % TILES) for tile in range(TILES)])
+    total, result, arrived = lax.optimization_barrier((total, result, arrived))
+    total = added(total, moved(total, orders[3], False))
+    slotted = call(
+        slots_kernel,
+        shape((owners.shape[0], chans, width), bf16),
+        2,
+        (meta, owners, result, arrived),
+    )
+    total, slotted = lax.optimization_barrier((total, slotted))
     far = moved(total, ("x0", "z0"), True)
     near = moved(total, ("x0", "z0"), False)
     mate = moved(total, ("", ""), True)
@@ -524,24 +576,9 @@
         ),
         1,
         (meta, total, near, mate, far),
-        (pltpu.VMEM((2 * chans + 64, units), bf16),),
-    )
-
-    inner, outer = halo(inner, outer, (0,))
-    result, sent = call(
-        last_conv_kernel,
-        (rows_shape, shape((CAP, chans, width), bf16)),
-        3,
-        (meta, land, owners, field, inner, outer, cots[-1], cols, *results),
-        (padded,),
-    )
-    arrived = lax.ppermute(sent, "tile", [(tile, tile + 1) for tile in range(TILES - 1)])
-    slotted = call(
-        slots_kernel,
-        shape((owners.shape[0], chans, width), bf16),
-        2,
-        (meta, owners, result, arrived),
-    )
+        (pltpu.VMEM((2 * chans + 32, units), f32),),
+    )
+
     grad_kernel, grad_gain, grad_up, grad_bias, grad_down, grad_scale = grads
     return (
         slotted[None],

time: 172 us -> 120 us (0.70)
  the two profiles are of different devices: /device:TPU:64 before, /device:TPU:1 now
where the time goes in v2:
time: 120 us
  starting transfers between devices  54.8 us (46%)
  waiting for transfers between devices  42.3 us (35%)
  Pallas kernels  15.5 us (13%)
  local copies, waits for them, and re-layouts  5.14 us (4%)
  other arithmetic  1.39 us (1%)
    ppermute x10, starting transfers between devices, moved(): return lax.ppermute(value, 'tile', pairs)  20.2 us
    ppermute x10, waiting for transfers between devices, moved(): return lax.ppermute(value, 'tile', pairs)  18 us
    ppermute x5, starting transfers between devices, halo(): lax.ppermute(inner, 'tile', [(tile, tile ^ 1) for tile in range(TILES)])  17.8 us
    pallas_call x12, Pallas kernels, call(): pl.pallas_call(body, out_shape=out_shape, in_specs=spec, out_specs=outs,...  15.5 us
    ppermute x3, starting transfers between devices, body(): cots.append(lax.ppermute(result, 'section', pairs))  12.3 us
    ppermute x5, waiting for transfers between devices, halo(): outer = lax.ppermute(outer, 'tile', across)  10.7 us
    ppermute x3, waiting for transfers between devices, body(): cots.append(lax.ppermute(result, 'section', pairs))  9.89 us
    unnamed x24, local copies, waits for them, and re-layouts  4.45 us
  transfers between devices with their start and end apart: 24, of which 17 were waited for; matrix products, arithmetic and copies ran while one was open for 1% of the time, Pallas kernels for 3%

profile of v2, /device:TPU:1, one launch (start us, length us, event | category | flops | bytes accessed | tf_op | source)
XLA Modules:
  0.0 120.1 jit_solution(7657927011293362487)
XLA Ops:
  0.7 1.0 select_bitcast_fusion
  1.7 2.7 %collective-permute-start.1 = (bf16[3,192,128]{2,1,0:T(8,128)(2,1)S(1)}, bf16[3,192,128]{2,1,0:T(8,128)(2,1)S(1)}, u32[]{:S(2)}, u32[]{:S(2)}) collective-permute-start(bf16[3,192,128]{2,1,0:T(8,128)(2,1)S(1)} %get-tuple-element.109), channel_id=1, source_target_pairs={{0,63},{1,2},{2,1},{3,4},{4,3},{5,6},{6,5},{7,8},{8,7},{9,10},{10,... | collective-permute-start | bytes 442376 | tf_op jit(solution)/shard_map/ppermute | solution.py:73
  4.4 6.4 %collective-permute-start = (bf16[3,192,128]{2,1,0:T(8,128)(2,1)S(1)}, bf16[3,192,128]{2,1,0:T(8,128)(2,1)S(1)}, u32[]{:S(2)}, u32[]{:S(2)}) collective-permute-start(bf16[3,192,128]{2,1,0:T(8,128)(2,1)S(1)} %get-tuple-element.110), channel_id=1, source_target_pairs={{0,1},{1,0},{2,3},{3,2},{4,5},{5,4},{6,7},{7,6},{8,9},{9,8},{10,11... | collective-permute-start | bytes 442376 | tf_op jit(solution)/shard_map/ppermute | solution.py:74
  15.1 3.6 %shard_map.154 = (f32[192,640]{1,0:T(8,128)S(1)}, f32[1,640]{1,0:T(1,128)S(1)}, bf16[768,640]{1,0:T(8,128)(2,1)S(1)}, bf16[768,640]{1,0:T(8,128)(2,1)S(1)}) custom-call(s32[8]{0:T(128)S(1)} %stack.35.meta, bf16[5,192,128]{2,1,0:T(8,128)(2,1)S(1)} %bitcast.32, bf16[3,192,128]{2,1,0:T(8,128)(2,1)S(1)} %collective-permute-done.inner, ...), custom_call_target="tpu_custom_call" | custom-call | tf_op jit(solution)/shard_map/pallas_call | solution.py:82
  21.5 3.6 %collective-permute-done.3.outer = bf16[3,192,128]{2,1,0:T(8,128)(2,1)S(1)} collective-permute-done((bf16[3,192,128]{2,1,0:T(8,128)(2,1)S(1)}, bf16[3,192,128]{2,1,0:T(8,128)(2,1)S(1)}, u32[]{:S(2)}, u32[]{:S(2)}) %collective-permute-start.3) | collective-permute-done | bytes 147488 | tf_op jit(solution)/shard_map/ppermute | solution.py:73
  25.6 5.3 %collective-permute-start.4 = (bf16[5,192,128]{2,1,0:T(8,128)(2,1)S(1)}, bf16[5,192,128]{2,1,0:T(8,128)(2,1)S(1)}, u32[]{:S(2)}, u32[]{:S(2)}) collective-permute-start(bf16[5,192,128]{2,1,0:T(8,128)(2,1)S(1)} %shard_map.156.third), channel_id=1, source_target_pairs={{0,192},{64,0},{128,64},{192,128},{1,193},{65,1},{129,65},{193,129... | collective-permute-start | bytes 737288 | tf_op jit(solution)/shard_map/ppermute | solution.py:516
  31.0 3.1 %collective-permute-done.4.cot.cot_2 = bf16[5,192,128]{2,1,0:T(8,128)(2,1)S(1)} collective-permute-done((bf16[5,192,128]{2,1,0:T(8,128)(2,1)S(1)}, bf16[5,192,128]{2,1,0:T(8,128)(2,1)S(1)}, u32[]{:S(2)}, u32[]{:S(2)}) %collective-permute-start.4) | collective-permute-done | bytes 245792 | tf_op jit(solution)/shard_map/ppermute | solution.py:516
  34.7 4.4 %collective-permute-start.5 = (bf16[3,192,128]{2,1,0:T(8,128)(2,1)S(1)}, bf16[3,192,128]{2,1,0:T(8,128)(2,1)S(1)}, u32[]{:S(2)}, u32[]{:S(2)}) collective-permute-start(bf16[3,192,128]{2,1,0:T(8,128)(2,1)S(1)} %get-tuple-element.60), channel_id=1, source_target_pairs={{0,1},{1,0},{2,3},{3,2},{4,5},{5,4},{6,7},{7,6},{8,9},{9,8},{10,11... | collective-permute-start | bytes 442376 | tf_op jit(solution)/shard_map/ppermute | solution.py:74
  40.0 3.6 %collective-permute-done.6.outer = bf16[3,192,128]{2,1,0:T(8,128)(2,1)S(1)} collective-permute-done((bf16[3,192,128]{2,1,0:T(8,128)(2,1)S(1)}, bf16[3,192,128]{2,1,0:T(8,128)(2,1)S(1)}, u32[]{:S(2)}, u32[]{:S(2)}) %collective-permute-start.6) | collective-permute-done | bytes 147488 | tf_op jit(solution)/shard_map/ppermute | solution.py:73
  44.2 3.5 %collective-permute-start.7 = (bf16[5,192,128]{2,1,0:T(8,128)(2,1)S(1)}, bf16[5,192,128]{2,1,0:T(8,128)(2,1)S(1)}, u32[]{:S(2)}, u32[]{:S(2)}) collective-permute-start(bf16[5,192,128]{2,1,0:T(8,128)(2,1)S(1)} %shard_map.158.second), channel_id=1, source_target_pairs={{0,192},{64,0},{128,64},{192,128},{1,193},{65,1},{129,65},{193,129... | collective-permute-start | bytes 737288 | tf_op jit(solution)/shard_map/ppermute | solution.py:516
  47.7 3.1 %collective-permute-done.7.cot.cot_1 = bf16[5,192,128]{2,1,0:T(8,128)(2,1)S(1)} collective-permute-done((bf16[5,192,128]{2,1,0:T(8,128)(2,1)S(1)}, bf16[5,192,128]{2,1,0:T(8,128)(2,1)S(1)}, u32[]{:S(2)}, u32[]{:S(2)}) %collective-permute-start.7) | collective-permute-done | bytes 245792 | tf_op jit(solution)/shard_map/ppermute | solution.py:516
  51.4 4.5 %collective-permute-start.8 = (bf16[3,192,128]{2,1,0:T(8,128)(2,1)S(1)}, bf16[3,192,128]{2,1,0:T(8,128)(2,1)S(1)}, u32[]{:S(2)}, u32[]{:S(2)}) collective-permute-start(bf16[3,192,128]{2,1,0:T(8,128)(2,1)S(1)} %get-tuple-element.63), channel_id=1, source_target_pairs={{0,1},{1,0},{2,3},{3,2},{4,5},{5,4},{6,7},{7,6},{8,9},{9,8},{10,11... | collective-permute-start | bytes 442376 | tf_op jit(solution)/shard_map/ppermute | solution.py:74
  56.9 3.6 %collective-permute-done.9.outer = bf16[3,192,128]{2,1,0:T(8,128)(2,1)S(1)} collective-permute-done((bf16[3,192,128]{2,1,0:T(8,128)(2,1)S(1)}, bf16[3,192,128]{2,1,0:T(8,128)(2,1)S(1)}, u32[]{:S(2)}, u32[]{:S(2)}) %collective-permute-start.9) | collective-permute-done | bytes 147488 | tf_op jit(solution)/shard_map/ppermute | solution.py:73
  61.0 3.5 %collective-permute-start.10 = (bf16[5,192,128]{2,1,0:T(8,128)(2,1)S(1)}, bf16[5,192,128]{2,1,0:T(8,128)(2,1)S(1)}, u32[]{:S(2)}, u32[]{:S(2)}) collective-permute-start(bf16[5,192,128]{2,1,0:T(8,128)(2,1)S(1)} %shard_map.160.first), channel_id=1, source_target_pairs={{0,192},{64,0},{128,64},{192,128},{1,193},{65,1},{129,65},{193,129... | collective-permute-start | bytes 737288 | tf_op jit(solution)/shard_map/ppermute | solution.py:516
  64.5 3.6 %collective-permute-done.10.cot_0.cot = bf16[5,192,128]{2,1,0:T(8,128)(2,1)S(1)} collective-permute-done((bf16[5,192,128]{2,1,0:T(8,128)(2,1)S(1)}, bf16[5,192,128]{2,1,0:T(8,128)(2,1)S(1)}, u32[]{:S(2)}, u32[]{:S(2)}) %collective-permute-start.10) | collective-permute-done | bytes 245792 | tf_op jit(solution)/shard_map/ppermute | solution.py:516
  68.1 2.8 %shard_map.161 = (bf16[5,192,128]{2,1,0:T(8,128)(2,1)S(1)}, bf16[3,192,128]{2,1,0:T(8,128)(2,1)S(1)}, bf16[3,192,128]{2,1,0:T(8,128)(2,1)S(1)}, bf16[104,768]{1,...) custom-call(s32[8]{0:T(128)S(1)} %stack.35.meta, ...), custom_call_target="tpu_custom_call" | custom-call | tf_op jit(solution)/shard_map/pallas_call | solution.py:82
  71.0 4.4 %collective-permute-start.12 = (bf16[104,768]{1,0:T(8,128)(2,1)S(1)}, bf16[104,768]{1,0:T(8,128)(2,1)S(1)}, u32[]{:S(2)}, u32[]{:S(2)}) collective-permute-start(bf16[104,768]{1,0:T(8,128)(2,1)S(1)} %get-tuple-element.68), channel_id=1, source_target_pairs={{0,1},{1,0},{2,3},{3,2},{4,5},{5,4},{6,7},{7,6},{8,9},{9,8},{10,11... | collective-permute-start | bytes 479240 | tf_op jit(solution)/shard_map/ppermute | solution.py:68
  75.4 1.5 %collective-permute-start.13 = (bf16[104,768]{1,0:T(8,128)(2,1)S(1)}, bf16[104,768]{1,0:T(8,128)(2,1)S(1)}, u32[]{:S(2)}, u32[]{:S(2)}) collective-permute-start(bf16[104,768]{1,0:T(8,128)(2,1)S(1)} %get-tuple-element.69), channel_id=1, source_target_pairs={{0,9},{1,2},{2,11},{3,0},{4,13},{5,6},{6,15},{7,4},{8,1},{9,10},{1... | collective-permute-start | bytes 479240 | tf_op jit(solution)/shard_map/ppermute | solution.py:68
  77.0 3.5 %collective-permute-done.13 = bf16[104,768]{1,0:T(8,128)(2,1)S(1)} collective-permute-done((bf16[104,768]{1,0:T(8,128)(2,1)S(1)}, bf16[104,768]{1,0:T(8,128)(2,1)S(1)}, u32[]{:S(2)}, u32[]{:S(2)}) %collective-permute-start.13) | collective-permute-done | bytes 159776 | tf_op jit(solution)/shard_map/ppermute | solution.py:68
  80.6 1.8 %collective-permute-start.15 = (bf16[3,192,128]{2,1,0:T(8,128)(2,1)S(1)}, bf16[3,192,128]{2,1,0:T(8,128)(2,1)S(1)}, u32[]{:S(2)}, u32[]{:S(2)}) collective-permute-start(bf16[3,192,128]{2,1,0:T(8,128)(2,1)S(1)} %get-tuple-element.73), channel_id=1, source_target_pairs={{0,1},{1,0},{2,3},{3,2},{4,5},{5,4},{6,7},{7,6},{8,9},{9,8},{10,11... | collective-permute-start | bytes 442376 | tf_op jit(solution)/shard_map/ppermute | solution.py:74
  82.4 5.1 %collective-permute-done.14 = bf16[104,768]{1,0:T(8,128)(2,1)S(1)} collective-permute-done((bf16[104,768]{1,0:T(8,128)(2,1)S(1)}, bf16[104,768]{1,0:T(8,128)(2,1)S(1)}, u32[]{:S(2)}, u32[]{:S(2)}) %collective-permute-start.14) | collective-permute-done | bytes 159776 | tf_op jit(solution)/shard_map/ppermute | solution.py:68
  88.3 2.2 %shard_map.162 = (bf16[5,192,128]{2,1,0:T(8,128)(2,1)S(1)}, bf16[2,192,128]{2,1,0:T(8,128)(2,1)S(1)}) custom-call(s32[8]{0:T(128)S(1)} %stack.35.meta, s32[5]{0:T(128)S(1)} %copy-done.4, s32[3]{0:T(128)S(1)} %copy-done.6, bf16[5,192,128]{2,1,0:T(8,128)(2,1)S(1)} %get-tuple-element.76.field, bf16[3,192,128]{2,1,0:T(8,128)(2,1)S(1)} %collective-permute-done.15.inner, ...), custom_call_target="tpu_custom_call" | custom-call | tf_op jit(solution)/shard_map/pallas_call | solution.py:82
  90.5 2.5 %collective-permute-done.17 = bf16[104,768]{1,0:T(8,128)(2,1)S(1)} collective-permute-done((bf16[104,768]{1,0:T(8,128)(2,1)S(1)}, bf16[104,768]{1,0:T(8,128)(2,1)S(1)}, u32[]{:S(2)}, u32[]{:S(2)}) %collective-permute-start.17) | collective-permute-done | bytes 159776 | tf_op jit(solution)/shard_map/ppermute | solution.py:68
  93.1 2.2 %collective-permute-start.18 = (bf16[104,768]{1,0:T(8,128)(2,1)S(1)}, bf16[104,768]{1,0:T(8,128)(2,1)S(1)}, u32[]{:S(2)}, u32[]{:S(2)}) collective-permute-start(bf16[104,768]{1,0:T(8,128)(2,1)S(1)} %add_convert_fusion.2), channel_id=1, source_target_pairs={{0,24},{1,3},{2,26},{3,1},{4,28},{5,7},{6,30},{7,5},{8,16},{9,11},... | collective-permute-start | bytes 479240 | tf_op jit(solution)/shard_map/ppermute | solution.py:68
  95.3 1.8 %collective-permute-start.19 = (bf16[2,192,128]{2,1,0:T(8,128)(2,1)S(1)}, bf16[2,192,128]{2,1,0:T(8,128)(2,1)S(1)}, u32[]{:S(2)}, u32[]{:S(2)}) collective-permute-start(bf16[2,192,128]{2,1,0:T(8,128)(2,1)S(1)} %get-tuple-element.83), channel_id=1, source_target_pairs={{0,1},{1,2},{2,3},{3,4},{4,5},{5,6},{6,7},{7,8},{8,9},{9,10},{10,1... | collective-permute-start | bytes 294920 | tf_op jit(solution)/shard_map/ppermute | solution.py:554
  98.7 4.5 %collective-permute-start.20 = (bf16[104,768]{1,0:T(8,128)(2,1)S(1)}, bf16[104,768]{1,0:T(8,128)(2,1)S(1)}, u32[]{:S(2)}, u32[]{:S(2)}) collective-permute-start(bf16[104,768]{1,0:T(8,128)(2,1)S(1)} %add_convert_fusion.1), channel_id=1, source_target_pairs={{0,56},{1,7},{2,58},{3,5},{4,60},{5,3},{6,62},{7,1},{8,48},{9,15},... | collective-permute-start | bytes 479240 | tf_op jit(solution)/shard_map/ppermute | solution.py:68
  103.2 1.3 %shard_map.163 = bf16[3,192,128]{2,1,0:T(8,128)(2,1)} custom-call(s32[8]{0:T(128)S(1)} %stack.35.meta, s32[3]{0:T(128)S(1)} %copy-done.6, bf16[5,192,128]{2,1,0:T(8,128)(2,1)S(1)} %get-tuple-element.85.result, bf16[2,192,128]{2,1,0:T(8,128)(2,1)S(1)} %collective-permute-done.19.arrived), custom_call_target="tpu_custom_call" | custom-call | tf_op jit(solution)/shard_map/pallas_call | solution.py:82
  104.6 1.6 %collective-permute-done.20 = bf16[104,768]{1,0:T(8,128)(2,1)S(1)} collective-permute-done((bf16[104,768]{1,0:T(8,128)(2,1)S(1)}, bf16[104,768]{1,0:T(8,128)(2,1)S(1)}, u32[]{:S(2)}, u32[]{:S(2)}) %collective-permute-start.20) | collective-permute-done | bytes 159776 | tf_op jit(solution)/shard_map/ppermute | solution.py:68
  106.2 5.2 %collective-permute-start.23 = (bf16[104,768]{1,0:T(8,128)(2,1)S(1)}, bf16[104,768]{1,0:T(8,128)(2,1)S(1)}, u32[]{:S(2)}, u32[]{:S(2)}) collective-permute-start(bf16[104,768]{1,0:T(8,128)(2,1)S(1)} %add_convert_fusion.keep), channel_id=1, source_target_pairs={{0,3},{1,8},{2,1},{3,10},{4,7},{5,12},{6,5},{7,14},{8,11},{9,0},{1... | collective-permute-start | bytes 479240 | tf_op jit(solution)/shard_map/ppermute | solution.py:68
  112.1 1.3 %collective-permute-start.21 = (bf16[104,768]{1,0:T(8,128)(2,1)S(1)}, bf16[104,768]{1,0:T(8,128)(2,1)S(1)}, u32[]{:S(2)}, u32[]{:S(2)}) collective-permute-start(bf16[104,768]{1,0:T(8,128)(2,1)S(1)} %add_convert_fusion.keep), channel_id=1, source_target_pairs={{0,2},{1,9},{2,0},{3,11},{4,6},{5,13},{6,4},{7,15},{8,10},{9,1},{1... | collective-permute-start | bytes 479240 | tf_op jit(solution)/shard_map/ppermute | solution.py:68
  113.6 4.1 %collective-permute-done.21.near = bf16[104,768]{1,0:T(8,128)(2,1)S(1)} collective-permute-done((bf16[104,768]{1,0:T(8,128)(2,1)S(1)}, bf16[104,768]{1,0:T(8,128)(2,1)S(1)}, u32[]{:S(2)}, u32[]{:S(2)}) %collective-permute-start.21) | collective-permute-done | bytes 159776 | tf_op jit(solution)/shard_map/ppermute | solution.py:68
  117.7 1.7 %shard_map.164 = (f32[49,192]{1,0:T(8,128)S(1)}, f32[1,192]{1,0:T(1,128)}, f32[192,768]{1,0:T(8,128)}, f32[1,768]{1,0:T(1,128)}, f32[192,768]{1,0:T(8,128)}, /*index=5*/f32[1,192]{1,0:T(1,128)}) custom-call(s32[8]{0:T(128)S(1)} %stack.35.meta, bf16[104,768]{1,0:T(8,128)(2,1)S(1)} %add_convert_fusion.keep, bf16[104,768]{1,0:T(8,128)(2,1)S(1)} %collective-permute-done.21.near, ...), custom_call_target="tpu_custom_call" | custom-call | tf_op jit(solution)/shard_map/pallas_call | solution.py:82
  (65 shorter events, 16.0 us)
Async XLA Ops:
  0.6 10.1 %copy-start.7 = (f32[1,49,192]{2,0,1:T(1,128)S(1)}, f32[1,49,192]{2,0,1:T(1,128)}, u32[]{:S(2)}) copy-start(f32[1,49,192]{2,0,1:T(1,128)} %param.14) | copy-start | bytes 112900
  1.7 13.0 %collective-permute-start.1 = (bf16[3,192,128]{2,1,0:T(8,128)(2,1)S(1)}, bf16[3,192,128]{2,1,0:T(8,128)(2,1)S(1)}, u32[]{:S(2)}, u32[]{:S(2)}) collective-permute-start(bf16[3,192,128]{2,1,0:T(8,128)(2,1)S(1)} %get-tuple-element.109), channel_id=1, source_target_pairs={{0,63},{1,2},{2,1},{3,4},{4,3},{5,6},{6,5},{7,8},{8,7},{9,10},{10,... | collective-permute-start | bytes 442376 | tf_op jit(solution)/shard_map/ppermute | solution.py:73
  4.4 6.5 %copy-start.9 = (f32[1,192]{1,0:T(1,128)S(1)}, f32[1,192]{1,0:T(1,128)}, u32[]{:S(2)}) copy-start(f32[1,192]{1,0:T(1,128)} %param.15) | copy-start | bytes 2308
  4.4 10.3 %collective-permute-start = (bf16[3,192,128]{2,1,0:T(8,128)(2,1)S(1)}, bf16[3,192,128]{2,1,0:T(8,128)(2,1)S(1)}, u32[]{:S(2)}, u32[]{:S(2)}) collective-permute-start(bf16[3,192,128]{2,1,0:T(8,128)(2,1)S(1)} %get-tuple-element.110), channel_id=1, source_target_pairs={{0,1},{1,0},{2,3},{3,2},{4,5},{5,4},{6,7},{7,6},{8,9},{9,8},{10,11... | collective-permute-start | bytes 442376 | tf_op jit(solution)/shard_map/ppermute | solution.py:74
  10.9 0.7 copy-start.5
  11.8 1.0 copy-start.3
  12.7 0.7 copy-start.8
  12.9 1.0 copy-start
  14.1 0.9 copy-start.1
  15.1 3.6 %copy-start.2 = (bf16[5,192,128]{2,1,0:T(8,128)(2,1)S(1)}, bf16[5,192,128]{2,1,0:T(8,128)(2,1)}, u32[]{:S(2)}) copy-start(bf16[5,192,128]{2,1,0:T(8,128)(2,1)} %cot_top.1) | copy-start | bytes 737284
  19.9 1.7 %collective-permute-start.2 = (bf16[3,192,128]{2,1,0:T(8,128)(2,1)S(1)}, bf16[3,192,128]{2,1,0:T(8,128)(2,1)S(1)}, u32[]{:S(2)}, u32[]{:S(2)}) collective-permute-start(bf16[3,192,128]{2,1,0:T(8,128)(2,1)S(1)} %get-tuple-element.56), channel_id=1, source_target_pairs={{0,1},{1,0},{2,3},{3,2},{4,5},{5,4},{6,7},{7,6},{8,9},{9,8},{10,11... | collective-permute-start | bytes 442376 | tf_op jit(solution)/shard_map/ppermute | solution.py:74
  20.5 4.6 %collective-permute-start.3 = (bf16[3,192,128]{2,1,0:T(8,128)(2,1)S(1)}, bf16[3,192,128]{2,1,0:T(8,128)(2,1)S(1)}, u32[]{:S(2)}, u32[]{:S(2)}) collective-permute-start(bf16[3,192,128]{2,1,0:T(8,128)(2,1)S(1)} %get-tuple-element.57), channel_id=1, source_target_pairs={{0,63},{1,2},{2,1},{3,4},{4,3},{5,6},{6,5},{7,8},{8,7},{9,10},{10,... | collective-permute-start | bytes 442376 | tf_op jit(solution)/shard_map/ppermute | solution.py:73
  25.6 8.5 %collective-permute-start.4 = (bf16[5,192,128]{2,1,0:T(8,128)(2,1)S(1)}, bf16[5,192,128]{2,1,0:T(8,128)(2,1)S(1)}, u32[]{:S(2)}, u32[]{:S(2)}) collective-permute-start(bf16[5,192,128]{2,1,0:T(8,128)(2,1)S(1)} %shard_map.156.third), channel_id=1, source_target_pairs={{0,192},{64,0},{128,64},{192,128},{1,193},{65,1},{129,65},{193,129... | collective-permute-start | bytes 737288 | tf_op jit(solution)/shard_map/ppermute | solution.py:516
  34.7 5.4 %collective-permute-start.5 = (bf16[3,192,128]{2,1,0:T(8,128)(2,1)S(1)}, bf16[3,192,128]{2,1,0:T(8,128)(2,1)S(1)}, u32[]{:S(2)}, u32[]{:S(2)}) collective-permute-start(bf16[3,192,128]{2,1,0:T(8,128)(2,1)S(1)} %get-tuple-element.60), channel_id=1, source_target_pairs={{0,1},{1,0},{2,3},{3,2},{4,5},{5,4},{6,7},{7,6},{8,9},{9,8},{10,11... | collective-permute-start | bytes 442376 | tf_op jit(solution)/shard_map/ppermute | solution.py:74
  39.0 4.6 %collective-permute-start.6 = (bf16[3,192,128]{2,1,0:T(8,128)(2,1)S(1)}, bf16[3,192,128]{2,1,0:T(8,128)(2,1)S(1)}, u32[]{:S(2)}, u32[]{:S(2)}) collective-permute-start(bf16[3,192,128]{2,1,0:T(8,128)(2,1)S(1)} %get-tuple-element.61), channel_id=1, source_target_pairs={{0,63},{1,2},{2,1},{3,4},{4,3},{5,6},{6,5},{7,8},{8,7},{9,10},{10,... | collective-permute-start | bytes 442376 | tf_op jit(solution)/shard_map/ppermute | solution.py:73
  44.2 6.6 %collective-permute-start.7 = (bf16[5,192,128]{2,1,0:T(8,128)(2,1)S(1)}, bf16[5,192,128]{2,1,0:T(8,128)(2,1)S(1)}, u32[]{:S(2)}, u32[]{:S(2)}) collective-permute-start(bf16[5,192,128]{2,1,0:T(8,128)(2,1)S(1)} %shard_map.158.second), channel_id=1, source_target_pairs={{0,192},{64,0},{128,64},{192,128},{1,193},{65,1},{129,65},{193,129... | collective-permute-start | bytes 737288 | tf_op jit(solution)/shard_map/ppermute | solution.py:516
  51.4 5.5 %collective-permute-start.8 = (bf16[3,192,128]{2,1,0:T(8,128)(2,1)S(1)}, bf16[3,192,128]{2,1,0:T(8,128)(2,1)S(1)}, u32[]{:S(2)}, u32[]{:S(2)}) collective-permute-start(bf16[3,192,128]{2,1,0:T(8,128)(2,1)S(1)} %get-tuple-element.63), channel_id=1, source_target_pairs={{0,1},{1,0},{2,3},{3,2},{4,5},{5,4},{6,7},{7,6},{8,9},{9,8},{10,11... | collective-permute-start | bytes 442376 | tf_op jit(solution)/shard_map/ppermute | solution.py:74
  55.9 4.6 %collective-permute-start.9 = (bf16[3,192,128]{2,1,0:T(8,128)(2,1)S(1)}, bf16[3,192,128]{2,1,0:T(8,128)(2,1)S(1)}, u32[]{:S(2)}, u32[]{:S(2)}) collective-permute-start(bf16[3,192,128]{2,1,0:T(8,128)(2,1)S(1)} %get-tuple-element.64), channel_id=1, source_target_pairs={{0,63},{1,2},{2,1},{3,4},{4,3},{5,6},{6,5},{7,8},{8,7},{9,10},{10,... | collective-permute-start | bytes 442376 | tf_op jit(solution)/shard_map/ppermute | solution.py:73
  61.0 7.1 %collective-permute-start.10 = (bf16[5,192,128]{2,1,0:T(8,128)(2,1)S(1)}, bf16[5,192,128]{2,1,0:T(8,128)(2,1)S(1)}, u32[]{:S(2)}, u32[]{:S(2)}) collective-permute-start(bf16[5,192,128]{2,1,0:T(8,128)(2,1)S(1)} %shard_map.160.first), channel_id=1, source_target_pairs={{0,192},{64,0},{128,64},{192,128},{1,193},{65,1},{129,65},{193,129... | collective-permute-start | bytes 737288 | tf_op jit(solution)/shard_map/ppermute | solution.py:516
  70.9 6.0 %collective-permute-start.11 = (bf16[104,768]{1,0:T(8,128)(2,1)S(1)}, bf16[104,768]{1,0:T(8,128)(2,1)S(1)}, u32[]{:S(2)}, u32[]{:S(2)}) collective-permute-start(bf16[104,768]{1,0:T(8,128)(2,1)S(1)} %get-tuple-element.67), channel_id=1, source_target_pairs={{0,2},{1,9},{2,0},{3,11},{4,6},{5,13},{6,4},{7,15},{8,10},{9,1},{1... | collective-permute-start | bytes 479240 | tf_op jit(solution)/shard_map/ppermute | solution.py:68
  71.0 5.9 %collective-permute-start.12 = (bf16[104,768]{1,0:T(8,128)(2,1)S(1)}, bf16[104,768]{1,0:T(8,128)(2,1)S(1)}, u32[]{:S(2)}, u32[]{:S(2)}) collective-permute-start(bf16[104,768]{1,0:T(8,128)(2,1)S(1)} %get-tuple-element.68), channel_id=1, source_target_pairs={{0,1},{1,0},{2,3},{3,2},{4,5},{5,4},{6,7},{7,6},{8,9},{9,8},{10,11... | collective-permute-start | bytes 479240 | tf_op jit(solution)/shard_map/ppermute | solution.py:68
  75.4 5.0 %collective-permute-start.13 = (bf16[104,768]{1,0:T(8,128)(2,1)S(1)}, bf16[104,768]{1,0:T(8,128)(2,1)S(1)}, u32[]{:S(2)}, u32[]{:S(2)}) collective-permute-start(bf16[104,768]{1,0:T(8,128)(2,1)S(1)} %get-tuple-element.69), channel_id=1, source_target_pairs={{0,9},{1,2},{2,11},{3,0},{4,13},{5,6},{6,15},{7,4},{8,1},{9,10},{1... | collective-permute-start | bytes 479240 | tf_op jit(solution)/shard_map/ppermute | solution.py:68
  80.5 7.1 %collective-permute-start.14 = (bf16[104,768]{1,0:T(8,128)(2,1)S(1)}, bf16[104,768]{1,0:T(8,128)(2,1)S(1)}, u32[]{:S(2)}, u32[]{:S(2)}) collective-permute-start(bf16[104,768]{1,0:T(8,128)(2,1)S(1)} %add_convert_fusion.4), channel_id=1, source_target_pairs={{0,6},{1,25},{2,4},{3,27},{4,2},{5,29},{6,0},{7,31},{8,14},{9,17},... | collective-permute-start | bytes 479240 | tf_op jit(solution)/shard_map/ppermute | solution.py:68
  80.6 7.0 %collective-permute-start.15 = (bf16[3,192,128]{2,1,0:T(8,128)(2,1)S(1)}, bf16[3,192,128]{2,1,0:T(8,128)(2,1)S(1)}, u32[]{:S(2)}, u32[]{:S(2)}) collective-permute-start(bf16[3,192,128]{2,1,0:T(8,128)(2,1)S(1)} %get-tuple-element.73), channel_id=1, source_target_pairs={{0,1},{1,0},{2,3},{3,2},{4,5},{5,4},{6,7},{7,6},{8,9},{9,8},{10,11... | collective-permute-start | bytes 442376 | tf_op jit(solution)/shard_map/ppermute | solution.py:74
  82.4 5.2 %collective-permute-start.16 = (bf16[3,192,128]{2,1,0:T(8,128)(2,1)S(1)}, bf16[3,192,128]{2,1,0:T(8,128)(2,1)S(1)}, u32[]{:S(2)}, u32[]{:S(2)}) collective-permute-start(bf16[3,192,128]{2,1,0:T(8,128)(2,1)S(1)} %get-tuple-element.74), channel_id=1, source_target_pairs={{0,63},{1,2},{2,1},{3,4},{4,3},{5,6},{6,5},{7,8},{8,7},{9,10},{10,... | collective-permute-start | bytes 442376 | tf_op jit(solution)/shard_map/ppermute | solution.py:73
  87.6 5.4 %collective-permute-start.17 = (bf16[104,768]{1,0:T(8,128)(2,1)S(1)}, bf16[104,768]{1,0:T(8,128)(2,1)S(1)}, u32[]{:S(2)}, u32[]{:S(2)}) collective-permute-start(bf16[104,768]{1,0:T(8,128)(2,1)S(1)} %add_convert_fusion.3), channel_id=1, source_target_pairs={{0,8},{1,57},{2,10},{3,59},{4,12},{5,61},{6,14},{7,63},{8,0},{9,49... | collective-permute-start | bytes 479240 | tf_op jit(solution)/shard_map/ppermute | solution.py:68
  93.1 4.8 %collective-permute-start.18 = (bf16[104,768]{1,0:T(8,128)(2,1)S(1)}, bf16[104,768]{1,0:T(8,128)(2,1)S(1)}, u32[]{:S(2)}, u32[]{:S(2)}) collective-permute-start(bf16[104,768]{1,0:T(8,128)(2,1)S(1)} %add_convert_fusion.2), channel_id=1, source_target_pairs={{0,24},{1,3},{2,26},{3,1},{4,28},{5,7},{6,30},{7,5},{8,16},{9,11},... | collective-permute-start | bytes 479240 | tf_op jit(solution)/shard_map/ppermute | solution.py:68
  95.3 3.4 %collective-permute-start.19 = (bf16[2,192,128]{2,1,0:T(8,128)(2,1)S(1)}, bf16[2,192,128]{2,1,0:T(8,128)(2,1)S(1)}, u32[]{:S(2)}, u32[]{:S(2)}) collective-permute-start(bf16[2,192,128]{2,1,0:T(8,128)(2,1)S(1)} %get-tuple-element.83), channel_id=1, source_target_pairs={{0,1},{1,2},{2,3},{3,4},{4,5},{5,6},{6,7},{7,8},{8,9},{9,10},{10,1... | collective-permute-start | bytes 294920 | tf_op jit(solution)/shard_map/ppermute | solution.py:554
  98.7 7.4 %collective-permute-start.20 = (bf16[104,768]{1,0:T(8,128)(2,1)S(1)}, bf16[104,768]{1,0:T(8,128)(2,1)S(1)}, u32[]{:S(2)}, u32[]{:S(2)}) collective-permute-start(bf16[104,768]{1,0:T(8,128)(2,1)S(1)} %add_convert_fusion.1), channel_id=1, source_target_pairs={{0,56},{1,7},{2,58},{3,5},{4,60},{5,3},{6,62},{7,1},{8,48},{9,15},... | collective-permute-start | bytes 479240 | tf_op jit(solution)/shard_map/ppermute | solution.py:68
  106.2 7.4 %collective-permute-start.23 = (bf16[104,768]{1,0:T(8,128)(2,1)S(1)}, bf16[104,768]{1,0:T(8,128)(2,1)S(1)}, u32[]{:S(2)}, u32[]{:S(2)}) collective-permute-start(bf16[104,768]{1,0:T(8,128)(2,1)S(1)} %add_convert_fusion.keep), channel_id=1, source_target_pairs={{0,3},{1,8},{2,1},{3,10},{4,7},{5,12},{6,5},{7,14},{8,11},{9,0},{1... | collective-permute-start | bytes 479240 | tf_op jit(solution)/shard_map/ppermute | solution.py:68
  111.4 2.2 %collective-permute-start.22 = (bf16[104,768]{1,0:T(8,128)(2,1)S(1)}, bf16[104,768]{1,0:T(8,128)(2,1)S(1)}, u32[]{:S(2)}, u32[]{:S(2)}) collective-permute-start(bf16[104,768]{1,0:T(8,128)(2,1)S(1)} %add_convert_fusion.keep), channel_id=1, source_target_pairs={{0,1},{1,0},{2,3},{3,2},{4,5},{5,4},{6,7},{7,6},{8,9},{9,8},{10,11... | collective-permute-start | bytes 479240 | tf_op jit(solution)/shard_map/ppermute | solution.py:68
  112.1 5.6 %collective-permute-start.21 = (bf16[104,768]{1,0:T(8,128)(2,1)S(1)}, bf16[104,768]{1,0:T(8,128)(2,1)S(1)}, u32[]{:S(2)}, u32[]{:S(2)}) collective-permute-start(bf16[104,768]{1,0:T(8,128)(2,1)S(1)} %add_convert_fusion.keep), channel_id=1, source_target_pairs={{0,2},{1,9},{2,0},{3,11},{4,6},{5,13},{6,4},{7,15},{8,10},{9,1},{1... | collective-permute-start | bytes 479240 | tf_op jit(solution)/shard_map/ppermute | solution.py:68
  (2 other events, 1.3 us)

commit v3 on v2

--- a/solution.py
+++ b/solution.py
@@ -23,8 +23,9 @@
 f32 = jnp.float32
 bf16 = jnp.bfloat16
 
-SECTION, ODD, KEEP, NEAR, MATE, FAR, OFFSET, INSIDE = range(8)
+SECTION, ODD, KEEP, NEAR, MATE, FAR, OFFSET, INSIDE, LAND = range(9)
 PLACES = 8
+OWNERS = LAND + 5
 
 
 def split_tile(tile):
@@ -113,7 +114,17 @@
     outer_ref[...] = jnp.where(odd, tail, head)
 
 
-def prepare_kernel(cols, forth_ref, back_ref):
+def prepare_kernel(
+    kernel, gain, layer, bias, up, down, cols, forth_ref, back_ref, up_t_ref, down_t_ref, bias_ref, lines_ref
+):
+    lines_ref[...] = jnp.zeros_like(lines_ref)
+    lines_ref[: KS * KS] = kernel[...]
+    lines_ref[KS * KS : KS * KS + 1] = gain[...]
+    lines_ref[KS * KS + 1 : KS * KS + 2] = layer[...]
+    cols[...] = jnp.transpose(lines_ref[...])
+    up_t_ref[...] = jnp.transpose(up[...].astype(f32)).astype(bf16)
+    down_t_ref[...] = jnp.transpose(down[...].astype(f32)).astype(bf16)
+    bias_ref[...] = jnp.transpose(jnp.broadcast_to(bias[...], (8, bias.shape[1])))
     high = cols[...].astype(bf16)
     low = (cols[...] - high.astype(f32)).astype(bf16)
     chans, taps = cols.shape
@@ -189,7 +200,7 @@
     chunk = 128
     for first in range(0, units, chunk):
         part = slice(first, first + chunk)
-        preact = jnp.dot(up_t[part], normed_ref[...], preferred_element_type=f32) + bias[part]
+        preact = jnp.dot(up_t[part], normed_ref[...], preferred_element_type=f32) + bias[part, :1]
         square = preact * preact
         hyper = jnp.tanh(preact * (tanh_root + tanh_root * cubic_coef * square))
         half = 0.5 + 0.5 * hyper
@@ -200,13 +211,13 @@
         slope_ref[part] = slope.astype(bf16)
 
 
-def mlp_backward(cots, land, cols, down_t, up, slope, nhat, inv, out_ref, low_ref, field_ref, sums=None):
+def mlp_backward(cots, meta, cols, down_t, up, slope, nhat, inv, out_ref, low_ref, field_ref, sums=None):
     width = cots[0].shape[1]
     count = len(cots)
     gain = cols[:, KS * KS : KS * KS + 1]
     layer = cols[:, KS * KS + 1 : KS * KS + 2]
     for row in range(count):
-        wet = land[row].astype(f32)
+        wet = meta[LAND + row].astype(f32)
         out_ref[:, row * width : (row + 1) * width] = (cots[row] * layer * wet).astype(bf16)
     units = down_t.shape[0]
     chunk = 128
@@ -237,12 +248,12 @@
 
 
 def turn_kernel(
-    section, meta, land, cot, cols, down_t, up, slope, nhat, inv, field_ref, inner_ref, outer_ref, out_ref, low_ref
+    section, meta, cot, cols, down_t, up, slope, nhat, inv, field_ref, inner_ref, outer_ref, out_ref, low_ref
 ):
     @pl.when(meta[SECTION] == section)
     def _():
         cots = [cot[row].astype(f32) for row in range(cot.shape[0])]
-        mlp_backward(cots, land, cols, down_t, up, slope, nhat, inv, out_ref, low_ref, field_ref)
+        mlp_backward(cots, meta, cols, down_t, up, slope, nhat, inv, out_ref, low_ref, field_ref)
         edges(meta[ODD] == 1, field_ref, inner_ref, outer_ref)
 
 
@@ -268,7 +279,7 @@
 
 
 def last_conv_kernel(
-    meta, land, owners, field, inner, outer, cot, taps_mat, third, second, first, result_ref, sent_ref, rows_ref
+    meta, field, inner, outer, cot, taps_mat, third, second, first, result_ref, sent_ref, rows_ref
 ):
     for section, kept in ((3, third), (2, second), (1, first)):
 
@@ -284,9 +295,9 @@
     rank = jnp.int32(0)
     for local in range(result_ref.shape[0]):
         kept = jnp.bool_(False)
-        for slot in range(owners.shape[0]):
-            kept = kept | (owners[slot] == meta[OFFSET] + local)
-        sent = (land[local] == 1) & jnp.logical_not(kept)
+        for slot in range(OWNERS, meta.shape[0]):
+            kept = kept | (meta[slot] == meta[OFFSET] + local)
+        sent = (meta[LAND + local] == 1) & jnp.logical_not(kept)
         for place in range(CAP):
 
             @pl.when(sent & (rank == place))
@@ -296,19 +307,18 @@
         rank = rank + sent.astype(jnp.int32)
 
 
-def slots_kernel(meta, owners, result, arrived, slots_ref):
+def slots_kernel(meta, result, arrived, slots_ref):
     for slot in range(slots_ref.shape[0]):
         slots_ref[slot] = arrived[min(slot, CAP - 1)]
         for local in range(result.shape[0]):
 
-            @pl.when(owners[slot] == meta[OFFSET] + local)
+            @pl.when(meta[OWNERS + slot] == meta[OFFSET] + local)
             def _():
                 slots_ref[slot] = result[local]
 
 
 def last_kernel(
     meta,
-    land,
     cot_top,
     cot_2,
     cot_1,
@@ -351,7 +361,7 @@
 
     cots = [cot_ref[row].astype(f32) for row in range(count)]
     mlp_backward(
-        cots, land, cols, down_t, up, slope, nhat, inv, out_ref, low_ref, field_ref, (bias_ref, gain_ref)
+        cots, meta, cols, down_t, up, slope, nhat, inv, out_ref, low_ref, field_ref, (bias_ref, gain_ref)
     )
     edges(odd, field_ref, field_inner_ref, field_outer_ref)
     gain = cols[:, KS * KS : KS * KS + 1]
@@ -411,10 +421,10 @@
     for place, source in ((KEEP, keep), (NEAR, near), (MATE, mate), (FAR, far)):
         start = pl.multiple_of(meta[place] * part_rows, 8)
         packed_ref[pl.ds(start, part_rows), :] = source[...].astype(f32) * scale
-    chans = up_ref.shape[0]
+    chans = up_ref.shape[1]
     base = 2 * chans
-    up_ref[...] = packed_ref[:chans]
-    down_ref[...] = packed_ref[chans:base]
+    up_ref[0] = packed_ref[:chans]
+    down_ref[0] = packed_ref[chans:base]
     lane = lax.broadcasted_iota(jnp.int32, (PLACES, 128), 1) >> 4
     blocks = chans // BLOCK
     for tap_row in range(KS):
@@ -430,7 +440,7 @@
                 half = jnp.where(lane == block - first, part, half)
             halves.append(half)
         line = jnp.concatenate(halves, axis=1)
-        kernel_ref[tap_row * KS : (tap_row + 1) * KS] = line[:KS, :chans]
+        kernel_ref[0, tap_row * KS : (tap_row + 1) * KS] = line[:KS, :chans]
     bias_ref[...] = packed_ref[base + 16 : base + 17]
     gain_ref[...] = packed_ref[base + 17 : base + 18, :chans]
     scale_ref[...] = packed_ref[base + 17 : base + 18, 256 : 256 + chans]
@@ -452,29 +462,38 @@
     bit_x, bit_z = (x + 1) // 2 % 2, (z + 1) // 2 % 2
     bit = jnp.where(core == 0, bit_x, bit_z)
     mate_bit = jnp.where(core == 0, bit_z, bit_x)
-    meta = jnp.stack(
-        [
-            section_now,
-            core,
-            2 * core + bit,
-            2 * core + 1 - bit,
-            2 * (1 - core) + mate_bit,
-            2 * (1 - core) + 1 - mate_bit,
-            tile_now * count,
-            jnp.where((tile_now == 0) | (tile_now == TILES - 1), 0, 1),
-        ]
-    ).astype(jnp.int32)
+    numbers = [
+        section_now,
+        core,
+        2 * core + bit,
+        2 * core + 1 - bit,
+        2 * (1 - core) + mate_bit,
+        2 * (1 - core) + 1 - mate_bit,
+        tile_now * count,
+        jnp.where((tile_now == 0) | (tile_now == TILES - 1), 0, 1),
+    ]
+    meta = jnp.concatenate([jnp.stack(numbers).astype(jnp.int32), land, owners])
 
     odd = core == 1
     head, tail = source[:MARGIN], source[count - MARGIN :]
     acts_inner, acts_outer = halo(jnp.where(odd, head, tail), jnp.where(odd, tail, head))
-    unused = jnp.zeros((64 - KS * KS - 2, chans), f32)
-    cols = jnp.concatenate([dw_kernel[0], ln_gain, layer_scale, unused]).T
+    up, down = w_up[0], w_down[0]
     taps_shape = shape((chans // BLOCK, KS * BLOCK, 256), bf16)
-    forth, back = call(prepare_kernel, (taps_shape, taps_shape), 0, (cols,), cost=(10**9, 10**7))
-    up, down = w_up[0], w_down[0]
-    up_t, down_t = up.T, down.T
-    bias = b_up.reshape(units, 1)
+    cols, forth, back, up_t, down_t, bias = call(
+        prepare_kernel,
+        (
+            shape((chans, 64), f32),
+            taps_shape,
+            taps_shape,
+            shape((units, chans), bf16),
+            shape((units, chans), bf16),
+            shape((units, 8), f32),
+        ),
+        0,
+        (dw_kernel[0], ln_gain, layer_scale, b_up, up, down),
+        (pltpu.VMEM((64, chans), f32),),
+        cost=(10**9, 10**7),
+    )
 
     padded = pltpu.VMEM((count + PLACES - 1, chans, width), bf16)
     nhat, inv, hidden, slope = call(
@@ -499,8 +518,8 @@
         field, inner, outer = call(
             functools.partial(turn_kernel, section),
             (rows_shape, edge_shape, edge_shape),
-            2,
-            (meta, land, cots[-1], cols, down_t, up, slope, nhat, inv),
+            1,
+            (meta, cots[-1], cols, down_t, up, slope, nhat, inv),
             (outgrads, lowgrads),
         )
         inner, outer = halo(inner, outer)
@@ -515,12 +534,12 @@
         pairs = [(place, (place - 1) % SECTIONS) for place in range(SECTIONS)]
         cots.append(lax.ppermute(result, "section", pairs))
 
-    part = shape(((2 * chans + 32) // 4, units), bf16)
+    part = shape(((2 * chans + 64) // 4, units), bf16)
     field, inner, outer, keep, near, mate, far = call(
         last_kernel,
         (rows_shape, edge_shape, edge_shape, part, part, part, part),
-        2,
-        (meta, land, *cots, cols, layer_scale, down_t, down, up, slope, nhat, inv, hidden)
+        1,
+        (meta, *cots, cols, layer_scale, down_t, down, up, slope, nhat, inv, hidden)
         + (source, acts_inner, acts_outer),
         (
             outgrads,
@@ -528,7 +547,7 @@
             pltpu.VMEM((units, width), f32),
             pltpu.VMEM((chans, width), f32),
             padded,
-            pltpu.VMEM((2 * chans + 32, units), f32),
+            pltpu.VMEM((2 * chans + 64, units), f32),
             pltpu.VMEM((count, chans, width), bf16),
         ),
     )
@@ -538,28 +557,33 @@
     total = added(keep, near, mate, far)
     orders = (("x1", "z1"), ("z0", "z2"), ("z1", "x0"), ("z2", "x1"))
     total, inner, outer = lax.optimization_barrier((total, inner, outer))
-    total = added(total, moved(total, orders[0], False))
+    half = total.shape[0] // 2
+    first = jnp.where(core == 0, x // 2, (z + 2) // 4 % 2) == 0
+    kept = jnp.where(first, total[:half], total[half:])
+    given = jnp.where(first, total[half:], total[:half])
+    total = added(kept, moved(given, orders[0], False))
     inner, outer = halo(inner, outer)
-    total, inner, outer = lax.optimization_barrier((total, inner, outer))
     total = added(total, moved(total, orders[1], False))
     result, sent = call(
         last_conv_kernel,
         (rows_shape, shape((CAP, chans, width), bf16)),
-        3,
-        (meta, land, owners, field, inner, outer, cots[-1], back, *results),
+        1,
+        (meta, field, inner, outer, cots[-1], back, *results),
         (padded,),
     )
     total, result, sent = lax.optimization_barrier((total, result, sent))
     total = added(total, moved(total, orders[2], False))
     arrived = lax.ppermute(sent, "tile", [(tile, (tile + 1) % TILES) for tile in range(TILES)])
-    total, result, arrived = lax.optimization_barrier((total, result, arrived))
     total = added(total, moved(total, orders[3], False))
+    total, arrived = lax.optimization_barrier((total, arrived))
     slotted = call(
         slots_kernel,
         shape((owners.shape[0], chans, width), bf16),
-        2,
-        (meta, owners, result, arrived),
-    )
+        1,
+        (meta, result, arrived),
+    )
+    other = moved(total, orders[0], False)
+    total = jnp.concatenate([jnp.where(first, total, other), jnp.where(first, other, total)])
     total, slotted = lax.optimization_barrier((total, slotted))
     far = moved(total, ("x0", "z0"), True)
     near = moved(total, ("x0", "z0"), False)
@@ -567,26 +591,26 @@
     grads = call(
         functools.partial(finish_kernel, scale),
         (
-            shape((KS * KS, chans), f32),
+            shape((1, KS * KS, chans), f32),
             shape((1, chans), f32),
-            shape((chans, units), f32),
+            shape((1, chans, units), f32),
             shape((1, units), f32),
-            shape((chans, units), f32),
+            shape((1, chans, units), f32),
             shape((1, chans), f32),
         ),
         1,
         (meta, total, near, mate, far),
-        (pltpu.VMEM((2 * chans + 32, units), f32),),
+        (pltpu.VMEM((2 * chans + 64, units), f32),),
     )
 
     grad_kernel, grad_gain, grad_up, grad_bias, grad_down, grad_scale = grads
     return (
         slotted[None],
-        grad_kernel[None],
+        grad_kernel,
         grad_gain,
-        grad_up[None],
+        grad_up,
         grad_bias,
-        grad_down[None],
+        grad_down,
         grad_scale,
     )
 

time: 120 us -> 123 us (1.025)
  starting transfers between devices: 54.8 us -> 59.5 us
    ppermute x10 -> x11, starting transfers between devices: 20.2 us -> 24.9 us  [moved(): return lax.ppermute(value, 'tile', pairs)]
    ppermute x10 -> x11, waiting for transfers between devices: 18 us -> 14.6 us  [moved(): return lax.ppermute(value, 'tile', pairs)]
    ppermute x1, waiting for transfers between devices: 0.69 us -> 2.34 us  [body(): lax.ppermute(sent, 'tile', [(tile, (tile + 1) % TILES) for tile in range(...]
    unnamed x24 -> x30, local copies, waits for them, and re-layouts: 4.45 us -> 4.29 us
  transfers between devices with their start and end apart: 24 -> 25, of which waited for: 17 -> 17; matrix products, arithmetic and copies ran while one was open for 1% -> 0% of each run, Pallas kernels for 3% -> 3%
where the time goes in v3:
time: 123 us
  starting transfers between devices  59.5 us (48%)
  waiting for transfers between devices  41.1 us (33%)
  Pallas kernels  15.8 us (13%)
  local copies, waits for them, and re-layouts  4.38 us (4%)
  other arithmetic  1.3 us (1%)
    ppermute x11, starting transfers between devices, moved(): return lax.ppermute(value, 'tile', pairs)  24.9 us
    ppermute x5, starting transfers between devices, halo(): lax.ppermute(inner, 'tile', [(tile, tile ^ 1) for tile in range(TILES)])  17.6 us
    pallas_call x12, Pallas kernels, call(): pl.pallas_call(body, out_shape=out_shape, in_specs=spec, out_specs=outs,...  15.8 us
    ppermute x11, waiting for transfers between devices, moved(): return lax.ppermute(value, 'tile', pairs)  14.6 us
    ppermute x3, starting transfers between devices, body(): cots.append(lax.ppermute(result, 'section', pairs))  12.4 us
    ppermute x5, waiting for transfers between devices, halo(): outer = lax.ppermute(outer, 'tile', across)  11.2 us
    ppermute x3, waiting for transfers between devices, body(): cots.append(lax.ppermute(result, 'section', pairs))  9.96 us
    unnamed x30, local copies, waits for them, and re-layouts  4.29 us
  transfers between devices with their start and end apart: 25, of which 17 were waited for; matrix products, arithmetic and copies ran while one was open for 0% of the time, Pallas kernels for 3%

profile of v3, /device:TPU:1, one launch (start us, length us, event | category | flops | bytes accessed | tf_op | source)
XLA Modules:
  0.0 123.0 jit_solution(6649562250059492567)
XLA Ops:
  1.7 2.7 %collective-permute-start.1 = (bf16[3,192,128]{2,1,0:T(8,128)(2,1)S(1)}, bf16[3,192,128]{2,1,0:T(8,128)(2,1)S(1)}, u32[]{:S(2)}, u32[]{:S(2)}) collective-permute-start(bf16[3,192,128]{2,1,0:T(8,128)(2,1)S(1)} %get-tuple-element.102), channel_id=1, source_target_pairs={{0,63},{1,2},{2,1},{3,4},{4,3},{5,6},{6,5},{7,8},{8,7},{9,10},{10,... | collective-permute-start | bytes 442376 | tf_op jit(solution)/shard_map/ppermute | solution.py:74
  4.4 6.4 %collective-permute-start = (bf16[3,192,128]{2,1,0:T(8,128)(2,1)S(1)}, bf16[3,192,128]{2,1,0:T(8,128)(2,1)S(1)}, u32[]{:S(2)}, u32[]{:S(2)}) collective-permute-start(bf16[3,192,128]{2,1,0:T(8,128)(2,1)S(1)} %get-tuple-element.103), channel_id=1, source_target_pairs={{0,1},{1,0},{2,3},{3,2},{4,5},{5,4},{6,7},{7,6},{8,9},{9,8},{10,11... | collective-permute-start | bytes 442376 | tf_op jit(solution)/shard_map/ppermute | solution.py:75
  13.2 3.6 %shard_map.154 = (f32[192,640]{1,0:T(8,128)S(1)}, f32[1,640]{1,0:T(1,128)S(1)}, bf16[768,640]{1,0:T(8,128)(2,1)S(1)}, bf16[768,640]{1,0:T(8,128)(2,1)S(1)}) custom-call(s32[16]{0:T(128)S(1)} %concatenate.6.meta, bf16[5,192,128]{2,1,0:T(8,128)(2,1)S(1)} %bitcast.24, bf16[3,192,128]{2,1,0:T(8,128)(2,1)S(1)} %collective-permute-done.inner, ...), custom_call_target="tpu_custom_call" | custom-call | tf_op jit(solution)/shard_map/pallas_call | solution.py:83
  18.9 3.6 %collective-permute-done.3.outer = bf16[3,192,128]{2,1,0:T(8,128)(2,1)S(1)} collective-permute-done((bf16[3,192,128]{2,1,0:T(8,128)(2,1)S(1)}, bf16[3,192,128]{2,1,0:T(8,128)(2,1)S(1)}, u32[]{:S(2)}, u32[]{:S(2)}) %collective-permute-start.3) | collective-permute-done | bytes 147488 | tf_op jit(solution)/shard_map/ppermute | solution.py:74
  23.0 5.4 %collective-permute-start.4 = (bf16[5,192,128]{2,1,0:T(8,128)(2,1)S(1)}, bf16[5,192,128]{2,1,0:T(8,128)(2,1)S(1)}, u32[]{:S(2)}, u32[]{:S(2)}) collective-permute-start(bf16[5,192,128]{2,1,0:T(8,128)(2,1)S(1)} %shard_map.156.third), channel_id=1, source_target_pairs={{0,192},{64,0},{128,64},{192,128},{1,193},{65,1},{129,65},{193,129... | collective-permute-start | bytes 737288 | tf_op jit(solution)/shard_map/ppermute | solution.py:535
  28.4 3.1 %collective-permute-done.4.cot.cot_2 = bf16[5,192,128]{2,1,0:T(8,128)(2,1)S(1)} collective-permute-done((bf16[5,192,128]{2,1,0:T(8,128)(2,1)S(1)}, bf16[5,192,128]{2,1,0:T(8,128)(2,1)S(1)}, u32[]{:S(2)}, u32[]{:S(2)}) %collective-permute-start.4) | collective-permute-done | bytes 245792 | tf_op jit(solution)/shard_map/ppermute | solution.py:535
  32.1 4.3 %collective-permute-start.5 = (bf16[3,192,128]{2,1,0:T(8,128)(2,1)S(1)}, bf16[3,192,128]{2,1,0:T(8,128)(2,1)S(1)}, u32[]{:S(2)}, u32[]{:S(2)}) collective-permute-start(bf16[3,192,128]{2,1,0:T(8,128)(2,1)S(1)} %get-tuple-element.64), channel_id=1, source_target_pairs={{0,1},{1,0},{2,3},{3,2},{4,5},{5,4},{6,7},{7,6},{8,9},{9,8},{10,11... | collective-permute-start | bytes 442376 | tf_op jit(solution)/shard_map/ppermute | solution.py:75
  37.5 3.6 %collective-permute-done.6.outer = bf16[3,192,128]{2,1,0:T(8,128)(2,1)S(1)} collective-permute-done((bf16[3,192,128]{2,1,0:T(8,128)(2,1)S(1)}, bf16[3,192,128]{2,1,0:T(8,128)(2,1)S(1)}, u32[]{:S(2)}, u32[]{:S(2)}) %collective-permute-start.6) | collective-permute-done | bytes 147488 | tf_op jit(solution)/shard_map/ppermute | solution.py:74
  41.6 3.5 %collective-permute-start.7 = (bf16[5,192,128]{2,1,0:T(8,128)(2,1)S(1)}, bf16[5,192,128]{2,1,0:T(8,128)(2,1)S(1)}, u32[]{:S(2)}, u32[]{:S(2)}) collective-permute-start(bf16[5,192,128]{2,1,0:T(8,128)(2,1)S(1)} %shard_map.158.second), channel_id=1, source_target_pairs={{0,192},{64,0},{128,64},{192,128},{1,193},{65,1},{129,65},{193,129... | collective-permute-start | bytes 737288 | tf_op jit(solution)/shard_map/ppermute | solution.py:535
  45.1 3.1 %collective-permute-done.7.cot.cot_1 = bf16[5,192,128]{2,1,0:T(8,128)(2,1)S(1)} collective-permute-done((bf16[5,192,128]{2,1,0:T(8,128)(2,1)S(1)}, bf16[5,192,128]{2,1,0:T(8,128)(2,1)S(1)}, u32[]{:S(2)}, u32[]{:S(2)}) %collective-permute-start.7) | collective-permute-done | bytes 245792 | tf_op jit(solution)/shard_map/ppermute | solution.py:535
  48.8 4.4 %collective-permute-start.8 = (bf16[3,192,128]{2,1,0:T(8,128)(2,1)S(1)}, bf16[3,192,128]{2,1,0:T(8,128)(2,1)S(1)}, u32[]{:S(2)}, u32[]{:S(2)}) collective-permute-start(bf16[3,192,128]{2,1,0:T(8,128)(2,1)S(1)} %get-tuple-element.67), channel_id=1, source_target_pairs={{0,1},{1,0},{2,3},{3,2},{4,5},{5,4},{6,7},{7,6},{8,9},{9,8},{10,11... | collective-permute-start | bytes 442376 | tf_op jit(solution)/shard_map/ppermute | solution.py:75
  54.1 3.6 %collective-permute-done.9.outer = bf16[3,192,128]{2,1,0:T(8,128)(2,1)S(1)} collective-permute-done((bf16[3,192,128]{2,1,0:T(8,128)(2,1)S(1)}, bf16[3,192,128]{2,1,0:T(8,128)(2,1)S(1)}, u32[]{:S(2)}, u32[]{:S(2)}) %collective-permute-start.9) | collective-permute-done | bytes 147488 | tf_op jit(solution)/shard_map/ppermute | solution.py:74
  58.3 3.5 %collective-permute-start.10 = (bf16[5,192,128]{2,1,0:T(8,128)(2,1)S(1)}, bf16[5,192,128]{2,1,0:T(8,128)(2,1)S(1)}, u32[]{:S(2)}, u32[]{:S(2)}) collective-permute-start(bf16[5,192,128]{2,1,0:T(8,128)(2,1)S(1)} %shard_map.160.first), channel_id=1, source_target_pairs={{0,192},{64,0},{128,64},{192,128},{1,193},{65,1},{129,65},{193,129... | collective-permute-start | bytes 737288 | tf_op jit(solution)/shard_map/ppermute | solution.py:535
  61.7 3.7 %collective-permute-done.10.cot_0.cot = bf16[5,192,128]{2,1,0:T(8,128)(2,1)S(1)} collective-permute-done((bf16[5,192,128]{2,1,0:T(8,128)(2,1)S(1)}, bf16[5,192,128]{2,1,0:T(8,128)(2,1)S(1)}, u32[]{:S(2)}, u32[]{:S(2)}) %collective-permute-start.10) | collective-permute-done | bytes 245792 | tf_op jit(solution)/shard_map/ppermute | solution.py:535
  65.4 2.9 %shard_map.161 = (bf16[5,192,128]{2,1,0:T(8,128)(2,1)S(1)}, bf16[3,192,128]{2,1,0:T(8,128)(2,1)S(1)}, bf16[3,192,128]{2,1,0:T(8,128)(2,1)S(1)}, bf16[112,768]{1,...) custom-call(s32[16]{0:T(128)S(1)} %concatenate.6.meta, ...), custom_call_target="tpu_custom_call" | custom-call | tf_op jit(solution)/shard_map/pallas_call | solution.py:83
  69.7 4.5 %collective-permute-start.12 = (bf16[112,768]{1,0:T(8,128)(2,1)S(1)}, bf16[112,768]{1,0:T(8,128)(2,1)S(1)}, u32[]{:S(2)}, u32[]{:S(2)}) collective-permute-start(bf16[112,768]{1,0:T(8,128)(2,1)S(1)} %get-tuple-element.72), channel_id=1, source_target_pairs={{0,1},{1,0},{2,3},{3,2},{4,5},{5,4},{6,7},{7,6},{8,9},{9,8},{10,11... | collective-permute-start | bytes 516104 | tf_op jit(solution)/shard_map/ppermute | solution.py:69
  74.2 1.6 %collective-permute-start.13 = (bf16[112,768]{1,0:T(8,128)(2,1)S(1)}, bf16[112,768]{1,0:T(8,128)(2,1)S(1)}, u32[]{:S(2)}, u32[]{:S(2)}) collective-permute-start(bf16[112,768]{1,0:T(8,128)(2,1)S(1)} %get-tuple-element.73), channel_id=1, source_target_pairs={{0,9},{1,2},{2,11},{3,0},{4,13},{5,6},{6,15},{7,4},{8,1},{9,10},{1... | collective-permute-start | bytes 516104 | tf_op jit(solution)/shard_map/ppermute | solution.py:69
  75.8 3.5 %collective-permute-done.13 = bf16[112,768]{1,0:T(8,128)(2,1)S(1)} collective-permute-done((bf16[112,768]{1,0:T(8,128)(2,1)S(1)}, bf16[112,768]{1,0:T(8,128)(2,1)S(1)}, u32[]{:S(2)}, u32[]{:S(2)}) %collective-permute-start.13) | collective-permute-done | bytes 172064 | tf_op jit(solution)/shard_map/ppermute | solution.py:69
  80.2 2.0 %collective-permute-start.16 = (bf16[3,192,128]{2,1,0:T(8,128)(2,1)S(1)}, bf16[3,192,128]{2,1,0:T(8,128)(2,1)S(1)}, u32[]{:S(2)}, u32[]{:S(2)}) collective-permute-start(bf16[3,192,128]{2,1,0:T(8,128)(2,1)S(1)} %copy-done.8), channel_id=1, source_target_pairs={{0,1},{1,0},{2,3},{3,2},{4,5},{5,4},{6,7},{7,6},{8,9},{9,8},{10,11... | collective-permute-start | bytes 442376 | tf_op jit(solution)/shard_map/ppermute | solution.py:75
  82.2 2.7 %collective-permute-done.14 = bf16[56,768]{1,0:T(8,128)(2,1)S(1)} collective-permute-done((bf16[56,768]{1,0:T(8,128)(2,1)S(1)}, bf16[56,768]{1,0:T(8,128)(2,1)S(1)}, u32[]{:S(2)}, u32[]{:S(2)}) %collective-permute-start.14) | collective-permute-done | bytes 86048 | tf_op jit(solution)/shard_map/ppermute | solution.py:69
  85.0 1.3 %collective-permute-start.15 = (bf16[56,768]{1,0:T(8,128)(2,1)S(1)}, bf16[56,768]{1,0:T(8,128)(2,1)S(1)}, u32[]{:S(2)}, u32[]{:S(2)}) collective-permute-start(bf16[56,768]{1,0:T(8,128)(2,1)S(1)} %add_convert_fusion.4), channel_id=1, source_target_pairs={{0,8},{1,57},{2,10},{3,59},{4,12},{5,61},{6,14},{7,63},{8,0},{9,49... | collective-permute-start | bytes 258056 | tf_op jit(solution)/shard_map/ppermute | solution.py:69
  86.8 2.2 %shard_map.162 = (bf16[5,192,128]{2,1,0:T(8,128)(2,1)S(1)}, bf16[2,192,128]{2,1,0:T(8,128)(2,1)S(1)}) custom-call(s32[16]{0:T(128)S(1)} %concatenate.6.meta, bf16[5,192,128]{2,1,0:T(8,128)(2,1)S(1)} %get-tuple-element.77.field, bf16[3,192,128]{2,1,0:T(8,128)(2,1)S(1)} %collective-permute-done.16.inner, ...), custom_call_target="tpu_custom_call" | custom-call | tf_op jit(solution)/shard_map/pallas_call | solution.py:83
  91.1 2.2 %collective-permute-done.18 = bf16[56,768]{1,0:T(8,128)(2,1)S(1)} collective-permute-done((bf16[56,768]{1,0:T(8,128)(2,1)S(1)}, bf16[56,768]{1,0:T(8,128)(2,1)S(1)}, u32[]{:S(2)}, u32[]{:S(2)}) %collective-permute-start.18) | collective-permute-done | bytes 86048 | tf_op jit(solution)/shard_map/ppermute | solution.py:69
  93.3 4.6 %collective-permute-start.19 = (bf16[56,768]{1,0:T(8,128)(2,1)S(1)}, bf16[56,768]{1,0:T(8,128)(2,1)S(1)}, u32[]{:S(2)}, u32[]{:S(2)}) collective-permute-start(bf16[56,768]{1,0:T(8,128)(2,1)S(1)} %add_convert_fusion.2), channel_id=1, source_target_pairs={{0,56},{1,7},{2,58},{3,5},{4,60},{5,3},{6,62},{7,1},{8,48},{9,15},... | collective-permute-start | bytes 258056 | tf_op jit(solution)/shard_map/ppermute | solution.py:69
  97.9 1.9 %collective-permute-start.20 = (bf16[2,192,128]{2,1,0:T(8,128)(2,1)S(1)}, bf16[2,192,128]{2,1,0:T(8,128)(2,1)S(1)}, u32[]{:S(2)}, u32[]{:S(2)}) collective-permute-start(bf16[2,192,128]{2,1,0:T(8,128)(2,1)S(1)} %get-tuple-element.83), channel_id=1, source_target_pairs={{0,1},{1,2},{2,3},{3,4},{4,5},{5,6},{6,7},{7,8},{8,9},{9,10},{10,1... | collective-permute-start | bytes 294920 | tf_op jit(solution)/shard_map/ppermute | solution.py:576
  99.8 2.3 %collective-permute-done.20.arrived = bf16[2,192,128]{2,1,0:T(8,128)(2,1)S(1)} collective-permute-done((bf16[2,192,128]{2,1,0:T(8,128)(2,1)S(1)}, bf16[2,192,128]{2,1,0:T(8,128)(2,1)S(1)}, u32[]{:S(2)}, u32[]{:S(2)}) %collective-permute-start.20) | collective-permute-done | bytes 98336 | tf_op jit(solution)/shard_map/ppermute | solution.py:576
  102.2 3.6 %collective-permute-start.21 = (bf16[56,768]{1,0:T(8,128)(2,1)S(1)}, bf16[56,768]{1,0:T(8,128)(2,1)S(1)}, u32[]{:S(2)}, u32[]{:S(2)}) collective-permute-start(bf16[56,768]{1,0:T(8,128)(2,1)S(1)} %add_convert_fusion.1), channel_id=1, source_target_pairs={{0,6},{1,25},{2,4},{3,27},{4,2},{5,29},{6,0},{7,31},{8,14},{9,17},... | collective-permute-start | bytes 258056 | tf_op jit(solution)/shard_map/ppermute | solution.py:69
  105.8 1.3 %shard_map.163 = bf16[3,192,128]{2,1,0:T(8,128)(2,1)} custom-call(s32[16]{0:T(128)S(1)} %concatenate.6.meta, bf16[5,192,128]{2,1,0:T(8,128)(2,1)S(1)} %get-tuple-element.85.result, bf16[2,192,128]{2,1,0:T(8,128)(2,1)S(1)} %collective-permute-done.20.arrived), custom_call_target="tpu_custom_call" | custom-call | tf_op jit(solution)/shard_map/pallas_call | solution.py:83
  108.0 3.4 %collective-permute-start.24 = (bf16[112,768]{1,0:T(8,128)(2,1)S(1)}, bf16[112,768]{1,0:T(8,128)(2,1)S(1)}, u32[]{:S(2)}, u32[]{:S(2)}) collective-permute-start(bf16[112,768]{1,0:T(8,128)(2,1)S(1)} %pad_maximum_fusion.keep), channel_id=1, source_target_pairs={{0,3},{1,8},{2,1},{3,10},{4,7},{5,12},{6,5},{7,14},{8,11},{9,0},{1... | collective-permute-start | bytes 516104 | tf_op jit(solution)/shard_map/ppermute | solution.py:69
  111.4 3.2 %collective-permute-start.23 = (bf16[112,768]{1,0:T(8,128)(2,1)S(1)}, bf16[112,768]{1,0:T(8,128)(2,1)S(1)}, u32[]{:S(2)}, u32[]{:S(2)}) collective-permute-start(bf16[112,768]{1,0:T(8,128)(2,1)S(1)} %pad_maximum_fusion.keep), channel_id=1, source_target_pairs={{0,1},{1,0},{2,3},{3,2},{4,5},{5,4},{6,7},{7,6},{8,9},{9,8},{10,11... | collective-permute-start | bytes 516104 | tf_op jit(solution)/shard_map/ppermute | solution.py:69
  115.9 4.6 %collective-permute-done.22.near = bf16[112,768]{1,0:T(8,128)(2,1)S(1)} collective-permute-done((bf16[112,768]{1,0:T(8,128)(2,1)S(1)}, bf16[112,768]{1,0:T(8,128)(2,1)S(1)}, u32[]{:S(2)}, u32[]{:S(2)}) %collective-permute-start.22) | collective-permute-done | bytes 172064 | tf_op jit(solution)/shard_map/ppermute | solution.py:69
  120.5 1.8 %shard_map.164 = (f32[1,49,192]{2,1,0:T(8,128)S(1)}, f32[1,192]{1,0:T(1,128)}, f32[1,192,768]{2,1,0:T(8,128)}, f32[1,768]{1,0:T(1,128)}, f32[1,192,768]{2,1,0:T(8,128)}, /*index=5*/f32[1,192]{1,0:T(1,128)}) custom-call(s32[16]{0:T(128)S(1)} %concatenate.6.meta, bf16[112,768]{1,0:T(8,128)(2,1)S(1)} %pad_maximum_fusion.keep, ...), custom_call_target="tpu_custom_call" | custom-call | tf_op jit(solution)/shard_map/pallas_call | solution.py:83
  (70 shorter events, 17.8 us)
Async XLA Ops:
  0.6 10.2 %copy-start.11 = (f32[1,49,192]{2,0,1:T(1,128)S(1)}, f32[1,49,192]{2,0,1:T(1,128)}, u32[]{:S(2)}) copy-start(f32[1,49,192]{2,0,1:T(1,128)} %param.14) | copy-start | bytes 112900
  0.7 10.9 %copy-start.3 = (bf16[1,192,768]{2,1,0:T(8,128)(2,1)S(1)}, bf16[1,192,768]{2,1,0:T(8,128)(2,1)}, u32[]{:S(2)}) copy-start(bf16[1,192,768]{2,1,0:T(8,128)(2,1)} %param.18) | copy-start | bytes 884740
  1.7 9.9 %copy-start = (bf16[1,192,768]{2,1,0:T(8,128)(2,1)S(1)}, bf16[1,192,768]{2,1,0:T(8,128)(2,1)}, u32[]{:S(2)}) copy-start(bf16[1,192,768]{2,1,0:T(8,128)(2,1)} %param.16) | copy-start | bytes 884740
  1.7 11.2 %collective-permute-start.1 = (bf16[3,192,128]{2,1,0:T(8,128)(2,1)S(1)}, bf16[3,192,128]{2,1,0:T(8,128)(2,1)S(1)}, u32[]{:S(2)}, u32[]{:S(2)}) collective-permute-start(bf16[3,192,128]{2,1,0:T(8,128)(2,1)S(1)} %get-tuple-element.102), channel_id=1, source_target_pairs={{0,63},{1,2},{2,1},{3,4},{4,3},{5,6},{6,5},{7,8},{8,7},{9,10},{10,... | collective-permute-start | bytes 442376 | tf_op jit(solution)/shard_map/ppermute | solution.py:74
  4.4 8.5 %collective-permute-start = (bf16[3,192,128]{2,1,0:T(8,128)(2,1)S(1)}, bf16[3,192,128]{2,1,0:T(8,128)(2,1)S(1)}, u32[]{:S(2)}, u32[]{:S(2)}) collective-permute-start(bf16[3,192,128]{2,1,0:T(8,128)(2,1)S(1)} %get-tuple-element.103), channel_id=1, source_target_pairs={{0,1},{1,0},{2,3},{3,2},{4,5},{5,4},{6,7},{7,6},{8,9},{9,8},{10,11... | collective-permute-start | bytes 442376 | tf_op jit(solution)/shard_map/ppermute | solution.py:75
  12.3 0.9 copy-start.1
  13.2 3.6 %copy-start.2 = (bf16[5,192,128]{2,1,0:T(8,128)(2,1)S(1)}, bf16[5,192,128]{2,1,0:T(8,128)(2,1)}, u32[]{:S(2)}) copy-start(bf16[5,192,128]{2,1,0:T(8,128)(2,1)} %cot_top.1) | copy-start | bytes 737284
  17.4 1.5 %collective-permute-start.2 = (bf16[3,192,128]{2,1,0:T(8,128)(2,1)S(1)}, bf16[3,192,128]{2,1,0:T(8,128)(2,1)S(1)}, u32[]{:S(2)}, u32[]{:S(2)}) collective-permute-start(bf16[3,192,128]{2,1,0:T(8,128)(2,1)S(1)} %get-tuple-element.60), channel_id=1, source_target_pairs={{0,1},{1,0},{2,3},{3,2},{4,5},{5,4},{6,7},{7,6},{8,9},{9,8},{10,11... | collective-permute-start | bytes 442376 | tf_op jit(solution)/shard_map/ppermute | solution.py:75
  17.9 4.6 %collective-permute-start.3 = (bf16[3,192,128]{2,1,0:T(8,128)(2,1)S(1)}, bf16[3,192,128]{2,1,0:T(8,128)(2,1)S(1)}, u32[]{:S(2)}, u32[]{:S(2)}) collective-permute-start(bf16[3,192,128]{2,1,0:T(8,128)(2,1)S(1)} %get-tuple-element.61), channel_id=1, source_target_pairs={{0,63},{1,2},{2,1},{3,4},{4,3},{5,6},{6,5},{7,8},{8,7},{9,10},{10,... | collective-permute-start | bytes 442376 | tf_op jit(solution)/shard_map/ppermute | solution.py:74
  23.0 8.5 %collective-permute-start.4 = (bf16[5,192,128]{2,1,0:T(8,128)(2,1)S(1)}, bf16[5,192,128]{2,1,0:T(8,128)(2,1)S(1)}, u32[]{:S(2)}, u32[]{:S(2)}) collective-permute-start(bf16[5,192,128]{2,1,0:T(8,128)(2,1)S(1)} %shard_map.156.third), channel_id=1, source_target_pairs={{0,192},{64,0},{128,64},{192,128},{1,193},{65,1},{129,65},{193,129... | collective-permute-start | bytes 737288 | tf_op jit(solution)/shard_map/ppermute | solution.py:535
  32.1 5.3 %collective-permute-start.5 = (bf16[3,192,128]{2,1,0:T(8,128)(2,1)S(1)}, bf16[3,192,128]{2,1,0:T(8,128)(2,1)S(1)}, u32[]{:S(2)}, u32[]{:S(2)}) collective-permute-start(bf16[3,192,128]{2,1,0:T(8,128)(2,1)S(1)} %get-tuple-element.64), channel_id=1, source_target_pairs={{0,1},{1,0},{2,3},{3,2},{4,5},{5,4},{6,7},{7,6},{8,9},{9,8},{10,11... | collective-permute-start | bytes 442376 | tf_op jit(solution)/shard_map/ppermute | solution.py:75
  36.5 4.6 %collective-permute-start.6 = (bf16[3,192,128]{2,1,0:T(8,128)(2,1)S(1)}, bf16[3,192,128]{2,1,0:T(8,128)(2,1)S(1)}, u32[]{:S(2)}, u32[]{:S(2)}) collective-permute-start(bf16[3,192,128]{2,1,0:T(8,128)(2,1)S(1)} %get-tuple-element.65), channel_id=1, source_target_pairs={{0,63},{1,2},{2,1},{3,4},{4,3},{5,6},{6,5},{7,8},{8,7},{9,10},{10,... | collective-permute-start | bytes 442376 | tf_op jit(solution)/shard_map/ppermute | solution.py:74
  41.6 6.6 %collective-permute-start.7 = (bf16[5,192,128]{2,1,0:T(8,128)(2,1)S(1)}, bf16[5,192,128]{2,1,0:T(8,128)(2,1)S(1)}, u32[]{:S(2)}, u32[]{:S(2)}) collective-permute-start(bf16[5,192,128]{2,1,0:T(8,128)(2,1)S(1)} %shard_map.158.second), channel_id=1, source_target_pairs={{0,192},{64,0},{128,64},{192,128},{1,193},{65,1},{129,65},{193,129... | collective-permute-start | bytes 737288 | tf_op jit(solution)/shard_map/ppermute | solution.py:535
  48.8 5.4 %collective-permute-start.8 = (bf16[3,192,128]{2,1,0:T(8,128)(2,1)S(1)}, bf16[3,192,128]{2,1,0:T(8,128)(2,1)S(1)}, u32[]{:S(2)}, u32[]{:S(2)}) collective-permute-start(bf16[3,192,128]{2,1,0:T(8,128)(2,1)S(1)} %get-tuple-element.67), channel_id=1, source_target_pairs={{0,1},{1,0},{2,3},{3,2},{4,5},{5,4},{6,7},{7,6},{8,9},{9,8},{10,11... | collective-permute-start | bytes 442376 | tf_op jit(solution)/shard_map/ppermute | solution.py:75
  53.1 4.6 %collective-permute-start.9 = (bf16[3,192,128]{2,1,0:T(8,128)(2,1)S(1)}, bf16[3,192,128]{2,1,0:T(8,128)(2,1)S(1)}, u32[]{:S(2)}, u32[]{:S(2)}) collective-permute-start(bf16[3,192,128]{2,1,0:T(8,128)(2,1)S(1)} %get-tuple-element.68), channel_id=1, source_target_pairs={{0,63},{1,2},{2,1},{3,4},{4,3},{5,6},{6,5},{7,8},{8,7},{9,10},{10,... | collective-permute-start | bytes 442376 | tf_op jit(solution)/shard_map/ppermute | solution.py:74
  58.3 7.2 %collective-permute-start.10 = (bf16[5,192,128]{2,1,0:T(8,128)(2,1)S(1)}, bf16[5,192,128]{2,1,0:T(8,128)(2,1)S(1)}, u32[]{:S(2)}, u32[]{:S(2)}) collective-permute-start(bf16[5,192,128]{2,1,0:T(8,128)(2,1)S(1)} %shard_map.160.first), channel_id=1, source_target_pairs={{0,192},{64,0},{128,64},{192,128},{1,193},{65,1},{129,65},{193,129... | collective-permute-start | bytes 737288 | tf_op jit(solution)/shard_map/ppermute | solution.py:535
  69.7 6.1 %collective-permute-start.11 = (bf16[112,768]{1,0:T(8,128)(2,1)S(1)}, bf16[112,768]{1,0:T(8,128)(2,1)S(1)}, u32[]{:S(2)}, u32[]{:S(2)}) collective-permute-start(bf16[112,768]{1,0:T(8,128)(2,1)S(1)} %get-tuple-element.71), channel_id=1, source_target_pairs={{0,2},{1,9},{2,0},{3,11},{4,6},{5,13},{6,4},{7,15},{8,10},{9,1},{1... | collective-permute-start | bytes 516104 | tf_op jit(solution)/shard_map/ppermute | solution.py:69
  69.7 6.1 %collective-permute-start.12 = (bf16[112,768]{1,0:T(8,128)(2,1)S(1)}, bf16[112,768]{1,0:T(8,128)(2,1)S(1)}, u32[]{:S(2)}, u32[]{:S(2)}) collective-permute-start(bf16[112,768]{1,0:T(8,128)(2,1)S(1)} %get-tuple-element.72), channel_id=1, source_target_pairs={{0,1},{1,0},{2,3},{3,2},{4,5},{5,4},{6,7},{7,6},{8,9},{9,8},{10,11... | collective-permute-start | bytes 516104 | tf_op jit(solution)/shard_map/ppermute | solution.py:69
  74.2 5.1 %collective-permute-start.13 = (bf16[112,768]{1,0:T(8,128)(2,1)S(1)}, bf16[112,768]{1,0:T(8,128)(2,1)S(1)}, u32[]{:S(2)}, u32[]{:S(2)}) collective-permute-start(bf16[112,768]{1,0:T(8,128)(2,1)S(1)} %get-tuple-element.73), channel_id=1, source_target_pairs={{0,9},{1,2},{2,11},{3,0},{4,13},{5,6},{6,15},{7,4},{8,1},{9,10},{1... | collective-permute-start | bytes 516104 | tf_op jit(solution)/shard_map/ppermute | solution.py:69
  79.3 0.9 copy-start.8
  79.4 2.8 %copy-start.6 = (bf16[3,192,128]{2,1,0:T(8,128)(2,1)S(1)}, bf16[3,192,128]{2,1,0:T(8,128)(2,1)}, u32[]{:S(2)}) copy-start(bf16[3,192,128]{2,1,0:T(8,128)(2,1)} %copy-done.5) | copy-start | bytes 442372
  79.4 5.5 %collective-permute-start.14 = (bf16[56,768]{1,0:T(8,128)(2,1)S(1)}, bf16[56,768]{1,0:T(8,128)(2,1)S(1)}, u32[]{:S(2)}, u32[]{:S(2)}) collective-permute-start(bf16[56,768]{1,0:T(8,128)(2,1)S(1)} %broadcast_select_fusion.2), channel_id=1, source_target_pairs={{0,6},{1,25},{2,4},{3,27},{4,2},{5,29},{6,0},{7,31},{8,14},{9,17},... | collective-permute-start | bytes 258056 | tf_op jit(solution)/shard_map/ppermute | solution.py:69
  80.2 6.1 %collective-permute-start.16 = (bf16[3,192,128]{2,1,0:T(8,128)(2,1)S(1)}, bf16[3,192,128]{2,1,0:T(8,128)(2,1)S(1)}, u32[]{:S(2)}, u32[]{:S(2)}) collective-permute-start(bf16[3,192,128]{2,1,0:T(8,128)(2,1)S(1)} %copy-done.8), channel_id=1, source_target_pairs={{0,1},{1,0},{2,3},{3,2},{4,5},{5,4},{6,7},{7,6},{8,9},{9,8},{10,11... | collective-permute-start | bytes 442376 | tf_op jit(solution)/shard_map/ppermute | solution.py:75
  82.2 4.6 %collective-permute-start.17 = (bf16[3,192,128]{2,1,0:T(8,128)(2,1)S(1)}, bf16[3,192,128]{2,1,0:T(8,128)(2,1)S(1)}, u32[]{:S(2)}, u32[]{:S(2)}) collective-permute-start(bf16[3,192,128]{2,1,0:T(8,128)(2,1)S(1)} %copy-done.6), channel_id=1, source_target_pairs={{0,63},{1,2},{2,1},{3,4},{4,3},{5,6},{6,5},{7,8},{8,7},{9,10},{10,... | collective-permute-start | bytes 442376 | tf_op jit(solution)/shard_map/ppermute | solution.py:74
  85.0 4.8 %collective-permute-start.15 = (bf16[56,768]{1,0:T(8,128)(2,1)S(1)}, bf16[56,768]{1,0:T(8,128)(2,1)S(1)}, u32[]{:S(2)}, u32[]{:S(2)}) collective-permute-start(bf16[56,768]{1,0:T(8,128)(2,1)S(1)} %add_convert_fusion.4), channel_id=1, source_target_pairs={{0,8},{1,57},{2,10},{3,59},{4,12},{5,61},{6,14},{7,63},{8,0},{9,49... | collective-permute-start | bytes 258056 | tf_op jit(solution)/shard_map/ppermute | solution.py:69
  89.8 3.4 %collective-permute-start.18 = (bf16[56,768]{1,0:T(8,128)(2,1)S(1)}, bf16[56,768]{1,0:T(8,128)(2,1)S(1)}, u32[]{:S(2)}, u32[]{:S(2)}) collective-permute-start(bf16[56,768]{1,0:T(8,128)(2,1)S(1)} %add_convert_fusion.3), channel_id=1, source_target_pairs={{0,24},{1,3},{2,26},{3,1},{4,28},{5,7},{6,30},{7,5},{8,16},{9,11},... | collective-permute-start | bytes 258056 | tf_op jit(solution)/shard_map/ppermute | solution.py:69
  93.3 6.5 %collective-permute-start.19 = (bf16[56,768]{1,0:T(8,128)(2,1)S(1)}, bf16[56,768]{1,0:T(8,128)(2,1)S(1)}, u32[]{:S(2)}, u32[]{:S(2)}) collective-permute-start(bf16[56,768]{1,0:T(8,128)(2,1)S(1)} %add_convert_fusion.2), channel_id=1, source_target_pairs={{0,56},{1,7},{2,58},{3,5},{4,60},{5,3},{6,62},{7,1},{8,48},{9,15},... | collective-permute-start | bytes 258056 | tf_op jit(solution)/shard_map/ppermute | solution.py:69
  97.9 4.3 %collective-permute-start.20 = (bf16[2,192,128]{2,1,0:T(8,128)(2,1)S(1)}, bf16[2,192,128]{2,1,0:T(8,128)(2,1)S(1)}, u32[]{:S(2)}, u32[]{:S(2)}) collective-permute-start(bf16[2,192,128]{2,1,0:T(8,128)(2,1)S(1)} %get-tuple-element.83), channel_id=1, source_target_pairs={{0,1},{1,2},{2,3},{3,4},{4,5},{5,6},{6,7},{7,8},{8,9},{9,10},{10,1... | collective-permute-start | bytes 294920 | tf_op jit(solution)/shard_map/ppermute | solution.py:576
  102.2 5.8 %collective-permute-start.21 = (bf16[56,768]{1,0:T(8,128)(2,1)S(1)}, bf16[56,768]{1,0:T(8,128)(2,1)S(1)}, u32[]{:S(2)}, u32[]{:S(2)}) collective-permute-start(bf16[56,768]{1,0:T(8,128)(2,1)S(1)} %add_convert_fusion.1), channel_id=1, source_target_pairs={{0,6},{1,25},{2,4},{3,27},{4,2},{5,29},{6,0},{7,31},{8,14},{9,17},... | collective-permute-start | bytes 258056 | tf_op jit(solution)/shard_map/ppermute | solution.py:69
  108.0 7.9 %collective-permute-start.24 = (bf16[112,768]{1,0:T(8,128)(2,1)S(1)}, bf16[112,768]{1,0:T(8,128)(2,1)S(1)}, u32[]{:S(2)}, u32[]{:S(2)}) collective-permute-start(bf16[112,768]{1,0:T(8,128)(2,1)S(1)} %pad_maximum_fusion.keep), channel_id=1, source_target_pairs={{0,3},{1,8},{2,1},{3,10},{4,7},{5,12},{6,5},{7,14},{8,11},{9,0},{1... | collective-permute-start | bytes 516104 | tf_op jit(solution)/shard_map/ppermute | solution.py:69
  111.4 4.5 %collective-permute-start.23 = (bf16[112,768]{1,0:T(8,128)(2,1)S(1)}, bf16[112,768]{1,0:T(8,128)(2,1)S(1)}, u32[]{:S(2)}, u32[]{:S(2)}) collective-permute-start(bf16[112,768]{1,0:T(8,128)(2,1)S(1)} %pad_maximum_fusion.keep), channel_id=1, source_target_pairs={{0,1},{1,0},{2,3},{3,2},{4,5},{5,4},{6,7},{7,6},{8,9},{9,8},{10,11... | collective-permute-start | bytes 516104 | tf_op jit(solution)/shard_map/ppermute | solution.py:69
  114.6 5.9 %collective-permute-start.22 = (bf16[112,768]{1,0:T(8,128)(2,1)S(1)}, bf16[112,768]{1,0:T(8,128)(2,1)S(1)}, u32[]{:S(2)}, u32[]{:S(2)}) collective-permute-start(bf16[112,768]{1,0:T(8,128)(2,1)S(1)} %pad_maximum_fusion.keep), channel_id=1, source_target_pairs={{0,2},{1,9},{2,0},{3,11},{4,6},{5,13},{6,4},{7,15},{8,10},{9,1},{1... | collective-permute-start | bytes 516104 | tf_op jit(solution)/shard_map/ppermute | solution.py:69
  (7 other events, 4.8 us)

commit v4 on v3

--- a/solution.py
+++ b/solution.py
@@ -114,6 +114,31 @@
     outer_ref[...] = jnp.where(odd, tail, head)
 
 
+def fill_taps(cols, targets):
+    high = cols[...].astype(bf16)
+    low = (cols[...] - high.astype(f32)).astype(bf16)
+    chans, taps = cols.shape
+    wide = KS * 128
+    tap = lax.broadcasted_iota(jnp.int32, (taps, wide), 0)
+    place = lax.broadcasted_iota(jnp.int32, (taps, wide), 1)
+    tap_col, tap_row = place >> 7, (place >> 4) & (PLACES - 1)
+    own = lax.broadcasted_iota(jnp.int32, (chans, wide), 0) & (BLOCK - 1)
+    diagonal = own == (lax.broadcasted_iota(jnp.int32, (chans, wide), 1) & (BLOCK - 1))
+    for target, row in zip(targets, (tap_row, KS - 1 - tap_row)):
+        if target is None:
+            continue
+        hit = (tap == row * KS + tap_col) & (tap_row < KS)
+        spread = jnp.where(hit, 1.0, 0.0).astype(bf16)
+        for half, value in enumerate((high, low)):
+            filled = jnp.dot(value, spread, preferred_element_type=f32)
+            filled = jnp.where(diagonal, filled, 0.0).astype(bf16)
+            for block in range(chans // BLOCK):
+                for col in range(KS):
+                    target[
+                        block, col * BLOCK : (col + 1) * BLOCK, half * 128 : (half + 1) * 128
+                    ] = filled[block * BLOCK : (block + 1) * BLOCK, col * 128 : (col + 1) * 128]
+
+
 def prepare_kernel(
     kernel, gain, layer, bias, up, down, cols, forth_ref, back_ref, up_t_ref, down_t_ref, bias_ref, lines_ref
 ):
@@ -125,26 +150,7 @@
     up_t_ref[...] = jnp.transpose(up[...].astype(f32)).astype(bf16)
     down_t_ref[...] = jnp.transpose(down[...].astype(f32)).astype(bf16)
     bias_ref[...] = jnp.transpose(jnp.broadcast_to(bias[...], (8, bias.shape[1])))
-    high = cols[...].astype(bf16)
-    low = (cols[...] - high.astype(f32)).astype(bf16)
-    chans, taps = cols.shape
-    wide = KS * 128
-    tap = lax.broadcasted_iota(jnp.int32, (taps, wide), 0)
-    place = lax.broadcasted_iota(jnp.int32, (taps, wide), 1)
-    tap_col, tap_row = place >> 7, (place >> 4) & (PLACES - 1)
-    own = lax.broadcasted_iota(jnp.int32, (chans, wide), 0) & (BLOCK - 1)
-    diagonal = own == (lax.broadcasted_iota(jnp.int32, (chans, wide), 1) & (BLOCK - 1))
-    for target, row in ((forth_ref, tap_row), (back_ref, KS - 1 - tap_row)):
-        hit = (tap == row * KS + tap_col) & (tap_row < KS)
-        spread = jnp.where(hit, 1.0, 0.0).astype(bf16)
-        for half, value in enumerate((high, low)):
-            filled = jnp.dot(value, spread, preferred_element_type=f32)
-            filled = jnp.where(diagonal, filled, 0.0).astype(bf16)
-            for block in range(chans // BLOCK):
-                for col in range(KS):
-                    target[
-                        block, col * BLOCK : (col + 1) * BLOCK, half * 128 : (half + 1) * 128
-                    ] = filled[block * BLOCK : (block + 1) * BLOCK, col * 128 : (col + 1) * 128]
+    fill_taps(cols, (forth_ref, back_ref))
 
 
 def stacked(rows_ref, start, count):
@@ -173,7 +179,7 @@
 
 
 def forward_kernel(
-    meta, acts, inner, outer, taps_mat, cols, up_t, bias, nhat_ref, inv_ref, hidden_ref, slope_ref, rows_ref, field_ref, normed_ref
+    meta, acts, inner, outer, taps_mat, cols, up_t, bias, bias_row, nhat_ref, inv_ref, hidden_ref, slope_ref, note_ref, rows_ref, field_ref, normed_ref
 ):
     count, chans, width = acts.shape
     fill_rows(rows_ref, meta, acts, inner, outer)
@@ -196,6 +202,24 @@
         nhat_ref[:, part] = nhat
         inv_ref[:, part] = inverse
         normed_ref[:, part] = (nhat * gain).astype(bf16)
+    cells = count * width
+    note_ref[:chans, :cells] = nhat_ref[...].astype(bf16)
+    high, low = two_parts(cols[...])
+    note_ref[:chans, cells:] = jnp.concatenate([high, low], axis=1).astype(bf16)
+    parts = two_parts(bias_row[...])
+    padding = jnp.zeros((1, bias_row.shape[1] - cells), f32)
+    parts += two_parts(jnp.concatenate([inv_ref[...], padding], axis=1))
+    rest = jnp.zeros((BLOCK - len(parts), bias_row.shape[1]), f32)
+    note_ref[chans:] = jnp.concatenate([*parts, rest]).astype(bf16)
+    mlp_forward(normed_ref, up_t, bias, hidden_ref, slope_ref)
+
+
+def two_parts(value):
+    high = value.astype(bf16).astype(f32)
+    return [high, value - high]
+
+
+def mlp_forward(normed_ref, up_t, bias, hidden_ref, slope_ref):
     units = up_t.shape[0]
     chunk = 128
     for first in range(0, units, chunk):
@@ -204,11 +228,40 @@
         square = preact * preact
         hyper = jnp.tanh(preact * (tanh_root + tanh_root * cubic_coef * square))
         half = 0.5 + 0.5 * hyper
-        hidden_ref[part] = (preact * half).astype(bf16)
+        if hidden_ref is not None:
+            hidden_ref[part] = (preact * half).astype(bf16)
         slope = half * (
             1.0 + preact * (1.0 - hyper) * (tanh_root + 3.0 * cubic_coef * tanh_root * square)
         )
         slope_ref[part] = slope.astype(bf16)
+
+
+def adopt_kernel(
+    meta, note, half, other, nhat_ref, inv_ref, slope_ref, cols_ref, back_ref, up_ref, down_t_ref, up_t_ref, bias_ref, normed_ref
+):
+    chans, cells = nhat_ref.shape
+    units = slope_ref.shape[0]
+    taps = cols_ref.shape[1]
+
+    @pl.when((meta[SECTION] == SECTIONS - 1) | (meta[SECTION] == 0))
+    def _():
+        odd = meta[ODD] == 1
+        up = jnp.where(odd, other[...], half[...])
+        up_ref[...] = up
+        up_t_ref[...] = jnp.transpose(up.astype(f32)).astype(bf16)
+        down = jnp.where(odd, half[...], other[...])
+        down_t_ref[...] = jnp.transpose(down.astype(f32)).astype(bf16)
+        nhat = note[:chans, :cells].astype(f32)
+        nhat_ref[...] = nhat
+        pieces = note[:chans, cells:].astype(f32)
+        cols_ref[...] = pieces[:, :taps] + pieces[:, taps:]
+        lines = note[chans:].astype(f32)
+        bias_row = lines[0:1] + lines[1:2]
+        inv_ref[...] = (lines[2:3] + lines[3:4])[:, :cells]
+        bias_ref[...] = jnp.transpose(jnp.broadcast_to(bias_row, (8, units)))
+        fill_taps(cols_ref, (None, back_ref))
+        normed_ref[...] = (nhat * cols_ref[:, KS * KS : KS * KS + 1]).astype(bf16)
+        mlp_forward(normed_ref, up_t_ref, bias_ref, None, slope_ref)
 
 
 def mlp_backward(cots, meta, cols, down_t, up, slope, nhat, inv, out_ref, low_ref, field_ref, sums=None):
@@ -278,19 +331,8 @@
         conv_rows(meta, field, inner, outer, cot, taps_mat, result_ref, rows_ref)
 
 
-def last_conv_kernel(
-    meta, field, inner, outer, cot, taps_mat, third, second, first, result_ref, sent_ref, rows_ref
-):
-    for section, kept in ((3, third), (2, second), (1, first)):
-
-        @pl.when(meta[SECTION] == section)
-        def _():
-            result_ref[...] = kept[...]
-
-    @pl.when(meta[SECTION] == 0)
-    def _():
-        conv_rows(meta, field, inner, outer, cot, taps_mat, result_ref, rows_ref)
-
+def last_conv_kernel(meta, field, inner, outer, cot, taps_mat, result_ref, sent_ref, rows_ref):
+    conv_rows(meta, field, inner, outer, cot, taps_mat, result_ref, rows_ref)
     sent_ref[...] = jnp.zeros_like(sent_ref)
     rank = jnp.int32(0)
     for local in range(result_ref.shape[0]):
@@ -335,6 +377,7 @@
     acts,
     inner,
     outer,
+    cot_ref,
     field_ref,
     field_inner_ref,
     field_outer_ref,
@@ -348,7 +391,6 @@
     gain_ref,
     rows_ref,
     packed_ref,
-    cot_ref,
 ):
     count, chans, width = acts.shape
     units = slope.shape[0]
@@ -478,68 +520,92 @@
     head, tail = source[:MARGIN], source[count - MARGIN :]
     acts_inner, acts_outer = halo(jnp.where(odd, head, tail), jnp.where(odd, tail, head))
     up, down = w_up[0], w_down[0]
+    swaps = [(section, section ^ 1) for section in range(SECTIONS)]
     taps_shape = shape((chans // BLOCK, KS * BLOCK, 256), bf16)
+    weights_t = shape((units, chans), bf16)
+    cols_shape = shape((chans, 64), f32)
     cols, forth, back, up_t, down_t, bias = call(
         prepare_kernel,
-        (
-            shape((chans, 64), f32),
-            taps_shape,
-            taps_shape,
-            shape((units, chans), bf16),
-            shape((units, chans), bf16),
-            shape((units, 8), f32),
-        ),
+        (cols_shape, taps_shape, taps_shape, weights_t, weights_t, shape((units, 8), f32)),
         0,
         (dw_kernel[0], ln_gain, layer_scale, b_up, up, down),
         (pltpu.VMEM((64, chans), f32),),
         cost=(10**9, 10**7),
     )
+    half = lax.ppermute(jnp.where(odd, down, up), "section", swaps)
 
     padded = pltpu.VMEM((count + PLACES - 1, chans, width), bf16)
-    nhat, inv, hidden, slope = call(
+    nhat_shape, inv_shape = shape((chans, cells), f32), shape((1, cells), f32)
+    unit_shape = shape((units, cells), bf16)
+    nhat, inv, hidden, slope, own_note = call(
         forward_kernel,
-        (
-            shape((chans, cells), f32),
-            shape((1, cells), f32),
-            shape((units, cells), bf16),
-            shape((units, cells), bf16),
-        ),
+        (nhat_shape, inv_shape, unit_shape, unit_shape, shape((chans + BLOCK, units), bf16)),
         1,
-        (meta, source, acts_inner, acts_outer, forth, cols, up_t, bias),
+        (meta, source, acts_inner, acts_outer, forth, cols, up_t, bias, b_up),
         (padded, pltpu.VMEM((chans, cells), f32), pltpu.VMEM((chans, cells), bf16)),
     )
+    note = lax.ppermute(own_note, "section", swaps)
 
     rows_shape = shape((count, chans, width), bf16)
     edge_shape = shape((MARGIN, chans, width), bf16)
     outgrads = pltpu.VMEM((chans, cells), bf16)
     lowgrads = pltpu.VMEM((units, cells), bf16)
-    cots, results = [cot_top], []
-    for section in range(SECTIONS - 1, 0, -1):
-        field, inner, outer = call(
-            functools.partial(turn_kernel, section),
+
+    def turn_field(plane, cot, params):
+        field_cols, field_down_t, field_up, field_slope, field_nhat, field_inv, _ = params
+        return call(
+            functools.partial(turn_kernel, plane),
             (rows_shape, edge_shape, edge_shape),
             1,
-            (meta, cots[-1], cols, down_t, up, slope, nhat, inv),
+            (meta, cot, field_cols, field_down_t, field_up, field_slope, field_nhat, field_inv),
             (outgrads, lowgrads),
         )
-        inner, outer = halo(inner, outer)
-        result = call(
-            functools.partial(conv_kernel, section),
+
+    def turn_input(plane, cot, params, field, inner, outer):
+        return call(
+            functools.partial(conv_kernel, plane),
             rows_shape,
             1,
-            (meta, field, inner, outer, cots[-1], back),
+            (meta, field, inner, outer, cot, params[-1]),
             (padded,),
         )
-        results.append(result)
-        pairs = [(place, (place - 1) % SECTIONS) for place in range(SECTIONS)]
-        cots.append(lax.ppermute(result, "section", pairs))
-
-    part = shape(((2 * chans + 64) // 4, units), bf16)
-    field, inner, outer, keep, near, mate, far = call(
+
+    top = SECTIONS - 1
+    params = (cols, down_t, up, slope, nhat, inv, back)
+    field, inner, outer = turn_field(top, cot_top, params)
+    half, field = lax.optimization_barrier((half, field))
+    inner, outer = halo(inner, outer)
+    other = moved(half, ("", ""), True)
+    adopted = call(
+        adopt_kernel,
+        (nhat_shape, inv_shape, unit_shape, cols_shape, taps_shape, shape((chans, units), bf16))
+        + (weights_t, weights_t, shape((units, 8), f32)),
+        1,
+        (meta, note, half, other),
+        (pltpu.VMEM((chans, cells), bf16),),
+        cost=(10**9, 10**7),
+    )
+    next_nhat, next_inv, next_slope, next_cols, next_back, next_up, next_down_t = adopted[:7]
+    adopted = (next_cols, next_down_t, next_up, next_slope, next_nhat, next_inv, next_back)
+    cot_2 = turn_input(top, cot_top, params, field, inner, outer)
+    own_2 = lax.ppermute(cot_2, "section", swaps)
+
+    field, inner, outer = turn_field(top, cot_2, adopted)
+    inner, outer = halo(inner, outer)
+    cot_1 = turn_input(top, cot_2, adopted, field, inner, outer)
+    cot_1 = lax.ppermute(cot_1, "section", [(0, top), (top, 0), (1, 2), (2, 1)])
+    own_1 = lax.ppermute(cot_1, "section", swaps)
+
+    field, inner, outer = turn_field(0, cot_1, adopted)
+    inner, outer = halo(inner, outer)
+    cot_0 = turn_input(0, cot_1, adopted, field, inner, outer)
+
+    part = shape(((2 * chans + 32) // 4, units), bf16)
+    cot_own, field, inner, outer, keep, near, mate, far = call(
         last_kernel,
-        (rows_shape, edge_shape, edge_shape, part, part, part, part),
+        (rows_shape, rows_shape, edge_shape, edge_shape, part, part, part, part),
         1,
-        (meta, *cots, cols, layer_scale, down_t, down, up, slope, nhat, inv, hidden)
+        (meta, cot_top, own_2, own_1, cot_0, cols, layer_scale, down_t, down, up, slope, nhat, inv, hidden)
         + (source, acts_inner, acts_outer),
         (
             outgrads,
@@ -547,8 +613,7 @@
             pltpu.VMEM((units, width), f32),
             pltpu.VMEM((chans, width), f32),
             padded,
-            pltpu.VMEM((2 * chans + 64, units), f32),
-            pltpu.VMEM((count, chans, width), bf16),
+            pltpu.VMEM((2 * chans + 32, units), f32),
         ),
     )
     far = moved(far, ("z0", "x0"), True)
@@ -557,18 +622,15 @@
     total = added(keep, near, mate, far)
     orders = (("x1", "z1"), ("z0", "z2"), ("z1", "x0"), ("z2", "x1"))
     total, inner, outer = lax.optimization_barrier((total, inner, outer))
-    half = total.shape[0] // 2
-    first = jnp.where(core == 0, x // 2, (z + 2) // 4 % 2) == 0
-    kept = jnp.where(first, total[:half], total[half:])
-    given = jnp.where(first, total[half:], total[:half])
-    total = added(kept, moved(given, orders[0], False))
+    total = added(total, moved(total, orders[0], False))
     inner, outer = halo(inner, outer)
+    total, inner, outer = lax.optimization_barrier((total, inner, outer))
     total = added(total, moved(total, orders[1], False))
     result, sent = call(
         last_conv_kernel,
         (rows_shape, shape((CAP, chans, width), bf16)),
         1,
-        (meta, field, inner, outer, cots[-1], back, *results),
+        (meta, field, inner, outer, cot_own, back),
         (padded,),
     )
     total, result, sent = lax.optimization_barrier((total, result, sent))
@@ -582,9 +644,6 @@
         1,
         (meta, result, arrived),
     )
-    other = moved(total, orders[0], False)
-    total = jnp.concatenate([jnp.where(first, total, other), jnp.where(first, other, total)])
-    total, slotted = lax.optimization_barrier((total, slotted))
     far = moved(total, ("x0", "z0"), True)
     near = moved(total, ("x0", "z0"), False)
     mate = moved(total, ("", ""), True)
@@ -600,7 +659,7 @@
         ),
         1,
         (meta, total, near, mate, far),
-        (pltpu.VMEM((2 * chans + 64, units), f32),),
+        (pltpu.VMEM((2 * chans + 32, units), f32),),
     )
 
     grad_kernel, grad_gain, grad_up, grad_bias, grad_down, grad_scale = grads

time: 123 us -> 116 us (0.943)
  starting transfers between devices: 59.5 us -> 52 us
  Pallas kernels: 15.8 us -> 21.7 us
  waiting for transfers between devices: 41.1 us -> 37.4 us
  local copies, waits for them, and re-layouts: 4.38 us -> 2.11 us
    pallas_call x12 -> x13, Pallas kernels: 15.8 us -> 21.7 us  [call(): pl.pallas_call(body, out_shape=out_shape, in_specs=spec, out_specs=outs,...]
    ppermute x3 -> x5, waiting for transfers between devices: 9.96 us -> 4.71 us  [the longest x1 3.58 us: body(): cot_1 = lax.ppermute(cot_1, 'section', [(0, top), (top, 0), (1, 2), (2, 1)])]
    ppermute x5, starting transfers between devices: 17.6 us -> 14.8 us  [halo(): lax.ppermute(inner, 'tile', [(tile, tile ^ 1) for tile in range(TILES)])]
    ppermute x11, waiting for transfers between devices: 14.6 us -> 17.1 us  [moved(): return lax.ppermute(value, 'tile', pairs)]
    unnamed x30 -> x22, local copies, waits for them, and re-layouts: 4.29 us -> 2.03 us
    ppermute x11, starting transfers between devices: 24.9 us -> 22.7 us  [moved(): return lax.ppermute(value, 'tile', pairs)]
    ppermute x3 -> x5, starting transfers between devices: 12.4 us -> 10.4 us  [the longest x1 7.92 us: body(): cot_1 = lax.ppermute(cot_1, 'section', [(0, top), (top, 0), (1, 2), (2, 1)])]
  transfers between devices with their start and end apart: 25 -> 27, of which waited for: 17 -> 17; matrix products, arithmetic and copies ran while one was open for 0% -> 0% of each run, Pallas kernels for 3% -> 11%
where the time goes in v4:
time: 116 us
  starting transfers between devices  52 us (45%)
  waiting for transfers between devices  37.4 us (32%)
  Pallas kernels  21.7 us (19%)
  local copies, waits for them, and re-layouts  2.11 us (2%)
  other arithmetic  1.4 us (1%)
    ppermute x11, starting transfers between devices, moved(): return lax.ppermute(value, 'tile', pairs)  22.7 us
    pallas_call x13, Pallas kernels, call(): pl.pallas_call(body, out_shape=out_shape, in_specs=spec, out_specs=outs,...  21.7 us
    ppermute x11, waiting for transfers between devices, moved(): return lax.ppermute(value, 'tile', pairs)  17.1 us
    ppermute x5, starting transfers between devices, halo(): lax.ppermute(inner, 'tile', [(tile, tile ^ 1) for tile in range(TILES)])  14.8 us
    ppermute x5, waiting for transfers between devices, halo(): outer = lax.ppermute(outer, 'tile', across)  11.1 us
    ppermute x1, starting transfers between devices, body(): cot_1 = lax.ppermute(cot_1, 'section', [(0, top), (top, 0), (1, 2), (2, 1)])  7.92 us
    ppermute x1, waiting for transfers between devices, body(): cot_1 = lax.ppermute(cot_1, 'section', [(0, top), (top, 0), (1, 2), (2, 1)])  3.58 us
    ppermute x5, waiting for transfers between devices, halo(): lax.ppermute(inner, 'tile', [(tile, tile ^ 1) for tile in range(TILES)])  3.33 us
  transfers between devices with their start and end apart: 27, of which 17 were waited for; matrix products, arithmetic and copies ran while one was open for 0% of the time, Pallas kernels for 11%

profile of v4, /device:TPU:1, one launch (start us, length us, event | category | flops | bytes accessed | tf_op | source)
XLA Modules:
  0.0 115.5 jit_solution(6949550332022672659)
XLA Ops:
  1.8 2.2 %collective-permute-start = (bf16[192,768]{1,0:T(8,128)(2,1)S(1)}, bf16[192,768]{1,0:T(8,128)(2,1)S(1)}, u32[]{:S(2)}, u32[]{:S(2)}) collective-permute-start(bf16[192,768]{1,0:T(8,128)(2,1)S(1)} %broadcast_select_fusion), channel_id=1, source_target_pairs={{0,64},{64,0},{128,192},{192,128},{1,65},{65,1},{129,193},{193,129... | collective-permute-start | bytes 884744 | tf_op jit(solution)/shard_map/ppermute | solution.py:535
  4.0 2.1 %collective-permute-start.2 = (bf16[3,192,128]{2,1,0:T(8,128)(2,1)S(1)}, bf16[3,192,128]{2,1,0:T(8,128)(2,1)S(1)}, u32[]{:S(2)}, u32[]{:S(2)}) collective-permute-start(bf16[3,192,128]{2,1,0:T(8,128)(2,1)S(1)} %get-tuple-element.126), channel_id=1, source_target_pairs={{0,63},{1,2},{2,1},{3,4},{4,3},{5,6},{6,5},{7,8},{8,7},{9,10},{10,... | collective-permute-start | bytes 442376 | tf_op jit(solution)/shard_map/ppermute | solution.py:74
  6.2 6.1 %collective-permute-start.1 = (bf16[3,192,128]{2,1,0:T(8,128)(2,1)S(1)}, bf16[3,192,128]{2,1,0:T(8,128)(2,1)S(1)}, u32[]{:S(2)}, u32[]{:S(2)}) collective-permute-start(bf16[3,192,128]{2,1,0:T(8,128)(2,1)S(1)} %get-tuple-element.127), channel_id=1, source_target_pairs={{0,1},{1,0},{2,3},{3,2},{4,5},{5,4},{6,7},{7,6},{8,9},{9,8},{10,11... | collective-permute-start | bytes 442376 | tf_op jit(solution)/shard_map/ppermute | solution.py:75
  14.5 3.6 %shard_map.154 = (f32[192,640]{1,0:T(8,128)S(1)}, f32[1,640]{1,0:T(1,128)S(1)}, bf16[768,640]{1,0:T(8,128)(2,1)S(1)}, bf16[768,640]{1,0:T(8,128)(2,1)S(1)}, bf16[208,768]{1,0:T(8,128)(2,1)S(1)}) custom-call(s32[16]{0:T(128)S(1)} %concatenate.3.meta, bf16[5,192,128]{2,1,0:T(8,128)(2,1)S(1)} %bitcast.24, ...), custom_call_target="tpu_custom_call" | custom-call | tf_op jit(solution)/shard_map/pallas_call | solution.py:83
  20.0 1.3 %collective-permute-done.3.inner = bf16[3,192,128]{2,1,0:T(8,128)(2,1)S(1)} collective-permute-done((bf16[3,192,128]{2,1,0:T(8,128)(2,1)S(1)}, bf16[3,192,128]{2,1,0:T(8,128)(2,1)S(1)}, u32[]{:S(2)}, u32[]{:S(2)}) %collective-permute-start.3) | collective-permute-done | bytes 147488 | tf_op jit(solution)/shard_map/ppermute | solution.py:75
  21.4 3.5 %collective-permute-done.4.outer = bf16[3,192,128]{2,1,0:T(8,128)(2,1)S(1)} collective-permute-done((bf16[3,192,128]{2,1,0:T(8,128)(2,1)S(1)}, bf16[3,192,128]{2,1,0:T(8,128)(2,1)S(1)}, u32[]{:S(2)}, u32[]{:S(2)}) %collective-permute-start.4) | collective-permute-done | bytes 147488 | tf_op jit(solution)/shard_map/ppermute | solution.py:74
  26.6 3.2 %shard_map.157 = (f32[192,640]{1,0:T(8,128)S(1)}, f32[1,640]{1,0:T(1,128)S(1)}, bf16[768,640]{1,0:T(8,128)(2,1)S(1)}, f32[192,64]{1,0:T(8,128)S(1)}, bf16[12,112...) custom-call(s32[16]{0:T(128)S(1)} %concatenate.3.meta, ...), custom_call_target="tpu_custom_call" | custom-call | flops 1000000000 | bytes 10000000 | tf_op jit(solution)/shard_map/pallas_call | solution.py:83
  30.3 2.4 %collective-permute-start.8 = (bf16[3,192,128]{2,1,0:T(8,128)(2,1)S(1)}, bf16[3,192,128]{2,1,0:T(8,128)(2,1)S(1)}, u32[]{:S(2)}, u32[]{:S(2)}) collective-permute-start(bf16[3,192,128]{2,1,0:T(8,128)(2,1)S(1)} %get-tuple-element.85), channel_id=1, source_target_pairs={{0,1},{1,0},{2,3},{3,2},{4,5},{5,4},{6,7},{7,6},{8,9},{9,8},{10,11... | collective-permute-start | bytes 442376 | tf_op jit(solution)/shard_map/ppermute | solution.py:75
  33.8 3.6 %collective-permute-done.9.outer = bf16[3,192,128]{2,1,0:T(8,128)(2,1)S(1)} collective-permute-done((bf16[3,192,128]{2,1,0:T(8,128)(2,1)S(1)}, bf16[3,192,128]{2,1,0:T(8,128)(2,1)S(1)}, u32[]{:S(2)}, u32[]{:S(2)}) %collective-permute-start.9) | collective-permute-done | bytes 147488 | tf_op jit(solution)/shard_map/ppermute | solution.py:74
  38.1 7.9 %collective-permute-start.10 = (bf16[5,192,128]{2,1,0:T(8,128)(2,1)S(1)}, bf16[5,192,128]{2,1,0:T(8,128)(2,1)S(1)}, u32[]{:S(2)}, u32[]{:S(2)}) collective-permute-start(bf16[5,192,128]{2,1,0:T(8,128)(2,1)S(1)} %shard_map.159), channel_id=1, source_target_pairs={{0,192},{192,0},{64,128},{128,64},{1,193},{193,1},{65,129},{129,65... | collective-permute-start | bytes 737288 | tf_op jit(solution)/shard_map/ppermute | solution.py:596
  46.0 3.6 %collective-permute-done.10.cot = bf16[5,192,128]{2,1,0:T(8,128)(2,1)S(1)} collective-permute-done((bf16[5,192,128]{2,1,0:T(8,128)(2,1)S(1)}, bf16[5,192,128]{2,1,0:T(8,128)(2,1)S(1)}, u32[]{:S(2)}, u32[]{:S(2)}) %collective-permute-start.10) | collective-permute-done | bytes 245792 | tf_op jit(solution)/shard_map/ppermute | solution.py:596
  49.6 1.5 %shard_map.160 = (bf16[5,192,128]{2,1,0:T(8,128)(2,1)S(1)}, bf16[3,192,128]{2,1,0:T(8,128)(2,1)S(1)}, bf16[3,192,128]{2,1,0:T(8,128)(2,1)S(1)}) custom-call(s32[16]{0:T(128)S(1)} %concatenate.3.meta, bf16[5,192,128]{2,1,0:T(8,128)(2,1)S(1)} %collective-permute-done.10.cot, f32[192,64]{1,0:T(8,128)S(1)} %get-tuple-element.78.cols, ...), custom_call_target="tpu_custom_call" | custom-call | tf_op jit(solution)/shard_map/pallas_call | solution.py:83
  51.1 4.4 %collective-permute-start.12 = (bf16[3,192,128]{2,1,0:T(8,128)(2,1)S(1)}, bf16[3,192,128]{2,1,0:T(8,128)(2,1)S(1)}, u32[]{:S(2)}, u32[]{:S(2)}) collective-permute-start(bf16[3,192,128]{2,1,0:T(8,128)(2,1)S(1)} %get-tuple-element.89), channel_id=1, source_target_pairs={{0,1},{1,0},{2,3},{3,2},{4,5},{5,4},{6,7},{7,6},{8,9},{9,8},{10,11... | collective-permute-start | bytes 442376 | tf_op jit(solution)/shard_map/ppermute | solution.py:75
  56.5 3.7 %collective-permute-done.13.outer = bf16[3,192,128]{2,1,0:T(8,128)(2,1)S(1)} collective-permute-done((bf16[3,192,128]{2,1,0:T(8,128)(2,1)S(1)}, bf16[3,192,128]{2,1,0:T(8,128)(2,1)S(1)}, u32[]{:S(2)}, u32[]{:S(2)}) %collective-permute-start.13) | collective-permute-done | bytes 147488 | tf_op jit(solution)/shard_map/ppermute | solution.py:74
  60.2 2.1 %shard_map.161.cot_0 = bf16[5,192,128]{2,1,0:T(8,128)(2,1)S(1)} custom-call(s32[16]{0:T(128)S(1)} %concatenate.3.meta, bf16[5,192,128]{2,1,0:T(8,128)(2,1)S(1)} %get-tuple-element.88.field, bf16[3,192,128]{2,1,0:T(8,128)(2,1)S(1)} %collective-permute-done.12.inner, bf16[3,192,128]{2,1,0:T(8,128)(2,1)S(1)} %collective-permute-done.13.outer, ...), custom_call_target="tpu_custom_call" | custom-call | tf_op jit(solution)/shard_map/pallas_call | solution.py:83
  62.4 3.0 %shard_map.162 = (bf16[5,192,128]{2,1,0:T(8,128)(2,1)S(1)}, bf16[5,192,128]{2,1,0:T(8,128)(2,1)S(1)}, bf16[3,192,128]{2,1,0:T(8,128)(2,1)S(1)}, bf16[3,192,128]{...) custom-call(s32[16]{0:T(128)S(1)} %concatenate.3.meta, ...), custom_call_target="tpu_custom_call" | custom-call | tf_op jit(solution)/shard_map/pallas_call | solution.py:83
  65.5 3.3 %collective-permute-start.15 = (bf16[104,768]{1,0:T(8,128)(2,1)S(1)}, bf16[104,768]{1,0:T(8,128)(2,1)S(1)}, u32[]{:S(2)}, u32[]{:S(2)}) collective-permute-start(bf16[104,768]{1,0:T(8,128)(2,1)S(1)} %get-tuple-element.94), channel_id=1, source_target_pairs={{0,1},{1,0},{2,3},{3,2},{4,5},{5,4},{6,7},{7,6},{8,9},{9,8},{10,11... | collective-permute-start | bytes 479240 | tf_op jit(solution)/shard_map/ppermute | solution.py:69
  68.8 1.5 %collective-permute-start.16 = (bf16[104,768]{1,0:T(8,128)(2,1)S(1)}, bf16[104,768]{1,0:T(8,128)(2,1)S(1)}, u32[]{:S(2)}, u32[]{:S(2)}) collective-permute-start(bf16[104,768]{1,0:T(8,128)(2,1)S(1)} %get-tuple-element.95), channel_id=1, source_target_pairs={{0,9},{1,2},{2,11},{3,0},{4,13},{5,6},{6,15},{7,4},{8,1},{9,10},{1... | collective-permute-start | bytes 479240 | tf_op jit(solution)/shard_map/ppermute | solution.py:69
  70.3 3.5 %collective-permute-done.16 = bf16[104,768]{1,0:T(8,128)(2,1)S(1)} collective-permute-done((bf16[104,768]{1,0:T(8,128)(2,1)S(1)}, bf16[104,768]{1,0:T(8,128)(2,1)S(1)}, u32[]{:S(2)}, u32[]{:S(2)}) %collective-permute-start.16) | collective-permute-done | bytes 159776 | tf_op jit(solution)/shard_map/ppermute | solution.py:69
  74.0 1.8 %collective-permute-start.18 = (bf16[3,192,128]{2,1,0:T(8,128)(2,1)S(1)}, bf16[3,192,128]{2,1,0:T(8,128)(2,1)S(1)}, u32[]{:S(2)}, u32[]{:S(2)}) collective-permute-start(bf16[3,192,128]{2,1,0:T(8,128)(2,1)S(1)} %get-tuple-element.99), channel_id=1, source_target_pairs={{0,1},{1,0},{2,3},{3,2},{4,5},{5,4},{6,7},{7,6},{8,9},{9,8},{10,11... | collective-permute-start | bytes 442376 | tf_op jit(solution)/shard_map/ppermute | solution.py:75
  75.8 4.5 %collective-permute-done.17 = bf16[104,768]{1,0:T(8,128)(2,1)S(1)} collective-permute-done((bf16[104,768]{1,0:T(8,128)(2,1)S(1)}, bf16[104,768]{1,0:T(8,128)(2,1)S(1)}, u32[]{:S(2)}, u32[]{:S(2)}) %collective-permute-start.17) | collective-permute-done | bytes 159776 | tf_op jit(solution)/shard_map/ppermute | solution.py:69
  80.7 3.0 %collective-permute-start.20 = (bf16[104,768]{1,0:T(8,128)(2,1)S(1)}, bf16[104,768]{1,0:T(8,128)(2,1)S(1)}, u32[]{:S(2)}, u32[]{:S(2)}) collective-permute-start(bf16[104,768]{1,0:T(8,128)(2,1)S(1)} %add_convert_fusion.3), channel_id=1, source_target_pairs={{0,8},{1,57},{2,10},{3,59},{4,12},{5,61},{6,14},{7,63},{8,0},{9,49... | collective-permute-start | bytes 479240 | tf_op jit(solution)/shard_map/ppermute | solution.py:69
  83.6 2.2 %shard_map.163 = (bf16[5,192,128]{2,1,0:T(8,128)(2,1)S(1)}, bf16[2,192,128]{2,1,0:T(8,128)(2,1)S(1)}) custom-call(s32[16]{0:T(128)S(1)} %concatenate.3.meta, bf16[5,192,128]{2,1,0:T(8,128)(2,1)S(1)} %get-tuple-element.102.field, bf16[3,192,128]{2,1,0:T(8,128)(2,1)S(1)} %collective-permute-done.18.inner, ...), custom_call_target="tpu_custom_call" | custom-call | tf_op jit(solution)/shard_map/pallas_call | solution.py:83
  85.8 2.2 %collective-permute-done.20 = bf16[104,768]{1,0:T(8,128)(2,1)S(1)} collective-permute-done((bf16[104,768]{1,0:T(8,128)(2,1)S(1)}, bf16[104,768]{1,0:T(8,128)(2,1)S(1)}, u32[]{:S(2)}, u32[]{:S(2)}) %collective-permute-start.20) | collective-permute-done | bytes 159776 | tf_op jit(solution)/shard_map/ppermute | solution.py:69
  88.0 1.4 %collective-permute-start.21 = (bf16[104,768]{1,0:T(8,128)(2,1)S(1)}, bf16[104,768]{1,0:T(8,128)(2,1)S(1)}, u32[]{:S(2)}, u32[]{:S(2)}) collective-permute-start(bf16[104,768]{1,0:T(8,128)(2,1)S(1)} %add_convert_fusion.2), channel_id=1, source_target_pairs={{0,24},{1,3},{2,26},{3,1},{4,28},{5,7},{6,30},{7,5},{8,16},{9,11},... | collective-permute-start | bytes 479240 | tf_op jit(solution)/shard_map/ppermute | solution.py:69
  89.5 3.0 %collective-permute-done.21 = bf16[104,768]{1,0:T(8,128)(2,1)S(1)} collective-permute-done((bf16[104,768]{1,0:T(8,128)(2,1)S(1)}, bf16[104,768]{1,0:T(8,128)(2,1)S(1)}, u32[]{:S(2)}, u32[]{:S(2)}) %collective-permute-start.21) | collective-permute-done | bytes 159776 | tf_op jit(solution)/shard_map/ppermute | solution.py:69
  92.5 4.2 %collective-permute-start.22 = (bf16[104,768]{1,0:T(8,128)(2,1)S(1)}, bf16[104,768]{1,0:T(8,128)(2,1)S(1)}, u32[]{:S(2)}, u32[]{:S(2)}) collective-permute-start(bf16[104,768]{1,0:T(8,128)(2,1)S(1)} %add_convert_fusion.1), channel_id=1, source_target_pairs={{0,56},{1,7},{2,58},{3,5},{4,60},{5,3},{6,62},{7,1},{8,48},{9,15},... | collective-permute-start | bytes 479240 | tf_op jit(solution)/shard_map/ppermute | solution.py:69
  96.7 1.9 %collective-permute-start.23 = (bf16[2,192,128]{2,1,0:T(8,128)(2,1)S(1)}, bf16[2,192,128]{2,1,0:T(8,128)(2,1)S(1)}, u32[]{:S(2)}, u32[]{:S(2)}) collective-permute-start(bf16[2,192,128]{2,1,0:T(8,128)(2,1)S(1)} %get-tuple-element.110), channel_id=1, source_target_pairs={{0,1},{1,2},{2,3},{3,4},{4,5},{5,6},{6,7},{7,8},{8,9},{9,10},{10,1... | collective-permute-start | bytes 294920 | tf_op jit(solution)/shard_map/ppermute | solution.py:638
  100.5 7.9 %collective-permute-start.26 = (bf16[104,768]{1,0:T(8,128)(2,1)S(1)}, bf16[104,768]{1,0:T(8,128)(2,1)S(1)}, u32[]{:S(2)}, u32[]{:S(2)}) collective-permute-start(bf16[104,768]{1,0:T(8,128)(2,1)S(1)} %add_convert_fusion.keep), channel_id=1, source_target_pairs={{0,3},{1,8},{2,1},{3,10},{4,7},{5,12},{6,5},{7,14},{8,11},{9,0},{1... | collective-permute-start | bytes 479240 | tf_op jit(solution)/shard_map/ppermute | solution.py:69
  108.6 1.3 %shard_map.164 = bf16[3,192,128]{2,1,0:T(8,128)(2,1)} custom-call(s32[16]{0:T(128)S(1)} %concatenate.3.meta, bf16[5,192,128]{2,1,0:T(8,128)(2,1)S(1)} %get-tuple-element.108.result, bf16[2,192,128]{2,1,0:T(8,128)(2,1)S(1)} %collective-permute-done.23.arrived), custom_call_target="tpu_custom_call" | custom-call | tf_op jit(solution)/shard_map/pallas_call | solution.py:83
  110.7 2.4 %collective-permute-done.24.near = bf16[104,768]{1,0:T(8,128)(2,1)S(1)} collective-permute-done((bf16[104,768]{1,0:T(8,128)(2,1)S(1)}, bf16[104,768]{1,0:T(8,128)(2,1)S(1)}, u32[]{:S(2)}, u32[]{:S(2)}) %collective-permute-start.24) | collective-permute-done | bytes 159776 | tf_op jit(solution)/shard_map/ppermute | solution.py:69
  113.1 1.7 %shard_map.165 = (f32[1,49,192]{2,1,0:T(8,128)S(1)}, f32[1,192]{1,0:T(1,128)}, f32[1,192,768]{2,1,0:T(8,128)}, f32[1,768]{1,0:T(1,128)}, f32[1,192,768]{2,1,0:T(8,128)}, /*index=5*/f32[1,192]{1,0:T(1,128)}) custom-call(s32[16]{0:T(128)S(1)} %concatenate.3.meta, bf16[104,768]{1,0:T(8,128)(2,1)S(1)} %add_convert_fusion.keep, ...), custom_call_target="tpu_custom_call" | custom-call | tf_op jit(solution)/shard_map/pallas_call | solution.py:83
  (65 shorter events, 14.4 us)
Async XLA Ops:
  0.6 3.4 %copy-start.1 = (bf16[1,5,192,128]{3,2,1,0:T(8,128)(2,1)S(1)}, bf16[1,5,192,128]{3,2,1,0:T(8,128)(2,1)}, u32[]{:S(2)}) copy-start(bf16[1,5,192,128]{3,2,1,0:T(8,128)(2,1)} %param.10) | copy-start | bytes 737284
  1.8 17.1 %collective-permute-start = (bf16[192,768]{1,0:T(8,128)(2,1)S(1)}, bf16[192,768]{1,0:T(8,128)(2,1)S(1)}, u32[]{:S(2)}, u32[]{:S(2)}) collective-permute-start(bf16[192,768]{1,0:T(8,128)(2,1)S(1)} %broadcast_select_fusion), channel_id=1, source_target_pairs={{0,64},{64,0},{128,192},{192,128},{1,65},{65,1},{129,193},{193,129... | collective-permute-start | bytes 884744 | tf_op jit(solution)/shard_map/ppermute | solution.py:535
  4.0 8.3 %copy-start.7 = (f32[1,49,192]{2,0,1:T(1,128)S(1)}, f32[1,49,192]{2,0,1:T(1,128)}, u32[]{:S(2)}) copy-start(f32[1,49,192]{2,0,1:T(1,128)} %param.14) | copy-start | bytes 112900
  4.0 9.1 %copy-start.3 = (bf16[1,192,768]{2,1,0:T(8,128)(2,1)S(1)}, bf16[1,192,768]{2,1,0:T(8,128)(2,1)}, u32[]{:S(2)}) copy-start(bf16[1,192,768]{2,1,0:T(8,128)(2,1)} %param.18) | copy-start | bytes 884740
  4.0 9.1 %copy-start = (bf16[1,192,768]{2,1,0:T(8,128)(2,1)S(1)}, bf16[1,192,768]{2,1,0:T(8,128)(2,1)}, u32[]{:S(2)}) copy-start(bf16[1,192,768]{2,1,0:T(8,128)(2,1)} %param.16) | copy-start | bytes 884740
  4.0 10.4 %collective-permute-start.2 = (bf16[3,192,128]{2,1,0:T(8,128)(2,1)S(1)}, bf16[3,192,128]{2,1,0:T(8,128)(2,1)S(1)}, u32[]{:S(2)}, u32[]{:S(2)}) collective-permute-start(bf16[3,192,128]{2,1,0:T(8,128)(2,1)S(1)} %get-tuple-element.126), channel_id=1, source_target_pairs={{0,63},{1,2},{2,1},{3,4},{4,3},{5,6},{6,5},{7,8},{8,7},{9,10},{10,... | collective-permute-start | bytes 442376 | tf_op jit(solution)/shard_map/ppermute | solution.py:74
  6.2 8.3 %collective-permute-start.1 = (bf16[3,192,128]{2,1,0:T(8,128)(2,1)S(1)}, bf16[3,192,128]{2,1,0:T(8,128)(2,1)S(1)}, u32[]{:S(2)}, u32[]{:S(2)}) collective-permute-start(bf16[3,192,128]{2,1,0:T(8,128)(2,1)S(1)} %get-tuple-element.127), channel_id=1, source_target_pairs={{0,1},{1,0},{2,3},{3,2},{4,5},{5,4},{6,7},{7,6},{8,9},{9,8},{10,11... | collective-permute-start | bytes 442376 | tf_op jit(solution)/shard_map/ppermute | solution.py:75
  14.5 3.9 %copy-start.2 = (bf16[5,192,128]{2,1,0:T(8,128)(2,1)S(1)}, bf16[5,192,128]{2,1,0:T(8,128)(2,1)}, u32[]{:S(2)}) copy-start(bf16[5,192,128]{2,1,0:T(8,128)(2,1)} %cot_top.1) | copy-start | bytes 737284
  18.1 8.5 %collective-permute-start.6 = (bf16[208,768]{1,0:T(8,128)(2,1)S(1)}, bf16[208,768]{1,0:T(8,128)(2,1)S(1)}, u32[]{:S(2)}, u32[]{:S(2)}) collective-permute-start(bf16[208,768]{1,0:T(8,128)(2,1)S(1)} %get-tuple-element.76), channel_id=1, source_target_pairs={{0,64},{64,0},{128,192},{192,128},{1,65},{65,1},{129,193},{193,129... | collective-permute-start | bytes 958472 | tf_op jit(solution)/shard_map/ppermute | solution.py:547
  18.9 7.7 %collective-permute-start.7 = (bf16[192,768]{1,0:T(8,128)(2,1)S(1)}, bf16[192,768]{1,0:T(8,128)(2,1)S(1)}, u32[]{:S(2)}, u32[]{:S(2)}) collective-permute-start(bf16[192,768]{1,0:T(8,128)(2,1)S(1)} %collective-permute-done.half), channel_id=1, source_target_pairs={{0,1},{1,0},{2,3},{3,2},{4,5},{5,4},{6,7},{7,6},{8,9},{9,8},{10,11... | collective-permute-start | bytes 884744 | tf_op jit(solution)/shard_map/ppermute | solution.py:69
  19.9 1.4 %collective-permute-start.3 = (bf16[3,192,128]{2,1,0:T(8,128)(2,1)S(1)}, bf16[3,192,128]{2,1,0:T(8,128)(2,1)S(1)}, u32[]{:S(2)}, u32[]{:S(2)}) collective-permute-start(bf16[3,192,128]{2,1,0:T(8,128)(2,1)S(1)} %get-tuple-element.73), channel_id=1, source_target_pairs={{0,1},{1,0},{2,3},{3,2},{4,5},{5,4},{6,7},{7,6},{8,9},{9,8},{10,11... | collective-permute-start | bytes 442376 | tf_op jit(solution)/shard_map/ppermute | solution.py:75
  20.0 4.9 %collective-permute-start.4 = (bf16[3,192,128]{2,1,0:T(8,128)(2,1)S(1)}, bf16[3,192,128]{2,1,0:T(8,128)(2,1)S(1)}, u32[]{:S(2)}, u32[]{:S(2)}) collective-permute-start(bf16[3,192,128]{2,1,0:T(8,128)(2,1)S(1)} %get-tuple-element.74), channel_id=1, source_target_pairs={{0,63},{1,2},{2,1},{3,4},{4,3},{5,6},{6,5},{7,8},{8,7},{9,10},{10,... | collective-permute-start | bytes 442376 | tf_op jit(solution)/shard_map/ppermute | solution.py:74
  30.3 3.4 %collective-permute-start.8 = (bf16[3,192,128]{2,1,0:T(8,128)(2,1)S(1)}, bf16[3,192,128]{2,1,0:T(8,128)(2,1)S(1)}, u32[]{:S(2)}, u32[]{:S(2)}) collective-permute-start(bf16[3,192,128]{2,1,0:T(8,128)(2,1)S(1)} %get-tuple-element.85), channel_id=1, source_target_pairs={{0,1},{1,0},{2,3},{3,2},{4,5},{5,4},{6,7},{7,6},{8,9},{9,8},{10,11... | collective-permute-start | bytes 442376 | tf_op jit(solution)/shard_map/ppermute | solution.py:75
  32.8 4.6 %collective-permute-start.9 = (bf16[3,192,128]{2,1,0:T(8,128)(2,1)S(1)}, bf16[3,192,128]{2,1,0:T(8,128)(2,1)S(1)}, u32[]{:S(2)}, u32[]{:S(2)}) collective-permute-start(bf16[3,192,128]{2,1,0:T(8,128)(2,1)S(1)} %get-tuple-element.86), channel_id=1, source_target_pairs={{0,63},{1,2},{2,1},{3,4},{4,3},{5,6},{6,5},{7,8},{8,7},{9,10},{10,... | collective-permute-start | bytes 442376 | tf_op jit(solution)/shard_map/ppermute | solution.py:74
  38.1 11.5 %collective-permute-start.10 = (bf16[5,192,128]{2,1,0:T(8,128)(2,1)S(1)}, bf16[5,192,128]{2,1,0:T(8,128)(2,1)S(1)}, u32[]{:S(2)}, u32[]{:S(2)}) collective-permute-start(bf16[5,192,128]{2,1,0:T(8,128)(2,1)S(1)} %shard_map.159), channel_id=1, source_target_pairs={{0,192},{192,0},{64,128},{128,64},{1,193},{193,1},{65,129},{129,65... | collective-permute-start | bytes 737288 | tf_op jit(solution)/shard_map/ppermute | solution.py:596
  46.0 16.4 %collective-permute-start.5 = (bf16[5,192,128]{2,1,0:T(8,128)(2,1)S(1)}, bf16[5,192,128]{2,1,0:T(8,128)(2,1)S(1)}, u32[]{:S(2)}, u32[]{:S(2)}) collective-permute-start(bf16[5,192,128]{2,1,0:T(8,128)(2,1)S(1)} %shard_map.156.cot), channel_id=1, source_target_pairs={{0,64},{64,0},{128,192},{192,128},{1,65},{65,1},{129,193},{193,129... | collective-permute-start | bytes 737288 | tf_op jit(solution)/shard_map/ppermute | solution.py:591
  49.6 12.8 %collective-permute-start.11 = (bf16[5,192,128]{2,1,0:T(8,128)(2,1)S(1)}, bf16[5,192,128]{2,1,0:T(8,128)(2,1)S(1)}, u32[]{:S(2)}, u32[]{:S(2)}) collective-permute-start(bf16[5,192,128]{2,1,0:T(8,128)(2,1)S(1)} %collective-permute-done.10.cot), channel_id=1, source_target_pairs={{0,64},{64,0},{128,192},{192,128},{1,65},{65,1},{129,193},{193,129... | collective-permute-start | bytes 737288 | tf_op jit(solution)/shard_map/ppermute | solution.py:597
  51.1 5.4 %collective-permute-start.12 = (bf16[3,192,128]{2,1,0:T(8,128)(2,1)S(1)}, bf16[3,192,128]{2,1,0:T(8,128)(2,1)S(1)}, u32[]{:S(2)}, u32[]{:S(2)}) collective-permute-start(bf16[3,192,128]{2,1,0:T(8,128)(2,1)S(1)} %get-tuple-element.89), channel_id=1, source_target_pairs={{0,1},{1,0},{2,3},{3,2},{4,5},{5,4},{6,7},{7,6},{8,9},{9,8},{10,11... | collective-permute-start | bytes 442376 | tf_op jit(solution)/shard_map/ppermute | solution.py:75
  55.5 4.7 %collective-permute-start.13 = (bf16[3,192,128]{2,1,0:T(8,128)(2,1)S(1)}, bf16[3,192,128]{2,1,0:T(8,128)(2,1)S(1)}, u32[]{:S(2)}, u32[]{:S(2)}) collective-permute-start(bf16[3,192,128]{2,1,0:T(8,128)(2,1)S(1)} %get-tuple-element.90), channel_id=1, source_target_pairs={{0,63},{1,2},{2,1},{3,4},{4,3},{5,6},{6,5},{7,8},{8,7},{9,10},{10,... | collective-permute-start | bytes 442376 | tf_op jit(solution)/shard_map/ppermute | solution.py:74
  65.4 5.0 %collective-permute-start.14 = (bf16[104,768]{1,0:T(8,128)(2,1)S(1)}, bf16[104,768]{1,0:T(8,128)(2,1)S(1)}, u32[]{:S(2)}, u32[]{:S(2)}) collective-permute-start(bf16[104,768]{1,0:T(8,128)(2,1)S(1)} %get-tuple-element.93), channel_id=1, source_target_pairs={{0,2},{1,9},{2,0},{3,11},{4,6},{5,13},{6,4},{7,15},{8,10},{9,1},{1... | collective-permute-start | bytes 479240 | tf_op jit(solution)/shard_map/ppermute | solution.py:69
  65.5 4.9 %collective-permute-start.15 = (bf16[104,768]{1,0:T(8,128)(2,1)S(1)}, bf16[104,768]{1,0:T(8,128)(2,1)S(1)}, u32[]{:S(2)}, u32[]{:S(2)}) collective-permute-start(bf16[104,768]{1,0:T(8,128)(2,1)S(1)} %get-tuple-element.94), channel_id=1, source_target_pairs={{0,1},{1,0},{2,3},{3,2},{4,5},{5,4},{6,7},{7,6},{8,9},{9,8},{10,11... | collective-permute-start | bytes 479240 | tf_op jit(solution)/shard_map/ppermute | solution.py:69
  68.8 5.0 %collective-permute-start.16 = (bf16[104,768]{1,0:T(8,128)(2,1)S(1)}, bf16[104,768]{1,0:T(8,128)(2,1)S(1)}, u32[]{:S(2)}, u32[]{:S(2)}) collective-permute-start(bf16[104,768]{1,0:T(8,128)(2,1)S(1)} %get-tuple-element.95), channel_id=1, source_target_pairs={{0,9},{1,2},{2,11},{3,0},{4,13},{5,6},{6,15},{7,4},{8,1},{9,10},{1... | collective-permute-start | bytes 479240 | tf_op jit(solution)/shard_map/ppermute | solution.py:69
  73.9 6.4 %collective-permute-start.17 = (bf16[104,768]{1,0:T(8,128)(2,1)S(1)}, bf16[104,768]{1,0:T(8,128)(2,1)S(1)}, u32[]{:S(2)}, u32[]{:S(2)}) collective-permute-start(bf16[104,768]{1,0:T(8,128)(2,1)S(1)} %add_convert_fusion.4), channel_id=1, source_target_pairs={{0,6},{1,25},{2,4},{3,27},{4,2},{5,29},{6,0},{7,31},{8,14},{9,17},... | collective-permute-start | bytes 479240 | tf_op jit(solution)/shard_map/ppermute | solution.py:69
  74.0 6.4 %collective-permute-start.18 = (bf16[3,192,128]{2,1,0:T(8,128)(2,1)S(1)}, bf16[3,192,128]{2,1,0:T(8,128)(2,1)S(1)}, u32[]{:S(2)}, u32[]{:S(2)}) collective-permute-start(bf16[3,192,128]{2,1,0:T(8,128)(2,1)S(1)} %get-tuple-element.99), channel_id=1, source_target_pairs={{0,1},{1,0},{2,3},{3,2},{4,5},{5,4},{6,7},{7,6},{8,9},{9,8},{10,11... | collective-permute-start | bytes 442376 | tf_op jit(solution)/shard_map/ppermute | solution.py:75
  75.8 4.9 %collective-permute-start.19 = (bf16[3,192,128]{2,1,0:T(8,128)(2,1)S(1)}, bf16[3,192,128]{2,1,0:T(8,128)(2,1)S(1)}, u32[]{:S(2)}, u32[]{:S(2)}) collective-permute-start(bf16[3,192,128]{2,1,0:T(8,128)(2,1)S(1)} %get-tuple-element.100), channel_id=1, source_target_pairs={{0,63},{1,2},{2,1},{3,4},{4,3},{5,6},{6,5},{7,8},{8,7},{9,10},{10,... | collective-permute-start | bytes 442376 | tf_op jit(solution)/shard_map/ppermute | solution.py:74
  80.7 7.3 %collective-permute-start.20 = (bf16[104,768]{1,0:T(8,128)(2,1)S(1)}, bf16[104,768]{1,0:T(8,128)(2,1)S(1)}, u32[]{:S(2)}, u32[]{:S(2)}) collective-permute-start(bf16[104,768]{1,0:T(8,128)(2,1)S(1)} %add_convert_fusion.3), channel_id=1, source_target_pairs={{0,8},{1,57},{2,10},{3,59},{4,12},{5,61},{6,14},{7,63},{8,0},{9,49... | collective-permute-start | bytes 479240 | tf_op jit(solution)/shard_map/ppermute | solution.py:69
  88.0 4.4 %collective-permute-start.21 = (bf16[104,768]{1,0:T(8,128)(2,1)S(1)}, bf16[104,768]{1,0:T(8,128)(2,1)S(1)}, u32[]{:S(2)}, u32[]{:S(2)}) collective-permute-start(bf16[104,768]{1,0:T(8,128)(2,1)S(1)} %add_convert_fusion.2), channel_id=1, source_target_pairs={{0,24},{1,3},{2,26},{3,1},{4,28},{5,7},{6,30},{7,5},{8,16},{9,11},... | collective-permute-start | bytes 479240 | tf_op jit(solution)/shard_map/ppermute | solution.py:69
  92.5 6.8 %collective-permute-start.22 = (bf16[104,768]{1,0:T(8,128)(2,1)S(1)}, bf16[104,768]{1,0:T(8,128)(2,1)S(1)}, u32[]{:S(2)}, u32[]{:S(2)}) collective-permute-start(bf16[104,768]{1,0:T(8,128)(2,1)S(1)} %add_convert_fusion.1), channel_id=1, source_target_pairs={{0,56},{1,7},{2,58},{3,5},{4,60},{5,3},{6,62},{7,1},{8,48},{9,15},... | collective-permute-start | bytes 479240 | tf_op jit(solution)/shard_map/ppermute | solution.py:69
  96.7 3.8 %collective-permute-start.23 = (bf16[2,192,128]{2,1,0:T(8,128)(2,1)S(1)}, bf16[2,192,128]{2,1,0:T(8,128)(2,1)S(1)}, u32[]{:S(2)}, u32[]{:S(2)}) collective-permute-start(bf16[2,192,128]{2,1,0:T(8,128)(2,1)S(1)} %get-tuple-element.110), channel_id=1, source_target_pairs={{0,1},{1,2},{2,3},{3,4},{4,5},{5,6},{6,7},{7,8},{8,9},{9,10},{10,1... | collective-permute-start | bytes 294920 | tf_op jit(solution)/shard_map/ppermute | solution.py:638
  100.5 10.1 %collective-permute-start.26 = (bf16[104,768]{1,0:T(8,128)(2,1)S(1)}, bf16[104,768]{1,0:T(8,128)(2,1)S(1)}, u32[]{:S(2)}, u32[]{:S(2)}) collective-permute-start(bf16[104,768]{1,0:T(8,128)(2,1)S(1)} %add_convert_fusion.keep), channel_id=1, source_target_pairs={{0,3},{1,8},{2,1},{3,10},{4,7},{5,12},{6,5},{7,14},{8,11},{9,0},{1... | collective-permute-start | bytes 479240 | tf_op jit(solution)/shard_map/ppermute | solution.py:69
  108.5 2.2 %collective-permute-start.25 = (bf16[104,768]{1,0:T(8,128)(2,1)S(1)}, bf16[104,768]{1,0:T(8,128)(2,1)S(1)}, u32[]{:S(2)}, u32[]{:S(2)}) collective-permute-start(bf16[104,768]{1,0:T(8,128)(2,1)S(1)} %add_convert_fusion.keep), channel_id=1, source_target_pairs={{0,1},{1,0},{2,3},{3,2},{4,5},{5,4},{6,7},{7,6},{8,9},{9,8},{10,11... | collective-permute-start | bytes 479240 | tf_op jit(solution)/shard_map/ppermute | solution.py:69
  108.5 4.7 %collective-permute-start.24 = (bf16[104,768]{1,0:T(8,128)(2,1)S(1)}, bf16[104,768]{1,0:T(8,128)(2,1)S(1)}, u32[]{:S(2)}, u32[]{:S(2)}) collective-permute-start(bf16[104,768]{1,0:T(8,128)(2,1)S(1)} %add_convert_fusion.keep), channel_id=1, source_target_pairs={{0,2},{1,9},{2,0},{3,11},{4,6},{5,13},{6,4},{7,15},{8,10},{9,1},{1... | collective-permute-start | bytes 479240 | tf_op jit(solution)/shard_map/ppermute | solution.py:69
  (5 other events, 3.5 us)

commit v5 on v4

--- a/solution.py
+++ b/solution.py
@@ -331,6 +331,36 @@
         conv_rows(meta, field, inner, outer, cot, taps_mat, result_ref, rows_ref)
 
 
+def middle_kernel(
+    plane,
+    meta,
+    field,
+    inner,
+    outer,
+    cot,
+    taps_mat,
+    cols,
+    down_t,
+    up,
+    slope,
+    nhat,
+    inv,
+    result_ref,
+    field_ref,
+    inner_ref,
+    outer_ref,
+    rows_ref,
+    out_ref,
+    low_ref,
+):
+    @pl.when(meta[SECTION] == plane)
+    def _():
+        conv_rows(meta, field, inner, outer, cot, taps_mat, result_ref, rows_ref)
+        cots = [result_ref[row].astype(f32) for row in range(result_ref.shape[0])]
+        mlp_backward(cots, meta, cols, down_t, up, slope, nhat, inv, out_ref, low_ref, field_ref)
+        edges(meta[ODD] == 1, field_ref, inner_ref, outer_ref)
+
+
 def last_conv_kernel(meta, field, inner, outer, cot, taps_mat, result_ref, sent_ref, rows_ref):
     conv_rows(meta, field, inner, outer, cot, taps_mat, result_ref, rows_ref)
     sent_ref[...] = jnp.zeros_like(sent_ref)
@@ -364,7 +394,11 @@
     cot_top,
     cot_2,
     cot_1,
-    cot_0,
+    turn_field,
+    turn_inner,
+    turn_outer,
+    turn_cot,
+    turn_mat,
     cols,
     layer_row,
     down_t,
@@ -395,11 +429,15 @@
     count, chans, width = acts.shape
     units = slope.shape[0]
     odd = meta[ODD] == 1
-    for section, cot in ((3, cot_top), (2, cot_2), (1, cot_1), (0, cot_0)):
+    for section, cot in ((3, cot_top), (2, cot_2), (1, cot_1)):
 
         @pl.when(meta[SECTION] == section)
         def _():
             cot_ref[...] = cot[...]
+
+    @pl.when(meta[SECTION] == 0)
+    def _():
+        conv_rows(meta, turn_field, turn_inner, turn_outer, turn_cot, turn_mat, cot_ref, rows_ref)
 
     cots = [cot_ref[row].astype(f32) for row in range(count)]
     mlp_backward(
@@ -482,7 +520,8 @@
                 half = jnp.where(lane == block - first, part, half)
             halves.append(half)
         line = jnp.concatenate(halves, axis=1)
-        kernel_ref[0, tap_row * KS : (tap_row + 1) * KS] = line[:KS, :chans]
+        for tap_col in range(KS):
+            kernel_ref[tap_row * KS + tap_col] = line[tap_col : tap_col + 1, :chans]
     bias_ref[...] = packed_ref[base + 16 : base + 17]
     gain_ref[...] = packed_ref[base + 17 : base + 18, :chans]
     scale_ref[...] = packed_ref[base + 17 : base + 18, 256 : 256 + chans]
@@ -552,7 +591,7 @@
     lowgrads = pltpu.VMEM((units, cells), bf16)
 
     def turn_field(plane, cot, params):
-        field_cols, field_down_t, field_up, field_slope, field_nhat, field_inv, _ = params
+        field_cols, field_down_t, field_up, field_slope, field_nhat, field_inv = params
         return call(
             functools.partial(turn_kernel, plane),
             (rows_shape, edge_shape, edge_shape),
@@ -561,18 +600,8 @@
             (outgrads, lowgrads),
         )
 
-    def turn_input(plane, cot, params, field, inner, outer):
-        return call(
-            functools.partial(conv_kernel, plane),
-            rows_shape,
-            1,
-            (meta, field, inner, outer, cot, params[-1]),
-            (padded,),
-        )
-
     top = SECTIONS - 1
-    params = (cols, down_t, up, slope, nhat, inv, back)
-    field, inner, outer = turn_field(top, cot_top, params)
+    field, inner, outer = turn_field(top, cot_top, (cols, down_t, up, slope, nhat, inv))
     half, field = lax.optimization_barrier((half, field))
     inner, outer = halo(inner, outer)
     other = moved(half, ("", ""), True)
@@ -586,26 +615,36 @@
         cost=(10**9, 10**7),
     )
     next_nhat, next_inv, next_slope, next_cols, next_back, next_up, next_down_t = adopted[:7]
-    adopted = (next_cols, next_down_t, next_up, next_slope, next_nhat, next_inv, next_back)
-    cot_2 = turn_input(top, cot_top, params, field, inner, outer)
+    cot_2, field, inner, outer = call(
+        functools.partial(middle_kernel, top),
+        (rows_shape, rows_shape, edge_shape, edge_shape),
+        1,
+        (meta, field, inner, outer, cot_top, back, next_cols, next_down_t, next_up)
+        + (next_slope, next_nhat, next_inv),
+        (padded, outgrads, lowgrads),
+    )
     own_2 = lax.ppermute(cot_2, "section", swaps)
-
-    field, inner, outer = turn_field(top, cot_2, adopted)
     inner, outer = halo(inner, outer)
-    cot_1 = turn_input(top, cot_2, adopted, field, inner, outer)
+    cot_1 = call(
+        functools.partial(conv_kernel, top),
+        rows_shape,
+        1,
+        (meta, field, inner, outer, cot_2, next_back),
+        (padded,),
+    )
     cot_1 = lax.ppermute(cot_1, "section", [(0, top), (top, 0), (1, 2), (2, 1)])
     own_1 = lax.ppermute(cot_1, "section", swaps)
 
+    adopted = (next_cols, next_down_t, next_up, next_slope, next_nhat, next_inv)
     field, inner, outer = turn_field(0, cot_1, adopted)
     inner, outer = halo(inner, outer)
-    cot_0 = turn_input(0, cot_1, adopted, field, inner, outer)
 
     part = shape(((2 * chans + 32) // 4, units), bf16)
     cot_own, field, inner, outer, keep, near, mate, far = call(
         last_kernel,
         (rows_shape, rows_shape, edge_shape, edge_shape, part, part, part, part),
         1,
-        (meta, cot_top, own_2, own_1, cot_0, cols, layer_scale, down_t, down, up, slope, nhat, inv, hidden)
+        (meta, cot_top, own_2, own_1, field, inner, outer, cot_1, next_back, cols, layer_scale, down_t, down, up, slope, nhat, inv, hidden)
         + (source, acts_inner, acts_outer),
         (
             outgrads,
@@ -621,11 +660,12 @@
     mate = moved(mate, ("", ""), True)
     total = added(keep, near, mate, far)
     orders = (("x1", "z1"), ("z0", "z2"), ("z1", "x0"), ("z2", "x1"))
+    total = added(total, moved(total, orders[0], False))
     total, inner, outer = lax.optimization_barrier((total, inner, outer))
-    total = added(total, moved(total, orders[0], False))
+    total = added(total, moved(total, orders[1], False))
     inner, outer = halo(inner, outer)
     total, inner, outer = lax.optimization_barrier((total, inner, outer))
-    total = added(total, moved(total, orders[1], False))
+    total = added(total, moved(total, orders[2], False))
     result, sent = call(
         last_conv_kernel,
         (rows_shape, shape((CAP, chans, width), bf16)),
@@ -634,9 +674,8 @@
         (padded,),
     )
     total, result, sent = lax.optimization_barrier((total, result, sent))
-    total = added(total, moved(total, orders[2], False))
+    total = added(total, moved(total, orders[3], False))
     arrived = lax.ppermute(sent, "tile", [(tile, (tile + 1) % TILES) for tile in range(TILES)])
-    total = added(total, moved(total, orders[3], False))
     total, arrived = lax.optimization_barrier((total, arrived))
     slotted = call(
         slots_kernel,
@@ -650,7 +689,7 @@
     grads = call(
         functools.partial(finish_kernel, scale),
         (
-            shape((1, KS * KS, chans), f32),
+            shape((KS * KS, 1, chans), f32),
             shape((1, chans), f32),
             shape((1, chans, units), f32),
             shape((1, units), f32),
@@ -665,7 +704,7 @@
     grad_kernel, grad_gain, grad_up, grad_bias, grad_down, grad_scale = grads
     return (
         slotted[None],
-        grad_kernel,
+        jnp.transpose(grad_kernel, (1, 0, 2)),
         grad_gain,
         grad_up,
         grad_bias,

time: 116 us -> 110 us (0.948)
  starting transfers between devices: 52 us -> 45.4 us
  waiting for transfers between devices: 37.4 us -> 40.2 us
    ppermute x1, waiting for transfers between devices: 1.12 us -> 6.55 us  [body(): note = lax.ppermute(own_note, 'section', swaps)]
    ppermute x11, starting transfers between devices: 22.7 us -> 19.4 us  [moved(): return lax.ppermute(value, 'tile', pairs)]
    ppermute x5, waiting for transfers between devices: 11.1 us -> 9.07 us  [halo(): outer = lax.ppermute(outer, 'tile', across)]
    ppermute x1, starting transfers between devices: 7.92 us -> 6.11 us  [body(): cot_1 = lax.ppermute(cot_1, 'section', [(0, top), (top, 0), (1, 2), (2, 1)])]
    ppermute x5, waiting for transfers between devices: 3.33 us -> 2.01 us  [halo(): lax.ppermute(inner, 'tile', [(tile, tile ^ 1) for tile in range(TILES)])]
    pallas_call x13 -> x11, Pallas kernels: 21.7 us -> 20.8 us  [call(): pl.pallas_call(body, out_shape=out_shape, in_specs=spec, out_specs=outs,...]
  transfers between devices with their start and end apart: 27 -> 27, of which waited for: 17 -> 15; matrix products, arithmetic and copies ran while one was open for 0% -> 0% of each run, Pallas kernels for 11% -> 12%
where the time goes in v5:
time: 110 us
  starting transfers between devices  45.4 us (41%)
  waiting for transfers between devices  40.2 us (37%)
  Pallas kernels  20.8 us (19%)
  local copies, waits for them, and re-layouts  1.44 us (1%)
  other arithmetic  1.41 us (1%)
    pallas_call x11, Pallas kernels, call(): pl.pallas_call(body, out_shape=out_shape, in_specs=spec, out_specs=outs,...  20.8 us
    ppermute x11, starting transfers between devices, moved(): return lax.ppermute(value, 'tile', pairs)  19.4 us
    ppermute x11, waiting for transfers between devices, moved(): return lax.ppermute(value, 'tile', pairs)  17.9 us
    ppermute x5, starting transfers between devices, halo(): lax.ppermute(inner, 'tile', [(tile, tile ^ 1) for tile in range(TILES)])  14 us
    ppermute x5, waiting for transfers between devices, halo(): outer = lax.ppermute(outer, 'tile', across)  9.07 us
    ppermute x1, waiting for transfers between devices, body(): note = lax.ppermute(own_note, 'section', swaps)  6.55 us
    ppermute x1, starting transfers between devices, body(): cot_1 = lax.ppermute(cot_1, 'section', [(0, top), (top, 0), (1, 2), (2, 1)])  6.11 us
    ppermute x1, waiting for transfers between devices, body(): cot_1 = lax.ppermute(cot_1, 'section', [(0, top), (top, 0), (1, 2), (2, 1)])  3.58 us
  transfers between devices with their start and end apart: 27, of which 15 were waited for; matrix products, arithmetic and copies ran while one was open for 0% of the time, Pallas kernels for 12%

profile of v5, /device:TPU:1, one launch (start us, length us, event | category | flops | bytes accessed | tf_op | source)
XLA Modules:
  0.0 110.2 jit_solution(18224181421305148443)
XLA Ops:
  0.7 1.1 %broadcast_select_fusion = bf16[192,768]{1,0:T(8,128)(2,1)S(1)} fusion(pred[]{:T(512)S(6)} %eq.21, bf16[1,192,768]{2,1,0:T(8,128)(2,1)} %param.16, bf16[1,192,768]{2,1,0:T(8,128)(2,1)} %param.18), kind=kLoop, calls=%fused_computation.5 | loop fusion | flops 147456 | bytes 884737 | tf_op jit(solution)/shard_map/jit(_where)/select_n | solution.py:574
  1.8 2.2 %collective-permute-start = (bf16[192,768]{1,0:T(8,128)(2,1)S(1)}, bf16[192,768]{1,0:T(8,128)(2,1)S(1)}, u32[]{:S(2)}, u32[]{:S(2)}) collective-permute-start(bf16[192,768]{1,0:T(8,128)(2,1)S(1)} %broadcast_select_fusion), channel_id=1, source_target_pairs={{0,64},{64,0},{128,192},{192,128},{1,65},{65,1},{129,193},{193,129... | collective-permute-start | bytes 884744 | tf_op jit(solution)/shard_map/ppermute | solution.py:574
  4.0 2.1 %collective-permute-start.2 = (bf16[3,192,128]{2,1,0:T(8,128)(2,1)S(1)}, bf16[3,192,128]{2,1,0:T(8,128)(2,1)S(1)}, u32[]{:S(2)}, u32[]{:S(2)}) collective-permute-start(bf16[3,192,128]{2,1,0:T(8,128)(2,1)S(1)} %get-tuple-element.121), channel_id=1, source_target_pairs={{0,63},{1,2},{2,1},{3,4},{4,3},{5,6},{6,5},{7,8},{8,7},{9,10},{10,... | collective-permute-start | bytes 442376 | tf_op jit(solution)/shard_map/ppermute | solution.py:74
  6.2 6.1 %collective-permute-start.1 = (bf16[3,192,128]{2,1,0:T(8,128)(2,1)S(1)}, bf16[3,192,128]{2,1,0:T(8,128)(2,1)S(1)}, u32[]{:S(2)}, u32[]{:S(2)}) collective-permute-start(bf16[3,192,128]{2,1,0:T(8,128)(2,1)S(1)} %get-tuple-element.122), channel_id=1, source_target_pairs={{0,1},{1,0},{2,3},{3,2},{4,5},{5,4},{6,7},{7,6},{8,9},{9,8},{10,11... | collective-permute-start | bytes 442376 | tf_op jit(solution)/shard_map/ppermute | solution.py:75
  14.5 3.6 %shard_map.154 = (f32[192,640]{1,0:T(8,128)S(1)}, f32[1,640]{1,0:T(1,128)S(1)}, bf16[768,640]{1,0:T(8,128)(2,1)S(1)}, bf16[768,640]{1,0:T(8,128)(2,1)S(1)}, bf16[208,768]{1,0:T(8,128)(2,1)S(1)}) custom-call(s32[16]{0:T(128)S(1)} %concatenate.3.meta, bf16[5,192,128]{2,1,0:T(8,128)(2,1)S(1)} %bitcast.25, ...), custom_call_target="tpu_custom_call" | custom-call | tf_op jit(solution)/shard_map/pallas_call | solution.py:83
  18.9 1.0 collective-permute-start.6
  20.0 6.6 %collective-permute-done.5.note = bf16[208,768]{1,0:T(8,128)(2,1)S(1)} collective-permute-done((bf16[208,768]{1,0:T(8,128)(2,1)S(1)}, bf16[208,768]{1,0:T(8,128)(2,1)S(1)}, u32[]{:S(2)}, u32[]{:S(2)}) %collective-permute-start.5) | collective-permute-done | bytes 319520 | tf_op jit(solution)/shard_map/ppermute | solution.py:586
  26.6 3.2 %shard_map.156 = (f32[192,640]{1,0:T(8,128)S(1)}, f32[1,640]{1,0:T(1,128)S(1)}, bf16[768,640]{1,0:T(8,128)(2,1)S(1)}, f32[192,64]{1,0:T(8,128)S(1)}, bf16[12,112...) custom-call(s32[16]{0:T(128)S(1)} %concatenate.3.meta, ...), custom_call_target="tpu_custom_call" | custom-call | flops 1000000000 | bytes 10000000 | tf_op jit(solution)/shard_map/pallas_call | solution.py:83
  30.4 1.6 %collective-permute-start.8 = (bf16[3,192,128]{2,1,0:T(8,128)(2,1)S(1)}, bf16[3,192,128]{2,1,0:T(8,128)(2,1)S(1)}, u32[]{:S(2)}, u32[]{:S(2)}) collective-permute-start(bf16[3,192,128]{2,1,0:T(8,128)(2,1)S(1)} %get-tuple-element.87), channel_id=1, source_target_pairs={{0,1},{1,0},{2,3},{3,2},{4,5},{5,4},{6,7},{7,6},{8,9},{9,8},{10,11... | collective-permute-start | bytes 442376 | tf_op jit(solution)/shard_map/ppermute | solution.py:75
  33.0 3.6 %collective-permute-done.9.outer = bf16[3,192,128]{2,1,0:T(8,128)(2,1)S(1)} collective-permute-done((bf16[3,192,128]{2,1,0:T(8,128)(2,1)S(1)}, bf16[3,192,128]{2,1,0:T(8,128)(2,1)S(1)}, u32[]{:S(2)}, u32[]{:S(2)}) %collective-permute-start.9) | collective-permute-done | bytes 147488 | tf_op jit(solution)/shard_map/ppermute | solution.py:74
  37.3 6.1 %collective-permute-start.10 = (bf16[5,192,128]{2,1,0:T(8,128)(2,1)S(1)}, bf16[5,192,128]{2,1,0:T(8,128)(2,1)S(1)}, u32[]{:S(2)}, u32[]{:S(2)}) collective-permute-start(bf16[5,192,128]{2,1,0:T(8,128)(2,1)S(1)} %shard_map.158), channel_id=1, source_target_pairs={{0,192},{192,0},{64,128},{128,64},{1,193},{193,1},{65,129},{129,65... | collective-permute-start | bytes 737288 | tf_op jit(solution)/shard_map/ppermute | solution.py:635
  43.4 3.6 %collective-permute-done.10.cot.turn_cot = bf16[5,192,128]{2,1,0:T(8,128)(2,1)S(1)} collective-permute-done((bf16[5,192,128]{2,1,0:T(8,128)(2,1)S(1)}, bf16[5,192,128]{2,1,0:T(8,128)(2,1)S(1)}, u32[]{:S(2)}, u32[]{:S(2)}) %collective-permute-start.10) | collective-permute-done | bytes 245792 | tf_op jit(solution)/shard_map/ppermute | solution.py:635
  47.0 1.5 %shard_map.159 = (bf16[5,192,128]{2,1,0:T(8,128)(2,1)S(1)}, bf16[3,192,128]{2,1,0:T(8,128)(2,1)S(1)}, bf16[3,192,128]{2,1,0:T(8,128)(2,1)S(1)}) custom-call(s32[16]{0:T(128)S(1)} %concatenate.3.meta, bf16[5,192,128]{2,1,0:T(8,128)(2,1)S(1)} %collective-permute-done.10.cot.turn_cot, f32[192,64]{1,0:T(8,128)S(1)} %get-tuple-element.79.cols, ...), custom_call_target="tpu_custom_call" | custom-call | tf_op jit(solution)/shard_map/pallas_call | solution.py:83
  48.5 4.4 %collective-permute-start.12 = (bf16[3,192,128]{2,1,0:T(8,128)(2,1)S(1)}, bf16[3,192,128]{2,1,0:T(8,128)(2,1)S(1)}, u32[]{:S(2)}, u32[]{:S(2)}) collective-permute-start(bf16[3,192,128]{2,1,0:T(8,128)(2,1)S(1)} %get-tuple-element.91), channel_id=1, source_target_pairs={{0,1},{1,0},{2,3},{3,2},{4,5},{5,4},{6,7},{7,6},{8,9},{9,8},{10,11... | collective-permute-start | bytes 442376 | tf_op jit(solution)/shard_map/ppermute | solution.py:75
  53.9 3.7 %collective-permute-done.13.turn_outer = bf16[3,192,128]{2,1,0:T(8,128)(2,1)S(1)} collective-permute-done((bf16[3,192,128]{2,1,0:T(8,128)(2,1)S(1)}, bf16[3,192,128]{2,1,0:T(8,128)(2,1)S(1)}, u32[]{:S(2)}, u32[]{:S(2)}) %collective-permute-start.13) | collective-permute-done | bytes 147488 | tf_op jit(solution)/shard_map/ppermute | solution.py:74
  57.6 4.5 %shard_map.160 = (bf16[5,192,128]{2,1,0:T(8,128)(2,1)S(1)}, bf16[5,192,128]{2,1,0:T(8,128)(2,1)S(1)}, bf16[3,192,128]{2,1,0:T(8,128)(2,1)S(1)}, bf16[3,192,128]{...) custom-call(s32[16]{0:T(128)S(1)} %concatenate.3.meta, ...), custom_call_target="tpu_custom_call" | custom-call | tf_op jit(solution)/shard_map/pallas_call | solution.py:83
  62.2 3.3 %collective-permute-start.15 = (bf16[104,768]{1,0:T(8,128)(2,1)S(1)}, bf16[104,768]{1,0:T(8,128)(2,1)S(1)}, u32[]{:S(2)}, u32[]{:S(2)}) collective-permute-start(bf16[104,768]{1,0:T(8,128)(2,1)S(1)} %get-tuple-element.96), channel_id=1, source_target_pairs={{0,1},{1,0},{2,3},{3,2},{4,5},{5,4},{6,7},{7,6},{8,9},{9,8},{10,11... | collective-permute-start | bytes 479240 | tf_op jit(solution)/shard_map/ppermute | solution.py:69
  65.6 1.5 %collective-permute-start.16 = (bf16[104,768]{1,0:T(8,128)(2,1)S(1)}, bf16[104,768]{1,0:T(8,128)(2,1)S(1)}, u32[]{:S(2)}, u32[]{:S(2)}) collective-permute-start(bf16[104,768]{1,0:T(8,128)(2,1)S(1)} %get-tuple-element.97), channel_id=1, source_target_pairs={{0,9},{1,2},{2,11},{3,0},{4,13},{5,6},{6,15},{7,4},{8,1},{9,10},{1... | collective-permute-start | bytes 479240 | tf_op jit(solution)/shard_map/ppermute | solution.py:69
  67.1 3.5 %collective-permute-done.16 = bf16[104,768]{1,0:T(8,128)(2,1)S(1)} collective-permute-done((bf16[104,768]{1,0:T(8,128)(2,1)S(1)}, bf16[104,768]{1,0:T(8,128)(2,1)S(1)}, u32[]{:S(2)}, u32[]{:S(2)}) %collective-permute-start.16) | collective-permute-done | bytes 159776 | tf_op jit(solution)/shard_map/ppermute | solution.py:69
  70.8 5.9 %collective-permute-done.17 = bf16[104,768]{1,0:T(8,128)(2,1)S(1)} collective-permute-done((bf16[104,768]{1,0:T(8,128)(2,1)S(1)}, bf16[104,768]{1,0:T(8,128)(2,1)S(1)}, u32[]{:S(2)}, u32[]{:S(2)}) %collective-permute-start.17) | collective-permute-done | bytes 159776 | tf_op jit(solution)/shard_map/ppermute | solution.py:69
  77.4 1.8 %collective-permute-start.19 = (bf16[3,192,128]{2,1,0:T(8,128)(2,1)S(1)}, bf16[3,192,128]{2,1,0:T(8,128)(2,1)S(1)}, u32[]{:S(2)}, u32[]{:S(2)}) collective-permute-start(bf16[3,192,128]{2,1,0:T(8,128)(2,1)S(1)} %get-tuple-element.101), channel_id=1, source_target_pairs={{0,1},{1,0},{2,3},{3,2},{4,5},{5,4},{6,7},{7,6},{8,9},{9,8},{10,11... | collective-permute-start | bytes 442376 | tf_op jit(solution)/shard_map/ppermute | solution.py:75
  79.3 2.9 %collective-permute-done.18 = bf16[104,768]{1,0:T(8,128)(2,1)S(1)} collective-permute-done((bf16[104,768]{1,0:T(8,128)(2,1)S(1)}, bf16[104,768]{1,0:T(8,128)(2,1)S(1)}, u32[]{:S(2)}, u32[]{:S(2)}) %collective-permute-start.18) | collective-permute-done | bytes 159776 | tf_op jit(solution)/shard_map/ppermute | solution.py:69
  82.2 1.8 %collective-permute-done.20.outer = bf16[3,192,128]{2,1,0:T(8,128)(2,1)S(1)} collective-permute-done((bf16[3,192,128]{2,1,0:T(8,128)(2,1)S(1)}, bf16[3,192,128]{2,1,0:T(8,128)(2,1)S(1)}, u32[]{:S(2)}, u32[]{:S(2)}) %collective-permute-start.20) | collective-permute-done | bytes 147488 | tf_op jit(solution)/shard_map/ppermute | solution.py:74
  84.7 2.4 %shard_map.161 = (bf16[5,192,128]{2,1,0:T(8,128)(2,1)S(1)}, bf16[2,192,128]{2,1,0:T(8,128)(2,1)S(1)}) custom-call(s32[16]{0:T(128)S(1)} %concatenate.3.meta, bf16[5,192,128]{2,1,0:T(8,128)(2,1)S(1)} %get-tuple-element.104.field, bf16[3,192,128]{2,1,0:T(8,128)(2,1)S(1)} %collective-permute-done.19.inner, ...), custom_call_target="tpu_custom_call" | custom-call | tf_op jit(solution)/shard_map/pallas_call | solution.py:83
  88.1 4.0 %collective-permute-start.22 = (bf16[104,768]{1,0:T(8,128)(2,1)S(1)}, bf16[104,768]{1,0:T(8,128)(2,1)S(1)}, u32[]{:S(2)}, u32[]{:S(2)}) collective-permute-start(bf16[104,768]{1,0:T(8,128)(2,1)S(1)} %add_convert_fusion.1), channel_id=1, source_target_pairs={{0,56},{1,7},{2,58},{3,5},{4,60},{5,3},{6,62},{7,1},{8,48},{9,15},... | collective-permute-start | bytes 479240 | tf_op jit(solution)/shard_map/ppermute | solution.py:69
  92.1 1.3 %collective-permute-start.23 = (bf16[2,192,128]{2,1,0:T(8,128)(2,1)S(1)}, bf16[2,192,128]{2,1,0:T(8,128)(2,1)S(1)}, u32[]{:S(2)}, u32[]{:S(2)}) collective-permute-start(bf16[2,192,128]{2,1,0:T(8,128)(2,1)S(1)} %get-tuple-element.112), channel_id=1, source_target_pairs={{0,1},{1,2},{2,3},{3,4},{4,5},{5,6},{6,7},{7,8},{8,9},{9,10},{10,1... | collective-permute-start | bytes 294920 | tf_op jit(solution)/shard_map/ppermute | solution.py:678
  93.4 1.4 %collective-permute-done.22 = bf16[104,768]{1,0:T(8,128)(2,1)S(1)} collective-permute-done((bf16[104,768]{1,0:T(8,128)(2,1)S(1)}, bf16[104,768]{1,0:T(8,128)(2,1)S(1)}, u32[]{:S(2)}, u32[]{:S(2)}) %collective-permute-start.22) | collective-permute-done | bytes 159776 | tf_op jit(solution)/shard_map/ppermute | solution.py:69
  94.8 1.1 collective-permute-done.23.arrived
  95.9 7.2 %collective-permute-start.26 = (bf16[104,768]{1,0:T(8,128)(2,1)S(1)}, bf16[104,768]{1,0:T(8,128)(2,1)S(1)}, u32[]{:S(2)}, u32[]{:S(2)}) collective-permute-start(bf16[104,768]{1,0:T(8,128)(2,1)S(1)} %add_convert_fusion.keep), channel_id=1, source_target_pairs={{0,3},{1,8},{2,1},{3,10},{4,7},{5,12},{6,5},{7,14},{8,11},{9,0},{1... | collective-permute-start | bytes 479240 | tf_op jit(solution)/shard_map/ppermute | solution.py:69
  103.8 1.3 %shard_map.162 = bf16[3,192,128]{2,1,0:T(8,128)(2,1)} custom-call(s32[16]{0:T(128)S(1)} %concatenate.3.meta, bf16[5,192,128]{2,1,0:T(8,128)(2,1)S(1)} %get-tuple-element.110.result, bf16[2,192,128]{2,1,0:T(8,128)(2,1)S(1)} %collective-permute-done.23.arrived), custom_call_target="tpu_custom_call" | custom-call | tf_op jit(solution)/shard_map/pallas_call | solution.py:83
  105.3 3.2 %collective-permute-done.24.near = bf16[104,768]{1,0:T(8,128)(2,1)S(1)} collective-permute-done((bf16[104,768]{1,0:T(8,128)(2,1)S(1)}, bf16[104,768]{1,0:T(8,128)(2,1)S(1)}, u32[]{:S(2)}, u32[]{:S(2)}) %collective-permute-start.24) | collective-permute-done | bytes 159776 | tf_op jit(solution)/shard_map/ppermute | solution.py:69
  108.5 1.8 %shard_map.163 = (f32[49,1,192]{2,1,0:T(1,128)}, f32[1,192]{1,0:T(1,128)}, f32[1,192,768]{2,1,0:T(8,128)}, f32[1,768]{1,0:T(1,128)}, f32[1,192,768]{2,1,0:T(8,128)}, /*index=5*/f32[1,192]{1,0:T(1,128)}) custom-call(s32[16]{0:T(128)S(1)} %concatenate.3.meta, bf16[104,768]{1,0:T(8,128)(2,1)S(1)} %add_convert_fusion.keep, ...), custom_call_target="tpu_custom_call" | custom-call | tf_op jit(solution)/shard_map/pallas_call | solution.py:83
  (62 shorter events, 10.1 us)
Async XLA Ops:
  0.6 3.4 %copy-start.1 = (bf16[1,5,192,128]{3,2,1,0:T(8,128)(2,1)S(1)}, bf16[1,5,192,128]{3,2,1,0:T(8,128)(2,1)}, u32[]{:S(2)}) copy-start(bf16[1,5,192,128]{3,2,1,0:T(8,128)(2,1)} %param.10) | copy-start | bytes 737284
  1.8 17.1 %collective-permute-start = (bf16[192,768]{1,0:T(8,128)(2,1)S(1)}, bf16[192,768]{1,0:T(8,128)(2,1)S(1)}, u32[]{:S(2)}, u32[]{:S(2)}) collective-permute-start(bf16[192,768]{1,0:T(8,128)(2,1)S(1)} %broadcast_select_fusion), channel_id=1, source_target_pairs={{0,64},{64,0},{128,192},{192,128},{1,65},{65,1},{129,193},{193,129... | collective-permute-start | bytes 884744 | tf_op jit(solution)/shard_map/ppermute | solution.py:574
  4.0 8.3 %copy-start.7 = (f32[1,49,192]{2,0,1:T(1,128)S(1)}, f32[1,49,192]{2,0,1:T(1,128)}, u32[]{:S(2)}) copy-start(f32[1,49,192]{2,0,1:T(1,128)} %param.14) | copy-start | bytes 112900
  4.0 9.1 %copy-start.3 = (bf16[1,192,768]{2,1,0:T(8,128)(2,1)S(1)}, bf16[1,192,768]{2,1,0:T(8,128)(2,1)}, u32[]{:S(2)}) copy-start(bf16[1,192,768]{2,1,0:T(8,128)(2,1)} %param.18) | copy-start | bytes 884740
  4.0 9.1 %copy-start = (bf16[1,192,768]{2,1,0:T(8,128)(2,1)S(1)}, bf16[1,192,768]{2,1,0:T(8,128)(2,1)}, u32[]{:S(2)}) copy-start(bf16[1,192,768]{2,1,0:T(8,128)(2,1)} %param.16) | copy-start | bytes 884740
  4.0 10.4 %collective-permute-start.2 = (bf16[3,192,128]{2,1,0:T(8,128)(2,1)S(1)}, bf16[3,192,128]{2,1,0:T(8,128)(2,1)S(1)}, u32[]{:S(2)}, u32[]{:S(2)}) collective-permute-start(bf16[3,192,128]{2,1,0:T(8,128)(2,1)S(1)} %get-tuple-element.121), channel_id=1, source_target_pairs={{0,63},{1,2},{2,1},{3,4},{4,3},{5,6},{6,5},{7,8},{8,7},{9,10},{10,... | collective-permute-start | bytes 442376 | tf_op jit(solution)/shard_map/ppermute | solution.py:74
  6.2 8.3 %collective-permute-start.1 = (bf16[3,192,128]{2,1,0:T(8,128)(2,1)S(1)}, bf16[3,192,128]{2,1,0:T(8,128)(2,1)S(1)}, u32[]{:S(2)}, u32[]{:S(2)}) collective-permute-start(bf16[3,192,128]{2,1,0:T(8,128)(2,1)S(1)} %get-tuple-element.122), channel_id=1, source_target_pairs={{0,1},{1,0},{2,3},{3,2},{4,5},{5,4},{6,7},{7,6},{8,9},{9,8},{10,11... | collective-permute-start | bytes 442376 | tf_op jit(solution)/shard_map/ppermute | solution.py:75
  14.5 3.9 %copy-start.2 = (bf16[5,192,128]{2,1,0:T(8,128)(2,1)S(1)}, bf16[5,192,128]{2,1,0:T(8,128)(2,1)}, u32[]{:S(2)}) copy-start(bf16[5,192,128]{2,1,0:T(8,128)(2,1)} %cot_top.1) | copy-start | bytes 737284
  18.1 8.5 %collective-permute-start.5 = (bf16[208,768]{1,0:T(8,128)(2,1)S(1)}, bf16[208,768]{1,0:T(8,128)(2,1)S(1)}, u32[]{:S(2)}, u32[]{:S(2)}) collective-permute-start(bf16[208,768]{1,0:T(8,128)(2,1)S(1)} %get-tuple-element.77), channel_id=1, source_target_pairs={{0,64},{64,0},{128,192},{192,128},{1,65},{65,1},{129,193},{193,129... | collective-permute-start | bytes 958472 | tf_op jit(solution)/shard_map/ppermute | solution.py:586
  18.9 7.7 %collective-permute-start.6 = (bf16[192,768]{1,0:T(8,128)(2,1)S(1)}, bf16[192,768]{1,0:T(8,128)(2,1)S(1)}, u32[]{:S(2)}, u32[]{:S(2)}) collective-permute-start(bf16[192,768]{1,0:T(8,128)(2,1)S(1)} %collective-permute-done.half), channel_id=1, source_target_pairs={{0,1},{1,0},{2,3},{3,2},{4,5},{5,4},{6,7},{7,6},{8,9},{9,8},{10,11... | collective-permute-start | bytes 884744 | tf_op jit(solution)/shard_map/ppermute | solution.py:69
  19.9 9.9 %collective-permute-start.3 = (bf16[3,192,128]{2,1,0:T(8,128)(2,1)S(1)}, bf16[3,192,128]{2,1,0:T(8,128)(2,1)S(1)}, u32[]{:S(2)}, u32[]{:S(2)}) collective-permute-start(bf16[3,192,128]{2,1,0:T(8,128)(2,1)S(1)} %get-tuple-element.74), channel_id=1, source_target_pairs={{0,1},{1,0},{2,3},{3,2},{4,5},{5,4},{6,7},{7,6},{8,9},{9,8},{10,11... | collective-permute-start | bytes 442376 | tf_op jit(solution)/shard_map/ppermute | solution.py:75
  20.0 9.8 %collective-permute-start.4 = (bf16[3,192,128]{2,1,0:T(8,128)(2,1)S(1)}, bf16[3,192,128]{2,1,0:T(8,128)(2,1)S(1)}, u32[]{:S(2)}, u32[]{:S(2)}) collective-permute-start(bf16[3,192,128]{2,1,0:T(8,128)(2,1)S(1)} %get-tuple-element.75), channel_id=1, source_target_pairs={{0,63},{1,2},{2,1},{3,4},{4,3},{5,6},{6,5},{7,8},{8,7},{9,10},{10,... | collective-permute-start | bytes 442376 | tf_op jit(solution)/shard_map/ppermute | solution.py:74
  30.4 2.6 %collective-permute-start.8 = (bf16[3,192,128]{2,1,0:T(8,128)(2,1)S(1)}, bf16[3,192,128]{2,1,0:T(8,128)(2,1)S(1)}, u32[]{:S(2)}, u32[]{:S(2)}) collective-permute-start(bf16[3,192,128]{2,1,0:T(8,128)(2,1)S(1)} %get-tuple-element.87), channel_id=1, source_target_pairs={{0,1},{1,0},{2,3},{3,2},{4,5},{5,4},{6,7},{7,6},{8,9},{9,8},{10,11... | collective-permute-start | bytes 442376 | tf_op jit(solution)/shard_map/ppermute | solution.py:75
  32.0 4.6 %collective-permute-start.9 = (bf16[3,192,128]{2,1,0:T(8,128)(2,1)S(1)}, bf16[3,192,128]{2,1,0:T(8,128)(2,1)S(1)}, u32[]{:S(2)}, u32[]{:S(2)}) collective-permute-start(bf16[3,192,128]{2,1,0:T(8,128)(2,1)S(1)} %get-tuple-element.88), channel_id=1, source_target_pairs={{0,63},{1,2},{2,1},{3,4},{4,3},{5,6},{6,5},{7,8},{8,7},{9,10},{10,... | collective-permute-start | bytes 442376 | tf_op jit(solution)/shard_map/ppermute | solution.py:74
  37.3 9.7 %collective-permute-start.10 = (bf16[5,192,128]{2,1,0:T(8,128)(2,1)S(1)}, bf16[5,192,128]{2,1,0:T(8,128)(2,1)S(1)}, u32[]{:S(2)}, u32[]{:S(2)}) collective-permute-start(bf16[5,192,128]{2,1,0:T(8,128)(2,1)S(1)} %shard_map.158), channel_id=1, source_target_pairs={{0,192},{192,0},{64,128},{128,64},{1,193},{193,1},{65,129},{129,65... | collective-permute-start | bytes 737288 | tf_op jit(solution)/shard_map/ppermute | solution.py:635
  43.4 9.5 %collective-permute-start.7 = (bf16[5,192,128]{2,1,0:T(8,128)(2,1)S(1)}, bf16[5,192,128]{2,1,0:T(8,128)(2,1)S(1)}, u32[]{:S(2)}, u32[]{:S(2)}) collective-permute-start(bf16[5,192,128]{2,1,0:T(8,128)(2,1)S(1)} %get-tuple-element.85.cot), channel_id=1, source_target_pairs={{0,64},{64,0},{128,192},{192,128},{1,65},{65,1},{129,193},{193,129... | collective-permute-start | bytes 737288 | tf_op jit(solution)/shard_map/ppermute | solution.py:626
  47.0 10.6 %collective-permute-start.11 = (bf16[5,192,128]{2,1,0:T(8,128)(2,1)S(1)}, bf16[5,192,128]{2,1,0:T(8,128)(2,1)S(1)}, u32[]{:S(2)}, u32[]{:S(2)}) collective-permute-start(bf16[5,192,128]{2,1,0:T(8,128)(2,1)S(1)} %collective-permute-done.10.cot.turn_cot), channel_id=1, source_target_pairs={{0,64},{64,0},{128,192},{192,128},{1,65},{65,1},{129,193},{193,129... | collective-permute-start | bytes 737288 | tf_op jit(solution)/shard_map/ppermute | solution.py:636
  48.5 5.4 %collective-permute-start.12 = (bf16[3,192,128]{2,1,0:T(8,128)(2,1)S(1)}, bf16[3,192,128]{2,1,0:T(8,128)(2,1)S(1)}, u32[]{:S(2)}, u32[]{:S(2)}) collective-permute-start(bf16[3,192,128]{2,1,0:T(8,128)(2,1)S(1)} %get-tuple-element.91), channel_id=1, source_target_pairs={{0,1},{1,0},{2,3},{3,2},{4,5},{5,4},{6,7},{7,6},{8,9},{9,8},{10,11... | collective-permute-start | bytes 442376 | tf_op jit(solution)/shard_map/ppermute | solution.py:75
  52.9 4.7 %collective-permute-start.13 = (bf16[3,192,128]{2,1,0:T(8,128)(2,1)S(1)}, bf16[3,192,128]{2,1,0:T(8,128)(2,1)S(1)}, u32[]{:S(2)}, u32[]{:S(2)}) collective-permute-start(bf16[3,192,128]{2,1,0:T(8,128)(2,1)S(1)} %get-tuple-element.92), channel_id=1, source_target_pairs={{0,63},{1,2},{2,1},{3,4},{4,3},{5,6},{6,5},{7,8},{8,7},{9,10},{10,... | collective-permute-start | bytes 442376 | tf_op jit(solution)/shard_map/ppermute | solution.py:74
  62.1 5.0 %collective-permute-start.14 = (bf16[104,768]{1,0:T(8,128)(2,1)S(1)}, bf16[104,768]{1,0:T(8,128)(2,1)S(1)}, u32[]{:S(2)}, u32[]{:S(2)}) collective-permute-start(bf16[104,768]{1,0:T(8,128)(2,1)S(1)} %get-tuple-element.95), channel_id=1, source_target_pairs={{0,2},{1,9},{2,0},{3,11},{4,6},{5,13},{6,4},{7,15},{8,10},{9,1},{1... | collective-permute-start | bytes 479240 | tf_op jit(solution)/shard_map/ppermute | solution.py:69
  62.2 4.9 %collective-permute-start.15 = (bf16[104,768]{1,0:T(8,128)(2,1)S(1)}, bf16[104,768]{1,0:T(8,128)(2,1)S(1)}, u32[]{:S(2)}, u32[]{:S(2)}) collective-permute-start(bf16[104,768]{1,0:T(8,128)(2,1)S(1)} %get-tuple-element.96), channel_id=1, source_target_pairs={{0,1},{1,0},{2,3},{3,2},{4,5},{5,4},{6,7},{7,6},{8,9},{9,8},{10,11... | collective-permute-start | bytes 479240 | tf_op jit(solution)/shard_map/ppermute | solution.py:69
  65.6 5.0 %collective-permute-start.16 = (bf16[104,768]{1,0:T(8,128)(2,1)S(1)}, bf16[104,768]{1,0:T(8,128)(2,1)S(1)}, u32[]{:S(2)}, u32[]{:S(2)}) collective-permute-start(bf16[104,768]{1,0:T(8,128)(2,1)S(1)} %get-tuple-element.97), channel_id=1, source_target_pairs={{0,9},{1,2},{2,11},{3,0},{4,13},{5,6},{6,15},{7,4},{8,1},{9,10},{1... | collective-permute-start | bytes 479240 | tf_op jit(solution)/shard_map/ppermute | solution.py:69
  70.7 6.0 %collective-permute-start.17 = (bf16[104,768]{1,0:T(8,128)(2,1)S(1)}, bf16[104,768]{1,0:T(8,128)(2,1)S(1)}, u32[]{:S(2)}, u32[]{:S(2)}) collective-permute-start(bf16[104,768]{1,0:T(8,128)(2,1)S(1)} %add_convert_fusion.4), channel_id=1, source_target_pairs={{0,6},{1,25},{2,4},{3,27},{4,2},{5,29},{6,0},{7,31},{8,14},{9,17},... | collective-permute-start | bytes 479240 | tf_op jit(solution)/shard_map/ppermute | solution.py:69
  76.7 5.4 %collective-permute-start.18 = (bf16[104,768]{1,0:T(8,128)(2,1)S(1)}, bf16[104,768]{1,0:T(8,128)(2,1)S(1)}, u32[]{:S(2)}, u32[]{:S(2)}) collective-permute-start(bf16[104,768]{1,0:T(8,128)(2,1)S(1)} %add_convert_fusion.3), channel_id=1, source_target_pairs={{0,8},{1,57},{2,10},{3,59},{4,12},{5,61},{6,14},{7,63},{8,0},{9,49... | collective-permute-start | bytes 479240 | tf_op jit(solution)/shard_map/ppermute | solution.py:69
  77.4 4.8 %collective-permute-start.19 = (bf16[3,192,128]{2,1,0:T(8,128)(2,1)S(1)}, bf16[3,192,128]{2,1,0:T(8,128)(2,1)S(1)}, u32[]{:S(2)}, u32[]{:S(2)}) collective-permute-start(bf16[3,192,128]{2,1,0:T(8,128)(2,1)S(1)} %get-tuple-element.101), channel_id=1, source_target_pairs={{0,1},{1,0},{2,3},{3,2},{4,5},{5,4},{6,7},{7,6},{8,9},{9,8},{10,11... | collective-permute-start | bytes 442376 | tf_op jit(solution)/shard_map/ppermute | solution.py:75
  79.2 4.8 %collective-permute-start.20 = (bf16[3,192,128]{2,1,0:T(8,128)(2,1)S(1)}, bf16[3,192,128]{2,1,0:T(8,128)(2,1)S(1)}, u32[]{:S(2)}, u32[]{:S(2)}) collective-permute-start(bf16[3,192,128]{2,1,0:T(8,128)(2,1)S(1)} %get-tuple-element.102), channel_id=1, source_target_pairs={{0,63},{1,2},{2,1},{3,4},{4,3},{5,6},{6,5},{7,8},{8,7},{9,10},{10,... | collective-permute-start | bytes 442376 | tf_op jit(solution)/shard_map/ppermute | solution.py:74
  84.0 4.1 %collective-permute-start.21 = (bf16[104,768]{1,0:T(8,128)(2,1)S(1)}, bf16[104,768]{1,0:T(8,128)(2,1)S(1)}, u32[]{:S(2)}, u32[]{:S(2)}) collective-permute-start(bf16[104,768]{1,0:T(8,128)(2,1)S(1)} %add_convert_fusion.2), channel_id=1, source_target_pairs={{0,24},{1,3},{2,26},{3,1},{4,28},{5,7},{6,30},{7,5},{8,16},{9,11},... | collective-permute-start | bytes 479240 | tf_op jit(solution)/shard_map/ppermute | solution.py:69
  88.1 6.6 %collective-permute-start.22 = (bf16[104,768]{1,0:T(8,128)(2,1)S(1)}, bf16[104,768]{1,0:T(8,128)(2,1)S(1)}, u32[]{:S(2)}, u32[]{:S(2)}) collective-permute-start(bf16[104,768]{1,0:T(8,128)(2,1)S(1)} %add_convert_fusion.1), channel_id=1, source_target_pairs={{0,56},{1,7},{2,58},{3,5},{4,60},{5,3},{6,62},{7,1},{8,48},{9,15},... | collective-permute-start | bytes 479240 | tf_op jit(solution)/shard_map/ppermute | solution.py:69
  92.1 3.8 %collective-permute-start.23 = (bf16[2,192,128]{2,1,0:T(8,128)(2,1)S(1)}, bf16[2,192,128]{2,1,0:T(8,128)(2,1)S(1)}, u32[]{:S(2)}, u32[]{:S(2)}) collective-permute-start(bf16[2,192,128]{2,1,0:T(8,128)(2,1)S(1)} %get-tuple-element.112), channel_id=1, source_target_pairs={{0,1},{1,2},{2,3},{3,4},{4,5},{5,6},{6,7},{7,8},{8,9},{9,10},{10,1... | collective-permute-start | bytes 294920 | tf_op jit(solution)/shard_map/ppermute | solution.py:678
  95.9 9.4 %collective-permute-start.26 = (bf16[104,768]{1,0:T(8,128)(2,1)S(1)}, bf16[104,768]{1,0:T(8,128)(2,1)S(1)}, u32[]{:S(2)}, u32[]{:S(2)}) collective-permute-start(bf16[104,768]{1,0:T(8,128)(2,1)S(1)} %add_convert_fusion.keep), channel_id=1, source_target_pairs={{0,3},{1,8},{2,1},{3,10},{4,7},{5,12},{6,5},{7,14},{8,11},{9,0},{1... | collective-permute-start | bytes 479240 | tf_op jit(solution)/shard_map/ppermute | solution.py:69
  103.1 2.2 %collective-permute-start.25 = (bf16[104,768]{1,0:T(8,128)(2,1)S(1)}, bf16[104,768]{1,0:T(8,128)(2,1)S(1)}, u32[]{:S(2)}, u32[]{:S(2)}) collective-permute-start(bf16[104,768]{1,0:T(8,128)(2,1)S(1)} %add_convert_fusion.keep), channel_id=1, source_target_pairs={{0,1},{1,0},{2,3},{3,2},{4,5},{5,4},{6,7},{7,6},{8,9},{9,8},{10,11... | collective-permute-start | bytes 479240 | tf_op jit(solution)/shard_map/ppermute | solution.py:69
  103.1 5.4 %collective-permute-start.24 = (bf16[104,768]{1,0:T(8,128)(2,1)S(1)}, bf16[104,768]{1,0:T(8,128)(2,1)S(1)}, u32[]{:S(2)}, u32[]{:S(2)}) collective-permute-start(bf16[104,768]{1,0:T(8,128)(2,1)S(1)} %add_convert_fusion.keep), channel_id=1, source_target_pairs={{0,2},{1,9},{2,0},{3,11},{4,6},{5,13},{6,4},{7,15},{8,10},{9,1},{1... | collective-permute-start | bytes 479240 | tf_op jit(solution)/shard_map/ppermute | solution.py:69
  (5 other events, 3.5 us)

commit v6 on v5

--- a/solution.py
+++ b/solution.py
@@ -14,7 +14,7 @@
 TILES = 64
 MARGIN = 3
 BLOCK = 16
-UNROLL = 4
+UNROLL = 12
 
 norm_eps = 1e-06
 tanh_root = math.sqrt(2.0 / math.pi)
@@ -69,11 +69,18 @@
     return lax.ppermute(value, "tile", pairs)
 
 
+def within(value):
+    return lax.ppermute(value, "tile", [(tile, tile ^ 1) for tile in range(TILES)])
+
+
+def across(value):
+    pairs = [(tile, (tile + 1 if tile % 2 else tile - 1) % TILES) for tile in range(TILES)]
+    return lax.ppermute(value, "tile", pairs)
+
+
 def halo(inner, outer):
-    across = [(tile, (tile + 1 if tile % 2 else tile - 1) % TILES) for tile in range(TILES)]
-    outer = lax.ppermute(outer, "tile", across)
-    inner = lax.ppermute(inner, "tile", [(tile, tile ^ 1) for tile in range(TILES)])
-    return inner, outer
+    outer = across(outer)
+    return within(inner), outer
 
 
 def call(body, out_shape, smem, operands, scratch=(), cost=(0, 0)):
@@ -660,11 +667,13 @@
     mate = moved(mate, ("", ""), True)
     total = added(keep, near, mate, far)
     orders = (("x1", "z1"), ("z0", "z2"), ("z1", "x0"), ("z2", "x1"))
+    total, inner = lax.optimization_barrier((total, inner))
     total = added(total, moved(total, orders[0], False))
+    inner = within(inner)
     total, inner, outer = lax.optimization_barrier((total, inner, outer))
     total = added(total, moved(total, orders[1], False))
-    inner, outer = halo(inner, outer)
-    total, inner, outer = lax.optimization_barrier((total, inner, outer))
+    outer = across(outer)
+    total, outer = lax.optimization_barrier((total, outer))
     total = added(total, moved(total, orders[2], False))
     result, sent = call(
         last_conv_kernel,

time: 110 us -> 108 us (0.982)
  Pallas kernels: 20.8 us -> 18.9 us
    ppermute x11, starting transfers between devices: 19.4 us -> 21.6 us  [moved(): return lax.ppermute(value, 'tile', pairs)]
    pallas_call x11, Pallas kernels: 20.8 us -> 18.9 us  [call(): pl.pallas_call(body, out_shape=out_shape, in_specs=spec, out_specs=outs,...]
    ppermute x10, waiting for transfers between devices: 11.1 us -> 9.38 us  [the longest x5 7.37 us: across(): return lax.ppermute(value, 'tile', pairs)]
    ppermute x1, starting transfers between devices: 1.27 us -> 0.01 us  [body(): lax.ppermute(sent, 'tile', [(tile, (tile + 1) % TILES) for tile in range(...]
    ppermute x1, starting transfers between devices: 6.11 us -> 4.97 us  [body(): cot_1 = lax.ppermute(cot_1, 'section', [(0, top), (top, 0), (1, 2), (2, 1)])]
  transfers between devices with their start and end apart: 27 -> 27, of which waited for: 15 -> 14; matrix products, arithmetic and copies ran while one was open for 0% -> 0% of each run, Pallas kernels for 12% -> 11%
where the time goes in v6:
time: 108 us
  starting transfers between devices  46 us (43%)
  waiting for transfers between devices  39.4 us (36%)
  Pallas kernels  18.9 us (17%)
  local copies, waits for them, and re-layouts  1.44 us (1%)
  other arithmetic  1.42 us (1%)
    ppermute x11, starting transfers between devices, moved(): return lax.ppermute(value, 'tile', pairs)  21.6 us
    pallas_call x11, Pallas kernels, call(): pl.pallas_call(body, out_shape=out_shape, in_specs=spec, out_specs=outs,...  18.9 us
    ppermute x11, waiting for transfers between devices, moved(): return lax.ppermute(value, 'tile', pairs)  18.5 us
    ppermute x5, starting transfers between devices, within(): lax.ppermute(value, 'tile', [(tile, tile ^ 1) for tile in range(TILES)])  14.2 us
    ppermute x5, waiting for transfers between devices, across(): return lax.ppermute(value, 'tile', pairs)  7.37 us
    ppermute x1, waiting for transfers between devices, body(): note = lax.ppermute(own_note, 'section', swaps)  6.53 us
    ppermute x1, starting transfers between devices, body(): cot_1 = lax.ppermute(cot_1, 'section', [(0, top), (top, 0), (1, 2), (2, 1)])  4.97 us
    ppermute x1, waiting for transfers between devices, body(): cot_1 = lax.ppermute(cot_1, 'section', [(0, top), (top, 0), (1, 2), (2, 1)])  3.58 us
  transfers between devices with their start and end apart: 27, of which 14 were waited for; matrix products, arithmetic and copies ran while one was open for 0% of the time, Pallas kernels for 11%

profile of v6, /device:TPU:1, one launch (start us, length us, event | category | flops | bytes accessed | tf_op | source)
XLA Modules:
  0.0 108.1 jit_solution(8586081950777008973)
XLA Ops:
  0.7 1.1 %broadcast_select_fusion = bf16[192,768]{1,0:T(8,128)(2,1)S(1)} fusion(pred[]{:T(512)S(6)} %eq.21, bf16[1,192,768]{2,1,0:T(8,128)(2,1)} %param.16, bf16[1,192,768]{2,1,0:T(8,128)(2,1)} %param.18), kind=kLoop, calls=%fused_computation.5 | loop fusion | flops 147456 | bytes 884737 | tf_op jit(solution)/shard_map/jit(_where)/select_n | solution.py:581
  1.8 2.2 %collective-permute-start = (bf16[192,768]{1,0:T(8,128)(2,1)S(1)}, bf16[192,768]{1,0:T(8,128)(2,1)S(1)}, u32[]{:S(2)}, u32[]{:S(2)}) collective-permute-start(bf16[192,768]{1,0:T(8,128)(2,1)S(1)} %broadcast_select_fusion), channel_id=1, source_target_pairs={{0,64},{64,0},{128,192},{192,128},{1,65},{65,1},{129,193},{193,129... | collective-permute-start | bytes 884744 | tf_op jit(solution)/shard_map/ppermute | solution.py:581
  4.0 2.1 %collective-permute-start.2 = (bf16[3,192,128]{2,1,0:T(8,128)(2,1)S(1)}, bf16[3,192,128]{2,1,0:T(8,128)(2,1)S(1)}, u32[]{:S(2)}, u32[]{:S(2)}) collective-permute-start(bf16[3,192,128]{2,1,0:T(8,128)(2,1)S(1)} %get-tuple-element.123), channel_id=1, source_target_pairs={{0,63},{1,2},{2,1},{3,4},{4,3},{5,6},{6,5},{7,8},{8,7},{9,10},{10,... | collective-permute-start | bytes 442376 | tf_op jit(solution)/shard_map/ppermute | solution.py:78
  6.2 6.1 %collective-permute-start.1 = (bf16[3,192,128]{2,1,0:T(8,128)(2,1)S(1)}, bf16[3,192,128]{2,1,0:T(8,128)(2,1)S(1)}, u32[]{:S(2)}, u32[]{:S(2)}) collective-permute-start(bf16[3,192,128]{2,1,0:T(8,128)(2,1)S(1)} %get-tuple-element.124), channel_id=1, source_target_pairs={{0,1},{1,0},{2,3},{3,2},{4,5},{5,4},{6,7},{7,6},{8,9},{9,8},{10,11... | collective-permute-start | bytes 442376 | tf_op jit(solution)/shard_map/ppermute | solution.py:73
  14.5 3.0 %shard_map.154 = (f32[192,640]{1,0:T(8,128)S(1)}, f32[1,640]{1,0:T(1,128)S(1)}, bf16[768,640]{1,0:T(8,128)(2,1)S(1)}, bf16[768,640]{1,0:T(8,128)(2,1)S(1)}, bf16[208,768]{1,0:T(8,128)(2,1)S(1)}) custom-call(s32[16]{0:T(128)S(1)} %concatenate.3.meta, bf16[5,192,128]{2,1,0:T(8,128)(2,1)S(1)} %bitcast.25, ...), custom_call_target="tpu_custom_call" | custom-call | tf_op jit(solution)/shard_map/pallas_call | solution.py:90
  18.3 1.0 collective-permute-start.6
  19.5 6.5 %collective-permute-done.5.note = bf16[208,768]{1,0:T(8,128)(2,1)S(1)} collective-permute-done((bf16[208,768]{1,0:T(8,128)(2,1)S(1)}, bf16[208,768]{1,0:T(8,128)(2,1)S(1)}, u32[]{:S(2)}, u32[]{:S(2)}) %collective-permute-start.5) | collective-permute-done | bytes 319520 | tf_op jit(solution)/shard_map/ppermute | solution.py:593
  26.0 3.2 %shard_map.156 = (f32[192,640]{1,0:T(8,128)S(1)}, f32[1,640]{1,0:T(1,128)S(1)}, bf16[768,640]{1,0:T(8,128)(2,1)S(1)}, f32[192,64]{1,0:T(8,128)S(1)}, bf16[12,112...) custom-call(s32[16]{0:T(128)S(1)} %concatenate.3.meta, ...), custom_call_target="tpu_custom_call" | custom-call | flops 1000000000 | bytes 10000000 | tf_op jit(solution)/shard_map/pallas_call | solution.py:90
  29.8 1.8 %collective-permute-start.8 = (bf16[3,192,128]{2,1,0:T(8,128)(2,1)S(1)}, bf16[3,192,128]{2,1,0:T(8,128)(2,1)S(1)}, u32[]{:S(2)}, u32[]{:S(2)}) collective-permute-start(bf16[3,192,128]{2,1,0:T(8,128)(2,1)S(1)} %get-tuple-element.88), channel_id=1, source_target_pairs={{0,1},{1,0},{2,3},{3,2},{4,5},{5,4},{6,7},{7,6},{8,9},{9,8},{10,11... | collective-permute-start | bytes 442376 | tf_op jit(solution)/shard_map/ppermute | solution.py:73
  31.6 1.0 collective-permute-done.8.inner
  32.6 3.6 %collective-permute-done.9.outer = bf16[3,192,128]{2,1,0:T(8,128)(2,1)S(1)} collective-permute-done((bf16[3,192,128]{2,1,0:T(8,128)(2,1)S(1)}, bf16[3,192,128]{2,1,0:T(8,128)(2,1)S(1)}, u32[]{:S(2)}, u32[]{:S(2)}) %collective-permute-start.9) | collective-permute-done | bytes 147488 | tf_op jit(solution)/shard_map/ppermute | solution.py:78
  36.7 5.0 %collective-permute-start.10 = (bf16[5,192,128]{2,1,0:T(8,128)(2,1)S(1)}, bf16[5,192,128]{2,1,0:T(8,128)(2,1)S(1)}, u32[]{:S(2)}, u32[]{:S(2)}) collective-permute-start(bf16[5,192,128]{2,1,0:T(8,128)(2,1)S(1)} %shard_map.158), channel_id=1, source_target_pairs={{0,192},{192,0},{64,128},{128,64},{1,193},{193,1},{65,129},{129,65... | collective-permute-start | bytes 737288 | tf_op jit(solution)/shard_map/ppermute | solution.py:642
  41.7 3.6 %collective-permute-done.10.cot.turn_cot = bf16[5,192,128]{2,1,0:T(8,128)(2,1)S(1)} collective-permute-done((bf16[5,192,128]{2,1,0:T(8,128)(2,1)S(1)}, bf16[5,192,128]{2,1,0:T(8,128)(2,1)S(1)}, u32[]{:S(2)}, u32[]{:S(2)}) %collective-permute-start.10) | collective-permute-done | bytes 245792 | tf_op jit(solution)/shard_map/ppermute | solution.py:642
  45.3 1.5 %shard_map.159 = (bf16[5,192,128]{2,1,0:T(8,128)(2,1)S(1)}, bf16[3,192,128]{2,1,0:T(8,128)(2,1)S(1)}, bf16[3,192,128]{2,1,0:T(8,128)(2,1)S(1)}) custom-call(s32[16]{0:T(128)S(1)} %concatenate.3.meta, bf16[5,192,128]{2,1,0:T(8,128)(2,1)S(1)} %collective-permute-done.10.cot.turn_cot, f32[192,64]{1,0:T(8,128)S(1)} %get-tuple-element.80.cols, ...), custom_call_target="tpu_custom_call" | custom-call | tf_op jit(solution)/shard_map/pallas_call | solution.py:90
  46.8 4.4 %collective-permute-start.12 = (bf16[3,192,128]{2,1,0:T(8,128)(2,1)S(1)}, bf16[3,192,128]{2,1,0:T(8,128)(2,1)S(1)}, u32[]{:S(2)}, u32[]{:S(2)}) collective-permute-start(bf16[3,192,128]{2,1,0:T(8,128)(2,1)S(1)} %get-tuple-element.92), channel_id=1, source_target_pairs={{0,1},{1,0},{2,3},{3,2},{4,5},{5,4},{6,7},{7,6},{8,9},{9,8},{10,11... | collective-permute-start | bytes 442376 | tf_op jit(solution)/shard_map/ppermute | solution.py:73
  52.2 3.7 %collective-permute-done.13.turn_outer = bf16[3,192,128]{2,1,0:T(8,128)(2,1)S(1)} collective-permute-done((bf16[3,192,128]{2,1,0:T(8,128)(2,1)S(1)}, bf16[3,192,128]{2,1,0:T(8,128)(2,1)S(1)}, u32[]{:S(2)}, u32[]{:S(2)}) %collective-permute-start.13) | collective-permute-done | bytes 147488 | tf_op jit(solution)/shard_map/ppermute | solution.py:78
  55.9 4.0 %shard_map.160 = (bf16[5,192,128]{2,1,0:T(8,128)(2,1)S(1)}, bf16[5,192,128]{2,1,0:T(8,128)(2,1)S(1)}, bf16[3,192,128]{2,1,0:T(8,128)(2,1)S(1)}, bf16[3,192,128]{...) custom-call(s32[16]{0:T(128)S(1)} %concatenate.3.meta, ...), custom_call_target="tpu_custom_call" | custom-call | tf_op jit(solution)/shard_map/pallas_call | solution.py:90
  60.1 3.3 %collective-permute-start.15 = (bf16[104,768]{1,0:T(8,128)(2,1)S(1)}, bf16[104,768]{1,0:T(8,128)(2,1)S(1)}, u32[]{:S(2)}, u32[]{:S(2)}) collective-permute-start(bf16[104,768]{1,0:T(8,128)(2,1)S(1)} %get-tuple-element.97), channel_id=1, source_target_pairs={{0,1},{1,0},{2,3},{3,2},{4,5},{5,4},{6,7},{7,6},{8,9},{9,8},{10,11... | collective-permute-start | bytes 479240 | tf_op jit(solution)/shard_map/ppermute | solution.py:69
  63.4 1.5 %collective-permute-start.16 = (bf16[104,768]{1,0:T(8,128)(2,1)S(1)}, bf16[104,768]{1,0:T(8,128)(2,1)S(1)}, u32[]{:S(2)}, u32[]{:S(2)}) collective-permute-start(bf16[104,768]{1,0:T(8,128)(2,1)S(1)} %get-tuple-element.98), channel_id=1, source_target_pairs={{0,9},{1,2},{2,11},{3,0},{4,13},{5,6},{6,15},{7,4},{8,1},{9,10},{1... | collective-permute-start | bytes 479240 | tf_op jit(solution)/shard_map/ppermute | solution.py:69
  64.9 3.5 %collective-permute-done.16 = bf16[104,768]{1,0:T(8,128)(2,1)S(1)} collective-permute-done((bf16[104,768]{1,0:T(8,128)(2,1)S(1)}, bf16[104,768]{1,0:T(8,128)(2,1)S(1)}, u32[]{:S(2)}, u32[]{:S(2)}) %collective-permute-start.16) | collective-permute-done | bytes 159776 | tf_op jit(solution)/shard_map/ppermute | solution.py:69
  68.6 1.8 %collective-permute-start.18 = (bf16[3,192,128]{2,1,0:T(8,128)(2,1)S(1)}, bf16[3,192,128]{2,1,0:T(8,128)(2,1)S(1)}, u32[]{:S(2)}, u32[]{:S(2)}) collective-permute-start(bf16[3,192,128]{2,1,0:T(8,128)(2,1)S(1)} %get-tuple-element.101), channel_id=1, source_target_pairs={{0,1},{1,0},{2,3},{3,2},{4,5},{5,4},{6,7},{7,6},{8,9},{9,8},{10,11... | collective-permute-start | bytes 442376 | tf_op jit(solution)/shard_map/ppermute | solution.py:73
  70.4 4.1 %collective-permute-done.17 = bf16[104,768]{1,0:T(8,128)(2,1)S(1)} collective-permute-done((bf16[104,768]{1,0:T(8,128)(2,1)S(1)}, bf16[104,768]{1,0:T(8,128)(2,1)S(1)}, u32[]{:S(2)}, u32[]{:S(2)}) %collective-permute-start.17) | collective-permute-done | bytes 159776 | tf_op jit(solution)/shard_map/ppermute | solution.py:69
  75.8 4.2 %collective-permute-done.19 = bf16[104,768]{1,0:T(8,128)(2,1)S(1)} collective-permute-done((bf16[104,768]{1,0:T(8,128)(2,1)S(1)}, bf16[104,768]{1,0:T(8,128)(2,1)S(1)}, u32[]{:S(2)}, u32[]{:S(2)}) %collective-permute-start.19) | collective-permute-done | bytes 159776 | tf_op jit(solution)/shard_map/ppermute | solution.py:69
  80.1 2.4 %collective-permute-start.21 = (bf16[104,768]{1,0:T(8,128)(2,1)S(1)}, bf16[104,768]{1,0:T(8,128)(2,1)S(1)}, u32[]{:S(2)}, u32[]{:S(2)}) collective-permute-start(bf16[104,768]{1,0:T(8,128)(2,1)S(1)} %add_convert_fusion.2), channel_id=1, source_target_pairs={{0,24},{1,3},{2,26},{3,1},{4,28},{5,7},{6,30},{7,5},{8,16},{9,11},... | collective-permute-start | bytes 479240 | tf_op jit(solution)/shard_map/ppermute | solution.py:69
  82.5 1.7 %shard_map.161 = (bf16[5,192,128]{2,1,0:T(8,128)(2,1)S(1)}, bf16[2,192,128]{2,1,0:T(8,128)(2,1)S(1)}) custom-call(s32[16]{0:T(128)S(1)} %concatenate.3.meta, bf16[5,192,128]{2,1,0:T(8,128)(2,1)S(1)} %get-tuple-element.106.field, bf16[3,192,128]{2,1,0:T(8,128)(2,1)S(1)} %collective-permute-done.18.inner, ...), custom_call_target="tpu_custom_call" | custom-call | tf_op jit(solution)/shard_map/pallas_call | solution.py:90
  85.2 4.5 %collective-permute-start.22 = (bf16[104,768]{1,0:T(8,128)(2,1)S(1)}, bf16[104,768]{1,0:T(8,128)(2,1)S(1)}, u32[]{:S(2)}, u32[]{:S(2)}) collective-permute-start(bf16[104,768]{1,0:T(8,128)(2,1)S(1)} %add_convert_fusion.1), channel_id=1, source_target_pairs={{0,56},{1,7},{2,58},{3,5},{4,60},{5,3},{6,62},{7,1},{8,48},{9,15},... | collective-permute-start | bytes 479240 | tf_op jit(solution)/shard_map/ppermute | solution.py:69
  89.7 2.7 %collective-permute-done.22 = bf16[104,768]{1,0:T(8,128)(2,1)S(1)} collective-permute-done((bf16[104,768]{1,0:T(8,128)(2,1)S(1)}, bf16[104,768]{1,0:T(8,128)(2,1)S(1)}, u32[]{:S(2)}, u32[]{:S(2)}) %collective-permute-start.22) | collective-permute-done | bytes 159776 | tf_op jit(solution)/shard_map/ppermute | solution.py:69
  92.4 1.4 %collective-permute-done.23.arrived = bf16[2,192,128]{2,1,0:T(8,128)(2,1)S(1)} collective-permute-done((bf16[2,192,128]{2,1,0:T(8,128)(2,1)S(1)}, bf16[2,192,128]{2,1,0:T(8,128)(2,1)S(1)}, u32[]{:S(2)}, u32[]{:S(2)}) %collective-permute-start.23) | collective-permute-done | bytes 98336 | tf_op jit(solution)/shard_map/ppermute | solution.py:687
  93.8 7.1 %collective-permute-start.26 = (bf16[104,768]{1,0:T(8,128)(2,1)S(1)}, bf16[104,768]{1,0:T(8,128)(2,1)S(1)}, u32[]{:S(2)}, u32[]{:S(2)}) collective-permute-start(bf16[104,768]{1,0:T(8,128)(2,1)S(1)} %add_convert_fusion.keep), channel_id=1, source_target_pairs={{0,3},{1,8},{2,1},{3,10},{4,7},{5,12},{6,5},{7,14},{8,11},{9,0},{1... | collective-permute-start | bytes 479240 | tf_op jit(solution)/shard_map/ppermute | solution.py:69
  101.7 1.3 %shard_map.162 = bf16[3,192,128]{2,1,0:T(8,128)(2,1)} custom-call(s32[16]{0:T(128)S(1)} %concatenate.3.meta, bf16[5,192,128]{2,1,0:T(8,128)(2,1)S(1)} %get-tuple-element.112.result, bf16[2,192,128]{2,1,0:T(8,128)(2,1)S(1)} %collective-permute-done.23.arrived), custom_call_target="tpu_custom_call" | custom-call | tf_op jit(solution)/shard_map/pallas_call | solution.py:90
  103.1 3.2 %collective-permute-done.24.near = bf16[104,768]{1,0:T(8,128)(2,1)S(1)} collective-permute-done((bf16[104,768]{1,0:T(8,128)(2,1)S(1)}, bf16[104,768]{1,0:T(8,128)(2,1)S(1)}, u32[]{:S(2)}, u32[]{:S(2)}) %collective-permute-start.24) | collective-permute-done | bytes 159776 | tf_op jit(solution)/shard_map/ppermute | solution.py:69
  106.3 1.8 %shard_map.163 = (f32[49,1,192]{2,1,0:T(1,128)}, f32[1,192]{1,0:T(1,128)}, f32[1,192,768]{2,1,0:T(8,128)}, f32[1,768]{1,0:T(1,128)}, f32[1,192,768]{2,1,0:T(8,128)}, /*index=5*/f32[1,192]{1,0:T(1,128)}) custom-call(s32[16]{0:T(128)S(1)} %concatenate.3.meta, bf16[104,768]{1,0:T(8,128)(2,1)S(1)} %add_convert_fusion.keep, ...), custom_call_target="tpu_custom_call" | custom-call | tf_op jit(solution)/shard_map/pallas_call | solution.py:90
  (62 shorter events, 8.7 us)
Async XLA Ops:
  0.6 3.4 %copy-start.1 = (bf16[1,5,192,128]{3,2,1,0:T(8,128)(2,1)S(1)}, bf16[1,5,192,128]{3,2,1,0:T(8,128)(2,1)}, u32[]{:S(2)}) copy-start(bf16[1,5,192,128]{3,2,1,0:T(8,128)(2,1)} %param.10) | copy-start | bytes 737284
  1.8 16.5 %collective-permute-start = (bf16[192,768]{1,0:T(8,128)(2,1)S(1)}, bf16[192,768]{1,0:T(8,128)(2,1)S(1)}, u32[]{:S(2)}, u32[]{:S(2)}) collective-permute-start(bf16[192,768]{1,0:T(8,128)(2,1)S(1)} %broadcast_select_fusion), channel_id=1, source_target_pairs={{0,64},{64,0},{128,192},{192,128},{1,65},{65,1},{129,193},{193,129... | collective-permute-start | bytes 884744 | tf_op jit(solution)/shard_map/ppermute | solution.py:581
  4.0 8.3 %copy-start.7 = (f32[1,49,192]{2,0,1:T(1,128)S(1)}, f32[1,49,192]{2,0,1:T(1,128)}, u32[]{:S(2)}) copy-start(f32[1,49,192]{2,0,1:T(1,128)} %param.14) | copy-start | bytes 112900
  4.0 9.1 %copy-start.3 = (bf16[1,192,768]{2,1,0:T(8,128)(2,1)S(1)}, bf16[1,192,768]{2,1,0:T(8,128)(2,1)}, u32[]{:S(2)}) copy-start(bf16[1,192,768]{2,1,0:T(8,128)(2,1)} %param.18) | copy-start | bytes 884740
  4.0 9.1 %copy-start = (bf16[1,192,768]{2,1,0:T(8,128)(2,1)S(1)}, bf16[1,192,768]{2,1,0:T(8,128)(2,1)}, u32[]{:S(2)}) copy-start(bf16[1,192,768]{2,1,0:T(8,128)(2,1)} %param.16) | copy-start | bytes 884740
  4.0 10.4 %collective-permute-start.2 = (bf16[3,192,128]{2,1,0:T(8,128)(2,1)S(1)}, bf16[3,192,128]{2,1,0:T(8,128)(2,1)S(1)}, u32[]{:S(2)}, u32[]{:S(2)}) collective-permute-start(bf16[3,192,128]{2,1,0:T(8,128)(2,1)S(1)} %get-tuple-element.123), channel_id=1, source_target_pairs={{0,63},{1,2},{2,1},{3,4},{4,3},{5,6},{6,5},{7,8},{8,7},{9,10},{10,... | collective-permute-start | bytes 442376 | tf_op jit(solution)/shard_map/ppermute | solution.py:78
  6.2 8.3 %collective-permute-start.1 = (bf16[3,192,128]{2,1,0:T(8,128)(2,1)S(1)}, bf16[3,192,128]{2,1,0:T(8,128)(2,1)S(1)}, u32[]{:S(2)}, u32[]{:S(2)}) collective-permute-start(bf16[3,192,128]{2,1,0:T(8,128)(2,1)S(1)} %get-tuple-element.124), channel_id=1, source_target_pairs={{0,1},{1,0},{2,3},{3,2},{4,5},{5,4},{6,7},{7,6},{8,9},{9,8},{10,11... | collective-permute-start | bytes 442376 | tf_op jit(solution)/shard_map/ppermute | solution.py:73
  14.5 3.3 %copy-start.2 = (bf16[5,192,128]{2,1,0:T(8,128)(2,1)S(1)}, bf16[5,192,128]{2,1,0:T(8,128)(2,1)}, u32[]{:S(2)}) copy-start(bf16[5,192,128]{2,1,0:T(8,128)(2,1)} %cot_top.1) | copy-start | bytes 737284
  17.5 8.5 %collective-permute-start.5 = (bf16[208,768]{1,0:T(8,128)(2,1)S(1)}, bf16[208,768]{1,0:T(8,128)(2,1)S(1)}, u32[]{:S(2)}, u32[]{:S(2)}) collective-permute-start(bf16[208,768]{1,0:T(8,128)(2,1)S(1)} %get-tuple-element.78), channel_id=1, source_target_pairs={{0,64},{64,0},{128,192},{192,128},{1,65},{65,1},{129,193},{193,129... | collective-permute-start | bytes 958472 | tf_op jit(solution)/shard_map/ppermute | solution.py:593
  18.3 7.7 %collective-permute-start.6 = (bf16[192,768]{1,0:T(8,128)(2,1)S(1)}, bf16[192,768]{1,0:T(8,128)(2,1)S(1)}, u32[]{:S(2)}, u32[]{:S(2)}) collective-permute-start(bf16[192,768]{1,0:T(8,128)(2,1)S(1)} %collective-permute-done.half), channel_id=1, source_target_pairs={{0,1},{1,0},{2,3},{3,2},{4,5},{5,4},{6,7},{7,6},{8,9},{9,8},{10,11... | collective-permute-start | bytes 884744 | tf_op jit(solution)/shard_map/ppermute | solution.py:69
  19.4 9.9 %collective-permute-start.3 = (bf16[3,192,128]{2,1,0:T(8,128)(2,1)S(1)}, bf16[3,192,128]{2,1,0:T(8,128)(2,1)S(1)}, u32[]{:S(2)}, u32[]{:S(2)}) collective-permute-start(bf16[3,192,128]{2,1,0:T(8,128)(2,1)S(1)} %get-tuple-element.75), channel_id=1, source_target_pairs={{0,1},{1,0},{2,3},{3,2},{4,5},{5,4},{6,7},{7,6},{8,9},{9,8},{10,11... | collective-permute-start | bytes 442376 | tf_op jit(solution)/shard_map/ppermute | solution.py:73
  19.5 9.8 %collective-permute-start.4 = (bf16[3,192,128]{2,1,0:T(8,128)(2,1)S(1)}, bf16[3,192,128]{2,1,0:T(8,128)(2,1)S(1)}, u32[]{:S(2)}, u32[]{:S(2)}) collective-permute-start(bf16[3,192,128]{2,1,0:T(8,128)(2,1)S(1)} %get-tuple-element.76), channel_id=1, source_target_pairs={{0,63},{1,2},{2,1},{3,4},{4,3},{5,6},{6,5},{7,8},{8,7},{9,10},{10,... | collective-permute-start | bytes 442376 | tf_op jit(solution)/shard_map/ppermute | solution.py:78
  29.8 2.8 %collective-permute-start.8 = (bf16[3,192,128]{2,1,0:T(8,128)(2,1)S(1)}, bf16[3,192,128]{2,1,0:T(8,128)(2,1)S(1)}, u32[]{:S(2)}, u32[]{:S(2)}) collective-permute-start(bf16[3,192,128]{2,1,0:T(8,128)(2,1)S(1)} %get-tuple-element.88), channel_id=1, source_target_pairs={{0,1},{1,0},{2,3},{3,2},{4,5},{5,4},{6,7},{7,6},{8,9},{9,8},{10,11... | collective-permute-start | bytes 442376 | tf_op jit(solution)/shard_map/ppermute | solution.py:73
  31.6 4.6 %collective-permute-start.9 = (bf16[3,192,128]{2,1,0:T(8,128)(2,1)S(1)}, bf16[3,192,128]{2,1,0:T(8,128)(2,1)S(1)}, u32[]{:S(2)}, u32[]{:S(2)}) collective-permute-start(bf16[3,192,128]{2,1,0:T(8,128)(2,1)S(1)} %get-tuple-element.89), channel_id=1, source_target_pairs={{0,63},{1,2},{2,1},{3,4},{4,3},{5,6},{6,5},{7,8},{8,7},{9,10},{10,... | collective-permute-start | bytes 442376 | tf_op jit(solution)/shard_map/ppermute | solution.py:78
  36.7 8.6 %collective-permute-start.10 = (bf16[5,192,128]{2,1,0:T(8,128)(2,1)S(1)}, bf16[5,192,128]{2,1,0:T(8,128)(2,1)S(1)}, u32[]{:S(2)}, u32[]{:S(2)}) collective-permute-start(bf16[5,192,128]{2,1,0:T(8,128)(2,1)S(1)} %shard_map.158), channel_id=1, source_target_pairs={{0,192},{192,0},{64,128},{128,64},{1,193},{193,1},{65,129},{129,65... | collective-permute-start | bytes 737288 | tf_op jit(solution)/shard_map/ppermute | solution.py:642
  41.7 9.5 %collective-permute-start.7 = (bf16[5,192,128]{2,1,0:T(8,128)(2,1)S(1)}, bf16[5,192,128]{2,1,0:T(8,128)(2,1)S(1)}, u32[]{:S(2)}, u32[]{:S(2)}) collective-permute-start(bf16[5,192,128]{2,1,0:T(8,128)(2,1)S(1)} %get-tuple-element.86.cot), channel_id=1, source_target_pairs={{0,64},{64,0},{128,192},{192,128},{1,65},{65,1},{129,193},{193,129... | collective-permute-start | bytes 737288 | tf_op jit(solution)/shard_map/ppermute | solution.py:633
  45.3 10.6 %collective-permute-start.11 = (bf16[5,192,128]{2,1,0:T(8,128)(2,1)S(1)}, bf16[5,192,128]{2,1,0:T(8,128)(2,1)S(1)}, u32[]{:S(2)}, u32[]{:S(2)}) collective-permute-start(bf16[5,192,128]{2,1,0:T(8,128)(2,1)S(1)} %collective-permute-done.10.cot.turn_cot), channel_id=1, source_target_pairs={{0,64},{64,0},{128,192},{192,128},{1,65},{65,1},{129,193},{193,129... | collective-permute-start | bytes 737288 | tf_op jit(solution)/shard_map/ppermute | solution.py:643
  46.8 5.4 %collective-permute-start.12 = (bf16[3,192,128]{2,1,0:T(8,128)(2,1)S(1)}, bf16[3,192,128]{2,1,0:T(8,128)(2,1)S(1)}, u32[]{:S(2)}, u32[]{:S(2)}) collective-permute-start(bf16[3,192,128]{2,1,0:T(8,128)(2,1)S(1)} %get-tuple-element.92), channel_id=1, source_target_pairs={{0,1},{1,0},{2,3},{3,2},{4,5},{5,4},{6,7},{7,6},{8,9},{9,8},{10,11... | collective-permute-start | bytes 442376 | tf_op jit(solution)/shard_map/ppermute | solution.py:73
  51.2 4.7 %collective-permute-start.13 = (bf16[3,192,128]{2,1,0:T(8,128)(2,1)S(1)}, bf16[3,192,128]{2,1,0:T(8,128)(2,1)S(1)}, u32[]{:S(2)}, u32[]{:S(2)}) collective-permute-start(bf16[3,192,128]{2,1,0:T(8,128)(2,1)S(1)} %get-tuple-element.93), channel_id=1, source_target_pairs={{0,63},{1,2},{2,1},{3,4},{4,3},{5,6},{6,5},{7,8},{8,7},{9,10},{10,... | collective-permute-start | bytes 442376 | tf_op jit(solution)/shard_map/ppermute | solution.py:78
  60.0 5.0 %collective-permute-start.14 = (bf16[104,768]{1,0:T(8,128)(2,1)S(1)}, bf16[104,768]{1,0:T(8,128)(2,1)S(1)}, u32[]{:S(2)}, u32[]{:S(2)}) collective-permute-start(bf16[104,768]{1,0:T(8,128)(2,1)S(1)} %get-tuple-element.96), channel_id=1, source_target_pairs={{0,2},{1,9},{2,0},{3,11},{4,6},{5,13},{6,4},{7,15},{8,10},{9,1},{1... | collective-permute-start | bytes 479240 | tf_op jit(solution)/shard_map/ppermute | solution.py:69
  60.1 4.9 %collective-permute-start.15 = (bf16[104,768]{1,0:T(8,128)(2,1)S(1)}, bf16[104,768]{1,0:T(8,128)(2,1)S(1)}, u32[]{:S(2)}, u32[]{:S(2)}) collective-permute-start(bf16[104,768]{1,0:T(8,128)(2,1)S(1)} %get-tuple-element.97), channel_id=1, source_target_pairs={{0,1},{1,0},{2,3},{3,2},{4,5},{5,4},{6,7},{7,6},{8,9},{9,8},{10,11... | collective-permute-start | bytes 479240 | tf_op jit(solution)/shard_map/ppermute | solution.py:69
  63.4 5.0 %collective-permute-start.16 = (bf16[104,768]{1,0:T(8,128)(2,1)S(1)}, bf16[104,768]{1,0:T(8,128)(2,1)S(1)}, u32[]{:S(2)}, u32[]{:S(2)}) collective-permute-start(bf16[104,768]{1,0:T(8,128)(2,1)S(1)} %get-tuple-element.98), channel_id=1, source_target_pairs={{0,9},{1,2},{2,11},{3,0},{4,13},{5,6},{6,15},{7,4},{8,1},{9,10},{1... | collective-permute-start | bytes 479240 | tf_op jit(solution)/shard_map/ppermute | solution.py:69
  68.5 6.0 %collective-permute-start.17 = (bf16[104,768]{1,0:T(8,128)(2,1)S(1)}, bf16[104,768]{1,0:T(8,128)(2,1)S(1)}, u32[]{:S(2)}, u32[]{:S(2)}) collective-permute-start(bf16[104,768]{1,0:T(8,128)(2,1)S(1)} %add_convert_fusion.4), channel_id=1, source_target_pairs={{0,6},{1,25},{2,4},{3,27},{4,2},{5,29},{6,0},{7,31},{8,14},{9,17},... | collective-permute-start | bytes 479240 | tf_op jit(solution)/shard_map/ppermute | solution.py:69
  68.6 6.0 %collective-permute-start.18 = (bf16[3,192,128]{2,1,0:T(8,128)(2,1)S(1)}, bf16[3,192,128]{2,1,0:T(8,128)(2,1)S(1)}, u32[]{:S(2)}, u32[]{:S(2)}) collective-permute-start(bf16[3,192,128]{2,1,0:T(8,128)(2,1)S(1)} %get-tuple-element.101), channel_id=1, source_target_pairs={{0,1},{1,0},{2,3},{3,2},{4,5},{5,4},{6,7},{7,6},{8,9},{9,8},{10,11... | collective-permute-start | bytes 442376 | tf_op jit(solution)/shard_map/ppermute | solution.py:73
  74.6 5.4 %collective-permute-start.19 = (bf16[104,768]{1,0:T(8,128)(2,1)S(1)}, bf16[104,768]{1,0:T(8,128)(2,1)S(1)}, u32[]{:S(2)}, u32[]{:S(2)}) collective-permute-start(bf16[104,768]{1,0:T(8,128)(2,1)S(1)} %add_convert_fusion.3), channel_id=1, source_target_pairs={{0,8},{1,57},{2,10},{3,59},{4,12},{5,61},{6,14},{7,63},{8,0},{9,49... | collective-permute-start | bytes 479240 | tf_op jit(solution)/shard_map/ppermute | solution.py:69
  75.2 4.9 %collective-permute-start.20 = (bf16[3,192,128]{2,1,0:T(8,128)(2,1)S(1)}, bf16[3,192,128]{2,1,0:T(8,128)(2,1)S(1)}, u32[]{:S(2)}, u32[]{:S(2)}) collective-permute-start(bf16[3,192,128]{2,1,0:T(8,128)(2,1)S(1)} %get-tuple-element.104), channel_id=1, source_target_pairs={{0,63},{1,2},{2,1},{3,4},{4,3},{5,6},{6,5},{7,8},{8,7},{9,10},{10,... | collective-permute-start | bytes 442376 | tf_op jit(solution)/shard_map/ppermute | solution.py:78
  80.1 5.1 %collective-permute-start.21 = (bf16[104,768]{1,0:T(8,128)(2,1)S(1)}, bf16[104,768]{1,0:T(8,128)(2,1)S(1)}, u32[]{:S(2)}, u32[]{:S(2)}) collective-permute-start(bf16[104,768]{1,0:T(8,128)(2,1)S(1)} %add_convert_fusion.2), channel_id=1, source_target_pairs={{0,24},{1,3},{2,26},{3,1},{4,28},{5,7},{6,30},{7,5},{8,16},{9,11},... | collective-permute-start | bytes 479240 | tf_op jit(solution)/shard_map/ppermute | solution.py:69
  85.2 7.2 %collective-permute-start.22 = (bf16[104,768]{1,0:T(8,128)(2,1)S(1)}, bf16[104,768]{1,0:T(8,128)(2,1)S(1)}, u32[]{:S(2)}, u32[]{:S(2)}) collective-permute-start(bf16[104,768]{1,0:T(8,128)(2,1)S(1)} %add_convert_fusion.1), channel_id=1, source_target_pairs={{0,56},{1,7},{2,58},{3,5},{4,60},{5,3},{6,62},{7,1},{8,48},{9,15},... | collective-permute-start | bytes 479240 | tf_op jit(solution)/shard_map/ppermute | solution.py:69
  89.7 4.1 %collective-permute-start.23 = (bf16[2,192,128]{2,1,0:T(8,128)(2,1)S(1)}, bf16[2,192,128]{2,1,0:T(8,128)(2,1)S(1)}, u32[]{:S(2)}, u32[]{:S(2)}) collective-permute-start(bf16[2,192,128]{2,1,0:T(8,128)(2,1)S(1)} %get-tuple-element.114), channel_id=1, source_target_pairs={{0,1},{1,2},{2,3},{3,4},{4,5},{5,6},{6,7},{7,8},{8,9},{9,10},{10,1... | collective-permute-start | bytes 294920 | tf_op jit(solution)/shard_map/ppermute | solution.py:687
  93.8 9.3 %collective-permute-start.26 = (bf16[104,768]{1,0:T(8,128)(2,1)S(1)}, bf16[104,768]{1,0:T(8,128)(2,1)S(1)}, u32[]{:S(2)}, u32[]{:S(2)}) collective-permute-start(bf16[104,768]{1,0:T(8,128)(2,1)S(1)} %add_convert_fusion.keep), channel_id=1, source_target_pairs={{0,3},{1,8},{2,1},{3,10},{4,7},{5,12},{6,5},{7,14},{8,11},{9,0},{1... | collective-permute-start | bytes 479240 | tf_op jit(solution)/shard_map/ppermute | solution.py:69
  100.9 2.2 %collective-permute-start.25 = (bf16[104,768]{1,0:T(8,128)(2,1)S(1)}, bf16[104,768]{1,0:T(8,128)(2,1)S(1)}, u32[]{:S(2)}, u32[]{:S(2)}) collective-permute-start(bf16[104,768]{1,0:T(8,128)(2,1)S(1)} %add_convert_fusion.keep), channel_id=1, source_target_pairs={{0,1},{1,0},{2,3},{3,2},{4,5},{5,4},{6,7},{7,6},{8,9},{9,8},{10,11... | collective-permute-start | bytes 479240 | tf_op jit(solution)/shard_map/ppermute | solution.py:69
  100.9 5.4 %collective-permute-start.24 = (bf16[104,768]{1,0:T(8,128)(2,1)S(1)}, bf16[104,768]{1,0:T(8,128)(2,1)S(1)}, u32[]{:S(2)}, u32[]{:S(2)}) collective-permute-start(bf16[104,768]{1,0:T(8,128)(2,1)S(1)} %add_convert_fusion.keep), channel_id=1, source_target_pairs={{0,2},{1,9},{2,0},{3,11},{4,6},{5,13},{6,4},{7,15},{8,10},{9,1},{1... | collective-permute-start | bytes 479240 | tf_op jit(solution)/shard_map/ppermute | solution.py:69
  (5 other events, 3.5 us)

commit v7 on v6

--- a/solution.py
+++ b/solution.py
@@ -79,8 +79,8 @@
 
 
 def halo(inner, outer):
-    outer = across(outer)
-    return within(inner), outer
+    inner = within(inner)
+    return inner, across(outer)
 
 
 def call(body, out_shape, smem, operands, scratch=(), cost=(0, 0)):
@@ -332,7 +332,7 @@
     lax.fori_loop(0, chans // BLOCK, step, 0, unroll=UNROLL)
 
 
-def conv_kernel(section, meta, field, inner, outer, cot, taps_mat, result_ref, rows_ref):
+def conv_kernel(section, meta, field, outer, inner, cot, taps_mat, result_ref, rows_ref):
     @pl.when(meta[SECTION] == section)
     def _():
         conv_rows(meta, field, inner, outer, cot, taps_mat, result_ref, rows_ref)
@@ -342,8 +342,8 @@
     plane,
     meta,
     field,
+    outer,
     inner,
-    outer,
     cot,
     taps_mat,
     cols,
@@ -402,8 +402,8 @@
     cot_2,
     cot_1,
     turn_field,
+    turn_outer,
     turn_inner,
-    turn_outer,
     turn_cot,
     turn_mat,
     cols,
@@ -626,7 +626,7 @@
         functools.partial(middle_kernel, top),
         (rows_shape, rows_shape, edge_shape, edge_shape),
         1,
-        (meta, field, inner, outer, cot_top, back, next_cols, next_down_t, next_up)
+        (meta, field, outer, inner, cot_top, back, next_cols, next_down_t, next_up)
         + (next_slope, next_nhat, next_inv),
         (padded, outgrads, lowgrads),
     )
@@ -636,7 +636,7 @@
         functools.partial(conv_kernel, top),
         rows_shape,
         1,
-        (meta, field, inner, outer, cot_2, next_back),
+        (meta, field, outer, inner, cot_2, next_back),
         (padded,),
     )
     cot_1 = lax.ppermute(cot_1, "section", [(0, top), (top, 0), (1, 2), (2, 1)])
@@ -651,7 +651,7 @@
         last_kernel,
         (rows_shape, rows_shape, edge_shape, edge_shape, part, part, part, part),
         1,
-        (meta, cot_top, own_2, own_1, field, inner, outer, cot_1, next_back, cols, layer_scale, down_t, down, up, slope, nhat, inv, hidden)
+        (meta, cot_top, own_2, own_1, field, outer, inner, cot_1, next_back, cols, layer_scale, down_t, down, up, slope, nhat, inv, hidden)
         + (source, acts_inner, acts_outer),
         (
             outgrads,
@@ -666,7 +666,7 @@
     near = moved(near, ("x0", "z0"), False)
     mate = moved(mate, ("", ""), True)
     total = added(keep, near, mate, far)
-    orders = (("x1", "z1"), ("z0", "z2"), ("z1", "x0"), ("z2", "x1"))
+    orders = (("x1", "x0"), ("z2", "z1"), ("z1", "z2"), ("z0", "x1"))
     total, inner = lax.optimization_barrier((total, inner))
     total = added(total, moved(total, orders[0], False))
     inner = within(inner)

time: 108 us -> 108 us (level)
  waiting for transfers between devices: 39.4 us -> 24.9 us
  starting transfers between devices: 46 us -> 60.2 us
    ppermute x5, starting transfers between devices: 14.2 us -> 22.6 us  [within(): lax.ppermute(value, 'tile', [(tile, tile ^ 1) for tile in range(TILES)])]
    ppermute x5, waiting for transfers between devices: 7.37 us -> 0.01 us  [across(): return lax.ppermute(value, 'tile', pairs)]
    ppermute x1, waiting for transfers between devices: 6.53 us -> 1.76 us  [body(): note = lax.ppermute(own_note, 'section', swaps)]
    ppermute x5, starting transfers between devices: 2.73 us -> 5.87 us  [across(): return lax.ppermute(value, 'tile', pairs)]
    ppermute x11, starting transfers between devices: 21.6 us -> 24.3 us  [moved(): return lax.ppermute(value, 'tile', pairs)]
    ppermute x1, waiting for transfers between devices: 1.38 us -> 0.01 us  [body(): lax.ppermute(sent, 'tile', [(tile, (tile + 1) % TILES) for tile in range(...]
  transfers between devices with their start and end apart: 27 -> 27, of which waited for: 14 -> 10; matrix products, arithmetic and copies ran while one was open for 0% -> 0% of each run, Pallas kernels for 11% -> 11%
where the time goes in v7:
time: 108 us
  starting transfers between devices  60.2 us (56%)
  waiting for transfers between devices  24.9 us (23%)
  Pallas kernels  18.9 us (17%)
  local copies, waits for them, and re-layouts  1.44 us (1%)
  other arithmetic  1.42 us (1%)
    ppermute x11, starting transfers between devices, moved(): return lax.ppermute(value, 'tile', pairs)  24.3 us
    ppermute x5, starting transfers between devices, within(): lax.ppermute(value, 'tile', [(tile, tile ^ 1) for tile in range(TILES)])  22.6 us
    pallas_call x11, Pallas kernels, call(): pl.pallas_call(body, out_shape=out_shape, in_specs=spec, out_specs=outs,...  18.9 us
    ppermute x11, waiting for transfers between devices, moved(): return lax.ppermute(value, 'tile', pairs)  17.5 us
    ppermute x5, starting transfers between devices, across(): return lax.ppermute(value, 'tile', pairs)  5.87 us
    ppermute x1, starting transfers between devices, body(): cot_1 = lax.ppermute(cot_1, 'section', [(0, top), (top, 0), (1, 2), (2, 1)])  5.01 us
    ppermute x1, waiting for transfers between devices, body(): cot_1 = lax.ppermute(cot_1, 'section', [(0, top), (top, 0), (1, 2), (2, 1)])  3.58 us
    ppermute x1, starting transfers between devices, body(): half = lax.ppermute(jnp.where(odd, down, up), 'section', swaps)  2.21 us
  transfers between devices with their start and end apart: 27, of which 10 were waited for; matrix products, arithmetic and copies ran while one was open for 0% of the time, Pallas kernels for 11%

profile of v7, /device:TPU:1, one launch (start us, length us, event | category | flops | bytes accessed | tf_op | source)
XLA Modules:
  0.0 107.8 jit_solution(6037974790605779108)
XLA Ops:
  0.7 1.1 %broadcast_select_fusion = bf16[192,768]{1,0:T(8,128)(2,1)S(1)} fusion(pred[]{:T(512)S(6)} %eq.21, bf16[1,192,768]{2,1,0:T(8,128)(2,1)} %param.16, bf16[1,192,768]{2,1,0:T(8,128)(2,1)} %param.18), kind=kLoop, calls=%fused_computation.5 | loop fusion | flops 147456 | bytes 884737 | tf_op jit(solution)/shard_map/jit(_where)/select_n | solution.py:581
  1.8 2.2 %collective-permute-start = (bf16[192,768]{1,0:T(8,128)(2,1)S(1)}, bf16[192,768]{1,0:T(8,128)(2,1)S(1)}, u32[]{:S(2)}, u32[]{:S(2)}) collective-permute-start(bf16[192,768]{1,0:T(8,128)(2,1)S(1)} %broadcast_select_fusion), channel_id=1, source_target_pairs={{0,64},{64,0},{128,192},{192,128},{1,65},{65,1},{129,193},{193,129... | collective-permute-start | bytes 884744 | tf_op jit(solution)/shard_map/ppermute | solution.py:581
  4.0 2.1 %collective-permute-start.2 = (bf16[3,192,128]{2,1,0:T(8,128)(2,1)S(1)}, bf16[3,192,128]{2,1,0:T(8,128)(2,1)S(1)}, u32[]{:S(2)}, u32[]{:S(2)}) collective-permute-start(bf16[3,192,128]{2,1,0:T(8,128)(2,1)S(1)} %get-tuple-element.123), channel_id=1, source_target_pairs={{0,63},{1,2},{2,1},{3,4},{4,3},{5,6},{6,5},{7,8},{8,7},{9,10},{10,... | collective-permute-start | bytes 442376 | tf_op jit(solution)/shard_map/ppermute | solution.py:78
  6.2 6.1 %collective-permute-start.1 = (bf16[3,192,128]{2,1,0:T(8,128)(2,1)S(1)}, bf16[3,192,128]{2,1,0:T(8,128)(2,1)S(1)}, u32[]{:S(2)}, u32[]{:S(2)}) collective-permute-start(bf16[3,192,128]{2,1,0:T(8,128)(2,1)S(1)} %get-tuple-element.124), channel_id=1, source_target_pairs={{0,1},{1,0},{2,3},{3,2},{4,5},{5,4},{6,7},{7,6},{8,9},{9,8},{10,11... | collective-permute-start | bytes 442376 | tf_op jit(solution)/shard_map/ppermute | solution.py:73
  14.5 3.0 %shard_map.154 = (f32[192,640]{1,0:T(8,128)S(1)}, f32[1,640]{1,0:T(1,128)S(1)}, bf16[768,640]{1,0:T(8,128)(2,1)S(1)}, bf16[768,640]{1,0:T(8,128)(2,1)S(1)}, bf16[208,768]{1,0:T(8,128)(2,1)S(1)}) custom-call(s32[16]{0:T(128)S(1)} %concatenate.3.meta, bf16[5,192,128]{2,1,0:T(8,128)(2,1)S(1)} %bitcast.25, ...), custom_call_target="tpu_custom_call" | custom-call | tf_op jit(solution)/shard_map/pallas_call | solution.py:90
  18.3 1.0 collective-permute-start.6
  19.4 4.9 %collective-permute-start.4 = (bf16[3,192,128]{2,1,0:T(8,128)(2,1)S(1)}, bf16[3,192,128]{2,1,0:T(8,128)(2,1)S(1)}, u32[]{:S(2)}, u32[]{:S(2)}) collective-permute-start(bf16[3,192,128]{2,1,0:T(8,128)(2,1)S(1)} %get-tuple-element.76), channel_id=1, source_target_pairs={{0,1},{1,0},{2,3},{3,2},{4,5},{5,4},{6,7},{7,6},{8,9},{9,8},{10,11... | collective-permute-start | bytes 442376 | tf_op jit(solution)/shard_map/ppermute | solution.py:73
  24.2 1.8 %collective-permute-done.5.note = bf16[208,768]{1,0:T(8,128)(2,1)S(1)} collective-permute-done((bf16[208,768]{1,0:T(8,128)(2,1)S(1)}, bf16[208,768]{1,0:T(8,128)(2,1)S(1)}, u32[]{:S(2)}, u32[]{:S(2)}) %collective-permute-start.5) | collective-permute-done | bytes 319520 | tf_op jit(solution)/shard_map/ppermute | solution.py:593
  26.0 3.2 %shard_map.156 = (f32[192,640]{1,0:T(8,128)S(1)}, f32[1,640]{1,0:T(1,128)S(1)}, bf16[768,640]{1,0:T(8,128)(2,1)S(1)}, f32[192,64]{1,0:T(8,128)S(1)}, bf16[12,112...) custom-call(s32[16]{0:T(128)S(1)} %concatenate.3.meta, ...), custom_call_target="tpu_custom_call" | custom-call | flops 1000000000 | bytes 10000000 | tf_op jit(solution)/shard_map/pallas_call | solution.py:90
  30.1 4.7 %collective-permute-start.9 = (bf16[3,192,128]{2,1,0:T(8,128)(2,1)S(1)}, bf16[3,192,128]{2,1,0:T(8,128)(2,1)S(1)}, u32[]{:S(2)}, u32[]{:S(2)}) collective-permute-start(bf16[3,192,128]{2,1,0:T(8,128)(2,1)S(1)} %get-tuple-element.89), channel_id=1, source_target_pairs={{0,1},{1,0},{2,3},{3,2},{4,5},{5,4},{6,7},{7,6},{8,9},{9,8},{10,11... | collective-permute-start | bytes 442376 | tf_op jit(solution)/shard_map/ppermute | solution.py:73
  36.3 5.0 %collective-permute-start.10 = (bf16[5,192,128]{2,1,0:T(8,128)(2,1)S(1)}, bf16[5,192,128]{2,1,0:T(8,128)(2,1)S(1)}, u32[]{:S(2)}, u32[]{:S(2)}) collective-permute-start(bf16[5,192,128]{2,1,0:T(8,128)(2,1)S(1)} %shard_map.158), channel_id=1, source_target_pairs={{0,192},{192,0},{64,128},{128,64},{1,193},{193,1},{65,129},{129,65... | collective-permute-start | bytes 737288 | tf_op jit(solution)/shard_map/ppermute | solution.py:642
  41.3 3.6 %collective-permute-done.10.cot.turn_cot = bf16[5,192,128]{2,1,0:T(8,128)(2,1)S(1)} collective-permute-done((bf16[5,192,128]{2,1,0:T(8,128)(2,1)S(1)}, bf16[5,192,128]{2,1,0:T(8,128)(2,1)S(1)}, u32[]{:S(2)}, u32[]{:S(2)}) %collective-permute-start.10) | collective-permute-done | bytes 245792 | tf_op jit(solution)/shard_map/ppermute | solution.py:642
  44.9 1.5 %shard_map.159 = (bf16[5,192,128]{2,1,0:T(8,128)(2,1)S(1)}, bf16[3,192,128]{2,1,0:T(8,128)(2,1)S(1)}, bf16[3,192,128]{2,1,0:T(8,128)(2,1)S(1)}) custom-call(s32[16]{0:T(128)S(1)} %concatenate.3.meta, bf16[5,192,128]{2,1,0:T(8,128)(2,1)S(1)} %collective-permute-done.10.cot.turn_cot, f32[192,64]{1,0:T(8,128)S(1)} %get-tuple-element.80.cols, ...), custom_call_target="tpu_custom_call" | custom-call | tf_op jit(solution)/shard_map/pallas_call | solution.py:90
  46.9 6.5 %collective-permute-start.13 = (bf16[3,192,128]{2,1,0:T(8,128)(2,1)S(1)}, bf16[3,192,128]{2,1,0:T(8,128)(2,1)S(1)}, u32[]{:S(2)}, u32[]{:S(2)}) collective-permute-start(bf16[3,192,128]{2,1,0:T(8,128)(2,1)S(1)} %get-tuple-element.93), channel_id=1, source_target_pairs={{0,1},{1,0},{2,3},{3,2},{4,5},{5,4},{6,7},{7,6},{8,9},{9,8},{10,11... | collective-permute-start | bytes 442376 | tf_op jit(solution)/shard_map/ppermute | solution.py:73
  54.4 4.0 %shard_map.160 = (bf16[5,192,128]{2,1,0:T(8,128)(2,1)S(1)}, bf16[5,192,128]{2,1,0:T(8,128)(2,1)S(1)}, bf16[3,192,128]{2,1,0:T(8,128)(2,1)S(1)}, bf16[3,192,128]{...) custom-call(s32[16]{0:T(128)S(1)} %concatenate.3.meta, ...), custom_call_target="tpu_custom_call" | custom-call | tf_op jit(solution)/shard_map/pallas_call | solution.py:90
  58.5 4.7 %collective-permute-start.15 = (bf16[104,768]{1,0:T(8,128)(2,1)S(1)}, bf16[104,768]{1,0:T(8,128)(2,1)S(1)}, u32[]{:S(2)}, u32[]{:S(2)}) collective-permute-start(bf16[104,768]{1,0:T(8,128)(2,1)S(1)} %get-tuple-element.97), channel_id=1, source_target_pairs={{0,1},{1,0},{2,3},{3,2},{4,5},{5,4},{6,7},{7,6},{8,9},{9,8},{10,11... | collective-permute-start | bytes 479240 | tf_op jit(solution)/shard_map/ppermute | solution.py:69
  63.2 1.5 %collective-permute-start.16 = (bf16[104,768]{1,0:T(8,128)(2,1)S(1)}, bf16[104,768]{1,0:T(8,128)(2,1)S(1)}, u32[]{:S(2)}, u32[]{:S(2)}) collective-permute-start(bf16[104,768]{1,0:T(8,128)(2,1)S(1)} %get-tuple-element.98), channel_id=1, source_target_pairs={{0,9},{1,2},{2,11},{3,0},{4,13},{5,6},{6,15},{7,4},{8,1},{9,10},{1... | collective-permute-start | bytes 479240 | tf_op jit(solution)/shard_map/ppermute | solution.py:69
  64.7 3.5 %collective-permute-done.16 = bf16[104,768]{1,0:T(8,128)(2,1)S(1)} collective-permute-done((bf16[104,768]{1,0:T(8,128)(2,1)S(1)}, bf16[104,768]{1,0:T(8,128)(2,1)S(1)}, u32[]{:S(2)}, u32[]{:S(2)}) %collective-permute-start.16) | collective-permute-done | bytes 159776 | tf_op jit(solution)/shard_map/ppermute | solution.py:69
  68.3 1.4 %collective-permute-start.17 = (bf16[104,768]{1,0:T(8,128)(2,1)S(1)}, bf16[104,768]{1,0:T(8,128)(2,1)S(1)}, u32[]{:S(2)}, u32[]{:S(2)}) collective-permute-start(bf16[104,768]{1,0:T(8,128)(2,1)S(1)} %add_convert_fusion.4), channel_id=1, source_target_pairs={{0,6},{1,3},{2,4},{3,1},{4,2},{5,7},{6,0},{7,5},{8,14},{9,11},{10,... | collective-permute-start | bytes 479240 | tf_op jit(solution)/shard_map/ppermute | solution.py:69
  70.2 2.3 %collective-permute-done.17 = bf16[104,768]{1,0:T(8,128)(2,1)S(1)} collective-permute-done((bf16[104,768]{1,0:T(8,128)(2,1)S(1)}, bf16[104,768]{1,0:T(8,128)(2,1)S(1)}, u32[]{:S(2)}, u32[]{:S(2)}) %collective-permute-start.17) | collective-permute-done | bytes 159776 | tf_op jit(solution)/shard_map/ppermute | solution.py:69
  72.7 3.0 %collective-permute-start.20 = (bf16[3,192,128]{2,1,0:T(8,128)(2,1)S(1)}, bf16[3,192,128]{2,1,0:T(8,128)(2,1)S(1)}, u32[]{:S(2)}, u32[]{:S(2)}) collective-permute-start(bf16[3,192,128]{2,1,0:T(8,128)(2,1)S(1)} %get-tuple-element.104), channel_id=1, source_target_pairs={{0,63},{1,2},{2,1},{3,4},{4,3},{5,6},{6,5},{7,8},{8,7},{9,10},{10,... | collective-permute-start | bytes 442376 | tf_op jit(solution)/shard_map/ppermute | solution.py:78
  75.6 3.0 %collective-permute-done.19 = bf16[104,768]{1,0:T(8,128)(2,1)S(1)} collective-permute-done((bf16[104,768]{1,0:T(8,128)(2,1)S(1)}, bf16[104,768]{1,0:T(8,128)(2,1)S(1)}, u32[]{:S(2)}, u32[]{:S(2)}) %collective-permute-start.19) | collective-permute-done | bytes 159776 | tf_op jit(solution)/shard_map/ppermute | solution.py:69
  78.7 2.7 %collective-permute-start.21 = (bf16[104,768]{1,0:T(8,128)(2,1)S(1)}, bf16[104,768]{1,0:T(8,128)(2,1)S(1)}, u32[]{:S(2)}, u32[]{:S(2)}) collective-permute-start(bf16[104,768]{1,0:T(8,128)(2,1)S(1)} %add_convert_fusion.2), channel_id=1, source_target_pairs={{0,24},{1,57},{2,26},{3,59},{4,28},{5,61},{6,30},{7,63},{8,16},{9,... | collective-permute-start | bytes 479240 | tf_op jit(solution)/shard_map/ppermute | solution.py:69
  81.4 1.7 %shard_map.161 = (bf16[5,192,128]{2,1,0:T(8,128)(2,1)S(1)}, bf16[2,192,128]{2,1,0:T(8,128)(2,1)S(1)}) custom-call(s32[16]{0:T(128)S(1)} %concatenate.3.meta, bf16[5,192,128]{2,1,0:T(8,128)(2,1)S(1)} %get-tuple-element.106.field, bf16[3,192,128]{2,1,0:T(8,128)(2,1)S(1)} %collective-permute-done.18.inner, ...), custom_call_target="tpu_custom_call" | custom-call | tf_op jit(solution)/shard_map/pallas_call | solution.py:90
  83.1 3.1 %collective-permute-done.21 = bf16[104,768]{1,0:T(8,128)(2,1)S(1)} collective-permute-done((bf16[104,768]{1,0:T(8,128)(2,1)S(1)}, bf16[104,768]{1,0:T(8,128)(2,1)S(1)}, u32[]{:S(2)}, u32[]{:S(2)}) %collective-permute-start.21) | collective-permute-done | bytes 159776 | tf_op jit(solution)/shard_map/ppermute | solution.py:69
  86.3 7.8 %collective-permute-start.22 = (bf16[104,768]{1,0:T(8,128)(2,1)S(1)}, bf16[104,768]{1,0:T(8,128)(2,1)S(1)}, u32[]{:S(2)}, u32[]{:S(2)}) collective-permute-start(bf16[104,768]{1,0:T(8,128)(2,1)S(1)} %add_convert_fusion.1), channel_id=1, source_target_pairs={{0,8},{1,7},{2,10},{3,5},{4,12},{5,3},{6,14},{7,1},{8,0},{9,15},{1... | collective-permute-start | bytes 479240 | tf_op jit(solution)/shard_map/ppermute | solution.py:69
  94.1 2.7 %collective-permute-done.22 = bf16[104,768]{1,0:T(8,128)(2,1)S(1)} collective-permute-done((bf16[104,768]{1,0:T(8,128)(2,1)S(1)}, bf16[104,768]{1,0:T(8,128)(2,1)S(1)}, u32[]{:S(2)}, u32[]{:S(2)}) %collective-permute-start.22) | collective-permute-done | bytes 159776 | tf_op jit(solution)/shard_map/ppermute | solution.py:69
  96.8 3.9 %collective-permute-start.26 = (bf16[104,768]{1,0:T(8,128)(2,1)S(1)}, bf16[104,768]{1,0:T(8,128)(2,1)S(1)}, u32[]{:S(2)}, u32[]{:S(2)}) collective-permute-start(bf16[104,768]{1,0:T(8,128)(2,1)S(1)} %add_convert_fusion.keep), channel_id=1, source_target_pairs={{0,3},{1,8},{2,1},{3,10},{4,7},{5,12},{6,5},{7,14},{8,11},{9,0},{1... | collective-permute-start | bytes 479240 | tf_op jit(solution)/shard_map/ppermute | solution.py:69
  100.7 1.0 collective-permute-start.24
  101.7 1.3 %shard_map.162 = bf16[3,192,128]{2,1,0:T(8,128)(2,1)} custom-call(s32[16]{0:T(128)S(1)} %concatenate.3.meta, bf16[5,192,128]{2,1,0:T(8,128)(2,1)S(1)} %get-tuple-element.112.result, bf16[2,192,128]{2,1,0:T(8,128)(2,1)S(1)} %collective-permute-done.23.arrived), custom_call_target="tpu_custom_call" | custom-call | tf_op jit(solution)/shard_map/pallas_call | solution.py:90
  103.0 3.0 %collective-permute-done.24.near = bf16[104,768]{1,0:T(8,128)(2,1)S(1)} collective-permute-done((bf16[104,768]{1,0:T(8,128)(2,1)S(1)}, bf16[104,768]{1,0:T(8,128)(2,1)S(1)}, u32[]{:S(2)}, u32[]{:S(2)}) %collective-permute-start.24) | collective-permute-done | bytes 159776 | tf_op jit(solution)/shard_map/ppermute | solution.py:69
  106.1 1.8 %shard_map.163 = (f32[49,1,192]{2,1,0:T(1,128)}, f32[1,192]{1,0:T(1,128)}, f32[1,192,768]{2,1,0:T(8,128)}, f32[1,768]{1,0:T(1,128)}, f32[1,192,768]{2,1,0:T(8,128)}, /*index=5*/f32[1,192]{1,0:T(1,128)}) custom-call(s32[16]{0:T(128)S(1)} %concatenate.3.meta, bf16[104,768]{1,0:T(8,128)(2,1)S(1)} %add_convert_fusion.keep, ...), custom_call_target="tpu_custom_call" | custom-call | tf_op jit(solution)/shard_map/pallas_call | solution.py:90
  (62 shorter events, 7.8 us)
Async XLA Ops:
  0.6 3.4 %copy-start.1 = (bf16[1,5,192,128]{3,2,1,0:T(8,128)(2,1)S(1)}, bf16[1,5,192,128]{3,2,1,0:T(8,128)(2,1)}, u32[]{:S(2)}) copy-start(bf16[1,5,192,128]{3,2,1,0:T(8,128)(2,1)} %param.10) | copy-start | bytes 737284
  1.8 16.5 %collective-permute-start = (bf16[192,768]{1,0:T(8,128)(2,1)S(1)}, bf16[192,768]{1,0:T(8,128)(2,1)S(1)}, u32[]{:S(2)}, u32[]{:S(2)}) collective-permute-start(bf16[192,768]{1,0:T(8,128)(2,1)S(1)} %broadcast_select_fusion), channel_id=1, source_target_pairs={{0,64},{64,0},{128,192},{192,128},{1,65},{65,1},{129,193},{193,129... | collective-permute-start | bytes 884744 | tf_op jit(solution)/shard_map/ppermute | solution.py:581
  4.0 8.3 %copy-start.7 = (f32[1,49,192]{2,0,1:T(1,128)S(1)}, f32[1,49,192]{2,0,1:T(1,128)}, u32[]{:S(2)}) copy-start(f32[1,49,192]{2,0,1:T(1,128)} %param.14) | copy-start | bytes 112900
  4.0 9.1 %copy-start.3 = (bf16[1,192,768]{2,1,0:T(8,128)(2,1)S(1)}, bf16[1,192,768]{2,1,0:T(8,128)(2,1)}, u32[]{:S(2)}) copy-start(bf16[1,192,768]{2,1,0:T(8,128)(2,1)} %param.18) | copy-start | bytes 884740
  4.0 9.1 %copy-start = (bf16[1,192,768]{2,1,0:T(8,128)(2,1)S(1)}, bf16[1,192,768]{2,1,0:T(8,128)(2,1)}, u32[]{:S(2)}) copy-start(bf16[1,192,768]{2,1,0:T(8,128)(2,1)} %param.16) | copy-start | bytes 884740
  4.0 10.4 %collective-permute-start.2 = (bf16[3,192,128]{2,1,0:T(8,128)(2,1)S(1)}, bf16[3,192,128]{2,1,0:T(8,128)(2,1)S(1)}, u32[]{:S(2)}, u32[]{:S(2)}) collective-permute-start(bf16[3,192,128]{2,1,0:T(8,128)(2,1)S(1)} %get-tuple-element.123), channel_id=1, source_target_pairs={{0,63},{1,2},{2,1},{3,4},{4,3},{5,6},{6,5},{7,8},{8,7},{9,10},{10,... | collective-permute-start | bytes 442376 | tf_op jit(solution)/shard_map/ppermute | solution.py:78
  6.2 8.3 %collective-permute-start.1 = (bf16[3,192,128]{2,1,0:T(8,128)(2,1)S(1)}, bf16[3,192,128]{2,1,0:T(8,128)(2,1)S(1)}, u32[]{:S(2)}, u32[]{:S(2)}) collective-permute-start(bf16[3,192,128]{2,1,0:T(8,128)(2,1)S(1)} %get-tuple-element.124), channel_id=1, source_target_pairs={{0,1},{1,0},{2,3},{3,2},{4,5},{5,4},{6,7},{7,6},{8,9},{9,8},{10,11... | collective-permute-start | bytes 442376 | tf_op jit(solution)/shard_map/ppermute | solution.py:73
  14.5 3.3 %copy-start.2 = (bf16[5,192,128]{2,1,0:T(8,128)(2,1)S(1)}, bf16[5,192,128]{2,1,0:T(8,128)(2,1)}, u32[]{:S(2)}) copy-start(bf16[5,192,128]{2,1,0:T(8,128)(2,1)} %cot_top.1) | copy-start | bytes 737284
  17.5 8.5 %collective-permute-start.5 = (bf16[208,768]{1,0:T(8,128)(2,1)S(1)}, bf16[208,768]{1,0:T(8,128)(2,1)S(1)}, u32[]{:S(2)}, u32[]{:S(2)}) collective-permute-start(bf16[208,768]{1,0:T(8,128)(2,1)S(1)} %get-tuple-element.78), channel_id=1, source_target_pairs={{0,64},{64,0},{128,192},{192,128},{1,65},{65,1},{129,193},{193,129... | collective-permute-start | bytes 958472 | tf_op jit(solution)/shard_map/ppermute | solution.py:593
  18.3 7.7 %collective-permute-start.6 = (bf16[192,768]{1,0:T(8,128)(2,1)S(1)}, bf16[192,768]{1,0:T(8,128)(2,1)S(1)}, u32[]{:S(2)}, u32[]{:S(2)}) collective-permute-start(bf16[192,768]{1,0:T(8,128)(2,1)S(1)} %collective-permute-done.half), channel_id=1, source_target_pairs={{0,1},{1,0},{2,3},{3,2},{4,5},{5,4},{6,7},{7,6},{8,9},{9,8},{10,11... | collective-permute-start | bytes 884744 | tf_op jit(solution)/shard_map/ppermute | solution.py:69
  19.4 9.9 %collective-permute-start.3 = (bf16[3,192,128]{2,1,0:T(8,128)(2,1)S(1)}, bf16[3,192,128]{2,1,0:T(8,128)(2,1)S(1)}, u32[]{:S(2)}, u32[]{:S(2)}) collective-permute-start(bf16[3,192,128]{2,1,0:T(8,128)(2,1)S(1)} %get-tuple-element.75), channel_id=1, source_target_pairs={{0,63},{1,2},{2,1},{3,4},{4,3},{5,6},{6,5},{7,8},{8,7},{9,10},{10,... | collective-permute-start | bytes 442376 | tf_op jit(solution)/shard_map/ppermute | solution.py:78
  19.4 9.9 %collective-permute-start.4 = (bf16[3,192,128]{2,1,0:T(8,128)(2,1)S(1)}, bf16[3,192,128]{2,1,0:T(8,128)(2,1)S(1)}, u32[]{:S(2)}, u32[]{:S(2)}) collective-permute-start(bf16[3,192,128]{2,1,0:T(8,128)(2,1)S(1)} %get-tuple-element.76), channel_id=1, source_target_pairs={{0,1},{1,0},{2,3},{3,2},{4,5},{5,4},{6,7},{7,6},{8,9},{9,8},{10,11... | collective-permute-start | bytes 442376 | tf_op jit(solution)/shard_map/ppermute | solution.py:73
  29.8 4.9 %collective-permute-start.8 = (bf16[3,192,128]{2,1,0:T(8,128)(2,1)S(1)}, bf16[3,192,128]{2,1,0:T(8,128)(2,1)S(1)}, u32[]{:S(2)}, u32[]{:S(2)}) collective-permute-start(bf16[3,192,128]{2,1,0:T(8,128)(2,1)S(1)} %get-tuple-element.88), channel_id=1, source_target_pairs={{0,63},{1,2},{2,1},{3,4},{4,3},{5,6},{6,5},{7,8},{8,7},{9,10},{10,... | collective-permute-start | bytes 442376 | tf_op jit(solution)/shard_map/ppermute | solution.py:78
  30.1 5.7 %collective-permute-start.9 = (bf16[3,192,128]{2,1,0:T(8,128)(2,1)S(1)}, bf16[3,192,128]{2,1,0:T(8,128)(2,1)S(1)}, u32[]{:S(2)}, u32[]{:S(2)}) collective-permute-start(bf16[3,192,128]{2,1,0:T(8,128)(2,1)S(1)} %get-tuple-element.89), channel_id=1, source_target_pairs={{0,1},{1,0},{2,3},{3,2},{4,5},{5,4},{6,7},{7,6},{8,9},{9,8},{10,11... | collective-permute-start | bytes 442376 | tf_op jit(solution)/shard_map/ppermute | solution.py:73
  36.3 8.6 %collective-permute-start.10 = (bf16[5,192,128]{2,1,0:T(8,128)(2,1)S(1)}, bf16[5,192,128]{2,1,0:T(8,128)(2,1)S(1)}, u32[]{:S(2)}, u32[]{:S(2)}) collective-permute-start(bf16[5,192,128]{2,1,0:T(8,128)(2,1)S(1)} %shard_map.158), channel_id=1, source_target_pairs={{0,192},{192,0},{64,128},{128,64},{1,193},{193,1},{65,129},{129,65... | collective-permute-start | bytes 737288 | tf_op jit(solution)/shard_map/ppermute | solution.py:642
  41.3 12.1 %collective-permute-start.7 = (bf16[5,192,128]{2,1,0:T(8,128)(2,1)S(1)}, bf16[5,192,128]{2,1,0:T(8,128)(2,1)S(1)}, u32[]{:S(2)}, u32[]{:S(2)}) collective-permute-start(bf16[5,192,128]{2,1,0:T(8,128)(2,1)S(1)} %get-tuple-element.86.cot), channel_id=1, source_target_pairs={{0,64},{64,0},{128,192},{192,128},{1,65},{65,1},{129,193},{193,129... | collective-permute-start | bytes 737288 | tf_op jit(solution)/shard_map/ppermute | solution.py:633
  44.9 9.5 %collective-permute-start.11 = (bf16[5,192,128]{2,1,0:T(8,128)(2,1)S(1)}, bf16[5,192,128]{2,1,0:T(8,128)(2,1)S(1)}, u32[]{:S(2)}, u32[]{:S(2)}) collective-permute-start(bf16[5,192,128]{2,1,0:T(8,128)(2,1)S(1)} %collective-permute-done.10.cot.turn_cot), channel_id=1, source_target_pairs={{0,64},{64,0},{128,192},{192,128},{1,65},{65,1},{129,193},{193,129... | collective-permute-start | bytes 737288 | tf_op jit(solution)/shard_map/ppermute | solution.py:643
  46.4 7.0 %collective-permute-start.12 = (bf16[3,192,128]{2,1,0:T(8,128)(2,1)S(1)}, bf16[3,192,128]{2,1,0:T(8,128)(2,1)S(1)}, u32[]{:S(2)}, u32[]{:S(2)}) collective-permute-start(bf16[3,192,128]{2,1,0:T(8,128)(2,1)S(1)} %get-tuple-element.92), channel_id=1, source_target_pairs={{0,63},{1,2},{2,1},{3,4},{4,3},{5,6},{6,5},{7,8},{8,7},{9,10},{10,... | collective-permute-start | bytes 442376 | tf_op jit(solution)/shard_map/ppermute | solution.py:78
  46.9 7.5 %collective-permute-start.13 = (bf16[3,192,128]{2,1,0:T(8,128)(2,1)S(1)}, bf16[3,192,128]{2,1,0:T(8,128)(2,1)S(1)}, u32[]{:S(2)}, u32[]{:S(2)}) collective-permute-start(bf16[3,192,128]{2,1,0:T(8,128)(2,1)S(1)} %get-tuple-element.93), channel_id=1, source_target_pairs={{0,1},{1,0},{2,3},{3,2},{4,5},{5,4},{6,7},{7,6},{8,9},{9,8},{10,11... | collective-permute-start | bytes 442376 | tf_op jit(solution)/shard_map/ppermute | solution.py:73
  58.4 6.3 %collective-permute-start.14 = (bf16[104,768]{1,0:T(8,128)(2,1)S(1)}, bf16[104,768]{1,0:T(8,128)(2,1)S(1)}, u32[]{:S(2)}, u32[]{:S(2)}) collective-permute-start(bf16[104,768]{1,0:T(8,128)(2,1)S(1)} %get-tuple-element.96), channel_id=1, source_target_pairs={{0,2},{1,9},{2,0},{3,11},{4,6},{5,13},{6,4},{7,15},{8,10},{9,1},{1... | collective-permute-start | bytes 479240 | tf_op jit(solution)/shard_map/ppermute | solution.py:69
  58.5 6.2 %collective-permute-start.15 = (bf16[104,768]{1,0:T(8,128)(2,1)S(1)}, bf16[104,768]{1,0:T(8,128)(2,1)S(1)}, u32[]{:S(2)}, u32[]{:S(2)}) collective-permute-start(bf16[104,768]{1,0:T(8,128)(2,1)S(1)} %get-tuple-element.97), channel_id=1, source_target_pairs={{0,1},{1,0},{2,3},{3,2},{4,5},{5,4},{6,7},{7,6},{8,9},{9,8},{10,11... | collective-permute-start | bytes 479240 | tf_op jit(solution)/shard_map/ppermute | solution.py:69
  63.2 5.0 %collective-permute-start.16 = (bf16[104,768]{1,0:T(8,128)(2,1)S(1)}, bf16[104,768]{1,0:T(8,128)(2,1)S(1)}, u32[]{:S(2)}, u32[]{:S(2)}) collective-permute-start(bf16[104,768]{1,0:T(8,128)(2,1)S(1)} %get-tuple-element.98), channel_id=1, source_target_pairs={{0,9},{1,2},{2,11},{3,0},{4,13},{5,6},{6,15},{7,4},{8,1},{9,10},{1... | collective-permute-start | bytes 479240 | tf_op jit(solution)/shard_map/ppermute | solution.py:69
  68.3 4.2 %collective-permute-start.17 = (bf16[104,768]{1,0:T(8,128)(2,1)S(1)}, bf16[104,768]{1,0:T(8,128)(2,1)S(1)}, u32[]{:S(2)}, u32[]{:S(2)}) collective-permute-start(bf16[104,768]{1,0:T(8,128)(2,1)S(1)} %add_convert_fusion.4), channel_id=1, source_target_pairs={{0,6},{1,3},{2,4},{3,1},{4,2},{5,7},{6,0},{7,5},{8,14},{9,11},{10,... | collective-permute-start | bytes 479240 | tf_op jit(solution)/shard_map/ppermute | solution.py:69
  69.7 2.8 %collective-permute-start.18 = (bf16[3,192,128]{2,1,0:T(8,128)(2,1)S(1)}, bf16[3,192,128]{2,1,0:T(8,128)(2,1)S(1)}, u32[]{:S(2)}, u32[]{:S(2)}) collective-permute-start(bf16[3,192,128]{2,1,0:T(8,128)(2,1)S(1)} %get-tuple-element.101), channel_id=1, source_target_pairs={{0,1},{1,0},{2,3},{3,2},{4,5},{5,4},{6,7},{7,6},{8,9},{9,8},{10,11... | collective-permute-start | bytes 442376 | tf_op jit(solution)/shard_map/ppermute | solution.py:73
  72.6 6.1 %collective-permute-start.19 = (bf16[104,768]{1,0:T(8,128)(2,1)S(1)}, bf16[104,768]{1,0:T(8,128)(2,1)S(1)}, u32[]{:S(2)}, u32[]{:S(2)}) collective-permute-start(bf16[104,768]{1,0:T(8,128)(2,1)S(1)} %add_convert_fusion.3), channel_id=1, source_target_pairs={{0,56},{1,25},{2,58},{3,27},{4,60},{5,29},{6,62},{7,31},{8,48},{9,... | collective-permute-start | bytes 479240 | tf_op jit(solution)/shard_map/ppermute | solution.py:69
  72.7 6.0 %collective-permute-start.20 = (bf16[3,192,128]{2,1,0:T(8,128)(2,1)S(1)}, bf16[3,192,128]{2,1,0:T(8,128)(2,1)S(1)}, u32[]{:S(2)}, u32[]{:S(2)}) collective-permute-start(bf16[3,192,128]{2,1,0:T(8,128)(2,1)S(1)} %get-tuple-element.104), channel_id=1, source_target_pairs={{0,63},{1,2},{2,1},{3,4},{4,3},{5,6},{6,5},{7,8},{8,7},{9,10},{10,... | collective-permute-start | bytes 442376 | tf_op jit(solution)/shard_map/ppermute | solution.py:78
  78.7 7.5 %collective-permute-start.21 = (bf16[104,768]{1,0:T(8,128)(2,1)S(1)}, bf16[104,768]{1,0:T(8,128)(2,1)S(1)}, u32[]{:S(2)}, u32[]{:S(2)}) collective-permute-start(bf16[104,768]{1,0:T(8,128)(2,1)S(1)} %add_convert_fusion.2), channel_id=1, source_target_pairs={{0,24},{1,57},{2,26},{3,59},{4,28},{5,61},{6,30},{7,63},{8,16},{9,... | collective-permute-start | bytes 479240 | tf_op jit(solution)/shard_map/ppermute | solution.py:69
  86.3 10.5 %collective-permute-start.22 = (bf16[104,768]{1,0:T(8,128)(2,1)S(1)}, bf16[104,768]{1,0:T(8,128)(2,1)S(1)}, u32[]{:S(2)}, u32[]{:S(2)}) collective-permute-start(bf16[104,768]{1,0:T(8,128)(2,1)S(1)} %add_convert_fusion.1), channel_id=1, source_target_pairs={{0,8},{1,7},{2,10},{3,5},{4,12},{5,3},{6,14},{7,1},{8,0},{9,15},{1... | collective-permute-start | bytes 479240 | tf_op jit(solution)/shard_map/ppermute | solution.py:69
  94.1 2.7 %collective-permute-start.23 = (bf16[2,192,128]{2,1,0:T(8,128)(2,1)S(1)}, bf16[2,192,128]{2,1,0:T(8,128)(2,1)S(1)}, u32[]{:S(2)}, u32[]{:S(2)}) collective-permute-start(bf16[2,192,128]{2,1,0:T(8,128)(2,1)S(1)} %get-tuple-element.114), channel_id=1, source_target_pairs={{0,1},{1,2},{2,3},{3,4},{4,5},{5,6},{6,7},{7,8},{8,9},{9,10},{10,1... | collective-permute-start | bytes 294920 | tf_op jit(solution)/shard_map/ppermute | solution.py:687
  96.8 6.2 %collective-permute-start.26 = (bf16[104,768]{1,0:T(8,128)(2,1)S(1)}, bf16[104,768]{1,0:T(8,128)(2,1)S(1)}, u32[]{:S(2)}, u32[]{:S(2)}) collective-permute-start(bf16[104,768]{1,0:T(8,128)(2,1)S(1)} %add_convert_fusion.keep), channel_id=1, source_target_pairs={{0,3},{1,8},{2,1},{3,10},{4,7},{5,12},{6,5},{7,14},{8,11},{9,0},{1... | collective-permute-start | bytes 479240 | tf_op jit(solution)/shard_map/ppermute | solution.py:69
  100.7 2.4 %collective-permute-start.25 = (bf16[104,768]{1,0:T(8,128)(2,1)S(1)}, bf16[104,768]{1,0:T(8,128)(2,1)S(1)}, u32[]{:S(2)}, u32[]{:S(2)}) collective-permute-start(bf16[104,768]{1,0:T(8,128)(2,1)S(1)} %add_convert_fusion.keep), channel_id=1, source_target_pairs={{0,1},{1,0},{2,3},{3,2},{4,5},{5,4},{6,7},{7,6},{8,9},{9,8},{10,11... | collective-permute-start | bytes 479240 | tf_op jit(solution)/shard_map/ppermute | solution.py:69
  100.7 5.4 %collective-permute-start.24 = (bf16[104,768]{1,0:T(8,128)(2,1)S(1)}, bf16[104,768]{1,0:T(8,128)(2,1)S(1)}, u32[]{:S(2)}, u32[]{:S(2)}) collective-permute-start(bf16[104,768]{1,0:T(8,128)(2,1)S(1)} %add_convert_fusion.keep), channel_id=1, source_target_pairs={{0,2},{1,9},{2,0},{3,11},{4,6},{5,13},{6,4},{7,15},{8,10},{9,1},{1... | collective-permute-start | bytes 479240 | tf_op jit(solution)/shard_map/ppermute | solution.py:69
  (5 other events, 3.5 us)

commit v8 on v7

--- a/solution.py
+++ b/solution.py
@@ -666,14 +666,14 @@
     near = moved(near, ("x0", "z0"), False)
     mate = moved(mate, ("", ""), True)
     total = added(keep, near, mate, far)
-    orders = (("x1", "x0"), ("z2", "z1"), ("z1", "z2"), ("z0", "x1"))
-    total, inner = lax.optimization_barrier((total, inner))
+    orders = (("x1", "z1"), ("z0", "z2"), ("z1", "x0"), ("z2", "x1"))
+    total, outer = lax.optimization_barrier((total, outer))
     total = added(total, moved(total, orders[0], False))
-    inner = within(inner)
+    outer = across(outer)
     total, inner, outer = lax.optimization_barrier((total, inner, outer))
     total = added(total, moved(total, orders[1], False))
-    outer = across(outer)
-    total, outer = lax.optimization_barrier((total, outer))
+    inner = within(inner)
+    total, inner = lax.optimization_barrier((total, inner))
     total = added(total, moved(total, orders[2], False))
     result, sent = call(
         last_conv_kernel,

time: 108 us -> 107 us (level)
  starting transfers between devices: 60.2 us -> 57.3 us
  waiting for transfers between devices: 24.9 us -> 27.1 us
    ppermute x11, starting transfers between devices: 24.3 us -> 21.7 us  [moved(): return lax.ppermute(value, 'tile', pairs)]
    ppermute x11, waiting for transfers between devices: 17.5 us -> 19.7 us  [moved(): return lax.ppermute(value, 'tile', pairs)]
    ppermute x5, starting transfers between devices: 5.87 us -> 4.5 us  [across(): return lax.ppermute(value, 'tile', pairs)]
where the time goes in v8:
time: 107 us
  starting transfers between devices  57.3 us (54%)
  waiting for transfers between devices  27.1 us (25%)
  Pallas kernels  18.9 us (18%)
  local copies, waits for them, and re-layouts  1.44 us (1%)
  other arithmetic  1.42 us (1%)
    ppermute x5, starting transfers between devices, within(): lax.ppermute(value, 'tile', [(tile, tile ^ 1) for tile in range(TILES)])  23.6 us
    ppermute x11, starting transfers between devices, moved(): return lax.ppermute(value, 'tile', pairs)  21.7 us
    ppermute x11, waiting for transfers between devices, moved(): return lax.ppermute(value, 'tile', pairs)  19.7 us
    pallas_call x11, Pallas kernels, call(): pl.pallas_call(body, out_shape=out_shape, in_specs=spec, out_specs=outs,...  18.9 us
    ppermute x1, starting transfers between devices, body(): cot_1 = lax.ppermute(cot_1, 'section', [(0, top), (top, 0), (1, 2), (2, 1)])  5.01 us
    ppermute x5, starting transfers between devices, across(): return lax.ppermute(value, 'tile', pairs)  4.5 us
    ppermute x1, waiting for transfers between devices, body(): cot_1 = lax.ppermute(cot_1, 'section', [(0, top), (top, 0), (1, 2), (2, 1)])  3.58 us
    ppermute x1, starting transfers between devices, body(): half = lax.ppermute(jnp.where(odd, down, up), 'section', swaps)  2.21 us
  transfers between devices with their start and end apart: 27, of which 10 were waited for; matrix products, arithmetic and copies ran while one was open for 0% of the time, Pallas kernels for 11%

profile of v8, /device:TPU:1, one launch (start us, length us, event | category | flops | bytes accessed | tf_op | source)
XLA Modules:
  0.0 107.1 jit_solution(9474186508997967149)
XLA Ops:
  0.7 1.1 %broadcast_select_fusion = bf16[192,768]{1,0:T(8,128)(2,1)S(1)} fusion(pred[]{:T(512)S(6)} %eq.21, bf16[1,192,768]{2,1,0:T(8,128)(2,1)} %param.16, bf16[1,192,768]{2,1,0:T(8,128)(2,1)} %param.18), kind=kLoop, calls=%fused_computation.5 | loop fusion | flops 147456 | bytes 884737 | tf_op jit(solution)/shard_map/jit(_where)/select_n | solution.py:581
  1.8 2.2 %collective-permute-start = (bf16[192,768]{1,0:T(8,128)(2,1)S(1)}, bf16[192,768]{1,0:T(8,128)(2,1)S(1)}, u32[]{:S(2)}, u32[]{:S(2)}) collective-permute-start(bf16[192,768]{1,0:T(8,128)(2,1)S(1)} %broadcast_select_fusion), channel_id=1, source_target_pairs={{0,64},{64,0},{128,192},{192,128},{1,65},{65,1},{129,193},{193,129... | collective-permute-start | bytes 884744 | tf_op jit(solution)/shard_map/ppermute | solution.py:581
  4.0 2.1 %collective-permute-start.2 = (bf16[3,192,128]{2,1,0:T(8,128)(2,1)S(1)}, bf16[3,192,128]{2,1,0:T(8,128)(2,1)S(1)}, u32[]{:S(2)}, u32[]{:S(2)}) collective-permute-start(bf16[3,192,128]{2,1,0:T(8,128)(2,1)S(1)} %get-tuple-element.123), channel_id=1, source_target_pairs={{0,63},{1,2},{2,1},{3,4},{4,3},{5,6},{6,5},{7,8},{8,7},{9,10},{10,... | collective-permute-start | bytes 442376 | tf_op jit(solution)/shard_map/ppermute | solution.py:78
  6.2 6.1 %collective-permute-start.1 = (bf16[3,192,128]{2,1,0:T(8,128)(2,1)S(1)}, bf16[3,192,128]{2,1,0:T(8,128)(2,1)S(1)}, u32[]{:S(2)}, u32[]{:S(2)}) collective-permute-start(bf16[3,192,128]{2,1,0:T(8,128)(2,1)S(1)} %get-tuple-element.124), channel_id=1, source_target_pairs={{0,1},{1,0},{2,3},{3,2},{4,5},{5,4},{6,7},{7,6},{8,9},{9,8},{10,11... | collective-permute-start | bytes 442376 | tf_op jit(solution)/shard_map/ppermute | solution.py:73
  14.5 3.0 %shard_map.154 = (f32[192,640]{1,0:T(8,128)S(1)}, f32[1,640]{1,0:T(1,128)S(1)}, bf16[768,640]{1,0:T(8,128)(2,1)S(1)}, bf16[768,640]{1,0:T(8,128)(2,1)S(1)}, bf16[208,768]{1,0:T(8,128)(2,1)S(1)}) custom-call(s32[16]{0:T(128)S(1)} %concatenate.3.meta, bf16[5,192,128]{2,1,0:T(8,128)(2,1)S(1)} %bitcast.25, ...), custom_call_target="tpu_custom_call" | custom-call | tf_op jit(solution)/shard_map/pallas_call | solution.py:90
  18.3 1.0 collective-permute-start.6
  19.4 4.9 %collective-permute-start.4 = (bf16[3,192,128]{2,1,0:T(8,128)(2,1)S(1)}, bf16[3,192,128]{2,1,0:T(8,128)(2,1)S(1)}, u32[]{:S(2)}, u32[]{:S(2)}) collective-permute-start(bf16[3,192,128]{2,1,0:T(8,128)(2,1)S(1)} %get-tuple-element.76), channel_id=1, source_target_pairs={{0,1},{1,0},{2,3},{3,2},{4,5},{5,4},{6,7},{7,6},{8,9},{9,8},{10,11... | collective-permute-start | bytes 442376 | tf_op jit(solution)/shard_map/ppermute | solution.py:73
  24.2 1.8 %collective-permute-done.5.note = bf16[208,768]{1,0:T(8,128)(2,1)S(1)} collective-permute-done((bf16[208,768]{1,0:T(8,128)(2,1)S(1)}, bf16[208,768]{1,0:T(8,128)(2,1)S(1)}, u32[]{:S(2)}, u32[]{:S(2)}) %collective-permute-start.5) | collective-permute-done | bytes 319520 | tf_op jit(solution)/shard_map/ppermute | solution.py:593
  26.0 3.2 %shard_map.156 = (f32[192,640]{1,0:T(8,128)S(1)}, f32[1,640]{1,0:T(1,128)S(1)}, bf16[768,640]{1,0:T(8,128)(2,1)S(1)}, f32[192,64]{1,0:T(8,128)S(1)}, bf16[12,112...) custom-call(s32[16]{0:T(128)S(1)} %concatenate.3.meta, ...), custom_call_target="tpu_custom_call" | custom-call | flops 1000000000 | bytes 10000000 | tf_op jit(solution)/shard_map/pallas_call | solution.py:90
  30.1 4.7 %collective-permute-start.9 = (bf16[3,192,128]{2,1,0:T(8,128)(2,1)S(1)}, bf16[3,192,128]{2,1,0:T(8,128)(2,1)S(1)}, u32[]{:S(2)}, u32[]{:S(2)}) collective-permute-start(bf16[3,192,128]{2,1,0:T(8,128)(2,1)S(1)} %get-tuple-element.89), channel_id=1, source_target_pairs={{0,1},{1,0},{2,3},{3,2},{4,5},{5,4},{6,7},{7,6},{8,9},{9,8},{10,11... | collective-permute-start | bytes 442376 | tf_op jit(solution)/shard_map/ppermute | solution.py:73
  36.3 5.0 %collective-permute-start.10 = (bf16[5,192,128]{2,1,0:T(8,128)(2,1)S(1)}, bf16[5,192,128]{2,1,0:T(8,128)(2,1)S(1)}, u32[]{:S(2)}, u32[]{:S(2)}) collective-permute-start(bf16[5,192,128]{2,1,0:T(8,128)(2,1)S(1)} %shard_map.158), channel_id=1, source_target_pairs={{0,192},{192,0},{64,128},{128,64},{1,193},{193,1},{65,129},{129,65... | collective-permute-start | bytes 737288 | tf_op jit(solution)/shard_map/ppermute | solution.py:642
  41.3 3.6 %collective-permute-done.10.cot.turn_cot = bf16[5,192,128]{2,1,0:T(8,128)(2,1)S(1)} collective-permute-done((bf16[5,192,128]{2,1,0:T(8,128)(2,1)S(1)}, bf16[5,192,128]{2,1,0:T(8,128)(2,1)S(1)}, u32[]{:S(2)}, u32[]{:S(2)}) %collective-permute-start.10) | collective-permute-done | bytes 245792 | tf_op jit(solution)/shard_map/ppermute | solution.py:642
  44.9 1.5 %shard_map.159 = (bf16[5,192,128]{2,1,0:T(8,128)(2,1)S(1)}, bf16[3,192,128]{2,1,0:T(8,128)(2,1)S(1)}, bf16[3,192,128]{2,1,0:T(8,128)(2,1)S(1)}) custom-call(s32[16]{0:T(128)S(1)} %concatenate.3.meta, bf16[5,192,128]{2,1,0:T(8,128)(2,1)S(1)} %collective-permute-done.10.cot.turn_cot, f32[192,64]{1,0:T(8,128)S(1)} %get-tuple-element.80.cols, ...), custom_call_target="tpu_custom_call" | custom-call | tf_op jit(solution)/shard_map/pallas_call | solution.py:90
  46.9 6.5 %collective-permute-start.13 = (bf16[3,192,128]{2,1,0:T(8,128)(2,1)S(1)}, bf16[3,192,128]{2,1,0:T(8,128)(2,1)S(1)}, u32[]{:S(2)}, u32[]{:S(2)}) collective-permute-start(bf16[3,192,128]{2,1,0:T(8,128)(2,1)S(1)} %get-tuple-element.93), channel_id=1, source_target_pairs={{0,1},{1,0},{2,3},{3,2},{4,5},{5,4},{6,7},{7,6},{8,9},{9,8},{10,11... | collective-permute-start | bytes 442376 | tf_op jit(solution)/shard_map/ppermute | solution.py:73
  54.4 4.0 %shard_map.160 = (bf16[5,192,128]{2,1,0:T(8,128)(2,1)S(1)}, bf16[5,192,128]{2,1,0:T(8,128)(2,1)S(1)}, bf16[3,192,128]{2,1,0:T(8,128)(2,1)S(1)}, bf16[3,192,128]{...) custom-call(s32[16]{0:T(128)S(1)} %concatenate.3.meta, ...), custom_call_target="tpu_custom_call" | custom-call | tf_op jit(solution)/shard_map/pallas_call | solution.py:90
  58.5 4.7 %collective-permute-start.15 = (bf16[104,768]{1,0:T(8,128)(2,1)S(1)}, bf16[104,768]{1,0:T(8,128)(2,1)S(1)}, u32[]{:S(2)}, u32[]{:S(2)}) collective-permute-start(bf16[104,768]{1,0:T(8,128)(2,1)S(1)} %get-tuple-element.97), channel_id=1, source_target_pairs={{0,1},{1,0},{2,3},{3,2},{4,5},{5,4},{6,7},{7,6},{8,9},{9,8},{10,11... | collective-permute-start | bytes 479240 | tf_op jit(solution)/shard_map/ppermute | solution.py:69
  63.2 1.5 %collective-permute-start.16 = (bf16[104,768]{1,0:T(8,128)(2,1)S(1)}, bf16[104,768]{1,0:T(8,128)(2,1)S(1)}, u32[]{:S(2)}, u32[]{:S(2)}) collective-permute-start(bf16[104,768]{1,0:T(8,128)(2,1)S(1)} %get-tuple-element.98), channel_id=1, source_target_pairs={{0,9},{1,2},{2,11},{3,0},{4,13},{5,6},{6,15},{7,4},{8,1},{9,10},{1... | collective-permute-start | bytes 479240 | tf_op jit(solution)/shard_map/ppermute | solution.py:69
  64.7 3.5 %collective-permute-done.16 = bf16[104,768]{1,0:T(8,128)(2,1)S(1)} collective-permute-done((bf16[104,768]{1,0:T(8,128)(2,1)S(1)}, bf16[104,768]{1,0:T(8,128)(2,1)S(1)}, u32[]{:S(2)}, u32[]{:S(2)}) %collective-permute-start.16) | collective-permute-done | bytes 159776 | tf_op jit(solution)/shard_map/ppermute | solution.py:69
  68.4 1.6 %collective-permute-start.18 = (bf16[3,192,128]{2,1,0:T(8,128)(2,1)S(1)}, bf16[3,192,128]{2,1,0:T(8,128)(2,1)S(1)}, u32[]{:S(2)}, u32[]{:S(2)}) collective-permute-start(bf16[3,192,128]{2,1,0:T(8,128)(2,1)S(1)} %get-tuple-element.102), channel_id=1, source_target_pairs={{0,63},{1,2},{2,1},{3,4},{4,3},{5,6},{6,5},{7,8},{8,7},{9,10},{10,... | collective-permute-start | bytes 442376 | tf_op jit(solution)/shard_map/ppermute | solution.py:78
  70.0 6.2 %collective-permute-done.17 = bf16[104,768]{1,0:T(8,128)(2,1)S(1)} collective-permute-done((bf16[104,768]{1,0:T(8,128)(2,1)S(1)}, bf16[104,768]{1,0:T(8,128)(2,1)S(1)}, u32[]{:S(2)}, u32[]{:S(2)}) %collective-permute-start.17) | collective-permute-done | bytes 159776 | tf_op jit(solution)/shard_map/ppermute | solution.py:69
  76.7 1.5 %collective-permute-start.20 = (bf16[3,192,128]{2,1,0:T(8,128)(2,1)S(1)}, bf16[3,192,128]{2,1,0:T(8,128)(2,1)S(1)}, u32[]{:S(2)}, u32[]{:S(2)}) collective-permute-start(bf16[3,192,128]{2,1,0:T(8,128)(2,1)S(1)} %get-tuple-element.104), channel_id=1, source_target_pairs={{0,1},{1,0},{2,3},{3,2},{4,5},{5,4},{6,7},{7,6},{8,9},{9,8},{10,11... | collective-permute-start | bytes 442376 | tf_op jit(solution)/shard_map/ppermute | solution.py:73
  78.2 3.5 %collective-permute-done.19 = bf16[104,768]{1,0:T(8,128)(2,1)S(1)} collective-permute-done((bf16[104,768]{1,0:T(8,128)(2,1)S(1)}, bf16[104,768]{1,0:T(8,128)(2,1)S(1)}, u32[]{:S(2)}, u32[]{:S(2)}) %collective-permute-start.19) | collective-permute-done | bytes 159776 | tf_op jit(solution)/shard_map/ppermute | solution.py:69
  81.7 1.7 %collective-permute-start.21 = (bf16[104,768]{1,0:T(8,128)(2,1)S(1)}, bf16[104,768]{1,0:T(8,128)(2,1)S(1)}, u32[]{:S(2)}, u32[]{:S(2)}) collective-permute-start(bf16[104,768]{1,0:T(8,128)(2,1)S(1)} %add_convert_fusion.2), channel_id=1, source_target_pairs={{0,24},{1,3},{2,26},{3,1},{4,28},{5,7},{6,30},{7,5},{8,16},{9,11},... | collective-permute-start | bytes 479240 | tf_op jit(solution)/shard_map/ppermute | solution.py:69
  83.4 1.7 %shard_map.161 = (bf16[5,192,128]{2,1,0:T(8,128)(2,1)S(1)}, bf16[2,192,128]{2,1,0:T(8,128)(2,1)S(1)}) custom-call(s32[16]{0:T(128)S(1)} %concatenate.3.meta, bf16[5,192,128]{2,1,0:T(8,128)(2,1)S(1)} %get-tuple-element.106.field, bf16[3,192,128]{2,1,0:T(8,128)(2,1)S(1)} %collective-permute-done.20.inner, ...), custom_call_target="tpu_custom_call" | custom-call | tf_op jit(solution)/shard_map/pallas_call | solution.py:90
  86.1 4.2 %collective-permute-start.22 = (bf16[104,768]{1,0:T(8,128)(2,1)S(1)}, bf16[104,768]{1,0:T(8,128)(2,1)S(1)}, u32[]{:S(2)}, u32[]{:S(2)}) collective-permute-start(bf16[104,768]{1,0:T(8,128)(2,1)S(1)} %add_convert_fusion.1), channel_id=1, source_target_pairs={{0,56},{1,7},{2,58},{3,5},{4,60},{5,3},{6,62},{7,1},{8,48},{9,15},... | collective-permute-start | bytes 479240 | tf_op jit(solution)/shard_map/ppermute | solution.py:69
  90.3 2.7 %collective-permute-done.22 = bf16[104,768]{1,0:T(8,128)(2,1)S(1)} collective-permute-done((bf16[104,768]{1,0:T(8,128)(2,1)S(1)}, bf16[104,768]{1,0:T(8,128)(2,1)S(1)}, u32[]{:S(2)}, u32[]{:S(2)}) %collective-permute-start.22) | collective-permute-done | bytes 159776 | tf_op jit(solution)/shard_map/ppermute | solution.py:69
  93.0 4.6 %collective-permute-start.26 = (bf16[104,768]{1,0:T(8,128)(2,1)S(1)}, bf16[104,768]{1,0:T(8,128)(2,1)S(1)}, u32[]{:S(2)}, u32[]{:S(2)}) collective-permute-start(bf16[104,768]{1,0:T(8,128)(2,1)S(1)} %add_convert_fusion.keep), channel_id=1, source_target_pairs={{0,3},{1,8},{2,1},{3,10},{4,7},{5,12},{6,5},{7,14},{8,11},{9,0},{1... | collective-permute-start | bytes 479240 | tf_op jit(solution)/shard_map/ppermute | solution.py:69
  97.6 1.9 %collective-permute-start.25 = (bf16[104,768]{1,0:T(8,128)(2,1)S(1)}, bf16[104,768]{1,0:T(8,128)(2,1)S(1)}, u32[]{:S(2)}, u32[]{:S(2)}) collective-permute-start(bf16[104,768]{1,0:T(8,128)(2,1)S(1)} %add_convert_fusion.keep), channel_id=1, source_target_pairs={{0,1},{1,0},{2,3},{3,2},{4,5},{5,4},{6,7},{7,6},{8,9},{9,8},{10,11... | collective-permute-start | bytes 479240 | tf_op jit(solution)/shard_map/ppermute | solution.py:69
  99.6 1.4 %collective-permute-start.24 = (bf16[104,768]{1,0:T(8,128)(2,1)S(1)}, bf16[104,768]{1,0:T(8,128)(2,1)S(1)}, u32[]{:S(2)}, u32[]{:S(2)}) collective-permute-start(bf16[104,768]{1,0:T(8,128)(2,1)S(1)} %add_convert_fusion.keep), channel_id=1, source_target_pairs={{0,2},{1,9},{2,0},{3,11},{4,6},{5,13},{6,4},{7,15},{8,10},{9,1},{1... | collective-permute-start | bytes 479240 | tf_op jit(solution)/shard_map/ppermute | solution.py:69
  100.9 1.3 %shard_map.162 = bf16[3,192,128]{2,1,0:T(8,128)(2,1)} custom-call(s32[16]{0:T(128)S(1)} %concatenate.3.meta, bf16[5,192,128]{2,1,0:T(8,128)(2,1)S(1)} %get-tuple-element.112.result, bf16[2,192,128]{2,1,0:T(8,128)(2,1)S(1)} %collective-permute-done.23.arrived), custom_call_target="tpu_custom_call" | custom-call | tf_op jit(solution)/shard_map/pallas_call | solution.py:90
  102.3 3.0 %collective-permute-done.24.near = bf16[104,768]{1,0:T(8,128)(2,1)S(1)} collective-permute-done((bf16[104,768]{1,0:T(8,128)(2,1)S(1)}, bf16[104,768]{1,0:T(8,128)(2,1)S(1)}, u32[]{:S(2)}, u32[]{:S(2)}) %collective-permute-start.24) | collective-permute-done | bytes 159776 | tf_op jit(solution)/shard_map/ppermute | solution.py:69
  105.3 1.8 %shard_map.163 = (f32[49,1,192]{2,1,0:T(1,128)}, f32[1,192]{1,0:T(1,128)}, f32[1,192,768]{2,1,0:T(8,128)}, f32[1,768]{1,0:T(1,128)}, f32[1,192,768]{2,1,0:T(8,128)}, /*index=5*/f32[1,192]{1,0:T(1,128)}) custom-call(s32[16]{0:T(128)S(1)} %concatenate.3.meta, bf16[104,768]{1,0:T(8,128)(2,1)S(1)} %add_convert_fusion.keep, ...), custom_call_target="tpu_custom_call" | custom-call | tf_op jit(solution)/shard_map/pallas_call | solution.py:90
  (62 shorter events, 8.7 us)
Async XLA Ops:
  0.6 3.4 %copy-start.1 = (bf16[1,5,192,128]{3,2,1,0:T(8,128)(2,1)S(1)}, bf16[1,5,192,128]{3,2,1,0:T(8,128)(2,1)}, u32[]{:S(2)}) copy-start(bf16[1,5,192,128]{3,2,1,0:T(8,128)(2,1)} %param.10) | copy-start | bytes 737284
  1.8 16.5 %collective-permute-start = (bf16[192,768]{1,0:T(8,128)(2,1)S(1)}, bf16[192,768]{1,0:T(8,128)(2,1)S(1)}, u32[]{:S(2)}, u32[]{:S(2)}) collective-permute-start(bf16[192,768]{1,0:T(8,128)(2,1)S(1)} %broadcast_select_fusion), channel_id=1, source_target_pairs={{0,64},{64,0},{128,192},{192,128},{1,65},{65,1},{129,193},{193,129... | collective-permute-start | bytes 884744 | tf_op jit(solution)/shard_map/ppermute | solution.py:581
  4.0 8.3 %copy-start.7 = (f32[1,49,192]{2,0,1:T(1,128)S(1)}, f32[1,49,192]{2,0,1:T(1,128)}, u32[]{:S(2)}) copy-start(f32[1,49,192]{2,0,1:T(1,128)} %param.14) | copy-start | bytes 112900
  4.0 9.1 %copy-start.3 = (bf16[1,192,768]{2,1,0:T(8,128)(2,1)S(1)}, bf16[1,192,768]{2,1,0:T(8,128)(2,1)}, u32[]{:S(2)}) copy-start(bf16[1,192,768]{2,1,0:T(8,128)(2,1)} %param.18) | copy-start | bytes 884740
  4.0 9.1 %copy-start = (bf16[1,192,768]{2,1,0:T(8,128)(2,1)S(1)}, bf16[1,192,768]{2,1,0:T(8,128)(2,1)}, u32[]{:S(2)}) copy-start(bf16[1,192,768]{2,1,0:T(8,128)(2,1)} %param.16) | copy-start | bytes 884740
  4.0 10.4 %collective-permute-start.2 = (bf16[3,192,128]{2,1,0:T(8,128)(2,1)S(1)}, bf16[3,192,128]{2,1,0:T(8,128)(2,1)S(1)}, u32[]{:S(2)}, u32[]{:S(2)}) collective-permute-start(bf16[3,192,128]{2,1,0:T(8,128)(2,1)S(1)} %get-tuple-element.123), channel_id=1, source_target_pairs={{0,63},{1,2},{2,1},{3,4},{4,3},{5,6},{6,5},{7,8},{8,7},{9,10},{10,... | collective-permute-start | bytes 442376 | tf_op jit(solution)/shard_map/ppermute | solution.py:78
  6.2 8.3 %collective-permute-start.1 = (bf16[3,192,128]{2,1,0:T(8,128)(2,1)S(1)}, bf16[3,192,128]{2,1,0:T(8,128)(2,1)S(1)}, u32[]{:S(2)}, u32[]{:S(2)}) collective-permute-start(bf16[3,192,128]{2,1,0:T(8,128)(2,1)S(1)} %get-tuple-element.124), channel_id=1, source_target_pairs={{0,1},{1,0},{2,3},{3,2},{4,5},{5,4},{6,7},{7,6},{8,9},{9,8},{10,11... | collective-permute-start | bytes 442376 | tf_op jit(solution)/shard_map/ppermute | solution.py:73
  14.5 3.3 %copy-start.2 = (bf16[5,192,128]{2,1,0:T(8,128)(2,1)S(1)}, bf16[5,192,128]{2,1,0:T(8,128)(2,1)}, u32[]{:S(2)}) copy-start(bf16[5,192,128]{2,1,0:T(8,128)(2,1)} %cot_top.1) | copy-start | bytes 737284
  17.5 8.5 %collective-permute-start.5 = (bf16[208,768]{1,0:T(8,128)(2,1)S(1)}, bf16[208,768]{1,0:T(8,128)(2,1)S(1)}, u32[]{:S(2)}, u32[]{:S(2)}) collective-permute-start(bf16[208,768]{1,0:T(8,128)(2,1)S(1)} %get-tuple-element.78), channel_id=1, source_target_pairs={{0,64},{64,0},{128,192},{192,128},{1,65},{65,1},{129,193},{193,129... | collective-permute-start | bytes 958472 | tf_op jit(solution)/shard_map/ppermute | solution.py:593
  18.3 7.7 %collective-permute-start.6 = (bf16[192,768]{1,0:T(8,128)(2,1)S(1)}, bf16[192,768]{1,0:T(8,128)(2,1)S(1)}, u32[]{:S(2)}, u32[]{:S(2)}) collective-permute-start(bf16[192,768]{1,0:T(8,128)(2,1)S(1)} %collective-permute-done.half), channel_id=1, source_target_pairs={{0,1},{1,0},{2,3},{3,2},{4,5},{5,4},{6,7},{7,6},{8,9},{9,8},{10,11... | collective-permute-start | bytes 884744 | tf_op jit(solution)/shard_map/ppermute | solution.py:69
  19.4 9.9 %collective-permute-start.3 = (bf16[3,192,128]{2,1,0:T(8,128)(2,1)S(1)}, bf16[3,192,128]{2,1,0:T(8,128)(2,1)S(1)}, u32[]{:S(2)}, u32[]{:S(2)}) collective-permute-start(bf16[3,192,128]{2,1,0:T(8,128)(2,1)S(1)} %get-tuple-element.75), channel_id=1, source_target_pairs={{0,63},{1,2},{2,1},{3,4},{4,3},{5,6},{6,5},{7,8},{8,7},{9,10},{10,... | collective-permute-start | bytes 442376 | tf_op jit(solution)/shard_map/ppermute | solution.py:78
  19.4 9.9 %collective-permute-start.4 = (bf16[3,192,128]{2,1,0:T(8,128)(2,1)S(1)}, bf16[3,192,128]{2,1,0:T(8,128)(2,1)S(1)}, u32[]{:S(2)}, u32[]{:S(2)}) collective-permute-start(bf16[3,192,128]{2,1,0:T(8,128)(2,1)S(1)} %get-tuple-element.76), channel_id=1, source_target_pairs={{0,1},{1,0},{2,3},{3,2},{4,5},{5,4},{6,7},{7,6},{8,9},{9,8},{10,11... | collective-permute-start | bytes 442376 | tf_op jit(solution)/shard_map/ppermute | solution.py:73
  29.8 4.9 %collective-permute-start.8 = (bf16[3,192,128]{2,1,0:T(8,128)(2,1)S(1)}, bf16[3,192,128]{2,1,0:T(8,128)(2,1)S(1)}, u32[]{:S(2)}, u32[]{:S(2)}) collective-permute-start(bf16[3,192,128]{2,1,0:T(8,128)(2,1)S(1)} %get-tuple-element.88), channel_id=1, source_target_pairs={{0,63},{1,2},{2,1},{3,4},{4,3},{5,6},{6,5},{7,8},{8,7},{9,10},{10,... | collective-permute-start | bytes 442376 | tf_op jit(solution)/shard_map/ppermute | solution.py:78
  30.1 5.7 %collective-permute-start.9 = (bf16[3,192,128]{2,1,0:T(8,128)(2,1)S(1)}, bf16[3,192,128]{2,1,0:T(8,128)(2,1)S(1)}, u32[]{:S(2)}, u32[]{:S(2)}) collective-permute-start(bf16[3,192,128]{2,1,0:T(8,128)(2,1)S(1)} %get-tuple-element.89), channel_id=1, source_target_pairs={{0,1},{1,0},{2,3},{3,2},{4,5},{5,4},{6,7},{7,6},{8,9},{9,8},{10,11... | collective-permute-start | bytes 442376 | tf_op jit(solution)/shard_map/ppermute | solution.py:73
  36.3 8.6 %collective-permute-start.10 = (bf16[5,192,128]{2,1,0:T(8,128)(2,1)S(1)}, bf16[5,192,128]{2,1,0:T(8,128)(2,1)S(1)}, u32[]{:S(2)}, u32[]{:S(2)}) collective-permute-start(bf16[5,192,128]{2,1,0:T(8,128)(2,1)S(1)} %shard_map.158), channel_id=1, source_target_pairs={{0,192},{192,0},{64,128},{128,64},{1,193},{193,1},{65,129},{129,65... | collective-permute-start | bytes 737288 | tf_op jit(solution)/shard_map/ppermute | solution.py:642
  41.3 12.1 %collective-permute-start.7 = (bf16[5,192,128]{2,1,0:T(8,128)(2,1)S(1)}, bf16[5,192,128]{2,1,0:T(8,128)(2,1)S(1)}, u32[]{:S(2)}, u32[]{:S(2)}) collective-permute-start(bf16[5,192,128]{2,1,0:T(8,128)(2,1)S(1)} %get-tuple-element.86.cot), channel_id=1, source_target_pairs={{0,64},{64,0},{128,192},{192,128},{1,65},{65,1},{129,193},{193,129... | collective-permute-start | bytes 737288 | tf_op jit(solution)/shard_map/ppermute | solution.py:633
  44.9 9.5 %collective-permute-start.11 = (bf16[5,192,128]{2,1,0:T(8,128)(2,1)S(1)}, bf16[5,192,128]{2,1,0:T(8,128)(2,1)S(1)}, u32[]{:S(2)}, u32[]{:S(2)}) collective-permute-start(bf16[5,192,128]{2,1,0:T(8,128)(2,1)S(1)} %collective-permute-done.10.cot.turn_cot), channel_id=1, source_target_pairs={{0,64},{64,0},{128,192},{192,128},{1,65},{65,1},{129,193},{193,129... | collective-permute-start | bytes 737288 | tf_op jit(solution)/shard_map/ppermute | solution.py:643
  46.4 7.0 %collective-permute-start.12 = (bf16[3,192,128]{2,1,0:T(8,128)(2,1)S(1)}, bf16[3,192,128]{2,1,0:T(8,128)(2,1)S(1)}, u32[]{:S(2)}, u32[]{:S(2)}) collective-permute-start(bf16[3,192,128]{2,1,0:T(8,128)(2,1)S(1)} %get-tuple-element.92), channel_id=1, source_target_pairs={{0,63},{1,2},{2,1},{3,4},{4,3},{5,6},{6,5},{7,8},{8,7},{9,10},{10,... | collective-permute-start | bytes 442376 | tf_op jit(solution)/shard_map/ppermute | solution.py:78
  46.9 7.5 %collective-permute-start.13 = (bf16[3,192,128]{2,1,0:T(8,128)(2,1)S(1)}, bf16[3,192,128]{2,1,0:T(8,128)(2,1)S(1)}, u32[]{:S(2)}, u32[]{:S(2)}) collective-permute-start(bf16[3,192,128]{2,1,0:T(8,128)(2,1)S(1)} %get-tuple-element.93), channel_id=1, source_target_pairs={{0,1},{1,0},{2,3},{3,2},{4,5},{5,4},{6,7},{7,6},{8,9},{9,8},{10,11... | collective-permute-start | bytes 442376 | tf_op jit(solution)/shard_map/ppermute | solution.py:73
  58.4 6.3 %collective-permute-start.14 = (bf16[104,768]{1,0:T(8,128)(2,1)S(1)}, bf16[104,768]{1,0:T(8,128)(2,1)S(1)}, u32[]{:S(2)}, u32[]{:S(2)}) collective-permute-start(bf16[104,768]{1,0:T(8,128)(2,1)S(1)} %get-tuple-element.96), channel_id=1, source_target_pairs={{0,2},{1,9},{2,0},{3,11},{4,6},{5,13},{6,4},{7,15},{8,10},{9,1},{1... | collective-permute-start | bytes 479240 | tf_op jit(solution)/shard_map/ppermute | solution.py:69
  58.5 6.2 %collective-permute-start.15 = (bf16[104,768]{1,0:T(8,128)(2,1)S(1)}, bf16[104,768]{1,0:T(8,128)(2,1)S(1)}, u32[]{:S(2)}, u32[]{:S(2)}) collective-permute-start(bf16[104,768]{1,0:T(8,128)(2,1)S(1)} %get-tuple-element.97), channel_id=1, source_target_pairs={{0,1},{1,0},{2,3},{3,2},{4,5},{5,4},{6,7},{7,6},{8,9},{9,8},{10,11... | collective-permute-start | bytes 479240 | tf_op jit(solution)/shard_map/ppermute | solution.py:69
  63.2 5.0 %collective-permute-start.16 = (bf16[104,768]{1,0:T(8,128)(2,1)S(1)}, bf16[104,768]{1,0:T(8,128)(2,1)S(1)}, u32[]{:S(2)}, u32[]{:S(2)}) collective-permute-start(bf16[104,768]{1,0:T(8,128)(2,1)S(1)} %get-tuple-element.98), channel_id=1, source_target_pairs={{0,9},{1,2},{2,11},{3,0},{4,13},{5,6},{6,15},{7,4},{8,1},{9,10},{1... | collective-permute-start | bytes 479240 | tf_op jit(solution)/shard_map/ppermute | solution.py:69
  68.3 7.9 %collective-permute-start.17 = (bf16[104,768]{1,0:T(8,128)(2,1)S(1)}, bf16[104,768]{1,0:T(8,128)(2,1)S(1)}, u32[]{:S(2)}, u32[]{:S(2)}) collective-permute-start(bf16[104,768]{1,0:T(8,128)(2,1)S(1)} %add_convert_fusion.4), channel_id=1, source_target_pairs={{0,6},{1,25},{2,4},{3,27},{4,2},{5,29},{6,0},{7,31},{8,14},{9,17},... | collective-permute-start | bytes 479240 | tf_op jit(solution)/shard_map/ppermute | solution.py:69
  68.4 7.8 %collective-permute-start.18 = (bf16[3,192,128]{2,1,0:T(8,128)(2,1)S(1)}, bf16[3,192,128]{2,1,0:T(8,128)(2,1)S(1)}, u32[]{:S(2)}, u32[]{:S(2)}) collective-permute-start(bf16[3,192,128]{2,1,0:T(8,128)(2,1)S(1)} %get-tuple-element.102), channel_id=1, source_target_pairs={{0,63},{1,2},{2,1},{3,4},{4,3},{5,6},{6,5},{7,8},{8,7},{9,10},{10,... | collective-permute-start | bytes 442376 | tf_op jit(solution)/shard_map/ppermute | solution.py:78
  76.2 5.4 %collective-permute-start.19 = (bf16[104,768]{1,0:T(8,128)(2,1)S(1)}, bf16[104,768]{1,0:T(8,128)(2,1)S(1)}, u32[]{:S(2)}, u32[]{:S(2)}) collective-permute-start(bf16[104,768]{1,0:T(8,128)(2,1)S(1)} %add_convert_fusion.3), channel_id=1, source_target_pairs={{0,8},{1,57},{2,10},{3,59},{4,12},{5,61},{6,14},{7,63},{8,0},{9,49... | collective-permute-start | bytes 479240 | tf_op jit(solution)/shard_map/ppermute | solution.py:69
  76.7 5.0 %collective-permute-start.20 = (bf16[3,192,128]{2,1,0:T(8,128)(2,1)S(1)}, bf16[3,192,128]{2,1,0:T(8,128)(2,1)S(1)}, u32[]{:S(2)}, u32[]{:S(2)}) collective-permute-start(bf16[3,192,128]{2,1,0:T(8,128)(2,1)S(1)} %get-tuple-element.104), channel_id=1, source_target_pairs={{0,1},{1,0},{2,3},{3,2},{4,5},{5,4},{6,7},{7,6},{8,9},{9,8},{10,11... | collective-permute-start | bytes 442376 | tf_op jit(solution)/shard_map/ppermute | solution.py:73
  81.7 4.3 %collective-permute-start.21 = (bf16[104,768]{1,0:T(8,128)(2,1)S(1)}, bf16[104,768]{1,0:T(8,128)(2,1)S(1)}, u32[]{:S(2)}, u32[]{:S(2)}) collective-permute-start(bf16[104,768]{1,0:T(8,128)(2,1)S(1)} %add_convert_fusion.2), channel_id=1, source_target_pairs={{0,24},{1,3},{2,26},{3,1},{4,28},{5,7},{6,30},{7,5},{8,16},{9,11},... | collective-permute-start | bytes 479240 | tf_op jit(solution)/shard_map/ppermute | solution.py:69
  86.1 6.9 %collective-permute-start.22 = (bf16[104,768]{1,0:T(8,128)(2,1)S(1)}, bf16[104,768]{1,0:T(8,128)(2,1)S(1)}, u32[]{:S(2)}, u32[]{:S(2)}) collective-permute-start(bf16[104,768]{1,0:T(8,128)(2,1)S(1)} %add_convert_fusion.1), channel_id=1, source_target_pairs={{0,56},{1,7},{2,58},{3,5},{4,60},{5,3},{6,62},{7,1},{8,48},{9,15},... | collective-permute-start | bytes 479240 | tf_op jit(solution)/shard_map/ppermute | solution.py:69
  90.3 2.7 %collective-permute-start.23 = (bf16[2,192,128]{2,1,0:T(8,128)(2,1)S(1)}, bf16[2,192,128]{2,1,0:T(8,128)(2,1)S(1)}, u32[]{:S(2)}, u32[]{:S(2)}) collective-permute-start(bf16[2,192,128]{2,1,0:T(8,128)(2,1)S(1)} %get-tuple-element.114), channel_id=1, source_target_pairs={{0,1},{1,2},{2,3},{3,4},{4,5},{5,6},{6,7},{7,8},{8,9},{9,10},{10,1... | collective-permute-start | bytes 294920 | tf_op jit(solution)/shard_map/ppermute | solution.py:687
  93.0 9.2 %collective-permute-start.26 = (bf16[104,768]{1,0:T(8,128)(2,1)S(1)}, bf16[104,768]{1,0:T(8,128)(2,1)S(1)}, u32[]{:S(2)}, u32[]{:S(2)}) collective-permute-start(bf16[104,768]{1,0:T(8,128)(2,1)S(1)} %add_convert_fusion.keep), channel_id=1, source_target_pairs={{0,3},{1,8},{2,1},{3,10},{4,7},{5,12},{6,5},{7,14},{8,11},{9,0},{1... | collective-permute-start | bytes 479240 | tf_op jit(solution)/shard_map/ppermute | solution.py:69
  97.6 4.6 %collective-permute-start.25 = (bf16[104,768]{1,0:T(8,128)(2,1)S(1)}, bf16[104,768]{1,0:T(8,128)(2,1)S(1)}, u32[]{:S(2)}, u32[]{:S(2)}) collective-permute-start(bf16[104,768]{1,0:T(8,128)(2,1)S(1)} %add_convert_fusion.keep), channel_id=1, source_target_pairs={{0,1},{1,0},{2,3},{3,2},{4,5},{5,4},{6,7},{7,6},{8,9},{9,8},{10,11... | collective-permute-start | bytes 479240 | tf_op jit(solution)/shard_map/ppermute | solution.py:69
  99.6 5.7 %collective-permute-start.24 = (bf16[104,768]{1,0:T(8,128)(2,1)S(1)}, bf16[104,768]{1,0:T(8,128)(2,1)S(1)}, u32[]{:S(2)}, u32[]{:S(2)}) collective-permute-start(bf16[104,768]{1,0:T(8,128)(2,1)S(1)} %add_convert_fusion.keep), channel_id=1, source_target_pairs={{0,2},{1,9},{2,0},{3,11},{4,6},{5,13},{6,4},{7,15},{8,10},{9,1},{1... | collective-permute-start | bytes 479240 | tf_op jit(solution)/shard_map/ppermute | solution.py:69
  (5 other events, 3.5 us)

commit v9 on v8

--- a/solution.py
+++ b/solution.py
@@ -589,6 +589,7 @@
         1,
         (meta, source, acts_inner, acts_outer, forth, cols, up_t, bias, b_up),
         (padded, pltpu.VMEM((chans, cells), f32), pltpu.VMEM((chans, cells), bf16)),
+        cost=(3 * 10**9, 12 * 10**6),
     )
     note = lax.ppermute(own_note, "section", swaps)
 
@@ -605,6 +606,7 @@
             1,
             (meta, cot, field_cols, field_down_t, field_up, field_slope, field_nhat, field_inv),
             (outgrads, lowgrads),
+            cost=(10**9, 6 * 10**6),
         )
 
     top = SECTIONS - 1

time: 107 us -> 107 us (level)
  starting transfers between devices: 57.3 us -> 53.7 us
  waiting for transfers between devices: 27.1 us -> 29.6 us
  local copies, waits for them, and re-layouts: 1.44 us -> 2.53 us
    ppermute x5, starting transfers between devices: 23.6 us -> 18.8 us  [within(): lax.ppermute(value, 'tile', [(tile, tile ^ 1) for tile in range(TILES)])]
    ppermute x5, waiting for transfers between devices: 0.01 us -> 2.46 us  [across(): return lax.ppermute(value, 'tile', pairs)]
    ppermute x1, waiting for transfers between devices: 1.76 us -> 3.54 us  [body(): note = lax.ppermute(own_note, 'section', swaps)]
    ppermute x5, starting transfers between devices: 4.5 us -> 6.15 us  [across(): return lax.ppermute(value, 'tile', pairs)]
    select_n x1, other arithmetic: 1.13 us -> 0.03 us  [body(): half = lax.ppermute(jnp.where(odd, down, up), 'section', swaps)]
    unnamed x21, local copies, waits for them, and re-layouts: 1.36 us -> 2.45 us
  transfers between devices with their start and end apart: 27 -> 27, of which waited for: 10 -> 11; matrix products, arithmetic and copies ran while one was open for 0% -> 0% of each run, Pallas kernels for 11% -> 11%
where the time goes in v9:
time: 107 us
  starting transfers between devices  53.7 us (50%)
  waiting for transfers between devices  29.6 us (28%)
  Pallas kernels  18.9 us (18%)
  local copies, waits for them, and re-layouts  2.53 us (2%)
  other arithmetic  1.35 us (1%)
    ppermute x11, starting transfers between devices, moved(): return lax.ppermute(value, 'tile', pairs)  22.1 us
    pallas_call x11, Pallas kernels, call(): pl.pallas_call(body, out_shape=out_shape, in_specs=spec, out_specs=outs,...  18.9 us
    ppermute x5, starting transfers between devices, within(): lax.ppermute(value, 'tile', [(tile, tile ^ 1) for tile in range(TILES)])  18.8 us
    ppermute x11, waiting for transfers between devices, moved(): return lax.ppermute(value, 'tile', pairs)  18.7 us
    ppermute x5, starting transfers between devices, across(): return lax.ppermute(value, 'tile', pairs)  6.15 us
    ppermute x1, starting transfers between devices, body(): cot_1 = lax.ppermute(cot_1, 'section', [(0, top), (top, 0), (1, 2), (2, 1)])  4.97 us
    ppermute x1, waiting for transfers between devices, body(): cot_1 = lax.ppermute(cot_1, 'section', [(0, top), (top, 0), (1, 2), (2, 1)])  3.58 us
    ppermute x1, waiting for transfers between devices, body(): note = lax.ppermute(own_note, 'section', swaps)  3.54 us
  transfers between devices with their start and end apart: 27, of which 11 were waited for; matrix products, arithmetic and copies ran while one was open for 0% of the time, Pallas kernels for 11%

profile of v9, /device:TPU:1, one launch (start us, length us, event | category | flops | bytes accessed | tf_op | source)
XLA Modules:
  0.0 107.0 jit_solution(10111961449931717022)
XLA Ops:
  0.7 1.1 select_bitcast_fusion
  1.7 2.7 %collective-permute-start.2 = (bf16[3,192,128]{2,1,0:T(8,128)(2,1)S(1)}, bf16[3,192,128]{2,1,0:T(8,128)(2,1)S(1)}, u32[]{:S(2)}, u32[]{:S(2)}) collective-permute-start(bf16[3,192,128]{2,1,0:T(8,128)(2,1)S(1)} %get-tuple-element.123), channel_id=1, source_target_pairs={{0,63},{1,2},{2,1},{3,4},{4,3},{5,6},{6,5},{7,8},{8,7},{9,10},{10,... | collective-permute-start | bytes 442376 | tf_op jit(solution)/shard_map/ppermute | solution.py:78
  4.4 6.4 %collective-permute-start.1 = (bf16[3,192,128]{2,1,0:T(8,128)(2,1)S(1)}, bf16[3,192,128]{2,1,0:T(8,128)(2,1)S(1)}, u32[]{:S(2)}, u32[]{:S(2)}) collective-permute-start(bf16[3,192,128]{2,1,0:T(8,128)(2,1)S(1)} %get-tuple-element.124), channel_id=1, source_target_pairs={{0,1},{1,0},{2,3},{3,2},{4,5},{5,4},{6,7},{7,6},{8,9},{9,8},{10,11... | collective-permute-start | bytes 442376 | tf_op jit(solution)/shard_map/ppermute | solution.py:73
  10.9 1.4 %collective-permute-start = (bf16[192,768]{1,0:T(8,128)(2,1)S(1)}, bf16[192,768]{1,0:T(8,128)(2,1)S(1)}, u32[]{:S(2)}, u32[]{:S(2)}) collective-permute-start(bf16[192,768]{1,0:T(8,128)(2,1)S(1)} %broadcast_select_fusion), channel_id=1, source_target_pairs={{0,64},{64,0},{128,192},{192,128},{1,65},{65,1},{129,193},{193,129... | collective-permute-start | bytes 884744 | tf_op jit(solution)/shard_map/ppermute | solution.py:581
  15.5 3.0 %shard_map.154 = (f32[192,640]{1,0:T(8,128)S(1)}, f32[1,640]{1,0:T(1,128)S(1)}, bf16[768,640]{1,0:T(8,128)(2,1)S(1)}, bf16[768,640]{1,0:T(8,128)(2,1)S(1)}, bf16[208,768]{1,0:T(8,128)(2,1)S(1)}) custom-call(s32[16]{0:T(128)S(1)} %concatenate.3.meta, bf16[5,192,128]{2,1,0:T(8,128)(2,1)S(1)} %bitcast.22, ...), custom_call_target="tpu_custom_call" | custom-call | flops 3000000000 | bytes 12000000 | tf_op jit(solution)/shard_map/pallas_call | solution.py:90
  20.4 3.5 %collective-permute-start.4 = (bf16[3,192,128]{2,1,0:T(8,128)(2,1)S(1)}, bf16[3,192,128]{2,1,0:T(8,128)(2,1)S(1)}, u32[]{:S(2)}, u32[]{:S(2)}) collective-permute-start(bf16[3,192,128]{2,1,0:T(8,128)(2,1)S(1)} %get-tuple-element.76), channel_id=1, source_target_pairs={{0,1},{1,0},{2,3},{3,2},{4,5},{5,4},{6,7},{7,6},{8,9},{9,8},{10,11... | collective-permute-start | bytes 442376 | tf_op jit(solution)/shard_map/ppermute | solution.py:73
  23.9 3.5 %collective-permute-done.5.note = bf16[208,768]{1,0:T(8,128)(2,1)S(1)} collective-permute-done((bf16[208,768]{1,0:T(8,128)(2,1)S(1)}, bf16[208,768]{1,0:T(8,128)(2,1)S(1)}, u32[]{:S(2)}, u32[]{:S(2)}) %collective-permute-start.5) | collective-permute-done | bytes 319520 | tf_op jit(solution)/shard_map/ppermute | solution.py:594
  27.4 3.2 %shard_map.156 = (f32[192,640]{1,0:T(8,128)S(1)}, f32[1,640]{1,0:T(1,128)S(1)}, bf16[768,640]{1,0:T(8,128)(2,1)S(1)}, f32[192,64]{1,0:T(8,128)S(1)}, bf16[12,112...) custom-call(s32[16]{0:T(128)S(1)} %concatenate.3.meta, ...), custom_call_target="tpu_custom_call" | custom-call | flops 1000000000 | bytes 10000000 | tf_op jit(solution)/shard_map/pallas_call | solution.py:90
  31.5 2.1 %collective-permute-start.9 = (bf16[3,192,128]{2,1,0:T(8,128)(2,1)S(1)}, bf16[3,192,128]{2,1,0:T(8,128)(2,1)S(1)}, u32[]{:S(2)}, u32[]{:S(2)}) collective-permute-start(bf16[3,192,128]{2,1,0:T(8,128)(2,1)S(1)} %get-tuple-element.89), channel_id=1, source_target_pairs={{0,1},{1,0},{2,3},{3,2},{4,5},{5,4},{6,7},{7,6},{8,9},{9,8},{10,11... | collective-permute-start | bytes 442376 | tf_op jit(solution)/shard_map/ppermute | solution.py:73
  33.6 2.4 %collective-permute-done.8.outer = bf16[3,192,128]{2,1,0:T(8,128)(2,1)S(1)} collective-permute-done((bf16[3,192,128]{2,1,0:T(8,128)(2,1)S(1)}, bf16[3,192,128]{2,1,0:T(8,128)(2,1)S(1)}, u32[]{:S(2)}, u32[]{:S(2)}) %collective-permute-start.8) | collective-permute-done | bytes 147488 | tf_op jit(solution)/shard_map/ppermute | solution.py:78
  36.6 5.0 %collective-permute-start.10 = (bf16[5,192,128]{2,1,0:T(8,128)(2,1)S(1)}, bf16[5,192,128]{2,1,0:T(8,128)(2,1)S(1)}, u32[]{:S(2)}, u32[]{:S(2)}) collective-permute-start(bf16[5,192,128]{2,1,0:T(8,128)(2,1)S(1)} %shard_map.158), channel_id=1, source_target_pairs={{0,192},{192,0},{64,128},{128,64},{1,193},{193,1},{65,129},{129,65... | collective-permute-start | bytes 737288 | tf_op jit(solution)/shard_map/ppermute | solution.py:644
  41.6 3.6 %collective-permute-done.10.cot.turn_cot = bf16[5,192,128]{2,1,0:T(8,128)(2,1)S(1)} collective-permute-done((bf16[5,192,128]{2,1,0:T(8,128)(2,1)S(1)}, bf16[5,192,128]{2,1,0:T(8,128)(2,1)S(1)}, u32[]{:S(2)}, u32[]{:S(2)}) %collective-permute-start.10) | collective-permute-done | bytes 245792 | tf_op jit(solution)/shard_map/ppermute | solution.py:644
  45.2 1.5 %shard_map.159 = (bf16[5,192,128]{2,1,0:T(8,128)(2,1)S(1)}, bf16[3,192,128]{2,1,0:T(8,128)(2,1)S(1)}, bf16[3,192,128]{2,1,0:T(8,128)(2,1)S(1)}) custom-call(s32[16]{0:T(128)S(1)} %concatenate.3.meta, bf16[5,192,128]{2,1,0:T(8,128)(2,1)S(1)} %collective-permute-done.10.cot.turn_cot, f32[192,64]{1,0:T(8,128)S(1)} %get-tuple-element.80.cols, ...), custom_call_target="tpu_custom_call" | custom-call | flops 1000000000 | bytes 6000000 | tf_op jit(solution)/shard_map/pallas_call | solution.py:90
  46.7 1.6 %collective-permute-start.12 = (bf16[3,192,128]{2,1,0:T(8,128)(2,1)S(1)}, bf16[3,192,128]{2,1,0:T(8,128)(2,1)S(1)}, u32[]{:S(2)}, u32[]{:S(2)}) collective-permute-start(bf16[3,192,128]{2,1,0:T(8,128)(2,1)S(1)} %get-tuple-element.92), channel_id=1, source_target_pairs={{0,63},{1,2},{2,1},{3,4},{4,3},{5,6},{6,5},{7,8},{8,7},{9,10},{10,... | collective-permute-start | bytes 442376 | tf_op jit(solution)/shard_map/ppermute | solution.py:78
  48.3 4.4 %collective-permute-start.13 = (bf16[3,192,128]{2,1,0:T(8,128)(2,1)S(1)}, bf16[3,192,128]{2,1,0:T(8,128)(2,1)S(1)}, u32[]{:S(2)}, u32[]{:S(2)}) collective-permute-start(bf16[3,192,128]{2,1,0:T(8,128)(2,1)S(1)} %get-tuple-element.93), channel_id=1, source_target_pairs={{0,1},{1,0},{2,3},{3,2},{4,5},{5,4},{6,7},{7,6},{8,9},{9,8},{10,11... | collective-permute-start | bytes 442376 | tf_op jit(solution)/shard_map/ppermute | solution.py:73
  53.7 4.0 %shard_map.160 = (bf16[5,192,128]{2,1,0:T(8,128)(2,1)S(1)}, bf16[5,192,128]{2,1,0:T(8,128)(2,1)S(1)}, bf16[3,192,128]{2,1,0:T(8,128)(2,1)S(1)}, bf16[3,192,128]{...) custom-call(s32[16]{0:T(128)S(1)} %concatenate.3.meta, ...), custom_call_target="tpu_custom_call" | custom-call | tf_op jit(solution)/shard_map/pallas_call | solution.py:90
  57.9 6.3 %collective-permute-start.15 = (bf16[104,768]{1,0:T(8,128)(2,1)S(1)}, bf16[104,768]{1,0:T(8,128)(2,1)S(1)}, u32[]{:S(2)}, u32[]{:S(2)}) collective-permute-start(bf16[104,768]{1,0:T(8,128)(2,1)S(1)} %get-tuple-element.97), channel_id=1, source_target_pairs={{0,1},{1,0},{2,3},{3,2},{4,5},{5,4},{6,7},{7,6},{8,9},{9,8},{10,11... | collective-permute-start | bytes 479240 | tf_op jit(solution)/shard_map/ppermute | solution.py:69
  64.2 1.5 %collective-permute-start.16 = (bf16[104,768]{1,0:T(8,128)(2,1)S(1)}, bf16[104,768]{1,0:T(8,128)(2,1)S(1)}, u32[]{:S(2)}, u32[]{:S(2)}) collective-permute-start(bf16[104,768]{1,0:T(8,128)(2,1)S(1)} %get-tuple-element.98), channel_id=1, source_target_pairs={{0,9},{1,2},{2,11},{3,0},{4,13},{5,6},{6,15},{7,4},{8,1},{9,10},{1... | collective-permute-start | bytes 479240 | tf_op jit(solution)/shard_map/ppermute | solution.py:69
  65.7 3.5 %collective-permute-done.16 = bf16[104,768]{1,0:T(8,128)(2,1)S(1)} collective-permute-done((bf16[104,768]{1,0:T(8,128)(2,1)S(1)}, bf16[104,768]{1,0:T(8,128)(2,1)S(1)}, u32[]{:S(2)}, u32[]{:S(2)}) %collective-permute-start.16) | collective-permute-done | bytes 159776 | tf_op jit(solution)/shard_map/ppermute | solution.py:69
  69.4 1.6 %collective-permute-start.18 = (bf16[3,192,128]{2,1,0:T(8,128)(2,1)S(1)}, bf16[3,192,128]{2,1,0:T(8,128)(2,1)S(1)}, u32[]{:S(2)}, u32[]{:S(2)}) collective-permute-start(bf16[3,192,128]{2,1,0:T(8,128)(2,1)S(1)} %get-tuple-element.102), channel_id=1, source_target_pairs={{0,63},{1,2},{2,1},{3,4},{4,3},{5,6},{6,5},{7,8},{8,7},{9,10},{10,... | collective-permute-start | bytes 442376 | tf_op jit(solution)/shard_map/ppermute | solution.py:78
  71.0 5.7 %collective-permute-done.17 = bf16[104,768]{1,0:T(8,128)(2,1)S(1)} collective-permute-done((bf16[104,768]{1,0:T(8,128)(2,1)S(1)}, bf16[104,768]{1,0:T(8,128)(2,1)S(1)}, u32[]{:S(2)}, u32[]{:S(2)}) %collective-permute-start.17) | collective-permute-done | bytes 159776 | tf_op jit(solution)/shard_map/ppermute | solution.py:69
  76.8 2.3 %collective-permute-start.20 = (bf16[3,192,128]{2,1,0:T(8,128)(2,1)S(1)}, bf16[3,192,128]{2,1,0:T(8,128)(2,1)S(1)}, u32[]{:S(2)}, u32[]{:S(2)}) collective-permute-start(bf16[3,192,128]{2,1,0:T(8,128)(2,1)S(1)} %get-tuple-element.104), channel_id=1, source_target_pairs={{0,1},{1,0},{2,3},{3,2},{4,5},{5,4},{6,7},{7,6},{8,9},{9,8},{10,11... | collective-permute-start | bytes 442376 | tf_op jit(solution)/shard_map/ppermute | solution.py:73
  79.2 3.0 %collective-permute-done.19 = bf16[104,768]{1,0:T(8,128)(2,1)S(1)} collective-permute-done((bf16[104,768]{1,0:T(8,128)(2,1)S(1)}, bf16[104,768]{1,0:T(8,128)(2,1)S(1)}, u32[]{:S(2)}, u32[]{:S(2)}) %collective-permute-start.19) | collective-permute-done | bytes 159776 | tf_op jit(solution)/shard_map/ppermute | solution.py:69
  82.2 2.1 %collective-permute-start.21 = (bf16[104,768]{1,0:T(8,128)(2,1)S(1)}, bf16[104,768]{1,0:T(8,128)(2,1)S(1)}, u32[]{:S(2)}, u32[]{:S(2)}) collective-permute-start(bf16[104,768]{1,0:T(8,128)(2,1)S(1)} %add_convert_fusion.2), channel_id=1, source_target_pairs={{0,24},{1,3},{2,26},{3,1},{4,28},{5,7},{6,30},{7,5},{8,16},{9,11},... | collective-permute-start | bytes 479240 | tf_op jit(solution)/shard_map/ppermute | solution.py:69
  84.3 1.7 %shard_map.161 = (bf16[5,192,128]{2,1,0:T(8,128)(2,1)S(1)}, bf16[2,192,128]{2,1,0:T(8,128)(2,1)S(1)}) custom-call(s32[16]{0:T(128)S(1)} %concatenate.3.meta, bf16[5,192,128]{2,1,0:T(8,128)(2,1)S(1)} %get-tuple-element.106.field, bf16[3,192,128]{2,1,0:T(8,128)(2,1)S(1)} %collective-permute-done.20.inner, ...), custom_call_target="tpu_custom_call" | custom-call | tf_op jit(solution)/shard_map/pallas_call | solution.py:90
  87.0 4.7 %collective-permute-start.22 = (bf16[104,768]{1,0:T(8,128)(2,1)S(1)}, bf16[104,768]{1,0:T(8,128)(2,1)S(1)}, u32[]{:S(2)}, u32[]{:S(2)}) collective-permute-start(bf16[104,768]{1,0:T(8,128)(2,1)S(1)} %add_convert_fusion.1), channel_id=1, source_target_pairs={{0,56},{1,7},{2,58},{3,5},{4,60},{5,3},{6,62},{7,1},{8,48},{9,15},... | collective-permute-start | bytes 479240 | tf_op jit(solution)/shard_map/ppermute | solution.py:69
  91.8 2.7 %collective-permute-done.22 = bf16[104,768]{1,0:T(8,128)(2,1)S(1)} collective-permute-done((bf16[104,768]{1,0:T(8,128)(2,1)S(1)}, bf16[104,768]{1,0:T(8,128)(2,1)S(1)}, u32[]{:S(2)}, u32[]{:S(2)}) %collective-permute-start.22) | collective-permute-done | bytes 159776 | tf_op jit(solution)/shard_map/ppermute | solution.py:69
  94.5 4.9 %collective-permute-start.26 = (bf16[104,768]{1,0:T(8,128)(2,1)S(1)}, bf16[104,768]{1,0:T(8,128)(2,1)S(1)}, u32[]{:S(2)}, u32[]{:S(2)}) collective-permute-start(bf16[104,768]{1,0:T(8,128)(2,1)S(1)} %add_convert_fusion.keep), channel_id=1, source_target_pairs={{0,3},{1,8},{2,1},{3,10},{4,7},{5,12},{6,5},{7,14},{8,11},{9,0},{1... | collective-permute-start | bytes 479240 | tf_op jit(solution)/shard_map/ppermute | solution.py:69
  99.5 1.4 %collective-permute-start.24 = (bf16[104,768]{1,0:T(8,128)(2,1)S(1)}, bf16[104,768]{1,0:T(8,128)(2,1)S(1)}, u32[]{:S(2)}, u32[]{:S(2)}) collective-permute-start(bf16[104,768]{1,0:T(8,128)(2,1)S(1)} %add_convert_fusion.keep), channel_id=1, source_target_pairs={{0,2},{1,9},{2,0},{3,11},{4,6},{5,13},{6,4},{7,15},{8,10},{9,1},{1... | collective-permute-start | bytes 479240 | tf_op jit(solution)/shard_map/ppermute | solution.py:69
  100.8 1.3 %shard_map.162 = bf16[3,192,128]{2,1,0:T(8,128)(2,1)} custom-call(s32[16]{0:T(128)S(1)} %concatenate.3.meta, bf16[5,192,128]{2,1,0:T(8,128)(2,1)S(1)} %get-tuple-element.112.result, bf16[2,192,128]{2,1,0:T(8,128)(2,1)S(1)} %collective-permute-done.23.arrived), custom_call_target="tpu_custom_call" | custom-call | tf_op jit(solution)/shard_map/pallas_call | solution.py:90
  102.2 3.0 %collective-permute-done.24.near = bf16[104,768]{1,0:T(8,128)(2,1)S(1)} collective-permute-done((bf16[104,768]{1,0:T(8,128)(2,1)S(1)}, bf16[104,768]{1,0:T(8,128)(2,1)S(1)}, u32[]{:S(2)}, u32[]{:S(2)}) %collective-permute-start.24) | collective-permute-done | bytes 159776 | tf_op jit(solution)/shard_map/ppermute | solution.py:69
  105.2 1.8 %shard_map.163 = (f32[49,1,192]{2,1,0:T(1,128)}, f32[1,192]{1,0:T(1,128)}, f32[1,192,768]{2,1,0:T(8,128)}, f32[1,768]{1,0:T(1,128)}, f32[1,192,768]{2,1,0:T(8,128)}, /*index=5*/f32[1,192]{1,0:T(1,128)}) custom-call(s32[16]{0:T(128)S(1)} %concatenate.3.meta, bf16[104,768]{1,0:T(8,128)(2,1)S(1)} %add_convert_fusion.keep, ...), custom_call_target="tpu_custom_call" | custom-call | tf_op jit(solution)/shard_map/pallas_call | solution.py:90
  (62 shorter events, 9.1 us)
Async XLA Ops:
  0.6 10.2 %copy-start.1 = (bf16[1,192,768]{2,1,0:T(8,128)(2,1)S(1)}, bf16[1,192,768]{2,1,0:T(8,128)(2,1)}, u32[]{:S(2)}) copy-start(bf16[1,192,768]{2,1,0:T(8,128)(2,1)} %param.16) | copy-start | bytes 884740
  0.7 10.2 %copy-start.2 = (bf16[1,192,768]{2,1,0:T(8,128)(2,1)S(1)}, bf16[1,192,768]{2,1,0:T(8,128)(2,1)}, u32[]{:S(2)}) copy-start(bf16[1,192,768]{2,1,0:T(8,128)(2,1)} %param.18) | copy-start | bytes 884740
  1.7 13.4 %collective-permute-start.2 = (bf16[3,192,128]{2,1,0:T(8,128)(2,1)S(1)}, bf16[3,192,128]{2,1,0:T(8,128)(2,1)S(1)}, u32[]{:S(2)}, u32[]{:S(2)}) collective-permute-start(bf16[3,192,128]{2,1,0:T(8,128)(2,1)S(1)} %get-tuple-element.123), channel_id=1, source_target_pairs={{0,63},{1,2},{2,1},{3,4},{4,3},{5,6},{6,5},{7,8},{8,7},{9,10},{10,... | collective-permute-start | bytes 442376 | tf_op jit(solution)/shard_map/ppermute | solution.py:78
  4.4 10.8 %collective-permute-start.1 = (bf16[3,192,128]{2,1,0:T(8,128)(2,1)S(1)}, bf16[3,192,128]{2,1,0:T(8,128)(2,1)S(1)}, u32[]{:S(2)}, u32[]{:S(2)}) collective-permute-start(bf16[3,192,128]{2,1,0:T(8,128)(2,1)S(1)} %get-tuple-element.124), channel_id=1, source_target_pairs={{0,1},{1,0},{2,3},{3,2},{4,5},{5,4},{6,7},{7,6},{8,9},{9,8},{10,11... | collective-permute-start | bytes 442376 | tf_op jit(solution)/shard_map/ppermute | solution.py:73
  10.9 8.7 %collective-permute-start = (bf16[192,768]{1,0:T(8,128)(2,1)S(1)}, bf16[192,768]{1,0:T(8,128)(2,1)S(1)}, u32[]{:S(2)}, u32[]{:S(2)}) collective-permute-start(bf16[192,768]{1,0:T(8,128)(2,1)S(1)} %broadcast_select_fusion), channel_id=1, source_target_pairs={{0,64},{64,0},{128,192},{192,128},{1,65},{65,1},{129,193},{193,129... | collective-permute-start | bytes 884744 | tf_op jit(solution)/shard_map/ppermute | solution.py:581
  12.2 0.8 copy-start.7
  14.5 0.9 copy-start
  15.5 3.3 %copy-start.3 = (bf16[5,192,128]{2,1,0:T(8,128)(2,1)S(1)}, bf16[5,192,128]{2,1,0:T(8,128)(2,1)}, u32[]{:S(2)}) copy-start(bf16[5,192,128]{2,1,0:T(8,128)(2,1)} %cot_top.1) | copy-start | bytes 737284
  18.5 8.9 %collective-permute-start.5 = (bf16[208,768]{1,0:T(8,128)(2,1)S(1)}, bf16[208,768]{1,0:T(8,128)(2,1)S(1)}, u32[]{:S(2)}, u32[]{:S(2)}) collective-permute-start(bf16[208,768]{1,0:T(8,128)(2,1)S(1)} %get-tuple-element.78), channel_id=1, source_target_pairs={{0,64},{64,0},{128,192},{192,128},{1,65},{65,1},{129,193},{193,129... | collective-permute-start | bytes 958472 | tf_op jit(solution)/shard_map/ppermute | solution.py:594
  19.6 7.8 %collective-permute-start.6 = (bf16[192,768]{1,0:T(8,128)(2,1)S(1)}, bf16[192,768]{1,0:T(8,128)(2,1)S(1)}, u32[]{:S(2)}, u32[]{:S(2)}) collective-permute-start(bf16[192,768]{1,0:T(8,128)(2,1)S(1)} %collective-permute-done.half), channel_id=1, source_target_pairs={{0,1},{1,0},{2,3},{3,2},{4,5},{5,4},{6,7},{7,6},{8,9},{9,8},{10,11... | collective-permute-start | bytes 884744 | tf_op jit(solution)/shard_map/ppermute | solution.py:69
  20.4 10.3 %collective-permute-start.3 = (bf16[3,192,128]{2,1,0:T(8,128)(2,1)S(1)}, bf16[3,192,128]{2,1,0:T(8,128)(2,1)S(1)}, u32[]{:S(2)}, u32[]{:S(2)}) collective-permute-start(bf16[3,192,128]{2,1,0:T(8,128)(2,1)S(1)} %get-tuple-element.75), channel_id=1, source_target_pairs={{0,63},{1,2},{2,1},{3,4},{4,3},{5,6},{6,5},{7,8},{8,7},{9,10},{10,... | collective-permute-start | bytes 442376 | tf_op jit(solution)/shard_map/ppermute | solution.py:78
  20.4 10.3 %collective-permute-start.4 = (bf16[3,192,128]{2,1,0:T(8,128)(2,1)S(1)}, bf16[3,192,128]{2,1,0:T(8,128)(2,1)S(1)}, u32[]{:S(2)}, u32[]{:S(2)}) collective-permute-start(bf16[3,192,128]{2,1,0:T(8,128)(2,1)S(1)} %get-tuple-element.76), channel_id=1, source_target_pairs={{0,1},{1,0},{2,3},{3,2},{4,5},{5,4},{6,7},{7,6},{8,9},{9,8},{10,11... | collective-permute-start | bytes 442376 | tf_op jit(solution)/shard_map/ppermute | solution.py:73
  31.2 4.8 %collective-permute-start.8 = (bf16[3,192,128]{2,1,0:T(8,128)(2,1)S(1)}, bf16[3,192,128]{2,1,0:T(8,128)(2,1)S(1)}, u32[]{:S(2)}, u32[]{:S(2)}) collective-permute-start(bf16[3,192,128]{2,1,0:T(8,128)(2,1)S(1)} %get-tuple-element.88), channel_id=1, source_target_pairs={{0,63},{1,2},{2,1},{3,4},{4,3},{5,6},{6,5},{7,8},{8,7},{9,10},{10,... | collective-permute-start | bytes 442376 | tf_op jit(solution)/shard_map/ppermute | solution.py:78
  31.5 4.6 %collective-permute-start.9 = (bf16[3,192,128]{2,1,0:T(8,128)(2,1)S(1)}, bf16[3,192,128]{2,1,0:T(8,128)(2,1)S(1)}, u32[]{:S(2)}, u32[]{:S(2)}) collective-permute-start(bf16[3,192,128]{2,1,0:T(8,128)(2,1)S(1)} %get-tuple-element.89), channel_id=1, source_target_pairs={{0,1},{1,0},{2,3},{3,2},{4,5},{5,4},{6,7},{7,6},{8,9},{9,8},{10,11... | collective-permute-start | bytes 442376 | tf_op jit(solution)/shard_map/ppermute | solution.py:73
  36.6 8.6 %collective-permute-start.10 = (bf16[5,192,128]{2,1,0:T(8,128)(2,1)S(1)}, bf16[5,192,128]{2,1,0:T(8,128)(2,1)S(1)}, u32[]{:S(2)}, u32[]{:S(2)}) collective-permute-start(bf16[5,192,128]{2,1,0:T(8,128)(2,1)S(1)} %shard_map.158), channel_id=1, source_target_pairs={{0,192},{192,0},{64,128},{128,64},{1,193},{193,1},{65,129},{129,65... | collective-permute-start | bytes 737288 | tf_op jit(solution)/shard_map/ppermute | solution.py:644
  41.6 11.1 %collective-permute-start.7 = (bf16[5,192,128]{2,1,0:T(8,128)(2,1)S(1)}, bf16[5,192,128]{2,1,0:T(8,128)(2,1)S(1)}, u32[]{:S(2)}, u32[]{:S(2)}) collective-permute-start(bf16[5,192,128]{2,1,0:T(8,128)(2,1)S(1)} %get-tuple-element.86.cot), channel_id=1, source_target_pairs={{0,64},{64,0},{128,192},{192,128},{1,65},{65,1},{129,193},{193,129... | collective-permute-start | bytes 737288 | tf_op jit(solution)/shard_map/ppermute | solution.py:635
  45.2 8.5 %collective-permute-start.11 = (bf16[5,192,128]{2,1,0:T(8,128)(2,1)S(1)}, bf16[5,192,128]{2,1,0:T(8,128)(2,1)S(1)}, u32[]{:S(2)}, u32[]{:S(2)}) collective-permute-start(bf16[5,192,128]{2,1,0:T(8,128)(2,1)S(1)} %collective-permute-done.10.cot.turn_cot), channel_id=1, source_target_pairs={{0,64},{64,0},{128,192},{192,128},{1,65},{65,1},{129,193},{193,129... | collective-permute-start | bytes 737288 | tf_op jit(solution)/shard_map/ppermute | solution.py:645
  46.7 6.0 %collective-permute-start.12 = (bf16[3,192,128]{2,1,0:T(8,128)(2,1)S(1)}, bf16[3,192,128]{2,1,0:T(8,128)(2,1)S(1)}, u32[]{:S(2)}, u32[]{:S(2)}) collective-permute-start(bf16[3,192,128]{2,1,0:T(8,128)(2,1)S(1)} %get-tuple-element.92), channel_id=1, source_target_pairs={{0,63},{1,2},{2,1},{3,4},{4,3},{5,6},{6,5},{7,8},{8,7},{9,10},{10,... | collective-permute-start | bytes 442376 | tf_op jit(solution)/shard_map/ppermute | solution.py:78
  48.3 5.4 %collective-permute-start.13 = (bf16[3,192,128]{2,1,0:T(8,128)(2,1)S(1)}, bf16[3,192,128]{2,1,0:T(8,128)(2,1)S(1)}, u32[]{:S(2)}, u32[]{:S(2)}) collective-permute-start(bf16[3,192,128]{2,1,0:T(8,128)(2,1)S(1)} %get-tuple-element.93), channel_id=1, source_target_pairs={{0,1},{1,0},{2,3},{3,2},{4,5},{5,4},{6,7},{7,6},{8,9},{9,8},{10,11... | collective-permute-start | bytes 442376 | tf_op jit(solution)/shard_map/ppermute | solution.py:73
  57.8 8.0 %collective-permute-start.14 = (bf16[104,768]{1,0:T(8,128)(2,1)S(1)}, bf16[104,768]{1,0:T(8,128)(2,1)S(1)}, u32[]{:S(2)}, u32[]{:S(2)}) collective-permute-start(bf16[104,768]{1,0:T(8,128)(2,1)S(1)} %get-tuple-element.96), channel_id=1, source_target_pairs={{0,2},{1,9},{2,0},{3,11},{4,6},{5,13},{6,4},{7,15},{8,10},{9,1},{1... | collective-permute-start | bytes 479240 | tf_op jit(solution)/shard_map/ppermute | solution.py:69
  57.9 7.9 %collective-permute-start.15 = (bf16[104,768]{1,0:T(8,128)(2,1)S(1)}, bf16[104,768]{1,0:T(8,128)(2,1)S(1)}, u32[]{:S(2)}, u32[]{:S(2)}) collective-permute-start(bf16[104,768]{1,0:T(8,128)(2,1)S(1)} %get-tuple-element.97), channel_id=1, source_target_pairs={{0,1},{1,0},{2,3},{3,2},{4,5},{5,4},{6,7},{7,6},{8,9},{9,8},{10,11... | collective-permute-start | bytes 479240 | tf_op jit(solution)/shard_map/ppermute | solution.py:69
  64.2 5.0 %collective-permute-start.16 = (bf16[104,768]{1,0:T(8,128)(2,1)S(1)}, bf16[104,768]{1,0:T(8,128)(2,1)S(1)}, u32[]{:S(2)}, u32[]{:S(2)}) collective-permute-start(bf16[104,768]{1,0:T(8,128)(2,1)S(1)} %get-tuple-element.98), channel_id=1, source_target_pairs={{0,9},{1,2},{2,11},{3,0},{4,13},{5,6},{6,15},{7,4},{8,1},{9,10},{1... | collective-permute-start | bytes 479240 | tf_op jit(solution)/shard_map/ppermute | solution.py:69
  69.3 7.4 %collective-permute-start.17 = (bf16[104,768]{1,0:T(8,128)(2,1)S(1)}, bf16[104,768]{1,0:T(8,128)(2,1)S(1)}, u32[]{:S(2)}, u32[]{:S(2)}) collective-permute-start(bf16[104,768]{1,0:T(8,128)(2,1)S(1)} %add_convert_fusion.4), channel_id=1, source_target_pairs={{0,6},{1,25},{2,4},{3,27},{4,2},{5,29},{6,0},{7,31},{8,14},{9,17},... | collective-permute-start | bytes 479240 | tf_op jit(solution)/shard_map/ppermute | solution.py:69
  69.4 7.3 %collective-permute-start.18 = (bf16[3,192,128]{2,1,0:T(8,128)(2,1)S(1)}, bf16[3,192,128]{2,1,0:T(8,128)(2,1)S(1)}, u32[]{:S(2)}, u32[]{:S(2)}) collective-permute-start(bf16[3,192,128]{2,1,0:T(8,128)(2,1)S(1)} %get-tuple-element.102), channel_id=1, source_target_pairs={{0,63},{1,2},{2,1},{3,4},{4,3},{5,6},{6,5},{7,8},{8,7},{9,10},{10,... | collective-permute-start | bytes 442376 | tf_op jit(solution)/shard_map/ppermute | solution.py:78
  76.7 5.4 %collective-permute-start.19 = (bf16[104,768]{1,0:T(8,128)(2,1)S(1)}, bf16[104,768]{1,0:T(8,128)(2,1)S(1)}, u32[]{:S(2)}, u32[]{:S(2)}) collective-permute-start(bf16[104,768]{1,0:T(8,128)(2,1)S(1)} %add_convert_fusion.3), channel_id=1, source_target_pairs={{0,8},{1,57},{2,10},{3,59},{4,12},{5,61},{6,14},{7,63},{8,0},{9,49... | collective-permute-start | bytes 479240 | tf_op jit(solution)/shard_map/ppermute | solution.py:69
  76.8 5.4 %collective-permute-start.20 = (bf16[3,192,128]{2,1,0:T(8,128)(2,1)S(1)}, bf16[3,192,128]{2,1,0:T(8,128)(2,1)S(1)}, u32[]{:S(2)}, u32[]{:S(2)}) collective-permute-start(bf16[3,192,128]{2,1,0:T(8,128)(2,1)S(1)} %get-tuple-element.104), channel_id=1, source_target_pairs={{0,1},{1,0},{2,3},{3,2},{4,5},{5,4},{6,7},{7,6},{8,9},{9,8},{10,11... | collective-permute-start | bytes 442376 | tf_op jit(solution)/shard_map/ppermute | solution.py:73
  82.2 4.8 %collective-permute-start.21 = (bf16[104,768]{1,0:T(8,128)(2,1)S(1)}, bf16[104,768]{1,0:T(8,128)(2,1)S(1)}, u32[]{:S(2)}, u32[]{:S(2)}) collective-permute-start(bf16[104,768]{1,0:T(8,128)(2,1)S(1)} %add_convert_fusion.2), channel_id=1, source_target_pairs={{0,24},{1,3},{2,26},{3,1},{4,28},{5,7},{6,30},{7,5},{8,16},{9,11},... | collective-permute-start | bytes 479240 | tf_op jit(solution)/shard_map/ppermute | solution.py:69
  87.0 7.4 %collective-permute-start.22 = (bf16[104,768]{1,0:T(8,128)(2,1)S(1)}, bf16[104,768]{1,0:T(8,128)(2,1)S(1)}, u32[]{:S(2)}, u32[]{:S(2)}) collective-permute-start(bf16[104,768]{1,0:T(8,128)(2,1)S(1)} %add_convert_fusion.1), channel_id=1, source_target_pairs={{0,56},{1,7},{2,58},{3,5},{4,60},{5,3},{6,62},{7,1},{8,48},{9,15},... | collective-permute-start | bytes 479240 | tf_op jit(solution)/shard_map/ppermute | solution.py:69
  91.8 2.7 %collective-permute-start.23 = (bf16[2,192,128]{2,1,0:T(8,128)(2,1)S(1)}, bf16[2,192,128]{2,1,0:T(8,128)(2,1)S(1)}, u32[]{:S(2)}, u32[]{:S(2)}) collective-permute-start(bf16[2,192,128]{2,1,0:T(8,128)(2,1)S(1)} %get-tuple-element.114), channel_id=1, source_target_pairs={{0,1},{1,2},{2,3},{3,4},{4,5},{5,6},{6,7},{7,8},{8,9},{9,10},{10,1... | collective-permute-start | bytes 294920 | tf_op jit(solution)/shard_map/ppermute | solution.py:689
  94.5 7.7 %collective-permute-start.26 = (bf16[104,768]{1,0:T(8,128)(2,1)S(1)}, bf16[104,768]{1,0:T(8,128)(2,1)S(1)}, u32[]{:S(2)}, u32[]{:S(2)}) collective-permute-start(bf16[104,768]{1,0:T(8,128)(2,1)S(1)} %add_convert_fusion.keep), channel_id=1, source_target_pairs={{0,3},{1,8},{2,1},{3,10},{4,7},{5,12},{6,5},{7,14},{8,11},{9,0},{1... | collective-permute-start | bytes 479240 | tf_op jit(solution)/shard_map/ppermute | solution.py:69
  99.3 2.8 %collective-permute-start.25 = (bf16[104,768]{1,0:T(8,128)(2,1)S(1)}, bf16[104,768]{1,0:T(8,128)(2,1)S(1)}, u32[]{:S(2)}, u32[]{:S(2)}) collective-permute-start(bf16[104,768]{1,0:T(8,128)(2,1)S(1)} %add_convert_fusion.keep), channel_id=1, source_target_pairs={{0,1},{1,0},{2,3},{3,2},{4,5},{5,4},{6,7},{7,6},{8,9},{9,8},{10,11... | collective-permute-start | bytes 479240 | tf_op jit(solution)/shard_map/ppermute | solution.py:69
  99.5 5.7 %collective-permute-start.24 = (bf16[104,768]{1,0:T(8,128)(2,1)S(1)}, bf16[104,768]{1,0:T(8,128)(2,1)S(1)}, u32[]{:S(2)}, u32[]{:S(2)}) collective-permute-start(bf16[104,768]{1,0:T(8,128)(2,1)S(1)} %add_convert_fusion.keep), channel_id=1, source_target_pairs={{0,2},{1,9},{2,0},{3,11},{4,6},{5,13},{6,4},{7,15},{8,10},{9,1},{1... | collective-permute-start | bytes 479240 | tf_op jit(solution)/shard_map/ppermute | solution.py:69
  (5 other events, 3.5 us)

commit v10 on v9

--- a/solution.py
+++ b/solution.py
@@ -687,7 +687,6 @@
     total, result, sent = lax.optimization_barrier((total, result, sent))
     total = added(total, moved(total, orders[3], False))
     arrived = lax.ppermute(sent, "tile", [(tile, (tile + 1) % TILES) for tile in range(TILES)])
-    total, arrived = lax.optimization_barrier((total, arrived))
     slotted = call(
         slots_kernel,
         shape((owners.shape[0], chans, width), bf16),

time: 107 us -> 108 us (level); the launches traced: 107 us -> 106 us
    ppermute x11, waiting for transfers between devices: 18.7 us -> 15.9 us  [moved(): return lax.ppermute(value, 'tile', pairs)]
    ppermute x1, waiting for transfers between devices: 0.01 us -> 2.68 us  [body(): lax.ppermute(sent, 'tile', [(tile, (tile + 1) % TILES) for tile in range(...]
  transfers between devices with their start and end apart: 27 -> 27, of which waited for: 11 -> 12; matrix products, arithmetic and copies ran while one was open for 0% -> 0% of each run, Pallas kernels for 11% -> 11%
where the time goes in v10:
time: 108 us; the launch traced here: 106 us
  starting transfers between devices  53.3 us (49%)
  waiting for transfers between devices  29.4 us (27%)
  Pallas kernels  18.9 us (17%)
  local copies, waits for them, and re-layouts  2.53 us (2%)
  other arithmetic  1.35 us (1%)
    ppermute x11, starting transfers between devices, moved(): return lax.ppermute(value, 'tile', pairs)  21.3 us
    pallas_call x11, Pallas kernels, call(): pl.pallas_call(body, out_shape=out_shape, in_specs=spec, out_specs=outs,...  18.9 us
    ppermute x5, starting transfers between devices, within(): lax.ppermute(value, 'tile', [(tile, tile ^ 1) for tile in range(TILES)])  18.8 us
    ppermute x11, waiting for transfers between devices, moved(): return lax.ppermute(value, 'tile', pairs)  15.9 us
    ppermute x5, starting transfers between devices, across(): return lax.ppermute(value, 'tile', pairs)  6.15 us
    ppermute x1, starting transfers between devices, body(): cot_1 = lax.ppermute(cot_1, 'section', [(0, top), (top, 0), (1, 2), (2, 1)])  4.97 us
    ppermute x1, waiting for transfers between devices, body(): cot_1 = lax.ppermute(cot_1, 'section', [(0, top), (top, 0), (1, 2), (2, 1)])  3.58 us
    ppermute x1, waiting for transfers between devices, body(): note = lax.ppermute(own_note, 'section', swaps)  3.54 us
  transfers between devices with their start and end apart: 27, of which 12 were waited for; matrix products, arithmetic and copies ran while one was open for 0% of the time, Pallas kernels for 11%

profile of v10, /device:TPU:1, one launch (start us, length us, event | category | flops | bytes accessed | tf_op | source)
XLA Modules:
  0.0 106.4 jit_solution(9327407662682876590)
XLA Ops:
  0.7 1.1 %select_bitcast_fusion = (bf16[3,192,128]{2,1,0:T(8,128)(2,1)S(1)}, bf16[3,192,128]{2,1,0:T(8,128)(2,1)S(1)}) fusion(pred[]{:T(512)S(6)} %eq.21, bf16[1,5,192,128]{3,2,1,0:T(8,128)(2,1)} %param.10), kind=kLoop, calls=%fused_computation.6 | loop fusion | flops 147456 | bytes 589825 | tf_op jit(solution)/shard_map/jit(_where)/select_n | solution.py:567
  1.7 2.7 %collective-permute-start.2 = (bf16[3,192,128]{2,1,0:T(8,128)(2,1)S(1)}, bf16[3,192,128]{2,1,0:T(8,128)(2,1)S(1)}, u32[]{:S(2)}, u32[]{:S(2)}) collective-permute-start(bf16[3,192,128]{2,1,0:T(8,128)(2,1)S(1)} %get-tuple-element.119), channel_id=1, source_target_pairs={{0,63},{1,2},{2,1},{3,4},{4,3},{5,6},{6,5},{7,8},{8,7},{9,10},{10,... | collective-permute-start | bytes 442376 | tf_op jit(solution)/shard_map/ppermute | solution.py:78
  4.4 6.4 %collective-permute-start.1 = (bf16[3,192,128]{2,1,0:T(8,128)(2,1)S(1)}, bf16[3,192,128]{2,1,0:T(8,128)(2,1)S(1)}, u32[]{:S(2)}, u32[]{:S(2)}) collective-permute-start(bf16[3,192,128]{2,1,0:T(8,128)(2,1)S(1)} %get-tuple-element.120), channel_id=1, source_target_pairs={{0,1},{1,0},{2,3},{3,2},{4,5},{5,4},{6,7},{7,6},{8,9},{9,8},{10,11... | collective-permute-start | bytes 442376 | tf_op jit(solution)/shard_map/ppermute | solution.py:73
  10.9 1.4 %collective-permute-start = (bf16[192,768]{1,0:T(8,128)(2,1)S(1)}, bf16[192,768]{1,0:T(8,128)(2,1)S(1)}, u32[]{:S(2)}, u32[]{:S(2)}) collective-permute-start(bf16[192,768]{1,0:T(8,128)(2,1)S(1)} %broadcast_select_fusion), channel_id=1, source_target_pairs={{0,64},{64,0},{128,192},{192,128},{1,65},{65,1},{129,193},{193,129... | collective-permute-start | bytes 884744 | tf_op jit(solution)/shard_map/ppermute | solution.py:581
  15.5 3.0 %shard_map.154 = (f32[192,640]{1,0:T(8,128)S(1)}, f32[1,640]{1,0:T(1,128)S(1)}, bf16[768,640]{1,0:T(8,128)(2,1)S(1)}, bf16[768,640]{1,0:T(8,128)(2,1)S(1)}, bf16[208,768]{1,0:T(8,128)(2,1)S(1)}) custom-call(s32[16]{0:T(128)S(1)} %concatenate.3.meta, bf16[5,192,128]{2,1,0:T(8,128)(2,1)S(1)} %bitcast.22, ...), custom_call_target="tpu_custom_call" | custom-call | flops 3000000000 | bytes 12000000 | tf_op jit(solution)/shard_map/pallas_call | solution.py:90
  20.4 3.5 %collective-permute-start.4 = (bf16[3,192,128]{2,1,0:T(8,128)(2,1)S(1)}, bf16[3,192,128]{2,1,0:T(8,128)(2,1)S(1)}, u32[]{:S(2)}, u32[]{:S(2)}) collective-permute-start(bf16[3,192,128]{2,1,0:T(8,128)(2,1)S(1)} %get-tuple-element.74), channel_id=1, source_target_pairs={{0,1},{1,0},{2,3},{3,2},{4,5},{5,4},{6,7},{7,6},{8,9},{9,8},{10,11... | collective-permute-start | bytes 442376 | tf_op jit(solution)/shard_map/ppermute | solution.py:73
  23.9 3.5 %collective-permute-done.5.note = bf16[208,768]{1,0:T(8,128)(2,1)S(1)} collective-permute-done((bf16[208,768]{1,0:T(8,128)(2,1)S(1)}, bf16[208,768]{1,0:T(8,128)(2,1)S(1)}, u32[]{:S(2)}, u32[]{:S(2)}) %collective-permute-start.5) | collective-permute-done | bytes 319520 | tf_op jit(solution)/shard_map/ppermute | solution.py:594
  27.4 3.2 %shard_map.156 = (f32[192,640]{1,0:T(8,128)S(1)}, f32[1,640]{1,0:T(1,128)S(1)}, bf16[768,640]{1,0:T(8,128)(2,1)S(1)}, f32[192,64]{1,0:T(8,128)S(1)}, bf16[12,112...) custom-call(s32[16]{0:T(128)S(1)} %concatenate.3.meta, ...), custom_call_target="tpu_custom_call" | custom-call | flops 1000000000 | bytes 10000000 | tf_op jit(solution)/shard_map/pallas_call | solution.py:90
  31.5 2.1 %collective-permute-start.9 = (bf16[3,192,128]{2,1,0:T(8,128)(2,1)S(1)}, bf16[3,192,128]{2,1,0:T(8,128)(2,1)S(1)}, u32[]{:S(2)}, u32[]{:S(2)}) collective-permute-start(bf16[3,192,128]{2,1,0:T(8,128)(2,1)S(1)} %get-tuple-element.87), channel_id=1, source_target_pairs={{0,1},{1,0},{2,3},{3,2},{4,5},{5,4},{6,7},{7,6},{8,9},{9,8},{10,11... | collective-permute-start | bytes 442376 | tf_op jit(solution)/shard_map/ppermute | solution.py:73
  33.6 2.4 %collective-permute-done.8.outer = bf16[3,192,128]{2,1,0:T(8,128)(2,1)S(1)} collective-permute-done((bf16[3,192,128]{2,1,0:T(8,128)(2,1)S(1)}, bf16[3,192,128]{2,1,0:T(8,128)(2,1)S(1)}, u32[]{:S(2)}, u32[]{:S(2)}) %collective-permute-start.8) | collective-permute-done | bytes 147488 | tf_op jit(solution)/shard_map/ppermute | solution.py:78
  36.6 5.0 %collective-permute-start.10 = (bf16[5,192,128]{2,1,0:T(8,128)(2,1)S(1)}, bf16[5,192,128]{2,1,0:T(8,128)(2,1)S(1)}, u32[]{:S(2)}, u32[]{:S(2)}) collective-permute-start(bf16[5,192,128]{2,1,0:T(8,128)(2,1)S(1)} %shard_map.158), channel_id=1, source_target_pairs={{0,192},{192,0},{64,128},{128,64},{1,193},{193,1},{65,129},{129,65... | collective-permute-start | bytes 737288 | tf_op jit(solution)/shard_map/ppermute | solution.py:644
  41.6 3.6 %collective-permute-done.10.cot.turn_cot = bf16[5,192,128]{2,1,0:T(8,128)(2,1)S(1)} collective-permute-done((bf16[5,192,128]{2,1,0:T(8,128)(2,1)S(1)}, bf16[5,192,128]{2,1,0:T(8,128)(2,1)S(1)}, u32[]{:S(2)}, u32[]{:S(2)}) %collective-permute-start.10) | collective-permute-done | bytes 245792 | tf_op jit(solution)/shard_map/ppermute | solution.py:644
  45.2 1.5 %shard_map.159 = (bf16[5,192,128]{2,1,0:T(8,128)(2,1)S(1)}, bf16[3,192,128]{2,1,0:T(8,128)(2,1)S(1)}, bf16[3,192,128]{2,1,0:T(8,128)(2,1)S(1)}) custom-call(s32[16]{0:T(128)S(1)} %concatenate.3.meta, bf16[5,192,128]{2,1,0:T(8,128)(2,1)S(1)} %collective-permute-done.10.cot.turn_cot, f32[192,64]{1,0:T(8,128)S(1)} %get-tuple-element.78.cols, ...), custom_call_target="tpu_custom_call" | custom-call | flops 1000000000 | bytes 6000000 | tf_op jit(solution)/shard_map/pallas_call | solution.py:90
  46.7 1.6 %collective-permute-start.12 = (bf16[3,192,128]{2,1,0:T(8,128)(2,1)S(1)}, bf16[3,192,128]{2,1,0:T(8,128)(2,1)S(1)}, u32[]{:S(2)}, u32[]{:S(2)}) collective-permute-start(bf16[3,192,128]{2,1,0:T(8,128)(2,1)S(1)} %get-tuple-element.90), channel_id=1, source_target_pairs={{0,63},{1,2},{2,1},{3,4},{4,3},{5,6},{6,5},{7,8},{8,7},{9,10},{10,... | collective-permute-start | bytes 442376 | tf_op jit(solution)/shard_map/ppermute | solution.py:78
  48.3 4.4 %collective-permute-start.13 = (bf16[3,192,128]{2,1,0:T(8,128)(2,1)S(1)}, bf16[3,192,128]{2,1,0:T(8,128)(2,1)S(1)}, u32[]{:S(2)}, u32[]{:S(2)}) collective-permute-start(bf16[3,192,128]{2,1,0:T(8,128)(2,1)S(1)} %get-tuple-element.91), channel_id=1, source_target_pairs={{0,1},{1,0},{2,3},{3,2},{4,5},{5,4},{6,7},{7,6},{8,9},{9,8},{10,11... | collective-permute-start | bytes 442376 | tf_op jit(solution)/shard_map/ppermute | solution.py:73
  53.7 4.0 %shard_map.160 = (bf16[5,192,128]{2,1,0:T(8,128)(2,1)S(1)}, bf16[5,192,128]{2,1,0:T(8,128)(2,1)S(1)}, bf16[3,192,128]{2,1,0:T(8,128)(2,1)S(1)}, bf16[3,192,128]{...) custom-call(s32[16]{0:T(128)S(1)} %concatenate.3.meta, ...), custom_call_target="tpu_custom_call" | custom-call | tf_op jit(solution)/shard_map/pallas_call | solution.py:90
  57.9 6.3 %collective-permute-start.15 = (bf16[104,768]{1,0:T(8,128)(2,1)S(1)}, bf16[104,768]{1,0:T(8,128)(2,1)S(1)}, u32[]{:S(2)}, u32[]{:S(2)}) collective-permute-start(bf16[104,768]{1,0:T(8,128)(2,1)S(1)} %get-tuple-element.95), channel_id=1, source_target_pairs={{0,1},{1,0},{2,3},{3,2},{4,5},{5,4},{6,7},{7,6},{8,9},{9,8},{10,11... | collective-permute-start | bytes 479240 | tf_op jit(solution)/shard_map/ppermute | solution.py:69
  64.2 1.5 %collective-permute-start.16 = (bf16[104,768]{1,0:T(8,128)(2,1)S(1)}, bf16[104,768]{1,0:T(8,128)(2,1)S(1)}, u32[]{:S(2)}, u32[]{:S(2)}) collective-permute-start(bf16[104,768]{1,0:T(8,128)(2,1)S(1)} %get-tuple-element.96), channel_id=1, source_target_pairs={{0,9},{1,2},{2,11},{3,0},{4,13},{5,6},{6,15},{7,4},{8,1},{9,10},{1... | collective-permute-start | bytes 479240 | tf_op jit(solution)/shard_map/ppermute | solution.py:69
  65.7 3.5 %collective-permute-done.16 = bf16[104,768]{1,0:T(8,128)(2,1)S(1)} collective-permute-done((bf16[104,768]{1,0:T(8,128)(2,1)S(1)}, bf16[104,768]{1,0:T(8,128)(2,1)S(1)}, u32[]{:S(2)}, u32[]{:S(2)}) %collective-permute-start.16) | collective-permute-done | bytes 159776 | tf_op jit(solution)/shard_map/ppermute | solution.py:69
  69.4 1.6 %collective-permute-start.18 = (bf16[3,192,128]{2,1,0:T(8,128)(2,1)S(1)}, bf16[3,192,128]{2,1,0:T(8,128)(2,1)S(1)}, u32[]{:S(2)}, u32[]{:S(2)}) collective-permute-start(bf16[3,192,128]{2,1,0:T(8,128)(2,1)S(1)} %get-tuple-element.100), channel_id=1, source_target_pairs={{0,63},{1,2},{2,1},{3,4},{4,3},{5,6},{6,5},{7,8},{8,7},{9,10},{10,... | collective-permute-start | bytes 442376 | tf_op jit(solution)/shard_map/ppermute | solution.py:78
  71.0 5.7 %collective-permute-done.17 = bf16[104,768]{1,0:T(8,128)(2,1)S(1)} collective-permute-done((bf16[104,768]{1,0:T(8,128)(2,1)S(1)}, bf16[104,768]{1,0:T(8,128)(2,1)S(1)}, u32[]{:S(2)}, u32[]{:S(2)}) %collective-permute-start.17) | collective-permute-done | bytes 159776 | tf_op jit(solution)/shard_map/ppermute | solution.py:69
  76.8 2.3 %collective-permute-start.20 = (bf16[3,192,128]{2,1,0:T(8,128)(2,1)S(1)}, bf16[3,192,128]{2,1,0:T(8,128)(2,1)S(1)}, u32[]{:S(2)}, u32[]{:S(2)}) collective-permute-start(bf16[3,192,128]{2,1,0:T(8,128)(2,1)S(1)} %get-tuple-element.102), channel_id=1, source_target_pairs={{0,1},{1,0},{2,3},{3,2},{4,5},{5,4},{6,7},{7,6},{8,9},{9,8},{10,11... | collective-permute-start | bytes 442376 | tf_op jit(solution)/shard_map/ppermute | solution.py:73
  79.2 3.0 %collective-permute-done.19 = bf16[104,768]{1,0:T(8,128)(2,1)S(1)} collective-permute-done((bf16[104,768]{1,0:T(8,128)(2,1)S(1)}, bf16[104,768]{1,0:T(8,128)(2,1)S(1)}, u32[]{:S(2)}, u32[]{:S(2)}) %collective-permute-start.19) | collective-permute-done | bytes 159776 | tf_op jit(solution)/shard_map/ppermute | solution.py:69
  82.2 2.1 %collective-permute-start.21 = (bf16[104,768]{1,0:T(8,128)(2,1)S(1)}, bf16[104,768]{1,0:T(8,128)(2,1)S(1)}, u32[]{:S(2)}, u32[]{:S(2)}) collective-permute-start(bf16[104,768]{1,0:T(8,128)(2,1)S(1)} %add_convert_fusion.2), channel_id=1, source_target_pairs={{0,24},{1,3},{2,26},{3,1},{4,28},{5,7},{6,30},{7,5},{8,16},{9,11},... | collective-permute-start | bytes 479240 | tf_op jit(solution)/shard_map/ppermute | solution.py:69
  84.3 1.7 %shard_map.161 = (bf16[5,192,128]{2,1,0:T(8,128)(2,1)S(1)}, bf16[2,192,128]{2,1,0:T(8,128)(2,1)S(1)}) custom-call(s32[16]{0:T(128)S(1)} %concatenate.3.meta, bf16[5,192,128]{2,1,0:T(8,128)(2,1)S(1)} %get-tuple-element.104.field, bf16[3,192,128]{2,1,0:T(8,128)(2,1)S(1)} %collective-permute-done.20.inner, ...), custom_call_target="tpu_custom_call" | custom-call | tf_op jit(solution)/shard_map/pallas_call | solution.py:90
  87.0 4.7 %collective-permute-start.23 = (bf16[104,768]{1,0:T(8,128)(2,1)S(1)}, bf16[104,768]{1,0:T(8,128)(2,1)S(1)}, u32[]{:S(2)}, u32[]{:S(2)}) collective-permute-start(bf16[104,768]{1,0:T(8,128)(2,1)S(1)} %add_convert_fusion.1), channel_id=1, source_target_pairs={{0,56},{1,7},{2,58},{3,5},{4,60},{5,3},{6,62},{7,1},{8,48},{9,15},... | collective-permute-start | bytes 479240 | tf_op jit(solution)/shard_map/ppermute | solution.py:69
  91.8 2.7 %collective-permute-done.23 = bf16[104,768]{1,0:T(8,128)(2,1)S(1)} collective-permute-done((bf16[104,768]{1,0:T(8,128)(2,1)S(1)}, bf16[104,768]{1,0:T(8,128)(2,1)S(1)}, u32[]{:S(2)}, u32[]{:S(2)}) %collective-permute-start.23) | collective-permute-done | bytes 159776 | tf_op jit(solution)/shard_map/ppermute | solution.py:69
  94.5 3.5 %collective-permute-start.26 = (bf16[104,768]{1,0:T(8,128)(2,1)S(1)}, bf16[104,768]{1,0:T(8,128)(2,1)S(1)}, u32[]{:S(2)}, u32[]{:S(2)}) collective-permute-start(bf16[104,768]{1,0:T(8,128)(2,1)S(1)} %add_convert_fusion.keep), channel_id=1, source_target_pairs={{0,3},{1,8},{2,1},{3,10},{4,7},{5,12},{6,5},{7,14},{8,11},{9,0},{1... | collective-permute-start | bytes 479240 | tf_op jit(solution)/shard_map/ppermute | solution.py:69
  98.7 1.3 %collective-permute-start.24 = (bf16[104,768]{1,0:T(8,128)(2,1)S(1)}, bf16[104,768]{1,0:T(8,128)(2,1)S(1)}, u32[]{:S(2)}, u32[]{:S(2)}) collective-permute-start(bf16[104,768]{1,0:T(8,128)(2,1)S(1)} %add_convert_fusion.keep), channel_id=1, source_target_pairs={{0,2},{1,9},{2,0},{3,11},{4,6},{5,13},{6,4},{7,15},{8,10},{9,1},{1... | collective-permute-start | bytes 479240 | tf_op jit(solution)/shard_map/ppermute | solution.py:69
  100.5 2.7 %collective-permute-done.22.arrived = bf16[2,192,128]{2,1,0:T(8,128)(2,1)S(1)} collective-permute-done((bf16[2,192,128]{2,1,0:T(8,128)(2,1)S(1)}, bf16[2,192,128]{2,1,0:T(8,128)(2,1)S(1)}, u32[]{:S(2)}, u32[]{:S(2)}) %collective-permute-start.22) | collective-permute-done | bytes 98336 | tf_op jit(solution)/shard_map/ppermute | solution.py:689
  103.1 1.3 %shard_map.162 = bf16[3,192,128]{2,1,0:T(8,128)(2,1)} custom-call(s32[16]{0:T(128)S(1)} %concatenate.3.meta, bf16[5,192,128]{2,1,0:T(8,128)(2,1)S(1)} %get-tuple-element.110.result, bf16[2,192,128]{2,1,0:T(8,128)(2,1)S(1)} %collective-permute-done.22.arrived), custom_call_target="tpu_custom_call" | custom-call | tf_op jit(solution)/shard_map/pallas_call | solution.py:90
  104.7 1.8 %shard_map.163 = (f32[49,1,192]{2,1,0:T(1,128)}, f32[1,192]{1,0:T(1,128)}, f32[1,192,768]{2,1,0:T(8,128)}, f32[1,768]{1,0:T(1,128)}, f32[1,192,768]{2,1,0:T(8,128)}, /*index=5*/f32[1,192]{1,0:T(1,128)}) custom-call(s32[16]{0:T(128)S(1)} %concatenate.3.meta, bf16[104,768]{1,0:T(8,128)(2,1)S(1)} %add_convert_fusion.keep, ...), custom_call_target="tpu_custom_call" | custom-call | tf_op jit(solution)/shard_map/pallas_call | solution.py:90
  (62 shorter events, 10.3 us)
Async XLA Ops:
  0.6 10.2 %copy-start.1 = (bf16[1,192,768]{2,1,0:T(8,128)(2,1)S(1)}, bf16[1,192,768]{2,1,0:T(8,128)(2,1)}, u32[]{:S(2)}) copy-start(bf16[1,192,768]{2,1,0:T(8,128)(2,1)} %param.16) | copy-start | bytes 884740
  0.7 10.2 %copy-start.2 = (bf16[1,192,768]{2,1,0:T(8,128)(2,1)S(1)}, bf16[1,192,768]{2,1,0:T(8,128)(2,1)}, u32[]{:S(2)}) copy-start(bf16[1,192,768]{2,1,0:T(8,128)(2,1)} %param.18) | copy-start | bytes 884740
  1.7 13.4 %collective-permute-start.2 = (bf16[3,192,128]{2,1,0:T(8,128)(2,1)S(1)}, bf16[3,192,128]{2,1,0:T(8,128)(2,1)S(1)}, u32[]{:S(2)}, u32[]{:S(2)}) collective-permute-start(bf16[3,192,128]{2,1,0:T(8,128)(2,1)S(1)} %get-tuple-element.119), channel_id=1, source_target_pairs={{0,63},{1,2},{2,1},{3,4},{4,3},{5,6},{6,5},{7,8},{8,7},{9,10},{10,... | collective-permute-start | bytes 442376 | tf_op jit(solution)/shard_map/ppermute | solution.py:78
  4.4 10.8 %collective-permute-start.1 = (bf16[3,192,128]{2,1,0:T(8,128)(2,1)S(1)}, bf16[3,192,128]{2,1,0:T(8,128)(2,1)S(1)}, u32[]{:S(2)}, u32[]{:S(2)}) collective-permute-start(bf16[3,192,128]{2,1,0:T(8,128)(2,1)S(1)} %get-tuple-element.120), channel_id=1, source_target_pairs={{0,1},{1,0},{2,3},{3,2},{4,5},{5,4},{6,7},{7,6},{8,9},{9,8},{10,11... | collective-permute-start | bytes 442376 | tf_op jit(solution)/shard_map/ppermute | solution.py:73
  10.9 8.7 %collective-permute-start = (bf16[192,768]{1,0:T(8,128)(2,1)S(1)}, bf16[192,768]{1,0:T(8,128)(2,1)S(1)}, u32[]{:S(2)}, u32[]{:S(2)}) collective-permute-start(bf16[192,768]{1,0:T(8,128)(2,1)S(1)} %broadcast_select_fusion), channel_id=1, source_target_pairs={{0,64},{64,0},{128,192},{192,128},{1,65},{65,1},{129,193},{193,129... | collective-permute-start | bytes 884744 | tf_op jit(solution)/shard_map/ppermute | solution.py:581
  12.2 0.8 copy-start.7
  14.5 0.9 copy-start
  15.5 3.3 %copy-start.3 = (bf16[5,192,128]{2,1,0:T(8,128)(2,1)S(1)}, bf16[5,192,128]{2,1,0:T(8,128)(2,1)}, u32[]{:S(2)}) copy-start(bf16[5,192,128]{2,1,0:T(8,128)(2,1)} %cot_top.1) | copy-start | bytes 737284
  18.5 8.9 %collective-permute-start.5 = (bf16[208,768]{1,0:T(8,128)(2,1)S(1)}, bf16[208,768]{1,0:T(8,128)(2,1)S(1)}, u32[]{:S(2)}, u32[]{:S(2)}) collective-permute-start(bf16[208,768]{1,0:T(8,128)(2,1)S(1)} %get-tuple-element.76), channel_id=1, source_target_pairs={{0,64},{64,0},{128,192},{192,128},{1,65},{65,1},{129,193},{193,129... | collective-permute-start | bytes 958472 | tf_op jit(solution)/shard_map/ppermute | solution.py:594
  19.6 7.8 %collective-permute-start.6 = (bf16[192,768]{1,0:T(8,128)(2,1)S(1)}, bf16[192,768]{1,0:T(8,128)(2,1)S(1)}, u32[]{:S(2)}, u32[]{:S(2)}) collective-permute-start(bf16[192,768]{1,0:T(8,128)(2,1)S(1)} %collective-permute-done.half), channel_id=1, source_target_pairs={{0,1},{1,0},{2,3},{3,2},{4,5},{5,4},{6,7},{7,6},{8,9},{9,8},{10,11... | collective-permute-start | bytes 884744 | tf_op jit(solution)/shard_map/ppermute | solution.py:69
  20.4 10.3 %collective-permute-start.3 = (bf16[3,192,128]{2,1,0:T(8,128)(2,1)S(1)}, bf16[3,192,128]{2,1,0:T(8,128)(2,1)S(1)}, u32[]{:S(2)}, u32[]{:S(2)}) collective-permute-start(bf16[3,192,128]{2,1,0:T(8,128)(2,1)S(1)} %get-tuple-element.73), channel_id=1, source_target_pairs={{0,63},{1,2},{2,1},{3,4},{4,3},{5,6},{6,5},{7,8},{8,7},{9,10},{10,... | collective-permute-start | bytes 442376 | tf_op jit(solution)/shard_map/ppermute | solution.py:78
  20.4 10.3 %collective-permute-start.4 = (bf16[3,192,128]{2,1,0:T(8,128)(2,1)S(1)}, bf16[3,192,128]{2,1,0:T(8,128)(2,1)S(1)}, u32[]{:S(2)}, u32[]{:S(2)}) collective-permute-start(bf16[3,192,128]{2,1,0:T(8,128)(2,1)S(1)} %get-tuple-element.74), channel_id=1, source_target_pairs={{0,1},{1,0},{2,3},{3,2},{4,5},{5,4},{6,7},{7,6},{8,9},{9,8},{10,11... | collective-permute-start | bytes 442376 | tf_op jit(solution)/shard_map/ppermute | solution.py:73
  31.2 4.8 %collective-permute-start.8 = (bf16[3,192,128]{2,1,0:T(8,128)(2,1)S(1)}, bf16[3,192,128]{2,1,0:T(8,128)(2,1)S(1)}, u32[]{:S(2)}, u32[]{:S(2)}) collective-permute-start(bf16[3,192,128]{2,1,0:T(8,128)(2,1)S(1)} %get-tuple-element.86), channel_id=1, source_target_pairs={{0,63},{1,2},{2,1},{3,4},{4,3},{5,6},{6,5},{7,8},{8,7},{9,10},{10,... | collective-permute-start | bytes 442376 | tf_op jit(solution)/shard_map/ppermute | solution.py:78
  31.5 4.6 %collective-permute-start.9 = (bf16[3,192,128]{2,1,0:T(8,128)(2,1)S(1)}, bf16[3,192,128]{2,1,0:T(8,128)(2,1)S(1)}, u32[]{:S(2)}, u32[]{:S(2)}) collective-permute-start(bf16[3,192,128]{2,1,0:T(8,128)(2,1)S(1)} %get-tuple-element.87), channel_id=1, source_target_pairs={{0,1},{1,0},{2,3},{3,2},{4,5},{5,4},{6,7},{7,6},{8,9},{9,8},{10,11... | collective-permute-start | bytes 442376 | tf_op jit(solution)/shard_map/ppermute | solution.py:73
  36.6 8.6 %collective-permute-start.10 = (bf16[5,192,128]{2,1,0:T(8,128)(2,1)S(1)}, bf16[5,192,128]{2,1,0:T(8,128)(2,1)S(1)}, u32[]{:S(2)}, u32[]{:S(2)}) collective-permute-start(bf16[5,192,128]{2,1,0:T(8,128)(2,1)S(1)} %shard_map.158), channel_id=1, source_target_pairs={{0,192},{192,0},{64,128},{128,64},{1,193},{193,1},{65,129},{129,65... | collective-permute-start | bytes 737288 | tf_op jit(solution)/shard_map/ppermute | solution.py:644
  41.6 11.1 %collective-permute-start.7 = (bf16[5,192,128]{2,1,0:T(8,128)(2,1)S(1)}, bf16[5,192,128]{2,1,0:T(8,128)(2,1)S(1)}, u32[]{:S(2)}, u32[]{:S(2)}) collective-permute-start(bf16[5,192,128]{2,1,0:T(8,128)(2,1)S(1)} %get-tuple-element.84.cot), channel_id=1, source_target_pairs={{0,64},{64,0},{128,192},{192,128},{1,65},{65,1},{129,193},{193,129... | collective-permute-start | bytes 737288 | tf_op jit(solution)/shard_map/ppermute | solution.py:635
  45.2 8.5 %collective-permute-start.11 = (bf16[5,192,128]{2,1,0:T(8,128)(2,1)S(1)}, bf16[5,192,128]{2,1,0:T(8,128)(2,1)S(1)}, u32[]{:S(2)}, u32[]{:S(2)}) collective-permute-start(bf16[5,192,128]{2,1,0:T(8,128)(2,1)S(1)} %collective-permute-done.10.cot.turn_cot), channel_id=1, source_target_pairs={{0,64},{64,0},{128,192},{192,128},{1,65},{65,1},{129,193},{193,129... | collective-permute-start | bytes 737288 | tf_op jit(solution)/shard_map/ppermute | solution.py:645
  46.7 6.0 %collective-permute-start.12 = (bf16[3,192,128]{2,1,0:T(8,128)(2,1)S(1)}, bf16[3,192,128]{2,1,0:T(8,128)(2,1)S(1)}, u32[]{:S(2)}, u32[]{:S(2)}) collective-permute-start(bf16[3,192,128]{2,1,0:T(8,128)(2,1)S(1)} %get-tuple-element.90), channel_id=1, source_target_pairs={{0,63},{1,2},{2,1},{3,4},{4,3},{5,6},{6,5},{7,8},{8,7},{9,10},{10,... | collective-permute-start | bytes 442376 | tf_op jit(solution)/shard_map/ppermute | solution.py:78
  48.3 5.4 %collective-permute-start.13 = (bf16[3,192,128]{2,1,0:T(8,128)(2,1)S(1)}, bf16[3,192,128]{2,1,0:T(8,128)(2,1)S(1)}, u32[]{:S(2)}, u32[]{:S(2)}) collective-permute-start(bf16[3,192,128]{2,1,0:T(8,128)(2,1)S(1)} %get-tuple-element.91), channel_id=1, source_target_pairs={{0,1},{1,0},{2,3},{3,2},{4,5},{5,4},{6,7},{7,6},{8,9},{9,8},{10,11... | collective-permute-start | bytes 442376 | tf_op jit(solution)/shard_map/ppermute | solution.py:73
  57.8 8.0 %collective-permute-start.14 = (bf16[104,768]{1,0:T(8,128)(2,1)S(1)}, bf16[104,768]{1,0:T(8,128)(2,1)S(1)}, u32[]{:S(2)}, u32[]{:S(2)}) collective-permute-start(bf16[104,768]{1,0:T(8,128)(2,1)S(1)} %get-tuple-element.94), channel_id=1, source_target_pairs={{0,2},{1,9},{2,0},{3,11},{4,6},{5,13},{6,4},{7,15},{8,10},{9,1},{1... | collective-permute-start | bytes 479240 | tf_op jit(solution)/shard_map/ppermute | solution.py:69
  57.9 7.9 %collective-permute-start.15 = (bf16[104,768]{1,0:T(8,128)(2,1)S(1)}, bf16[104,768]{1,0:T(8,128)(2,1)S(1)}, u32[]{:S(2)}, u32[]{:S(2)}) collective-permute-start(bf16[104,768]{1,0:T(8,128)(2,1)S(1)} %get-tuple-element.95), channel_id=1, source_target_pairs={{0,1},{1,0},{2,3},{3,2},{4,5},{5,4},{6,7},{7,6},{8,9},{9,8},{10,11... | collective-permute-start | bytes 479240 | tf_op jit(solution)/shard_map/ppermute | solution.py:69
  64.2 5.0 %collective-permute-start.16 = (bf16[104,768]{1,0:T(8,128)(2,1)S(1)}, bf16[104,768]{1,0:T(8,128)(2,1)S(1)}, u32[]{:S(2)}, u32[]{:S(2)}) collective-permute-start(bf16[104,768]{1,0:T(8,128)(2,1)S(1)} %get-tuple-element.96), channel_id=1, source_target_pairs={{0,9},{1,2},{2,11},{3,0},{4,13},{5,6},{6,15},{7,4},{8,1},{9,10},{1... | collective-permute-start | bytes 479240 | tf_op jit(solution)/shard_map/ppermute | solution.py:69
  69.3 7.4 %collective-permute-start.17 = (bf16[104,768]{1,0:T(8,128)(2,1)S(1)}, bf16[104,768]{1,0:T(8,128)(2,1)S(1)}, u32[]{:S(2)}, u32[]{:S(2)}) collective-permute-start(bf16[104,768]{1,0:T(8,128)(2,1)S(1)} %add_convert_fusion.4), channel_id=1, source_target_pairs={{0,6},{1,25},{2,4},{3,27},{4,2},{5,29},{6,0},{7,31},{8,14},{9,17},... | collective-permute-start | bytes 479240 | tf_op jit(solution)/shard_map/ppermute | solution.py:69
  69.4 7.3 %collective-permute-start.18 = (bf16[3,192,128]{2,1,0:T(8,128)(2,1)S(1)}, bf16[3,192,128]{2,1,0:T(8,128)(2,1)S(1)}, u32[]{:S(2)}, u32[]{:S(2)}) collective-permute-start(bf16[3,192,128]{2,1,0:T(8,128)(2,1)S(1)} %get-tuple-element.100), channel_id=1, source_target_pairs={{0,63},{1,2},{2,1},{3,4},{4,3},{5,6},{6,5},{7,8},{8,7},{9,10},{10,... | collective-permute-start | bytes 442376 | tf_op jit(solution)/shard_map/ppermute | solution.py:78
  76.7 5.4 %collective-permute-start.19 = (bf16[104,768]{1,0:T(8,128)(2,1)S(1)}, bf16[104,768]{1,0:T(8,128)(2,1)S(1)}, u32[]{:S(2)}, u32[]{:S(2)}) collective-permute-start(bf16[104,768]{1,0:T(8,128)(2,1)S(1)} %add_convert_fusion.3), channel_id=1, source_target_pairs={{0,8},{1,57},{2,10},{3,59},{4,12},{5,61},{6,14},{7,63},{8,0},{9,49... | collective-permute-start | bytes 479240 | tf_op jit(solution)/shard_map/ppermute | solution.py:69
  76.8 5.4 %collective-permute-start.20 = (bf16[3,192,128]{2,1,0:T(8,128)(2,1)S(1)}, bf16[3,192,128]{2,1,0:T(8,128)(2,1)S(1)}, u32[]{:S(2)}, u32[]{:S(2)}) collective-permute-start(bf16[3,192,128]{2,1,0:T(8,128)(2,1)S(1)} %get-tuple-element.102), channel_id=1, source_target_pairs={{0,1},{1,0},{2,3},{3,2},{4,5},{5,4},{6,7},{7,6},{8,9},{9,8},{10,11... | collective-permute-start | bytes 442376 | tf_op jit(solution)/shard_map/ppermute | solution.py:73
  82.2 4.8 %collective-permute-start.21 = (bf16[104,768]{1,0:T(8,128)(2,1)S(1)}, bf16[104,768]{1,0:T(8,128)(2,1)S(1)}, u32[]{:S(2)}, u32[]{:S(2)}) collective-permute-start(bf16[104,768]{1,0:T(8,128)(2,1)S(1)} %add_convert_fusion.2), channel_id=1, source_target_pairs={{0,24},{1,3},{2,26},{3,1},{4,28},{5,7},{6,30},{7,5},{8,16},{9,11},... | collective-permute-start | bytes 479240 | tf_op jit(solution)/shard_map/ppermute | solution.py:69
  87.0 7.4 %collective-permute-start.23 = (bf16[104,768]{1,0:T(8,128)(2,1)S(1)}, bf16[104,768]{1,0:T(8,128)(2,1)S(1)}, u32[]{:S(2)}, u32[]{:S(2)}) collective-permute-start(bf16[104,768]{1,0:T(8,128)(2,1)S(1)} %add_convert_fusion.1), channel_id=1, source_target_pairs={{0,56},{1,7},{2,58},{3,5},{4,60},{5,3},{6,62},{7,1},{8,48},{9,15},... | collective-permute-start | bytes 479240 | tf_op jit(solution)/shard_map/ppermute | solution.py:69
  94.5 10.0 %collective-permute-start.26 = (bf16[104,768]{1,0:T(8,128)(2,1)S(1)}, bf16[104,768]{1,0:T(8,128)(2,1)S(1)}, u32[]{:S(2)}, u32[]{:S(2)}) collective-permute-start(bf16[104,768]{1,0:T(8,128)(2,1)S(1)} %add_convert_fusion.keep), channel_id=1, source_target_pairs={{0,3},{1,8},{2,1},{3,10},{4,7},{5,12},{6,5},{7,14},{8,11},{9,0},{1... | collective-permute-start | bytes 479240 | tf_op jit(solution)/shard_map/ppermute | solution.py:69
  98.0 6.5 %collective-permute-start.25 = (bf16[104,768]{1,0:T(8,128)(2,1)S(1)}, bf16[104,768]{1,0:T(8,128)(2,1)S(1)}, u32[]{:S(2)}, u32[]{:S(2)}) collective-permute-start(bf16[104,768]{1,0:T(8,128)(2,1)S(1)} %add_convert_fusion.keep), channel_id=1, source_target_pairs={{0,1},{1,0},{2,3},{3,2},{4,5},{5,4},{6,7},{7,6},{8,9},{9,8},{10,11... | collective-permute-start | bytes 479240 | tf_op jit(solution)/shard_map/ppermute | solution.py:69
  98.7 5.9 %collective-permute-start.24 = (bf16[104,768]{1,0:T(8,128)(2,1)S(1)}, bf16[104,768]{1,0:T(8,128)(2,1)S(1)}, u32[]{:S(2)}, u32[]{:S(2)}) collective-permute-start(bf16[104,768]{1,0:T(8,128)(2,1)S(1)} %add_convert_fusion.keep), channel_id=1, source_target_pairs={{0,2},{1,9},{2,0},{3,11},{4,6},{5,13},{6,4},{7,15},{8,10},{9,1},{1... | collective-permute-start | bytes 479240 | tf_op jit(solution)/shard_map/ppermute | solution.py:69
  100.0 3.2 %collective-permute-start.22 = (bf16[2,192,128]{2,1,0:T(8,128)(2,1)S(1)}, bf16[2,192,128]{2,1,0:T(8,128)(2,1)S(1)}, u32[]{:S(2)}, u32[]{:S(2)}) collective-permute-start(bf16[2,192,128]{2,1,0:T(8,128)(2,1)S(1)} %get-tuple-element.111), channel_id=1, source_target_pairs={{0,1},{1,2},{2,3},{3,4},{4,5},{5,6},{6,7},{7,8},{8,9},{9,10},{10,1... | collective-permute-start | bytes 294920 | tf_op jit(solution)/shard_map/ppermute | solution.py:689
  (5 other events, 3.5 us)
